TPU v7x, 32 devices: a whole 2x2x4 slice. The times are simulated.
32 devices in a mesh: dp: 16 (over z, y, x), rep: 2 (over core).
Axes of the slice: x: 2, y: 2, z: 4, core: 2. Of those that a mesh axis runs over, the one named last changes fastest.
Arguments:
- query_tokens: bfloat16 [512, 32, 768], P(('dp', 'rep')), may hold values from -6 to 6
- passage_tokens: bfloat16 [128, 128, 768], P(('dp', 'rep')), may hold values from -6 to 6
- query_cot: bfloat16 [512, 32, 768], P(('dp', 'rep')), may hold values from -6 to 6
- passage_cot: bfloat16 [128, 128, 768], P(('dp', 'rep')), may hold values from -6 to 6
- positives: int32 [512, 128], P(('dp', 'rep')), may hold values from 0 to 1, as said below
- w_qkv: bfloat16 [2, 768, 2304], P(None, 'dp'), may hold values from -0.21875 to 0.21875
- w_out: bfloat16 [2, 768, 768], P(None, 'dp'), may hold values from -0.625 to 0.625
- w_up: bfloat16 [2, 768, 3072], P(None, 'dp'), may hold values from -0.21875 to 0.21875
- w_down: bfloat16 [2, 3072, 768], P(None, 'dp'), may hold values from -0.109375 to 0.109375
- biases: bfloat16 [2, 10, 768], P(None, None, 'dp'), may hold values from -3 to 3
- gains: bfloat16 [2, 2, 768], P(None, None, 'dp'), may hold values from 0.5 to 1.5
Outputs:
- query_out: bfloat16 [512, 32, 768], P(('dp', 'rep'))
- passage_out: bfloat16 [128, 128, 768], P(('dp', 'rep'))
- query_grad: float32 [512, 32, 768], P(('dp', 'rep'))
- passage_grad: float32 [128, 128, 768], P(('dp', 'rep'))
- query_loss: float32 [512], P(('dp', 'rep'))
- grad_qkv: float32 [2, 768, 2304], P(None, 'dp')
- grad_out: float32 [2, 768, 768], P(None, 'dp')
- grad_up: float32 [2, 768, 3072], P(None, 'dp')
- grad_down: float32 [2, 3072, 768], P(None, 'dp')
- grad_biases: float32 [2, 10, 768], P(None, None, 'dp')
- grad_gains: float32 [2, 2, 768], P(None, None, 'dp')
Inputs may be any that keep to these rules, and one draw needn't show every extreme that they name: `positives`: each query has one to three positive passages; some query has three and some one.
All inputs are finite; a program needn't handle non-finite values.
Results may differ from a plain program's by a relative error of at most 0.015.
Values may be sent and summed in bfloat16 or wider, within the bound.
No kernel may reach another device: no remote copies, remote signals or barrier semaphores. Data moves between devices by JAX's collectives and lax.ppermute only.
A program may use at most 256 MiB of HBM per device.

v0:
```python
from functools import partial

import jax
import jax.numpy as jnp
from jax import lax
from jax.sharding import PartitionSpec as P

D = 768
HEADS = 12
HEAD = 64


eps = 1e-05
loss_weight = 32.0


def rows_norm(h, gain, shift):
    center = h - jnp.mean(h, -1, keepdims=True)
    spread = jnp.mean(center * center, -1, keepdims=True)
    return center * lax.rsqrt(spread + eps) * gain + shift


def inner(left, right):
    return lax.dot_general(
        left, right, (((0,), (0,)), ((), ())), preferred_element_type=jnp.float32
    )


def times_t(left, right):
    return lax.dot_general(
        left, right, (((1,), (1,)), ((), ())), preferred_element_type=jnp.float32
    )


def tower_args(weights, tower):
    return (
        weights[0][tower],
        weights[1][tower],
        weights[2][tower],
        weights[3][tower],
        weights[4][tower].astype(jnp.float32),
        weights[5][tower].astype(jnp.float32),
    )


def tower_forward(tokens, weights):
    wqkv, wout, wup, wdown, vecs, gns = weights
    count, length, width = tokens.shape
    flat = tokens.reshape(count * length, width)
    zeros = jnp.zeros((width,), jnp.float32)
    proj = jnp.dot(flat, wqkv, preferred_element_type=jnp.float32) + jnp.concatenate(
        [vecs[0], zeros, vecs[1]]
    )
    proj_b = proj.astype(jnp.bfloat16)
    parts = proj_b.reshape(count, length, 3, HEADS, HEAD)
    scores = jnp.einsum(
        "slhd,smhd->shlm", parts[:, :, 0], parts[:, :, 1], preferred_element_type=jnp.float32
    ) * HEAD ** (-0.5)
    top = jnp.max(scores, -1, keepdims=True)
    lse = top + jnp.log(jnp.sum(jnp.exp(scores - top), -1, keepdims=True))
    probs_b = jnp.exp(scores - lse).astype(jnp.bfloat16)
    attn = jnp.einsum(
        "shlm,smhd->slhd", probs_b, parts[:, :, 2], preferred_element_type=jnp.float32
    )
    attn_b = attn.reshape(count * length, width).astype(jnp.bfloat16)
    hidden = flat.astype(jnp.float32) + (
        jnp.dot(attn_b, wout, preferred_element_type=jnp.float32) + vecs[2]
    )
    normed = rows_norm(hidden, gns[0], vecs[3])
    normed_b = normed.astype(jnp.bfloat16)
    upper = jnp.dot(normed_b, wup, preferred_element_type=jnp.float32) + vecs[4:8].reshape(-1)
    active_b = jax.nn.gelu(upper, approximate=False).astype(jnp.bfloat16)
    second = normed + (jnp.dot(active_b, wdown, preferred_element_type=jnp.float32) + vecs[8])
    result = rows_norm(second, gns[1], vecs[9])
    saved = (flat, proj_b, lse, attn_b, hidden, normed_b, upper, active_b, second)
    return (result.reshape(count, length, width).astype(jnp.bfloat16), saved)


def tower_backward(grad_out, saved, weights):
    wqkv, wout, wup, wdown, vecs, gns = weights
    flat, proj_b, lse, attn_b, hidden, normed_b, upper, active_b, second = saved
    rows, width = flat.shape
    count = lse.shape[0]
    length = lse.shape[2]
    unused, pull_two = jax.vjp(rows_norm, second, gns[1], vecs[9])
    grad_second, gain_two, shift_two = pull_two(grad_out)
    grad_down_b = grad_second.astype(jnp.bfloat16)
    grad_wdown = inner(active_b, grad_down_b)
    grad_active = times_t(grad_down_b, wdown)
    unused, pull_gelu = jax.vjp(partial(jax.nn.gelu, approximate=False), upper)
    grad_upper_b = pull_gelu(grad_active)[0].astype(jnp.bfloat16)
    grad_wup = inner(normed_b, grad_upper_b)
    grad_normed = times_t(grad_upper_b, wup) + grad_second
    unused, pull_one = jax.vjp(rows_norm, hidden, gns[0], vecs[3])
    grad_hidden, gain_one, shift_one = pull_one(grad_normed)
    grad_proj_out = grad_hidden.astype(jnp.bfloat16)
    grad_wout = inner(attn_b, grad_proj_out)
    grad_attn_b = (
        times_t(grad_proj_out, wout).astype(jnp.bfloat16).reshape(count, length, HEADS, HEAD)
    )
    parts = proj_b.reshape(count, length, 3, HEADS, HEAD)
    query, keys, values = (parts[:, :, 0], parts[:, :, 1], parts[:, :, 2])
    factor = HEAD ** (-0.5)
    scores = jnp.einsum("slhd,smhd->shlm", query, keys, preferred_element_type=jnp.float32) * factor
    probs = jnp.exp(scores - lse)
    grad_probs = jnp.einsum(
        "slhd,smhd->shlm", grad_attn_b, values, preferred_element_type=jnp.float32
    )
    grad_values = jnp.einsum(
        "shlm,slhd->smhd",
        probs.astype(jnp.bfloat16),
        grad_attn_b,
        preferred_element_type=jnp.float32,
    )
    grad_scores = (probs * (grad_probs - jnp.sum(probs * grad_probs, -1, keepdims=True))).astype(
        jnp.bfloat16
    )
    grad_query = (
        jnp.einsum("shlm,smhd->slhd", grad_scores, keys, preferred_element_type=jnp.float32)
        * factor
    )
    grad_keys = (
        jnp.einsum("shlm,slhd->smhd", grad_scores, query, preferred_element_type=jnp.float32)
        * factor
    )
    grad_proj = (
        jnp.stack([grad_query, grad_keys, grad_values], 2)
        .reshape(rows, 3 * width)
        .astype(jnp.bfloat16)
    )
    grad_wqkv = inner(flat, grad_proj)
    grad_tokens = times_t(grad_proj, wqkv) + grad_hidden
    column_sums = jnp.sum(grad_proj, 0, dtype=jnp.float32)
    vectors = jnp.concatenate(
        [
            column_sums[:width][None],
            column_sums[2 * width :][None],
            jnp.sum(grad_proj_out, 0, dtype=jnp.float32)[None],
            shift_one[None],
            jnp.sum(grad_upper_b, 0, dtype=jnp.float32).reshape(4, width),
            jnp.sum(grad_down_b, 0, dtype=jnp.float32)[None],
            shift_two[None],
        ],
        0,
    )
    gain_grads = jnp.stack([gain_one, gain_two])
    return (
        grad_tokens.reshape(count, length, width),
        (grad_wqkv, grad_wout, grad_wup, grad_wdown, vectors, gain_grads),
    )


def on_device(
    query_tokens,
    passage_tokens,
    query_cot,
    passage_cot,
    positives,
    w_qkv,
    w_out,
    w_up,
    w_down,
    biases,
    gains,
):
    whole = (
        lax.all_gather(w_qkv, "dp", axis=1, tiled=True),
        lax.all_gather(w_out, "dp", axis=1, tiled=True),
        lax.all_gather(w_up, "dp", axis=1, tiled=True),
        lax.all_gather(w_down, "dp", axis=1, tiled=True),
        lax.all_gather(biases, "dp", axis=2, tiled=True),
        lax.all_gather(gains, "dp", axis=2, tiled=True),
    )
    query_out, query_saved = tower_forward(query_tokens, tower_args(whole, 0))
    passage_out, passage_saved = tower_forward(passage_tokens, tower_args(whole, 1))
    factor = D ** (-0.5)
    cls_query = query_out[:, 0, :]
    cls_all = lax.all_gather(passage_out[:, 0, :], ("dp", "rep"), axis=0, tiled=True)
    raw = times_t(cls_query, cls_all) * factor
    top = jnp.max(raw, -1, keepdims=True)
    expd = jnp.exp(raw - top)
    marks = positives.astype(jnp.float32)
    total = jnp.sum(expd, -1, keepdims=True)
    marked = jnp.sum(marks * expd, -1, keepdims=True)
    query_loss = (jnp.log(total) - jnp.log(marked))[:, 0]
    grad_raw = (loss_weight * (expd / total - marks * expd / marked)).astype(jnp.bfloat16)
    grad_query_cls = jnp.dot(grad_raw, cls_all, preferred_element_type=jnp.float32) * factor
    grad_passage_cls = lax.psum_scatter(
        inner(grad_raw, cls_query) * factor, ("dp", "rep"), scatter_dimension=0, tiled=True
    )
    query_dout = query_cot.astype(jnp.float32).at[:, 0, :].add(grad_query_cls)
    passage_dout = passage_cot.astype(jnp.float32).at[:, 0, :].add(grad_passage_cls)
    backing = (
        lax.all_gather(w_qkv, "dp", axis=1, tiled=True),
        lax.all_gather(w_out, "dp", axis=1, tiled=True),
        lax.all_gather(w_up, "dp", axis=1, tiled=True),
        lax.all_gather(w_down, "dp", axis=1, tiled=True),
        lax.all_gather(biases, "dp", axis=2, tiled=True),
        lax.all_gather(gains, "dp", axis=2, tiled=True),
    )
    query_grad, query_terms = tower_backward(
        query_dout.reshape(-1, query_dout.shape[2]), query_saved, tower_args(backing, 0)
    )
    passage_grad, passage_terms = tower_backward(
        passage_dout.reshape(-1, passage_dout.shape[2]), passage_saved, tower_args(backing, 1)
    )
    term_qkv = jnp.stack([query_terms[0], passage_terms[0]])
    term_out = jnp.stack([query_terms[1], passage_terms[1]])
    term_up = jnp.stack([query_terms[2], passage_terms[2]])
    term_down = jnp.stack([query_terms[3], passage_terms[3]])
    term_vecs = jnp.stack([query_terms[4], passage_terms[4]])
    term_gains = jnp.stack([query_terms[5], passage_terms[5]])
    owned = (
        lax.psum_scatter(term_qkv, "dp", scatter_dimension=1, tiled=True),
        lax.psum_scatter(term_out, "dp", scatter_dimension=1, tiled=True),
        lax.psum_scatter(term_up, "dp", scatter_dimension=1, tiled=True),
        lax.psum_scatter(term_down, "dp", scatter_dimension=1, tiled=True),
        lax.psum_scatter(term_vecs, "dp", scatter_dimension=2, tiled=True),
        lax.psum_scatter(term_gains, "dp", scatter_dimension=2, tiled=True),
    )
    shares = (
        lax.psum_scatter(
            owned[0].astype(jnp.bfloat16), "rep", scatter_dimension=1, tiled=True
        ).astype(jnp.float32),
        lax.psum_scatter(
            owned[1].astype(jnp.bfloat16), "rep", scatter_dimension=1, tiled=True
        ).astype(jnp.float32),
        lax.psum_scatter(
            owned[2].astype(jnp.bfloat16), "rep", scatter_dimension=1, tiled=True
        ).astype(jnp.float32),
        lax.psum_scatter(
            owned[3].astype(jnp.bfloat16), "rep", scatter_dimension=1, tiled=True
        ).astype(jnp.float32),
        lax.psum_scatter(
            owned[4].astype(jnp.bfloat16), "rep", scatter_dimension=2, tiled=True
        ).astype(jnp.float32),
        lax.psum_scatter(
            owned[5].astype(jnp.bfloat16), "rep", scatter_dimension=2, tiled=True
        ).astype(jnp.float32),
    )
    summed = (
        lax.all_gather(shares[0].astype(jnp.bfloat16), "rep", axis=1, tiled=True).astype(
            jnp.float32
        ),
        lax.all_gather(shares[1].astype(jnp.bfloat16), "rep", axis=1, tiled=True).astype(
            jnp.float32
        ),
        lax.all_gather(shares[2].astype(jnp.bfloat16), "rep", axis=1, tiled=True).astype(
            jnp.float32
        ),
        lax.all_gather(shares[3].astype(jnp.bfloat16), "rep", axis=1, tiled=True).astype(
            jnp.float32
        ),
        lax.all_gather(shares[4].astype(jnp.bfloat16), "rep", axis=2, tiled=True).astype(
            jnp.float32
        ),
        lax.all_gather(shares[5].astype(jnp.bfloat16), "rep", axis=2, tiled=True).astype(
            jnp.float32
        ),
    )
    return (
        query_out,
        passage_out,
        query_grad,
        passage_grad,
        query_loss,
        summed[0],
        summed[1],
        summed[2],
        summed[3],
        summed[4],
        summed[5],
    )


def solution(mesh):
    return jax.shard_map(
        on_device,
        mesh=mesh,
        in_specs=(
            P(("dp", "rep"), None, None),
            P(("dp", "rep"), None, None),
            P(("dp", "rep"), None, None),
            P(("dp", "rep"), None, None),
            P(("dp", "rep"), None),
            P(None, "dp", None),
            P(None, "dp", None),
            P(None, "dp", None),
            P(None, "dp", None),
            P(None, None, "dp"),
            P(None, None, "dp"),
        ),
        out_specs=(
            P(("dp", "rep"), None, None),
            P(("dp", "rep"), None, None),
            P(("dp", "rep"), None, None),
            P(("dp", "rep"), None, None),
            P(("dp", "rep")),
            P(None, "dp", None),
            P(None, "dp", None),
            P(None, "dp", None),
            P(None, "dp", None),
            P(None, None, "dp"),
            P(None, None, "dp"),
        ),
        check_vma=False,
    )
```

profile of v0, /device:TPU:0, one launch (start us, length us, event | category | flops | bytes accessed | tf_op | source)
XLA Modules:
  0.0 1985.0 jit_solution(9746100989549643098)
XLA Ops:
  11.6 46.4 %all_gather.45 = bf16[2,10,768]{1,0,2:T(2,128)(2,1)S(1)} all-gather(bf16[2,10,48]{1,0,2:T(2,128)(2,1)S(1)} %copy.108), channel_id=1, replica_groups=mesh['dp'=16,'rep'=2] {'dp'}, dimensions={2}, use_global_device_ids=true | all-gather | bytes 32640 | tf_op jit(solution)/shard_map/all_gather | solution.py:171
  60.9 41.6 %all_gather.47 = bf16[2,2,768]{1,0,2:T(2,128)(2,1)S(1)} all-gather(bf16[2,2,48]{1,0,2:T(2,128)(2,1)S(1)} %copy.114), channel_id=1, replica_groups=mesh['dp'=16,'rep'=2] {'dp'}, dimensions={2}, use_global_device_ids=true | all-gather | bytes 6528 | tf_op jit(solution)/shard_map/all_gather | solution.py:172
  102.5 12.8 slice_reduce_fusion
  115.3 13.0 slice_reduce_fusion.8
  128.9 4.6 slice_reduce_fusion.1
  133.5 4.6 slice_reduce_fusion.9
  141.5 4.3 fusion.13
  148.2 4.4 reshape.377
  159.2 3.4 fusion.12
  162.5 8.2 reshape.375
  170.7 4.8 fusion.90
  189.9 119.7 %all-gather.10.cloned.1.call-done = bf16[2,768,3072]{2,1,0:T(8,128)(2,1)} async-done(((bf16[2,48,3072]{2,1,0:T(8,128)(2,1)}), bf16[2,768,3072]{2,1,0:T(8,128)(2,1)}) %all-gather.10.cloned.1.call-update) | async-done | bytes 9437200 | tf_op jit(solution)/shard_map/all_gather | solution.py:169
  309.6 19.9 %multiply_convert_fusion.1 = (bf16[512,3072]{1,0:T(8,128)(2,1)}, f32[512,3072]{1,0:T(8,128)}, f32[512,3072]{1,0:T(8,128)}) fusion(f32[3072]{0:T(1024)S(1)} %add.251, bf16[2,768,3072]{2,1,0:T(8,128)(2,1)} %all-gather.10.cloned.1.call-done, f32[512,768]{1,0:T(8,128)S(1)} %get-tuple-element.152, f32[768]{0:T(1024)S(1)} %get-tuple-element.101, ...), kind=kOutput, calls=%fused_computation.25 | convolution fusion | flops 2521694208 | bytes 22042624 | tf_op jit(solution)/shard_map/dot_general | solution.py:71
  329.5 103.2 %all-gather.12.cloned.1.call-done = bf16[2,3072,768]{2,1,0:T(8,128)(2,1)} async-done(((bf16[2,192,768]{2,1,0:T(8,128)(2,1)}), bf16[2,3072,768]{2,1,0:T(8,128)(2,1)}) %all-gather.12.cloned.1.call-update) | async-done | bytes 9437200 | tf_op jit(solution)/shard_map/all_gather | solution.py:170
  432.8 6.6 fusion.95
  441.1 18.8 multiply_convert_fusion
  460.0 5.2 fusion.97
  466.8 39.7 %all-gather = bf16[128,1,768]{2,1,0:T(2,128)(2,1)S(1)} all-gather(bf16[4,1,768]{2,1,0:T(2,128)(2,1)S(1)} %slice.294), channel_id=2, replica_groups=mesh['dp'=16,'rep'=2] {'dp','rep'}, dimensions={0}, use_global_device_ids=true | all-gather | bytes 202752 | tf_op jit(solution)/shard_map/all_gather | solution.py:178
  517.2 8.8 convert_reduce_fusion.2
  526.1 7.6 multiply_reduce_fusion.5
  533.7 105.0 %all-reduce.10.cloned.1.call-done = f32[128,768]{1,0:T(8,128)} async-done(((f32[128,768]{1,0:T(8,128)}), f32[128,768]{1,0:T(8,128)}) %all-reduce.10.cloned.1.call-update) | async-done | bytes 393232
  641.4 9.2 convert_reduce_fusion.1
  650.7 3.1 multiply_reduce_fusion.4
  662.3 5.4 convolution_bitcast_fusion.5
  670.6 7.0 pad_maximum_fusion
  678.8 4.8 convolution_bitcast_fusion.3
  686.3 6.9 pad_maximum_fusion.1
  700.9 3.4 convolution_convert_fusion.3
  704.3 3.8 reshape.380
  708.1 3.7 multiply_reduce_fusion.1
  717.5 3.5 convert_reduce_fusion
  728.7 3.7 copy.138
  732.3 7.2 copy.129
  739.5 7.5 convert_element_type.262
  747.1 6.6 convolution_bitcast_fusion
  753.6 5.0 convolution_bitcast_fusion.1
  758.6 11.5 pad_maximum_fusion.2
  770.1 21.8 %copy.139 = f32[2,768,2304]{2,0,1:T(2,128)} copy(f32[2,768,2304]{1,2,0:T(8,128)} %pad_maximum_fusion.2) | data formatting | bytes 28311552 | tf_op jit(solution)/shard_map/stack | solution.py:207
  791.9 724.7 %all-reduce.13 = bf16[2,768,2304]{2,0,1:T(2,128)(2,1)} all-reduce(f32[2,768,2304]{2,0,1:T(2,128)} %copy.139), channel_id=4, replica_groups=mesh['dp'=16,'rep'=2] {'dp'}, use_global_device_ids=true, to_apply=%region_26.0.clone | all-reduce | flops 3538944 | bytes 21233664
  1527.4 6.6 add_add_fusion.8
  1534.0 133.3 %reduce-scatter.23.cloned.1.call-done = f32[2,192,768]{2,1,0:T(8,128)} async-done(((f32[2,3072,768]{2,1,0:T(8,128)}), f32[2,192,768]{2,1,0:T(8,128)}) %reduce-scatter.23.cloned.1.call-update) | async-done | bytes 1179664 | tf_op jit(solution)/shard_map/reduce_scatter | solution.py:217
  1669.5 5.6 add_add_fusion.10
  1675.2 117.7 %reduce-scatter.33.cloned.1.call-done = f32[48,4]{1,0:T(8,128)} async-done(((f32[768,4]{1,0:T(8,128)}), f32[48,4]{1,0:T(8,128)}) %reduce-scatter.33.cloned.1.call-update) | async-done | bytes 784
  1793.8 125.3 %reduce-scatter.31.cloned.1.call-done = f32[48,20]{1,0:T(8,128)} async-done(((f32[768,20]{1,0:T(8,128)}), f32[48,20]{1,0:T(8,128)}) %reduce-scatter.31.cloned.1.call-update) | async-done | bytes 3856
  1927.9 11.9 all-reduce.12.cloned.1.call-done
  1943.9 7.3 reduce-scatter.27.cloned.1.call-done
  1954.8 8.6 reduce-scatter.29.cloned.1.call-done
  1968.0 6.8 reduce-scatter.25.cloned.1.call-done
  (413 shorter events, 123.5 us)
Async XLA Ops:
  7.2 134.3 %all-gather.6.cloned.1.call-start = ((), (), s32[]{:S(2)}) async-start(), calls=%async_computation.8 | async-start | bytes 7520256 | tf_op jit(solution)/shard_map/all_gather | solution.py:167
  7.9 177.7 %all-gather.8.cloned.1.call-start = ((), (), s32[]{:S(2)}) async-start(), calls=%async_computation.9 | async-start | bytes 2506752 | tf_op jit(solution)/shard_map/all_gather | solution.py:168
  8.7 300.9 %all-gather.10.cloned.1.call-start = ((), (), s32[]{:S(2)}) async-start(), calls=%async_computation.10 | async-start | bytes 10027008 | tf_op jit(solution)/shard_map/all_gather | solution.py:169
  9.4 423.4 %all-gather.12.cloned.1.call-start = ((), (), s32[]{:S(2)}) async-start(), calls=%async_computation.11 | async-start | bytes 10027008 | tf_op jit(solution)/shard_map/all_gather | solution.py:170
  10.0 628.7 %all-reduce.10.cloned.1.call-start = ((), (), s32[]{:S(2)}) async-start(), calls=%async_computation.20 | async-start | bytes 786432
  59.7 381.3 %copy-start.74 = (f32[3072]{0:T(1024)}, f32[3072]{0:T(1024)S(1)}, u32[]{:S(2)}) copy-start(f32[3072]{0:T(1024)S(1)} %add.273) | copy-start | bytes 36868
  60.9 248.7 %copy-start.76 = (f32[3072]{0:T(1024)}, f32[3072]{0:T(1024)S(1)}, u32[]{:S(2)}) copy-start(f32[3072]{0:T(1024)S(1)} %add.251) | copy-start | bytes 36868
  115.3 344.6 %copy-start.83 = (f32[768]{0:T(1024)}, f32[768]{0:T(1024)S(1)}, u32[]{:S(2)}) copy-start(f32[768]{0:T(1024)S(1)} %get-tuple-element.93) | copy-start | bytes 9220
  115.3 22.8 %copy-start.40 = (bf16[16,32,768]{2,1,0:T(8,128)(2,1)S(1)}, bf16[16,32,768]{2,1,0:T(8,128)(2,1)}, u32[]{:S(2)}) copy-start(bf16[16,32,768]{2,1,0:T(8,128)(2,1)} %param.17) | copy-start | bytes 2359300
  128.3 304.5 %copy-start.85 = (f32[768]{0:T(1024)}, f32[768]{0:T(1024)S(1)}, u32[]{:S(2)}) copy-start(f32[768]{0:T(1024)S(1)} %get-tuple-element.101) | copy-start | bytes 9220
  128.3 11.4 copy-start.41
  133.5 326.5 %copy-start.70 = (f32[768]{0:T(1024)}, f32[768]{0:T(1024)S(1)}, u32[]{:S(2)}) copy-start(f32[768]{0:T(1024)S(1)} %get-tuple-element.90) | copy-start | bytes 9220
  138.1 294.7 %copy-start.72 = (f32[768]{0:T(1024)}, f32[768]{0:T(1024)S(1)}, u32[]{:S(2)}) copy-start(f32[768]{0:T(1024)S(1)} %get-tuple-element.98) | copy-start | bytes 9220
  157.1 28.6 %copy-start.28 = (bf16[4,128,12,64]{1,0,3,2:T(4,128)(2,1)}, bf16[4,128,12,64]{1,0,3,2:T(4,128)(2,1)S(1)}, u32[]{:S(2)}) copy-start(bf16[4,128,12,64]{1,0,3,2:T(4,128)(2,1)S(1)} %copy.121) | copy-start | bytes 2359300
  188.2 252.8 %copy-start.19 = (f32[512,768]{1,0:T(8,128)}, f32[512,768]{1,0:T(8,128)S(1)}, u32[]{:S(2)}) copy-start(f32[512,768]{1,0:T(8,128)S(1)} %get-tuple-element.159) | copy-start | bytes 4718596
  188.3 271.7 %copy-start.66 = (f32[512]{0:T(512)}, f32[512]{0:T(512)S(1)}, u32[]{:S(2)}) copy-start(f32[512]{0:T(512)S(1)} %broadcast_multiply_fusion.1) | copy-start | bytes 6148
  189.5 140.1 %copy-start.21 = (f32[512,768]{1,0:T(8,128)}, f32[512,768]{1,0:T(8,128)S(1)}, u32[]{:S(2)}) copy-start(f32[512,768]{1,0:T(8,128)S(1)} %get-tuple-element.152) | copy-start | bytes 4718596
  189.5 243.3 %copy-start.68 = (f32[512]{0:T(512)}, f32[512]{0:T(512)S(1)}, u32[]{:S(2)}) copy-start(f32[512]{0:T(512)S(1)} %broadcast_multiply_fusion.3) | copy-start | bytes 6148
  189.8 139.7 %copy-start.60 = (f32[512]{0:T(512)}, f32[512]{0:T(512)S(1)}, u32[]{:S(2)}) copy-start(f32[512]{0:T(512)S(1)} %multiply_reduce_fusion.13) | copy-start | bytes 6148
  189.8 270.1 %copy-start.78 = (f32[512]{0:T(512)}, f32[512]{0:T(512)S(1)}, u32[]{:S(2)}) copy-start(f32[512]{0:T(512)S(1)} %fusion.74) | copy-start | bytes 6148
  189.9 242.9 %copy-start.80 = (f32[512]{0:T(512)}, f32[512]{0:T(512)S(1)}, u32[]{:S(2)}) copy-start(f32[512]{0:T(512)S(1)} %fusion.72) | copy-start | bytes 6148
  439.4 20.4 %copy-start.51 = (f32[512]{0:T(512)}, f32[512]{0:T(512)S(1)}, u32[]{:S(2)}) copy-start(f32[512]{0:T(512)S(1)} %broadcast_multiply_fusion.2) | copy-start | bytes 6148
  439.7 20.1 %copy-start.64 = (f32[512]{0:T(512)}, f32[512]{0:T(512)S(1)}, u32[]{:S(2)}) copy-start(f32[512]{0:T(512)S(1)} %multiply_reduce_fusion.12) | copy-start | bytes 6148
  439.8 20.1 %copy-start.56 = (f32[512]{0:T(512)}, f32[512]{0:T(512)S(1)}, u32[]{:S(2)}) copy-start(f32[512]{0:T(512)S(1)} %fusion.73) | copy-start | bytes 6148
  439.8 20.2 %slice-start.6 = ((s8[9437184]{0:T(1024)(128)(4,1)}), s8[4194304]{0:T(1024)(128)(4,1)S(1)}, s32[]{:S(2)}) async-start(s8[9437184]{0:T(1024)(128)(4,1)} %bitcast.306), calls=%async_computation.28 | async-start | bytes 8388608
  441.1 18.9 slice-start.7
  441.1 18.9 slice-start.8
  465.2 41.6 %copy-start.53 = (s32[16,128]{1,0:T(8,128)S(1)}, s32[16,128]{1,0:T(8,128)}, u32[]{:S(2)}) copy-start(s32[16,128]{1,0:T(8,128)} %param.19) | copy-start | bytes 24580
  515.0 1005.7 %reduce-scatter.19.cloned.1.call-start = ((), (), s32[]{:S(2)}) async-start(), calls=%async_computation.12 | async-start | bytes 5013504 | tf_op jit(solution)/shard_map/reduce_scatter | solution.py:215
  526.1 112.6 %copy-start.4 = (f32[4,128,768]{2,0,1:T(4,128)S(1)}, f32[4,128,768]{2,0,1:T(4,128)}, u32[]{:S(2)}) copy-start(f32[4,128,768]{2,0,1:T(4,128)} %copy_convert_fusion) | copy-start | bytes 4718596
  533.6 106.2 %copy-start.50 = (f32[512]{0:T(512)S(1)}, f32[512]{0:T(512)}, u32[]{:S(2)}) copy-start(f32[512]{0:T(512)} %copy-done.49) | copy-start | bytes 6148
  533.6 106.2 %copy-start.55 = (f32[512]{0:T(512)S(1)}, f32[512]{0:T(512)}, u32[]{:S(2)}) copy-start(f32[512]{0:T(512)} %copy-done.54) | copy-start | bytes 6148
  640.5 10.1 slice-start.3
  641.3 9.3 copy-start.47
  641.3 9.3 copy-start.20
  641.4 9.3 copy-start.67
  641.4 9.3 copy-start.71
  641.4 9.3 copy-start.79
  641.4 9.3 slice-start.4
  641.4 9.3 slice-start.5
  661.7 861.0 %reduce-scatter.21.cloned.1.call-start = ((), (), s32[]{:S(2)}) async-start(), calls=%async_computation.13 | async-start | bytes 20054016 | tf_op jit(solution)/shard_map/reduce_scatter | solution.py:216
  677.7 989.7 %reduce-scatter.23.cloned.1.call-start = ((), (), s32[]{:S(2)}) async-start(), calls=%async_computation.14 | async-start | bytes 20054016 | tf_op jit(solution)/shard_map/reduce_scatter | solution.py:217
  693.3 1099.6 %reduce-scatter.33.cloned.1.call-start = ((), (), s32[]{:S(2)}) async-start(), calls=%async_computation.19 | async-start | bytes 417792
  1516.6 402.5 %reduce-scatter.31.cloned.1.call-start = ((), (), s32[]{:S(2)}) async-start(), calls=%async_computation.18 | async-start | bytes 417792
  1518.5 421.3 %all-reduce.12.cloned.1.call-start = ((), (), s32[]{:S(2)}) async-start(), calls=%async_computation.21 | async-start | bytes 884736
  1520.7 430.5 %reduce-scatter.27.cloned.1.call-start = ((), (), s32[]{:S(2)}) async-start(), calls=%async_computation.16 | async-start | bytes 221184
  1522.6 440.8 %reduce-scatter.29.cloned.1.call-start = ((), (), s32[]{:S(2)}) async-start(), calls=%async_computation.17 | async-start | bytes 884736
  1525.6 449.2 %reduce-scatter.25.cloned.1.call-start = ((), (), s32[]{:S(2)}) async-start(), calls=%async_computation.15 | async-start | bytes 884736 | tf_op jit(solution)/shard_map/reduce_scatter | solution.py:231
  (77 other events, 274.5 us)
Sparse Core Ops, SparseCore 0:
  10.7 109.5 all-gather.5
  123.0 62.5 all-gather.7
  188.3 121.2 all-gather.9
  312.1 120.5 all-gather.11
  515.2 123.5 all-reduce.9
  661.8 136.4 reduce-scatter.18
  804.1 478.9 reduce-scatter.20
  1288.8 378.4 reduce-scatter.22
  1672.0 120.8 reduce-scatter.32
  1798.6 120.4 reduce-scatter.30
  1922.0 17.6 all-reduce.11
  1942.5 8.6 reduce-scatter.26
  1954.2 9.2 reduce-scatter.28
  1965.5 9.1 reduce-scatter.24
where the time goes:
time: 1990 us; the launch traced here: 1980 us
  blocking collectives  867 us (44%)
  waiting for transfers between devices  744 us (37%)
  matrix products  154 us (8%)
  local copies, waits for them, and re-layouts  141 us (7%)
  other arithmetic  59 us (3%)
    unnamed x2, blocking collectives  727 us
    unnamed x20, waiting for transfers between devices  379 us
    reduce_scatter x1, waiting for transfers between devices, on_device(): lax.psum_scatter(term_down, 'dp', scatter_dimension=1, tiled=True)  133 us
    all_gather x1, waiting for transfers between devices, on_device(): lax.all_gather(w_up, 'dp', axis=1, tiled=True)  120 us
    all_gather x1, waiting for transfers between devices, on_device(): lax.all_gather(w_down, 'dp', axis=1, tiled=True)  103 us
    dot_general x9, matrix products, times_t(): lax.dot_general(left, right, (((1,), (1,)), ((), ())), preferred_element_...  46.6 us
    all_gather x1, blocking collectives, on_device(): lax.all_gather(biases, 'dp', axis=2, tiled=True)  46.4 us
    all_gather x1, blocking collectives, on_device(): lax.all_gather(gains, 'dp', axis=2, tiled=True)  41.6 us
  transfers between devices with their start and end apart: 14, of which 11 were waited for; matrix products, arithmetic and copies ran while one was open for 14% of the time, Pallas kernels for 0%

commit v1 on v0

v1 whole, which is shorter than its diff:
```python
from functools import partial

import jax
import jax.numpy as jnp
from jax import lax
from jax.experimental import pallas as pl
from jax.experimental.pallas import tpu as pltpu
from jax.sharding import PartitionSpec as P

AXES = ("dp", "rep")
BF = jnp.bfloat16
F32 = jnp.float32
D = 768
FF = 3072
HEADS = 12
HEAD = 64
PAIRS = HEADS // 2
BLOCK = 128
TILE = 256
EPS = 1e-05
LOSS_WEIGHT = 32.0
MIB = 2**20
AT_OUT = 3 * D
AT_VEC = 4 * D
W_ONE = 4 * D + 256


def smem():
    return pl.BlockSpec(memory_space=pltpu.SMEM)


def vmem():
    return pl.BlockSpec(memory_space=pltpu.VMEM)


def params(mib):
    return pltpu.CompilerParams(vmem_limit_bytes=mib * MIB)


def send(v, pairs):
    return lax.ppermute(v, AXES, pairs)


class Plan:
    def __init__(self, n, reps):
        self.n, self.reps, self.depth = n, reps, n // 4

    def pairs(self, move):
        return [
            (d * self.reps + r, (d ^ move(r)[0]) * self.reps + (r ^ move(r)[1]))
            for d in range(self.n)
            for r in range(self.reps)
        ]

    def along(self, k):
        return self.pairs(lambda r: (4 * k, 0))

    def first(self):
        return self.pairs(lambda r: (1 + r % 2, 0))

    def second(self):
        return self.pairs(lambda r: (2 - r % 2, 0))

    def sibling(self, q):
        return self.pairs(lambda r: (0, q))


def assemble_kernel(depth, reps, width, where_ref, *refs):
    nb = 4 * reps
    bufs, out = refs[:nb], refs[nb]
    me, core = where_ref[0], where_ref[1]
    for q in range(reps):
        owner = core ^ q
        p1 = 1 + owner % 2
        p2 = 2 - owner % 2
        lanes = pl.ds(pl.multiple_of(owner * width, 128), width)
        for b in range(4):
            flip = [0, p1, p2, 3][b]
            for k in range(depth):
                dst = (me ^ flip) ^ (4 * k)
                out[pl.ds(dst, 1), :, lanes] = bufs[q * 4 + b][pl.ds(k, 1)]


def gather_chunk(plan, where, shard):
    me, core, tower = where[0], where[1], where[2]
    rows, whole = shard.shape[1:]
    width = whole // plan.reps
    mine = lax.dynamic_slice(shard, (tower, 0, core * width), (1, rows, width))
    other = lax.dynamic_slice(shard, (1 - tower, 0, core * width), (1, rows, width))
    got = [mine] + [
        send(other if k % 2 else mine, plan.along(k)) for k in range(1, plan.depth)
    ]
    z = jnp.concatenate(got, 0)
    r1 = send(z, plan.first())
    r2 = send(z, plan.second())
    r3 = send(r1, plan.second())
    bufs = [z, r1, r2, r3]
    for q in range(1, plan.reps):
        bufs += [send(b, plan.sibling(q)) for b in (z, r1, r2, r3)]
    full = pl.pallas_call(
        partial(assemble_kernel, plan.depth, plan.reps, width),
        out_shape=jax.ShapeDtypeStruct((plan.n, rows, whole), BF),
        in_specs=[smem()] + [vmem()] * len(bufs),
        out_specs=vmem(),
        compiler_params=params(24),
        name="assemble",
    )(where, *bufs)
    return full.reshape(plan.n * rows, whole)


def add_kernel(n, wh, table_ref, a_ref, b_ref, s_ref, k_ref):
    lanes = pl.ds(pl.multiple_of(table_ref[n] * wh, 128), wh)
    for j in range(n):
        at = table_ref[j]
        total = a_ref[pl.ds(at, 1), :, lanes].astype(F32) + b_ref[pl.ds(at, 1)].astype(F32)
        o_ref, to = (s_ref, j) if j < n // 2 else (k_ref, j - n // 2)
        o_ref[pl.ds(to, 1)] = total.astype(BF)


def plus(a, b):
    return (a.astype(F32) + b.astype(F32)).astype(BF)


def scatter_chunk(plan, where, grad, rows):
    me, core, tower = where[0], where[1], where[2]
    n = plan.n
    whole = grad.shape[1]
    wh = whole // plan.reps
    g = grad.reshape(n, rows, whole)
    got = [
        send(lax.dynamic_slice_in_dim(g, (core ^ q) * wh, wh, 2), plan.sibling(q))
        for q in range(1, plan.reps)
    ]
    rest = got[0]
    for o in got[1:]:
        rest = plus(rest, o)
    p1 = 1 + core % 2
    p2 = 2 - core % 2
    idx = []
    for b1 in (1, 0):
        for b2 in (1, 0):
            for k in range(plan.depth):
                idx.append(me ^ (b1 * p1) ^ (b2 * p2) ^ (4 * k))
    table = jnp.stack(idx + [core]).astype(jnp.int32)
    half = jax.ShapeDtypeStruct((n // 2, rows, wh), BF)
    hs, hk = pl.pallas_call(
        partial(add_kernel, n, wh),
        out_shape=(half, half),
        in_specs=[smem(), vmem(), vmem()],
        out_specs=[vmem(), vmem()],
        compiler_params=params(24),
        name="pick_add",
    )(table, g, rest)
    r1 = send(hs, plan.first())
    q = n // 4
    ks = plus(hk[:q], r1[:q])
    r2 = send(ks, plan.second())
    kk = plus(hk[q:], r1[q:])
    k2 = [kk[k].astype(F32) + r2[k].astype(F32) for k in range(plan.depth)]
    own, oth = k2[0], None
    for k in range(1, plan.depth):
        s = send(k2[k].astype(BF), plan.along(k)).astype(F32)
        if k % 2:
            oth = s if oth is None else oth + s
        else:
            own = own + s
    pair = jnp.stack([own, oth]).astype(BF)
    pair = jnp.where(tower == 0, pair, pair[::-1])
    parts = [pair] + [send(pair, plan.sibling(q)) for q in range(1, plan.reps)]
    if plan.reps == 2:
        a, b = parts[0].astype(F32), parts[1].astype(F32)
        return jnp.where(core == 0, jnp.concatenate([a, b], 2), jnp.concatenate([b, a], 2))
    full = jnp.zeros((2, rows, whole), F32)
    for q, part in enumerate(parts):
        full = lax.dynamic_update_slice_in_dim(full, part.astype(F32), (core ^ q) * wh, 2)
    return full


def dot(a, b):
    return jnp.dot(a, b, preferred_element_type=F32)


def dot_t(a, b):
    return lax.dot_general(a, b, (((1,), (1,)), ((), ())), preferred_element_type=F32)


def t_dot(a, b):
    return lax.dot_general(a, b, (((0,), (0,)), ((), ())), preferred_element_type=F32)


def normalize(h):
    center = h - jnp.mean(h, -1, keepdims=True)
    rstd = lax.rsqrt(jnp.mean(center * center, -1, keepdims=True) + EPS)
    return center * rstd, rstd


def lane_masks():
    lane = lax.broadcasted_iota(jnp.int32, (1, 2 * HEAD), 1)
    low = (lane < HEAD).astype(F32).astype(BF)
    return low, (1.0 - low.astype(F32)).astype(BF)


def attend_kernel(
    where_ref, x_ref, w_ref, proj_ref, probs_ref, attn_ref, hat_ref, rstd_ref, norm_ref, vec_ref, bias_ref
):
    @pl.when(pl.program_id(0) == 0)
    def prepare():
        vec_ref[...] = jnp.transpose(w_ref[:, AT_VEC : AT_VEC + 128].astype(F32))
        span = where_ref[3]
        row = lax.broadcasted_iota(jnp.int32, (2 * BLOCK, BLOCK), 0) % BLOCK
        col = lax.broadcasted_iota(jnp.int32, (2 * BLOCK, BLOCK), 1)
        bias_ref[...] = jnp.where((row ^ col) < span, 0.0, -1e30)

    x = x_ref[...]
    for j in range(3):
        part = dot(x, w_ref[:, j * D : (j + 1) * D])
        if j != 1:
            part = part + vec_ref[j // 2 : j // 2 + 1, :]
        proj_ref[:, j * D : (j + 1) * D] = part.astype(BF)
    low, high = lane_masks()
    bias = bias_ref[...]
    for blk in range(TILE // BLOCK):
        rows = slice(blk * BLOCK, (blk + 1) * BLOCK)
        for pair in range(PAIRS):
            lanes = slice(pair * 128, (pair + 1) * 128)
            q = proj_ref[rows, lanes]
            k = proj_ref[rows, D + pair * 128 : D + (pair + 1) * 128]
            v = proj_ref[rows, 2 * D + pair * 128 : 2 * D + (pair + 1) * 128]
            s = dot_t(jnp.concatenate([q * low, q * high], 0), k) * HEAD**-0.5 + bias
            e = jnp.exp(s - jnp.max(s, -1, keepdims=True))
            p = (e * (1.0 / jnp.sum(e, -1, keepdims=True))).astype(BF)
            probs_ref[blk, pair] = p
            wide = jnp.concatenate([p[:BLOCK], p[BLOCK:]], 1)
            attn_ref[rows, lanes] = dot(wide, jnp.concatenate([v * low, v * high], 0)).astype(BF)
    hidden = x.astype(F32) + (dot(attn_ref[...], w_ref[:, AT_OUT:AT_VEC]) + vec_ref[2:3, :])
    hat, rstd = normalize(hidden)
    hat_ref[...] = hat
    rstd_ref[...] = rstd
    norm_ref[...] = (hat * vec_ref[10:11, :] + vec_ref[3:4, :]).astype(BF)


def row_block(width, rows=TILE):
    return pl.BlockSpec((rows, width), lambda i: (i, 0))


def whole_block(shape):
    return pl.BlockSpec(shape, lambda i: (0,) * len(shape))


def attend(where, x, w_one):
    rows = x.shape[0]
    shape = jax.ShapeDtypeStruct
    per = TILE // BLOCK
    return pl.pallas_call(
        attend_kernel,
        grid=(rows // TILE,),
        out_shape=(
            shape((rows, 3 * D), BF),
            shape((rows // BLOCK, PAIRS, 2 * BLOCK, BLOCK), BF),
            shape((rows, D), BF),
            shape((rows, D), F32),
            shape((rows, 1), F32),
            shape((rows, D), BF),
            shape((128, D), F32),
        ),
        in_specs=[smem(), row_block(D), whole_block(w_one.shape)],
        out_specs=[
            row_block(3 * D),
            pl.BlockSpec((per, PAIRS, 2 * BLOCK, BLOCK), lambda i: (i, 0, 0, 0)),
            row_block(D),
            row_block(D),
            row_block(1),
            row_block(D),
            whole_block((128, D)),
        ],
        scratch_shapes=[pltpu.VMEM((2 * BLOCK, BLOCK), F32)],
        compiler_params=params(48),
        name="attend",
    )(where, x, w_one)


def gelu_pair(u):
    t = 1.0 / (1.0 + (0.3275911 * 2**-0.5) * jnp.abs(u))
    e = jnp.exp(-0.5 * u * u)
    poly = t * (
        0.5 * 0.254829592
        + t * (0.5 * -0.284496736 + t * (0.5 * 1.421413741 + t * (0.5 * -1.453152027 + t * (0.5 * 1.061405429))))
    )
    tail = poly * e
    phi = jnp.where(u < 0, tail, 1.0 - tail)
    return u * phi, phi + u * (e * 0.3989422804014327)


def up_kernel(norm_ref, w_ref, vec_ref, act_ref, slope_ref):
    i = pl.program_id(0)
    bias = vec_ref[pl.ds(4 + i, 1), :]
    for m in range(norm_ref.shape[0] // TILE):
        rows = slice(m * TILE, (m + 1) * TILE)
        act, slope = gelu_pair(dot(norm_ref[rows, :], w_ref[...]) + bias)
        act_ref[rows, :] = act.astype(BF)
        slope_ref[rows, :] = slope.astype(BF)


def up(norm, w_up, vec):
    rows = norm.shape[0]
    wide = jax.ShapeDtypeStruct((rows, FF), BF)
    col = pl.BlockSpec((rows, D), lambda i: (0, i))
    return pl.pallas_call(
        up_kernel,
        grid=(FF // D,),
        out_shape=(wide, wide),
        in_specs=[whole_block(norm.shape), pl.BlockSpec((D, D), lambda i: (0, i)), whole_block(vec.shape)],
        out_specs=[col, col],
        compiler_params=params(48),
        name="up",
    )(norm, w_up, vec)


def down_kernel(act_ref, w_ref, hat_ref, vec_ref, out_ref, hat2_ref, rstd2_ref, cls_ref):
    normed = hat_ref[...] * vec_ref[10:11, :] + vec_ref[3:4, :]
    second = normed + (dot(act_ref[...], w_ref[...]) + vec_ref[8:9, :])
    hat, rstd = normalize(second)
    hat2_ref[...] = hat
    rstd2_ref[...] = rstd
    out = hat * vec_ref[11:12, :] + vec_ref[9:10, :]
    out_ref[...] = out.astype(BF)
    for j in range(TILE // 32):
        cls_ref[j : j + 1, :] = out[32 * j : 32 * j + 1, :]


def down(act, w_down, hat, vec):
    rows = act.shape[0]
    shape = jax.ShapeDtypeStruct
    return pl.pallas_call(
        down_kernel,
        grid=(rows // TILE,),
        out_shape=(shape((rows, D), BF), shape((rows, D), F32), shape((rows, 1), F32), shape((rows // 32, D), F32)),
        in_specs=[row_block(FF), whole_block(w_down.shape), row_block(D), whole_block(vec.shape)],
        out_specs=[row_block(D), row_block(D), row_block(1), row_block(D, TILE // 32)],
        compiler_params=params(48),
        name="down",
    )(act, w_down, hat, vec)


def contrast_kernel(reps, depth, per, where_ref, q_ref, p_ref, loss_ref, grad_ref, acc_ref):
    i = pl.program_id(0)
    me, core, tower = where_ref[0], where_ref[1], where_ref[2]
    pieces = p_ref.shape[0]
    total_p = pieces * per * 2
    cls_q = q_ref[:, :32, :D].reshape(-1, D)
    marks = q_ref[:, :32, D:].reshape(-1, q_ref.shape[2] - D)
    cls_p = p_ref[:, 32:, :D].reshape(-1, D)
    cols = cls_p.shape[0]
    col = lax.broadcasted_iota(jnp.int32, (marks.shape[1], cols), 1)
    row = lax.broadcasted_iota(jnp.int32, (marks.shape[1], cols), 0)
    j, slot = col // 16, col % 16
    line = j % (depth // 2)
    f1 = (j // (depth // 2)) % 2
    f2 = (j // depth) % 2
    flip_core = j // (2 * depth)
    from_core = core ^ flip_core
    p1, p2 = 1 + from_core % 2, 2 - from_core % 2
    base = (me | 4) ^ (8 * line) ^ (f1 * p1) ^ (f2 * p2)
    owner = jnp.where(slot < per, base, base ^ 4)
    passage = (owner * reps + from_core) * per + slot % per
    good = slot < 2 * per
    pick = jnp.where((row == passage) & good, 1.0, 0.0).astype(BF)
    marked_cols = dot(marks, pick)
    valid = lax.broadcasted_iota(jnp.int32, (1, cols), 1) % 16 < 2 * per
    raw = jnp.where(valid, dot_t(cls_q, cls_p) * D**-0.5, -1e30)
    e = jnp.exp(raw - jnp.max(raw, -1, keepdims=True))
    total = jnp.sum(e, -1, keepdims=True)
    me_ = marked_cols * e
    marked = jnp.sum(me_, -1, keepdims=True)
    grad = (LOSS_WEIGHT * (e / total - me_ / marked)).astype(BF)
    part = t_dot(grad[:, :128], cls_q) * D**-0.5

    @pl.when(i == 0)
    def first():
        loss_ref[...] = (jnp.log(total) - jnp.log(marked))[:32]
        acc_ref[...] = jnp.zeros_like(acc_ref)
        grad_ref[...] = dot(grad[:32], cls_p) * D**-0.5

    acc_ref[...] += part

    @pl.when((i == pl.num_programs(0) - 1) & (tower == 1))
    def last():
        grad_ref[...] = jnp.zeros_like(grad_ref)
        for s in range(2 * per):
            at = s * (32 // (2 * per))
            grad_ref[at : at + 1, :] = acc_ref[s : s + 1, :]


def contrast(plan, where, cls, positives):
    tower = where[2]
    queries, passages = positives.shape
    per = queries // 4
    msg = jnp.concatenate(
        [cls.astype(BF), jnp.pad(positives.astype(BF), ((0, 32 - queries), (0, 0)))], 1
    )
    back = send(msg, plan.along(1))
    q = jnp.where(tower == 0, msg[:, :D], back[:, :D])
    p = jnp.where(tower == 0, back[:, :D], msg[:, :D])[:: 32 // (2 * per)]
    m_own, m_far = msg[:queries, D:], back[:queries, D:]
    marks = jnp.concatenate([jnp.where(tower == 0, m_own, m_far), jnp.where(tower == 0, m_far, m_own)], 0)
    top = jnp.concatenate([q, marks], 1)
    low = jnp.pad(p, ((0, 16 - 2 * per), (0, passages)))
    buf = jnp.concatenate([top, low], 0)[None]
    buf = jnp.concatenate([buf] + [send(buf, plan.along(k)) for k in range(2, plan.depth, 2)], 0)
    buf = jnp.concatenate([buf, send(buf, plan.first())], 0)
    buf = jnp.concatenate([buf, send(buf, plan.second())], 0)
    buf = jnp.concatenate([buf] + [send(buf, plan.sibling(s)) for s in range(1, plan.reps)], 0)
    pieces = buf.shape[0]
    group = min(16, pieces)
    width = buf.shape[2]
    loss, grad = pl.pallas_call(
        partial(contrast_kernel, plan.reps, plan.depth, per),
        grid=(pieces // group,),
        out_shape=(jax.ShapeDtypeStruct((32, 1), F32), jax.ShapeDtypeStruct((32, D), F32)),
        in_specs=[
            smem(),
            pl.BlockSpec((group, 48, width), lambda i: (i, 0, 0)),
            whole_block(buf.shape),
        ],
        out_specs=[whole_block((32, 1)), whole_block((32, D))],
        scratch_shapes=[pltpu.VMEM((128, D), F32)],
        compiler_params=params(56),
        name="contrast",
    )(where, buf, buf)
    loss = lax.dynamic_slice(loss, (tower * queries, 0), (queries, 1))[:, 0]
    return loss, grad


def norm_back(grad, hat, rstd, gain):
    scaled = grad * gain
    a = jnp.mean(scaled, -1, keepdims=True)
    b = jnp.mean(scaled * hat, -1, keepdims=True)
    return rstd * (scaled - a - hat * b)


def col_sum(v):
    return jnp.sum(v, 0, keepdims=True)


def top_kernel(cot_ref, cls_ref, hat_ref, rstd_ref, vec_ref, second_ref, gs_ref, sums_ref):
    @pl.when(pl.program_id(0) == 0)
    def clear():
        sums_ref[...] = jnp.zeros_like(sums_ref)

    groups = TILE // 32
    at_first = lax.broadcasted_iota(jnp.int32, (groups, 32, D), 1) == 0
    extra = jnp.where(at_first, cls_ref[...].reshape(groups, 1, D), 0.0)
    dout = cot_ref[...].astype(F32) + extra.reshape(TILE, D)
    hat = hat_ref[...]
    grad = norm_back(dout, hat, rstd_ref[...], vec_ref[11:12, :])
    second_ref[...] = grad
    gs = grad.astype(BF)
    gs_ref[...] = gs
    sums_ref[0:1, :] += col_sum(gs.astype(F32))
    sums_ref[1:2, :] += col_sum(dout)
    sums_ref[2:3, :] += col_sum(dout * hat)


def top(cot, cls_grad, hat2, rstd2, vec):
    rows = cot.shape[0]
    shape = jax.ShapeDtypeStruct
    return pl.pallas_call(
        top_kernel,
        grid=(rows // TILE,),
        out_shape=(shape((rows, D), F32), shape((rows, D), BF), shape((8, D), F32)),
        in_specs=[row_block(D), row_block(D, TILE // 32), row_block(D), row_block(1), whole_block(vec.shape)],
        out_specs=[row_block(D), row_block(D), whole_block((8, D))],
        compiler_params=params(48),
        name="top",
    )(cot, cls_grad, hat2, rstd2, vec)


def gelu_back_kernel(gs_ref, w_ref, slope_ref, gu_ref, sums_ref):
    total = jnp.zeros((1, D), F32)
    for m in range(gs_ref.shape[0] // TILE):
        rows = slice(m * TILE, (m + 1) * TILE)
        gu = (dot_t(gs_ref[rows, :], w_ref[...]) * slope_ref[rows, :].astype(F32)).astype(BF)
        gu_ref[rows, :] = gu
        total = total + col_sum(gu.astype(F32))
    sums_ref[pl.ds(pl.program_id(0), 1), :] = total


def gelu_back(gs, w_down, slope):
    rows = gs.shape[0]
    shape = jax.ShapeDtypeStruct
    col = pl.BlockSpec((rows, D), lambda i: (0, i))
    return pl.pallas_call(
        gelu_back_kernel,
        grid=(FF // D,),
        out_shape=(shape((rows, FF), BF), shape((8, D), F32)),
        in_specs=[whole_block(gs.shape), row_block(D, D), col],
        out_specs=[col, whole_block((8, D))],
        compiler_params=params(48),
        name="gelu_back",
    )(gs, w_down, slope)


def attend_back_kernel(
    gu_ref, w_up_ref, second_ref, hat_ref, rstd_ref, w_ref, vec_ref, proj_ref, probs_ref,
    go_ref, gp_ref, own_ref, far_ref, sums_ref, ga_ref,
):
    i = pl.program_id(0)

    @pl.when(i == 0)
    def clear():
        sums_ref[...] = jnp.zeros_like(sums_ref)

    grad = dot_t(gu_ref[...], w_up_ref[...]) + second_ref[...]
    hat = hat_ref[...]
    hidden = norm_back(grad, hat, rstd_ref[...], vec_ref[10:11, :])
    go = hidden.astype(BF)
    go_ref[...] = go
    sums_ref[2:3, :] += col_sum(go.astype(F32))
    sums_ref[3:4, :] += col_sum(grad)
    sums_ref[4:5, :] += col_sum(grad * hat)
    ga_ref[...] = dot_t(go, w_ref[:, AT_OUT:AT_VEC]).astype(BF)
    low, high = lane_masks()
    for blk in range(TILE // BLOCK):
        rows = slice(blk * BLOCK, (blk + 1) * BLOCK)
        for pair in range(PAIRS):
            lanes = slice(pair * 128, (pair + 1) * 128)
            lanes_k = slice(D + pair * 128, D + (pair + 1) * 128)
            lanes_v = slice(2 * D + pair * 128, 2 * D + (pair + 1) * 128)
            q, k, v = proj_ref[rows, lanes], proj_ref[rows, lanes_k], proj_ref[rows, lanes_v]
            a = ga_ref[rows, lanes]
            a2 = jnp.concatenate([a * low, a * high], 0)
            q2 = jnp.concatenate([q * low, q * high], 0)
            k2 = jnp.concatenate([k * low, k * high], 0)
            p = probs_ref[blk, pair]
            dp = dot_t(a2, v)
            pf = p.astype(F32)
            ds = (pf * (dp - jnp.sum(pf * dp, -1, keepdims=True)) * HEAD**-0.5).astype(BF)
            wide = jnp.concatenate([ds[:BLOCK], ds[BLOCK:]], 1)
            gp_ref[rows, lanes] = dot(wide, k2).astype(BF)
            gp_ref[rows, lanes_k] = t_dot(ds, q2).astype(BF)
            gp_ref[rows, lanes_v] = t_dot(p, a2).astype(BF)
    gp = gp_ref[...]
    sums_ref[0:1, :] += col_sum(gp[:, :D].astype(F32))
    sums_ref[1:2, :] += col_sum(gp[:, 2 * D :].astype(F32))
    gx = dot_t(gp, w_ref[:, :AT_OUT]) + hidden
    half = pl.num_programs(0) // 2

    @pl.when(i < half)
    def near():
        own_ref[...] = gx

    @pl.when(i >= half)
    def away():
        far_ref[...] = gx.astype(BF)


def attend_back(gu, w_up, second, hat, rstd, w_one, vec, proj, probs):
    rows = gu.shape[0]
    shape = jax.ShapeDtypeStruct
    per = TILE // BLOCK
    steps = rows // TILE
    half = steps // 2
    return pl.pallas_call(
        attend_back_kernel,
        grid=(steps,),
        out_shape=(
            shape((rows, D), BF),
            shape((rows, 3 * D), BF),
            shape((rows // 2, D), F32),
            shape((rows // 2, D), BF),
            shape((8, D), F32),
        ),
        in_specs=[
            row_block(FF),
            whole_block(w_up.shape),
            row_block(D),
            row_block(D),
            row_block(1),
            whole_block(w_one.shape),
            whole_block(vec.shape),
            row_block(3 * D),
            pl.BlockSpec((per, PAIRS, 2 * BLOCK, BLOCK), lambda i: (i, 0, 0, 0)),
        ],
        out_specs=[
            row_block(D),
            row_block(3 * D),
            pl.BlockSpec((TILE, D), lambda i: (jnp.minimum(i, half - 1), 0)),
            pl.BlockSpec((TILE, D), lambda i: (jnp.maximum(i - half, 0), 0)),
            whole_block((8, D)),
        ],
        scratch_shapes=[pltpu.VMEM((TILE, D), BF)],
        compiler_params=params(56),
        name="attend_back",
    )(gu, w_up, second, hat, rstd, w_one, vec, proj, probs)


def on_device(
    plan, query_tokens, passage_tokens, query_cot, passage_cot, positives, w_qkv, w_out, w_up, w_down, biases, gains
):
    me = lax.axis_index("dp")
    core = lax.axis_index("rep")
    tower = (me >> 2) & 1
    span = jnp.where(tower == 0, query_tokens.shape[1], passage_tokens.shape[1])
    where = jnp.stack([me, core, tower, span]).astype(jnp.int32)
    swap = plan.along(1)

    def exchange(a, b):
        a, b = a.reshape(-1, D), b.reshape(-1, D)
        return jnp.concatenate([jnp.where(tower == 0, a, b), send(jnp.where(tower == 0, b, a), swap)], 0)

    vecs = jnp.swapaxes(jnp.concatenate([biases, gains], 1), 1, 2)
    one = jnp.concatenate([w_qkv, w_out, jnp.pad(vecs, ((0, 0), (0, 0), (0, W_ONE - AT_VEC - vecs.shape[2])))], 2)
    x = exchange(query_tokens, passage_tokens)
    w_one = gather_chunk(plan, where, one)
    w_two = gather_chunk(plan, where, w_up)
    w_three = gather_chunk(plan, where, w_down)
    cot = exchange(query_cot, passage_cot)

    proj, probs, attn, hat1, rstd1, norm, vec = attend(where, x, w_one)
    act, slope = up(norm, w_two, vec)
    out, hat2, rstd2, cls = down(act, w_three, hat1, vec)
    half = out.shape[0] // 2
    out_back = send(out[half:], swap)
    query_out = jnp.where(tower == 0, out[:half], out_back).reshape(query_tokens.shape)
    passage_out = jnp.where(tower == 0, out_back, out[:half]).reshape(passage_tokens.shape)
    query_loss, cls_grad = contrast(plan, where, cls, positives)

    second, gs, sums_top = top(cot, cls_grad, hat2, rstd2, vec)
    g_three = t_dot(act, gs).astype(BF)
    grad_down = scatter_chunk(plan, where, g_three, w_down.shape[1])
    gu, sums_up = gelu_back(gs, w_three, slope)
    g_two = t_dot(norm, gu).astype(BF)
    grad_up = scatter_chunk(plan, where, g_two, w_up.shape[1])
    go, gp, gx_own, gx_far, sums = attend_back(gu, w_two, second, hat1, rstd1, w_one, vec, proj, probs)
    gx_back = send(gx_far, swap).astype(F32)
    query_grad = jnp.where(tower == 0, gx_own, gx_back).reshape(query_tokens.shape)
    passage_grad = jnp.where(tower == 0, gx_back, gx_own).reshape(passage_tokens.shape)
    lines = jnp.concatenate(
        [sums[0:4], sums_up[0:4], sums_top[0:2], sums[4:5], sums_top[2:3], jnp.zeros((W_ONE - AT_VEC - 12, D), F32)], 0
    )
    g_one = jnp.concatenate([t_dot(x, gp).astype(BF), t_dot(attn, go).astype(BF), lines.T.astype(BF)], 1)
    grad_one = scatter_chunk(plan, where, g_one, w_qkv.shape[1])
    grad_vecs = jnp.swapaxes(grad_one[:, :, AT_VEC : AT_VEC + 12], 1, 2)
    return (
        query_out,
        passage_out,
        query_grad,
        passage_grad,
        query_loss,
        grad_one[:, :, :AT_OUT],
        grad_one[:, :, AT_OUT:AT_VEC],
        grad_up,
        grad_down,
        grad_vecs[:, :10],
        grad_vecs[:, 10:],
    )


def solution(mesh):
    plan = Plan(mesh.shape["dp"], mesh.shape["rep"])
    rows = P(("dp", "rep"), None, None)
    shards = P(None, "dp", None)
    lanes = P(None, None, "dp")
    return jax.shard_map(
        partial(on_device, plan),
        mesh=mesh,
        in_specs=(rows,) * 4 + (P(("dp", "rep"), None),) + (shards,) * 4 + (lanes,) * 2,
        out_specs=(rows,) * 4 + (P(("dp", "rep")),) + (shards,) * 4 + (lanes,) * 2,
        check_vma=False,
    )
```

time: 1990 us -> 416 us (0.21)
  blocking collectives: 867 us -> 0 us
  waiting for transfers between devices: 744 us -> 144 us
  matrix products: 154 us -> 27.2 us
  Pallas kernels: 0 us -> 114 us
  local copies, waits for them, and re-layouts: 141 us -> 50.5 us
  starting transfers between devices: 1.18 us -> 49.8 us
  other arithmetic: 59 us -> 24 us
    unnamed x2 -> x0, blocking collectives: 727 us -> none
    unnamed x20 -> x0, waiting for transfers between devices: 379 us -> none
    all_gather x4 -> x0, waiting for transfers between devices: 226 us -> none  [the longest x1 120 us: on_device(): lax.all_gather(w_up, 'dp', axis=1, tiled=True)]
    ppermute x0 -> x60, waiting for transfers between devices: none -> 144 us  [send(): return lax.ppermute(v, AXES, pairs)]
    reduce_scatter x4 -> x0, waiting for transfers between devices: 140 us -> none  [the longest x1 133 us: on_device(): lax.psum_scatter(term_down, 'dp', scatter_dimension=1, tiled=True)]
    all_gather x9 -> x0, blocking collectives: 140 us -> none  [the longest x1 46.4 us: on_device(): lax.all_gather(biases, 'dp', axis=2, tiled=True)]
    dot_general x39 -> x4, matrix products: 154 us -> 27.2 us  [t_dot(): lax.dot_general(a, b, (((0,), (0,)), ((), ())), preferred_element_type=F32)]
    pallas_call x0 -> x13, Pallas kernels: none -> 114 us  [the longest x1 36 us: attend_back(): pl.pallas_call(attend_back_kernel, grid=(steps,), out_shape=(shape((rows,...]
  transfers between devices with their start and end apart: 14 -> 60, of which waited for: 11 -> 22; matrix products, arithmetic and copies ran while one was open for 14% -> 11% of each run, Pallas kernels for 0% -> 3%
where the time goes in v1:
time: 416 us; the launch traced here: 411 us
  waiting for transfers between devices  144 us (35%)
  Pallas kernels  114 us (27%)
  local copies, waits for them, and re-layouts  50.5 us (12%)
  starting transfers between devices  49.8 us (12%)
  matrix products  27.2 us (7%)
  other arithmetic  24 us (6%)
    ppermute x60, waiting for transfers between devices, send(): return lax.ppermute(v, AXES, pairs)  144 us
    ppermute x60, starting transfers between devices, send(): return lax.ppermute(v, AXES, pairs)  49.8 us
    pallas_call x1, Pallas kernels, attend_back(): pl.pallas_call(attend_back_kernel, grid=(steps,), out_shape=(shape((rows,...  36 us
    unnamed x129, local copies, waits for them, and re-layouts  30.5 us
    dot_general x4, matrix products, t_dot(): lax.dot_general(a, b, (((0,), (0,)), ((), ())), preferred_element_type=F32)  27.2 us
    pallas_call x1, Pallas kernels, up(): pl.pallas_call(up_kernel, grid=(FF // D,), out_shape=(wide, wide), in_spe...  18.3 us
    pallas_call x1, Pallas kernels, attend(): pl.pallas_call(attend_kernel, grid=(rows // TILE,), out_shape=(shape((row...  16.6 us
    pallas_call x1, Pallas kernels, gelu_back(): pl.pallas_call(gelu_back_kernel, grid=(FF // D,), out_shape=(shape((rows,...  10.1 us
  transfers between devices with their start and end apart: 60, of which 22 were waited for; matrix products, arithmetic and copies ran while one was open for 11% of the time, Pallas kernels for 3%

profile of v1, /device:TPU:0, one launch (start us, length us, event | category | flops | bytes accessed | tf_op | source)
XLA Modules:
  0.0 410.9 jit_solution(15983769253172306343)
XLA Ops:
  2.4 3.0 collective-permute-start.11
  5.4 2.5 collective-permute-start.13
  16.9 14.4 %collective-permute-done.12 = bf16[1,48,1536]{2,1,0:T(8,128)(2,1)S(1)} collective-permute-done((bf16[1,48,1536]{2,1,0:T(8,128)(2,1)S(1)}, bf16[1,48,1536]{2,1,0:T(8,128)(2,1)S(1)}, u32[]{:S(2)}, u32[]{:S(2)}) %collective-permute-start.12) | collective-permute-done | bytes 147488 | tf_op jit(solution)/shard_map/ppermute | solution.py:41
  36.6 2.9 collective-permute-start.3
  41.2 2.4 collective-permute-done.1
  43.7 8.6 %collective-permute-done.2 = bf16[1,48,1664]{2,1,0:T(8,128)(2,1)S(1)} collective-permute-done((bf16[1,48,1664]{2,1,0:T(8,128)(2,1)S(1)}, bf16[1,48,1664]{2,1,0:T(8,128)(2,1)S(1)}, u32[]{:S(2)}, u32[]{:S(2)}) %collective-permute-start.2) | collective-permute-done | bytes 159776 | tf_op jit(solution)/shard_map/ppermute | solution.py:41
  56.9 12.5 %collective-permute-done.24.refs_1_ = bf16[4,192,384]{2,1,0:T(8,128)(2,1)S(1)} collective-permute-done((bf16[4,192,384]{2,1,0:T(8,128)(2,1)S(1)}, bf16[4,192,384]{2,1,0:T(8,128)(2,1)S(1)}, u32[]{:S(2)}, u32[]{:S(2)}) %collective-permute-start.24) | collective-permute-done | bytes 589856 | tf_op jit(solution)/shard_map/ppermute | solution.py:41
  72.8 8.7 %collective-permute-done.4.refs_1_ = bf16[4,48,1664]{2,1,0:T(8,128)(2,1)S(1)} collective-permute-done((bf16[4,48,1664]{2,1,0:T(8,128)(2,1)S(1)}, bf16[4,48,1664]{2,1,0:T(8,128)(2,1)S(1)}, u32[]{:S(2)}, u32[]{:S(2)}) %collective-permute-start.4) | collective-permute-done | bytes 639008 | tf_op jit(solution)/shard_map/ppermute | solution.py:41
  83.6 5.7 %collective-permute-done.16.refs_3_ = bf16[4,48,1536]{2,1,0:T(8,128)(2,1)S(1)} collective-permute-done((bf16[4,48,1536]{2,1,0:T(8,128)(2,1)}, bf16[4,48,1536]{2,1,0:T(8,128)(2,1)S(1)}, u32[]{:S(2)}, u32[]{:S(2)}) %collective-permute-start.16) | collective-permute-done | bytes 589856 | tf_op jit(solution)/shard_map/ppermute | solution.py:41
  94.2 8.2 %collective-permute-done.26.refs_3_ = bf16[4,192,384]{2,1,0:T(8,128)(2,1)} collective-permute-done((bf16[4,192,384]{2,1,0:T(8,128)(2,1)S(1)}, bf16[4,192,384]{2,1,0:T(8,128)(2,1)}, u32[]{:S(2)}, u32[]{:S(2)}) %collective-permute-start.26) | collective-permute-done | bytes 589856 | tf_op jit(solution)/shard_map/ppermute | solution.py:41
  110.3 2.1 copy-done.2
  116.3 2.3 assemble.3
  118.6 2.2 copy-done
  120.8 16.6 %attend.1 = (bf16[1024,2304]{1,0:T(8,128)(2,1)}, bf16[8,6,256,128]{3,2,1,0:T(8,128)(2,1)}, bf16[1024,768]{1,0:T(8,128)(2,1)S(1)}, f32[1024,768]{1,0:T(8,128)}, f...) custom-call(s32[4]{0:T(128)S(1)} %pad_add_fusion.where_ref, ...), custom_call_target="tpu_custom_call" | custom-call | tf_op jit(solution)/shard_map/attend/pallas_call | solution.py:254
  137.4 18.3 %up.1 = (bf16[1024,3072]{1,0:T(8,128)(2,1)}, bf16[1024,3072]{1,0:T(8,128)(2,1)}) custom-call(bf16[1024,768]{1,0:T(8,128)(2,1)S(1)} %get-tuple-element.42.norm_ref, bf16[768,3072]{1,0:T(8,128)(2,1)} %bitcast.110, f32[128,768]{1,0:T(8,128)S(1)} %get-tuple-element.43.vec_ref), custom_call_target="tpu_custom_call" | custom-call | tf_op jit(solution)/shard_map/up/pallas_call | solution.py:308
  155.7 9.8 %down.1 = (bf16[1024,768]{1,0:T(8,128)(2,1)S(1)}, f32[1024,768]{1,0:T(8,128)S(1)}, f32[1024,1]{1,0:T(8,128)S(1)}, f32[32,768]{1,0:T(8,128)S(1)}) custom-call(bf16[1024,3072]{1,0:T(8,128)(2,1)} %get-tuple-element.44.act_ref, bf16[3072,768]{1,0:T(8,128)(2,1)} %bitcast.108, f32[1024,768]{1,0:T(8,128)} %get-tuple-element.45.hat_ref, ...), custom_call_target="tpu_custom_call" | custom-call | tf_op jit(solution)/shard_map/down/pallas_call | solution.py:334
  168.5 4.2 %collective-permute-done.33 = bf16[32,896]{1,0:T(8,128)(2,1)S(1)} collective-permute-done((bf16[32,896]{1,0:T(8,128)(2,1)S(1)}, bf16[32,896]{1,0:T(8,128)(2,1)S(1)}, u32[]{:S(2)}, u32[]{:S(2)}) %collective-permute-start.33) | collective-permute-done | bytes 57376 | tf_op jit(solution)/shard_map/ppermute | solution.py:41
  173.6 6.0 %collective-permute-done.34 = bf16[1,48,896]{2,1,0:T(8,128)(2,1)S(1)} collective-permute-done((bf16[1,48,896]{2,1,0:T(8,128)(2,1)S(1)}, bf16[1,48,896]{2,1,0:T(8,128)(2,1)S(1)}, u32[]{:S(2)}, u32[]{:S(2)}) %collective-permute-start.34) | collective-permute-done | bytes 86048 | tf_op jit(solution)/shard_map/ppermute | solution.py:41
  180.2 2.4 bitcast_select_fusion.1
  182.6 2.5 collective-permute-done.35
  185.3 7.1 %collective-permute-done.36 = bf16[4,48,896]{2,1,0:T(8,128)(2,1)S(1)} collective-permute-done((bf16[4,48,896]{2,1,0:T(8,128)(2,1)S(1)}, bf16[4,48,896]{2,1,0:T(8,128)(2,1)S(1)}, u32[]{:S(2)}, u32[]{:S(2)}) %collective-permute-start.36) | collective-permute-done | bytes 344096 | tf_op jit(solution)/shard_map/ppermute | solution.py:41
  194.1 7.6 %collective-permute-done.32 = bf16[512,768]{1,0:T(8,128)(2,1)} collective-permute-done((bf16[512,768]{1,0:T(8,128)(2,1)}, bf16[512,768]{1,0:T(8,128)(2,1)}, u32[]{:S(2)}, u32[]{:S(2)}) %collective-permute-start.32) | collective-permute-done | bytes 786464 | tf_op jit(solution)/shard_map/ppermute | solution.py:41
  205.4 3.7 contrast.1
  210.0 5.3 %top.1 = (f32[1024,768]{1,0:T(8,128)}, bf16[1024,768]{1,0:T(8,128)(2,1)S(1)}, f32[8,768]{1,0:T(8,128)S(1)}) custom-call(bf16[1024,768]{1,0:T(8,128)(2,1)S(1)} %pad_maximum_fusion.2.cot_ref, f32[32,768]{1,0:T(8,128)S(1)} %copy-done.36, f32[1024,768]{1,0:T(8,128)} %copy-done.7, f32[1024,1]{1,0:T(8,128)S(1)} %get-tuple-element.50.rstd_ref, ...), custom_call_target="tpu_custom_call" | custom-call | tf_op jit(solution)/shard_map/top/pallas_call | solution.py:467
  215.3 9.7 %convolution_convert_fusion = bf16[3072,768]{1,0:T(8,128)(2,1)} fusion(bf16[1024,3072]{1,0:T(8,128)(2,1)} %get-tuple-element.44.act_ref, bf16[1024,768]{1,0:T(8,128)(2,1)S(1)} %get-tuple-element.51.gs_ref), kind=kOutput, calls=%fused_computation.1 | convolution fusion | flops 4834197504 | bytes 12582912 | tf_op jit(solution)/shard_map/dot_general | solution.py:188
  225.0 10.1 %gelu_back.1 = (bf16[1024,3072]{1,0:T(8,128)(2,1)}, f32[8,768]{1,0:T(8,128)S(1)}) custom-call(bf16[1024,768]{1,0:T(8,128)(2,1)S(1)} %get-tuple-element.51.gs_ref, bf16[3072,768]{1,0:T(8,128)(2,1)} %bitcast.109, bf16[1024,3072]{1,0:T(8,128)(2,1)} %get-tuple-element.52.slope_ref), custom_call_target="tpu_custom_call" | custom-call | tf_op jit(solution)/shard_map/gelu_back/pallas_call | solution.py:492
  235.1 8.1 %convolution_convert_fusion.1 = bf16[768,3072]{1,0:T(8,128)(2,1)S(1)} fusion(bf16[1024,768]{1,0:T(8,128)(2,1)S(1)} %get-tuple-element.42.norm_ref, bf16[1024,3072]{1,0:T(8,128)(2,1)} %get-tuple-element.53.gu_ref), kind=kOutput, calls=%fused_computation.2 | convolution fusion | flops 4834197504 | bytes 12582912 | tf_op jit(solution)/shard_map/dot_general | solution.py:188
  243.3 36.0 %attend_back.1 = (bf16[1024,768]{1,0:T(8,128)(2,1)}, bf16[1024,2304]{1,0:T(8,128)(2,1)}, f32[512,768]{1,0:T(8,128)}, bf16[512,768]{1,0:T(8,128)(2,1)}, f32[8,768]{1,0:T(8,128)}) custom-call(bf16[1024,3072]{1,0:T(8,128)(2,1)} %get-tuple-element.53.gu_ref, bf16[768,3072]{1,0:T(8,128)(2,1)} %bitcast.111, f32[1024,768]{1,0:T(8,128)} %get-tuple-element.54.second_ref, ...), custom_call_target="tpu_custom_call" | custom-call | tf_op jit(solution)/shard_map/attend_back/pallas_call | solution.py:563
  280.1 3.3 constant_dynamic-slice_fusion
  287.9 2.9 convolution_convert_fusion.3
  292.4 6.5 %convolution_convert_fusion.2 = bf16[768,2304]{1,0:T(8,128)(2,1)S(1)} fusion(bf16[1024,2304]{1,0:T(8,128)(2,1)} %get-tuple-element.61, bf16[512,768]{1,0:T(8,128)(2,1)} %copy-done.45, bf16[512,768]{1,0:T(8,128)(2,1)S(1)} %copy-done.41), kind=kOutput, calls=%fused_computation.3 | convolution fusion | flops 3628793856 | bytes 9830400 | tf_op jit(solution)/shard_map/dot_general | solution.py:188
  302.9 2.5 copy-done.5
  305.4 3.4 pick_add.5
  309.3 2.1 slice.162
  311.8 3.0 pick_add.4
  317.3 2.1 pick_add.3
  321.0 10.9 %collective-permute-done.31 = bf16[512,768]{1,0:T(8,128)(2,1)} collective-permute-done((bf16[512,768]{1,0:T(8,128)(2,1)}, bf16[512,768]{1,0:T(8,128)(2,1)}, u32[]{:S(2)}, u32[]{:S(2)}) %collective-permute-start.31) | collective-permute-done | bytes 786464 | tf_op jit(solution)/shard_map/ppermute | solution.py:41
  331.9 2.6 broadcast_select_fusion
  341.4 21.5 %collective-permute-done.40 = bf16[8,48,1664]{2,1,0:T(8,128)(2,1)S(1)} collective-permute-done((bf16[8,48,1664]{2,1,0:T(8,128)(2,1)}, bf16[8,48,1664]{2,1,0:T(8,128)(2,1)S(1)}, u32[]{:S(2)}, u32[]{:S(2)}) %collective-permute-start.40) | collective-permute-done | bytes 1277984 | tf_op jit(solution)/shard_map/ppermute | solution.py:41
  363.3 3.0 collective-permute-start.41
  366.5 2.2 collective-permute-start.57
  368.8 2.1 collective-permute-start.58
  371.0 9.0 %collective-permute-done.56 = bf16[192,384]{1,0:T(8,128)(2,1)S(1)} collective-permute-done((bf16[192,384]{1,0:T(8,128)(2,1)S(1)}, bf16[192,384]{1,0:T(8,128)(2,1)S(1)}, u32[]{:S(2)}, u32[]{:S(2)}) %collective-permute-start.56) | collective-permute-done | bytes 147488 | tf_op jit(solution)/shard_map/ppermute | solution.py:41
  380.1 2.5 collective-permute-start.50
  384.7 2.7 collective-permute-done.49
  387.5 2.1 collective-permute-done.51
  397.7 3.7 collective-permute-done.42
  401.4 4.1 collective-permute-done.43
  (298 shorter events, 93.9 us)
Async XLA Ops:
  2.4 13.4 %collective-permute-start.11 = (bf16[1,48,1536]{2,1,0:T(8,128)(2,1)}, bf16[1,48,1536]{2,1,0:T(8,128)(2,1)S(1)}, u32[]{:S(2)}, u32[]{:S(2)}) collective-permute-start(bf16[1,48,1536]{2,1,0:T(8,128)(2,1)} %get-tuple-element.151), channel_id=1, source_target_pairs={{0,8},{1,9},{2,10},{3,11},{4,12},{5,13},{6,14},{7,15},{8,0},{9,1},... | collective-permute-start | bytes 442376 | tf_op jit(solution)/shard_map/ppermute | solution.py:41
  5.4 26.5 %collective-permute-start.13 = (bf16[1,48,1536]{2,1,0:T(8,128)(2,1)}, bf16[1,48,1536]{2,1,0:T(8,128)(2,1)}, u32[]{:S(2)}, u32[]{:S(2)}) collective-permute-start(bf16[1,48,1536]{2,1,0:T(8,128)(2,1)} %get-tuple-element.151), channel_id=1, source_target_pairs={{0,24},{1,25},{2,26},{3,27},{4,28},{5,29},{6,30},{7,31},{8,16},{9,... | collective-permute-start | bytes 442376 | tf_op jit(solution)/shard_map/ppermute | solution.py:41
  9.6 26.5 %collective-permute-start.21 = (bf16[1,192,384]{2,1,0:T(8,128)(2,1)}, bf16[1,192,384]{2,1,0:T(8,128)(2,1)S(1)}, u32[]{:S(2)}, u32[]{:S(2)}) collective-permute-start(bf16[1,192,384]{2,1,0:T(8,128)(2,1)} %get-tuple-element.149), channel_id=1, source_target_pairs={{0,8},{1,9},{2,10},{3,11},{4,12},{5,13},{6,14},{7,15},{8,0},{9,1},... | collective-permute-start | bytes 442376 | tf_op jit(solution)/shard_map/ppermute | solution.py:41
  10.2 29.3 %collective-permute-start.23 = (bf16[1,192,384]{2,1,0:T(8,128)(2,1)}, bf16[1,192,384]{2,1,0:T(8,128)(2,1)}, u32[]{:S(2)}, u32[]{:S(2)}) collective-permute-start(bf16[1,192,384]{2,1,0:T(8,128)(2,1)} %get-tuple-element.149), channel_id=1, source_target_pairs={{0,24},{1,25},{2,26},{3,27},{4,28},{5,29},{6,30},{7,31},{8,16},{9,... | collective-permute-start | bytes 442376 | tf_op jit(solution)/shard_map/ppermute | solution.py:41
  11.1 20.1 %collective-permute-start.12 = (bf16[1,48,1536]{2,1,0:T(8,128)(2,1)S(1)}, bf16[1,48,1536]{2,1,0:T(8,128)(2,1)S(1)}, u32[]{:S(2)}, u32[]{:S(2)}) collective-permute-start(bf16[1,48,1536]{2,1,0:T(8,128)(2,1)S(1)} %get-tuple-element.150), channel_id=1, source_target_pairs={{0,16},{1,17},{2,18},{3,19},{4,20},{5,21},{6,22},{7,23},{8,24},{9,... | collective-permute-start | bytes 442376 | tf_op jit(solution)/shard_map/ppermute | solution.py:41
  15.8 20.8 %collective-permute-start.22 = (bf16[1,192,384]{2,1,0:T(8,128)(2,1)S(1)}, bf16[1,192,384]{2,1,0:T(8,128)(2,1)}, u32[]{:S(2)}, u32[]{:S(2)}) collective-permute-start(bf16[1,192,384]{2,1,0:T(8,128)(2,1)S(1)} %get-tuple-element.148), channel_id=1, source_target_pairs={{0,16},{1,17},{2,18},{3,19},{4,20},{5,21},{6,22},{7,23},{8,24},{9,... | collective-permute-start | bytes 442376 | tf_op jit(solution)/shard_map/ppermute | solution.py:41
  33.0 21.0 %collective-permute-start.14 = (bf16[4,48,1536]{2,1,0:T(8,128)(2,1)S(1)}, bf16[4,48,1536]{2,1,0:T(8,128)(2,1)}, u32[]{:S(2)}, u32[]{:S(2)}) collective-permute-start(bf16[4,48,1536]{2,1,0:T(8,128)(2,1)S(1)} %pad_maximum_fusion.5.refs_0_), channel_id=1, source_target_pairs={{0,2},{1,5},{2,0},{3,7},{4,6},{5,1},{6,4},{7,3},{8,10},{9,13},{10,... | collective-permute-start | bytes 1769480 | tf_op jit(solution)/shard_map/ppermute | solution.py:41
  34.5 20.0 %collective-permute-start.15 = (bf16[4,48,1536]{2,1,0:T(8,128)(2,1)S(1)}, bf16[4,48,1536]{2,1,0:T(8,128)(2,1)}, u32[]{:S(2)}, u32[]{:S(2)}) collective-permute-start(bf16[4,48,1536]{2,1,0:T(8,128)(2,1)S(1)} %pad_maximum_fusion.5.refs_0_), channel_id=1, source_target_pairs={{0,4},{1,3},{2,6},{3,1},{4,0},{5,7},{6,2},{7,5},{8,12},{9,11},{10,... | collective-permute-start | bytes 1769480 | tf_op jit(solution)/shard_map/ppermute | solution.py:41
  36.6 16.8 %collective-permute-start.3 = (bf16[1,48,1664]{2,1,0:T(8,128)(2,1)S(1)}, bf16[1,48,1664]{2,1,0:T(8,128)(2,1)S(1)}, u32[]{:S(2)}, u32[]{:S(2)}) collective-permute-start(bf16[1,48,1664]{2,1,0:T(8,128)(2,1)S(1)} %get-tuple-element.147), channel_id=1, source_target_pairs={{0,24},{1,25},{2,26},{3,27},{4,28},{5,29},{6,30},{7,31},{8,16},{9,... | collective-permute-start | bytes 479240 | tf_op jit(solution)/shard_map/ppermute | solution.py:41
  39.5 12.8 %collective-permute-start.2 = (bf16[1,48,1664]{2,1,0:T(8,128)(2,1)S(1)}, bf16[1,48,1664]{2,1,0:T(8,128)(2,1)S(1)}, u32[]{:S(2)}, u32[]{:S(2)}) collective-permute-start(bf16[1,48,1664]{2,1,0:T(8,128)(2,1)S(1)} %get-tuple-element.146), channel_id=1, source_target_pairs={{0,16},{1,17},{2,18},{3,19},{4,20},{5,21},{6,22},{7,23},{8,24},{9,... | collective-permute-start | bytes 479240 | tf_op jit(solution)/shard_map/ppermute | solution.py:41
  43.6 28.7 %collective-permute-start = (bf16[512,768]{1,0:T(8,128)(2,1)S(1)}, bf16[512,768]{1,0:T(8,128)(2,1)S(1)}, u32[]{:S(2)}, u32[]{:S(2)}) collective-permute-start(bf16[512,768]{1,0:T(8,128)(2,1)S(1)} %get-tuple-element.136), channel_id=1, source_target_pairs={{0,8},{1,9},{2,10},{3,11},{4,12},{5,13},{6,14},{7,15},{8,0},{9,1},... | collective-permute-start | bytes 2359304 | tf_op jit(solution)/shard_map/ppermute | solution.py:41
  53.4 16.0 %collective-permute-start.24 = (bf16[4,192,384]{2,1,0:T(8,128)(2,1)S(1)}, bf16[4,192,384]{2,1,0:T(8,128)(2,1)S(1)}, u32[]{:S(2)}, u32[]{:S(2)}) collective-permute-start(bf16[4,192,384]{2,1,0:T(8,128)(2,1)S(1)} %pad_maximum_fusion.6.refs_0_), channel_id=1, source_target_pairs={{0,2},{1,5},{2,0},{3,7},{4,6},{5,1},{6,4},{7,3},{8,10},{9,13},{10,... | collective-permute-start | bytes 1769480 | tf_op jit(solution)/shard_map/ppermute | solution.py:41
  54.0 16.2 %collective-permute-start.25 = (bf16[4,192,384]{2,1,0:T(8,128)(2,1)S(1)}, bf16[4,192,384]{2,1,0:T(8,128)(2,1)S(1)}, u32[]{:S(2)}, u32[]{:S(2)}) collective-permute-start(bf16[4,192,384]{2,1,0:T(8,128)(2,1)S(1)} %pad_maximum_fusion.6.refs_0_), channel_id=1, source_target_pairs={{0,4},{1,3},{2,6},{3,1},{4,0},{5,7},{6,2},{7,5},{8,12},{9,11},{10,... | collective-permute-start | bytes 1769480 | tf_op jit(solution)/shard_map/ppermute | solution.py:41
  54.5 17.0 %collective-permute-start.27 = (bf16[4,192,384]{2,1,0:T(8,128)(2,1)S(1)}, bf16[4,192,384]{2,1,0:T(8,128)(2,1)S(1)}, u32[]{:S(2)}, u32[]{:S(2)}) collective-permute-start(bf16[4,192,384]{2,1,0:T(8,128)(2,1)S(1)} %pad_maximum_fusion.6.refs_0_), channel_id=1, source_target_pairs={{0,1},{1,0},{2,3},{3,2},{4,5},{5,4},{6,7},{7,6},{8,9},{9,8},{10,11... | collective-permute-start | bytes 1769480 | tf_op jit(solution)/shard_map/ppermute | solution.py:41
  55.4 26.1 %collective-permute-start.4 = (bf16[4,48,1664]{2,1,0:T(8,128)(2,1)S(1)}, bf16[4,48,1664]{2,1,0:T(8,128)(2,1)S(1)}, u32[]{:S(2)}, u32[]{:S(2)}) collective-permute-start(bf16[4,48,1664]{2,1,0:T(8,128)(2,1)S(1)} %pad_maximum_fusion.4.refs_0_), channel_id=1, source_target_pairs={{0,2},{1,5},{2,0},{3,7},{4,6},{5,1},{6,4},{7,3},{8,10},{9,13},{10,... | collective-permute-start | bytes 1916936 | tf_op jit(solution)/shard_map/ppermute | solution.py:41
  69.4 13.5 %collective-permute-start.5 = (bf16[4,48,1664]{2,1,0:T(8,128)(2,1)S(1)}, bf16[4,48,1664]{2,1,0:T(8,128)(2,1)S(1)}, u32[]{:S(2)}, u32[]{:S(2)}) collective-permute-start(bf16[4,48,1664]{2,1,0:T(8,128)(2,1)S(1)} %pad_maximum_fusion.4.refs_0_), channel_id=1, source_target_pairs={{0,4},{1,3},{2,6},{3,1},{4,0},{5,7},{6,2},{7,5},{8,12},{9,11},{10,... | collective-permute-start | bytes 1916936 | tf_op jit(solution)/shard_map/ppermute | solution.py:41
  70.2 19.0 %collective-permute-start.16 = (bf16[4,48,1536]{2,1,0:T(8,128)(2,1)}, bf16[4,48,1536]{2,1,0:T(8,128)(2,1)S(1)}, u32[]{:S(2)}, u32[]{:S(2)}) collective-permute-start(bf16[4,48,1536]{2,1,0:T(8,128)(2,1)} %collective-permute-done.14.refs_1_), channel_id=1, source_target_pairs={{0,4},{1,3},{2,6},{3,1},{4,0},{5,7},{6,2},{7,5},{8,12},{9,11},{10,... | collective-permute-start | bytes 1769480 | tf_op jit(solution)/shard_map/ppermute | solution.py:41
  72.3 18.2 %collective-permute-start.18 = (bf16[4,48,1536]{2,1,0:T(8,128)(2,1)}, bf16[4,48,1536]{2,1,0:T(8,128)(2,1)S(1)}, u32[]{:S(2)}, u32[]{:S(2)}) collective-permute-start(bf16[4,48,1536]{2,1,0:T(8,128)(2,1)} %collective-permute-done.14.refs_1_), channel_id=1, source_target_pairs={{0,1},{1,0},{2,3},{3,2},{4,5},{5,4},{6,7},{7,6},{8,9},{9,8},{10,11... | collective-permute-start | bytes 1769480 | tf_op jit(solution)/shard_map/ppermute | solution.py:41
  72.3 19.9 %collective-permute-start.19 = (bf16[4,48,1536]{2,1,0:T(8,128)(2,1)}, bf16[4,48,1536]{2,1,0:T(8,128)(2,1)S(1)}, u32[]{:S(2)}, u32[]{:S(2)}) collective-permute-start(bf16[4,48,1536]{2,1,0:T(8,128)(2,1)} %collective-permute-done.15.refs_2_), channel_id=1, source_target_pairs={{0,1},{1,0},{2,3},{3,2},{4,5},{5,4},{6,7},{7,6},{8,9},{9,8},{10,11... | collective-permute-start | bytes 1769480 | tf_op jit(solution)/shard_map/ppermute | solution.py:41
  81.5 23.3 %collective-permute-start.6 = (bf16[4,48,1664]{2,1,0:T(8,128)(2,1)S(1)}, bf16[4,48,1664]{2,1,0:T(8,128)(2,1)}, u32[]{:S(2)}, u32[]{:S(2)}) collective-permute-start(bf16[4,48,1664]{2,1,0:T(8,128)(2,1)S(1)} %collective-permute-done.4.refs_1_), channel_id=1, source_target_pairs={{0,4},{1,3},{2,6},{3,1},{4,0},{5,7},{6,2},{7,5},{8,12},{9,11},{10,... | collective-permute-start | bytes 1916936 | tf_op jit(solution)/shard_map/ppermute | solution.py:41
  82.9 19.6 %collective-permute-start.26 = (bf16[4,192,384]{2,1,0:T(8,128)(2,1)S(1)}, bf16[4,192,384]{2,1,0:T(8,128)(2,1)}, u32[]{:S(2)}, u32[]{:S(2)}) collective-permute-start(bf16[4,192,384]{2,1,0:T(8,128)(2,1)S(1)} %collective-permute-done.24.refs_1_), channel_id=1, source_target_pairs={{0,4},{1,3},{2,6},{3,1},{4,0},{5,7},{6,2},{7,5},{8,12},{9,11},{10,... | collective-permute-start | bytes 1769480 | tf_op jit(solution)/shard_map/ppermute | solution.py:41
  89.2 13.4 %collective-permute-start.28 = (bf16[4,192,384]{2,1,0:T(8,128)(2,1)S(1)}, bf16[4,192,384]{2,1,0:T(8,128)(2,1)S(1)}, u32[]{:S(2)}, u32[]{:S(2)}) collective-permute-start(bf16[4,192,384]{2,1,0:T(8,128)(2,1)S(1)} %collective-permute-done.24.refs_1_), channel_id=1, source_target_pairs={{0,1},{1,0},{2,3},{3,2},{4,5},{5,4},{6,7},{7,6},{8,9},{9,8},{10,11... | collective-permute-start | bytes 1769480 | tf_op jit(solution)/shard_map/ppermute | solution.py:41
  91.3 12.6 %collective-permute-start.29 = (bf16[4,192,384]{2,1,0:T(8,128)(2,1)S(1)}, bf16[4,192,384]{2,1,0:T(8,128)(2,1)S(1)}, u32[]{:S(2)}, u32[]{:S(2)}) collective-permute-start(bf16[4,192,384]{2,1,0:T(8,128)(2,1)S(1)} %collective-permute-done.25.refs_2_), channel_id=1, source_target_pairs={{0,1},{1,0},{2,3},{3,2},{4,5},{5,4},{6,7},{7,6},{8,9},{9,8},{10,11... | collective-permute-start | bytes 1769480 | tf_op jit(solution)/shard_map/ppermute | solution.py:41
  93.0 12.2 %collective-permute-start.20 = (bf16[4,48,1536]{2,1,0:T(8,128)(2,1)S(1)}, bf16[4,48,1536]{2,1,0:T(8,128)(2,1)S(1)}, u32[]{:S(2)}, u32[]{:S(2)}) collective-permute-start(bf16[4,48,1536]{2,1,0:T(8,128)(2,1)S(1)} %collective-permute-done.16.refs_3_), channel_id=1, source_target_pairs={{0,1},{1,0},{2,3},{3,2},{4,5},{5,4},{6,7},{7,6},{8,9},{9,8},{10,11... | collective-permute-start | bytes 1769480 | tf_op jit(solution)/shard_map/ppermute | solution.py:41
  102.5 13.8 %collective-permute-start.7 = (bf16[4,48,1664]{2,1,0:T(8,128)(2,1)S(1)}, bf16[4,48,1664]{2,1,0:T(8,128)(2,1)}, u32[]{:S(2)}, u32[]{:S(2)}) collective-permute-start(bf16[4,48,1664]{2,1,0:T(8,128)(2,1)S(1)} %pad_maximum_fusion.4.refs_0_), channel_id=1, source_target_pairs={{0,1},{1,0},{2,3},{3,2},{4,5},{5,4},{6,7},{7,6},{8,9},{9,8},{10,11... | collective-permute-start | bytes 1916936 | tf_op jit(solution)/shard_map/ppermute | solution.py:41
  103.4 12.8 %collective-permute-start.8 = (bf16[4,48,1664]{2,1,0:T(8,128)(2,1)S(1)}, bf16[4,48,1664]{2,1,0:T(8,128)(2,1)}, u32[]{:S(2)}, u32[]{:S(2)}) collective-permute-start(bf16[4,48,1664]{2,1,0:T(8,128)(2,1)S(1)} %collective-permute-done.4.refs_1_), channel_id=1, source_target_pairs={{0,1},{1,0},{2,3},{3,2},{4,5},{5,4},{6,7},{7,6},{8,9},{9,8},{10,11... | collective-permute-start | bytes 1916936 | tf_op jit(solution)/shard_map/ppermute | solution.py:41
  104.7 11.6 %collective-permute-start.9 = (bf16[4,48,1664]{2,1,0:T(8,128)(2,1)S(1)}, bf16[4,48,1664]{2,1,0:T(8,128)(2,1)}, u32[]{:S(2)}, u32[]{:S(2)}) collective-permute-start(bf16[4,48,1664]{2,1,0:T(8,128)(2,1)S(1)} %collective-permute-done.5.refs_2_), channel_id=1, source_target_pairs={{0,1},{1,0},{2,3},{3,2},{4,5},{5,4},{6,7},{7,6},{8,9},{9,8},{10,11... | collective-permute-start | bytes 1916936 | tf_op jit(solution)/shard_map/ppermute | solution.py:41
  104.8 11.5 %collective-permute-start.10 = (bf16[4,48,1664]{2,1,0:T(8,128)(2,1)}, bf16[4,48,1664]{2,1,0:T(8,128)(2,1)}, u32[]{:S(2)}, u32[]{:S(2)}) collective-permute-start(bf16[4,48,1664]{2,1,0:T(8,128)(2,1)} %collective-permute-done.6.refs_3_), channel_id=1, source_target_pairs={{0,1},{1,0},{2,3},{3,2},{4,5},{5,4},{6,7},{7,6},{8,9},{9,8},{10,11... | collective-permute-start | bytes 1916936 | tf_op jit(solution)/shard_map/ppermute | solution.py:41
  182.6 19.1 %collective-permute-start.32 = (bf16[512,768]{1,0:T(8,128)(2,1)}, bf16[512,768]{1,0:T(8,128)(2,1)}, u32[]{:S(2)}, u32[]{:S(2)}) collective-permute-start(bf16[512,768]{1,0:T(8,128)(2,1)} %get-tuple-element.134), channel_id=1, source_target_pairs={{0,8},{1,9},{2,10},{3,11},{4,12},{5,13},{6,14},{7,15},{8,0},{9,1},... | collective-permute-start | bytes 2359304 | tf_op jit(solution)/shard_map/ppermute | solution.py:41
  194.1 9.0 %collective-permute-start.37 = (bf16[8,48,896]{2,1,0:T(8,128)(2,1)}, bf16[8,48,896]{2,1,0:T(8,128)(2,1)}, u32[]{:S(2)}, u32[]{:S(2)}) collective-permute-start(bf16[8,48,896]{2,1,0:T(8,128)(2,1)} %pad_maximum_fusion.3), channel_id=1, source_target_pairs={{0,1},{1,0},{2,3},{3,2},{4,5},{5,4},{6,7},{7,6},{8,9},{9,8},{10,11... | collective-permute-start | bytes 2064392 | tf_op jit(solution)/shard_map/ppermute | solution.py:41
  283.4 19.4 %collective-permute-start.53 = (bf16[16,192,384]{2,1,0:T(8,128)(2,1)}, bf16[16,192,384]{2,1,0:T(8,128)(2,1)}, u32[]{:S(2)}, u32[]{:S(2)}) collective-permute-start(bf16[16,192,384]{2,1,0:T(8,128)(2,1)} %constant_dynamic-slice_fusion), channel_id=1, source_target_pairs={{0,1},{1,0},{2,3},{3,2},{4,5},{5,4},{6,7},{7,6},{8,9},{9,8},{10,11... | collective-permute-start | bytes 7077896 | tf_op jit(solution)/shard_map/ppermute | solution.py:41
  285.1 26.6 %collective-permute-start.46 = (bf16[16,48,1536]{2,1,0:T(8,128)(2,1)}, bf16[16,48,1536]{2,1,0:T(8,128)(2,1)}, u32[]{:S(2)}, u32[]{:S(2)}) collective-permute-start(bf16[16,48,1536]{2,1,0:T(8,128)(2,1)} %constant_dynamic-slice_fusion.1), channel_id=1, source_target_pairs={{0,1},{1,0},{2,3},{3,2},{4,5},{5,4},{6,7},{7,6},{8,9},{9,8},{10,11... | collective-permute-start | bytes 7077896 | tf_op jit(solution)/shard_map/ppermute | solution.py:41
  302.7 14.5 %collective-permute-start.39 = (bf16[16,48,1664]{2,1,0:T(8,128)(2,1)}, bf16[16,48,1664]{2,1,0:T(8,128)(2,1)S(1)}, u32[]{:S(2)}, u32[]{:S(2)}) collective-permute-start(bf16[16,48,1664]{2,1,0:T(8,128)(2,1)} %constant_dynamic-slice_fusion.2), channel_id=1, source_target_pairs={{0,1},{1,0},{2,3},{3,2},{4,5},{5,4},{6,7},{7,6},{8,9},{9,8},{10,11... | collective-permute-start | bytes 7667720 | tf_op jit(solution)/shard_map/ppermute | solution.py:41
  308.7 26.7 %collective-permute-start.54 = (bf16[8,192,384]{2,1,0:T(8,128)(2,1)}, bf16[8,192,384]{2,1,0:T(8,128)(2,1)}, u32[]{:S(2)}, u32[]{:S(2)}) collective-permute-start(bf16[8,192,384]{2,1,0:T(8,128)(2,1)} %get-tuple-element.72), channel_id=1, source_target_pairs={{0,2},{1,5},{2,0},{3,7},{4,6},{5,1},{6,4},{7,3},{8,10},{9,13},{10,... | collective-permute-start | bytes 3538952 | tf_op jit(solution)/shard_map/ppermute | solution.py:41
  311.5 20.4 %collective-permute-start.31 = (bf16[512,768]{1,0:T(8,128)(2,1)}, bf16[512,768]{1,0:T(8,128)(2,1)}, u32[]{:S(2)}, u32[]{:S(2)}) collective-permute-start(bf16[512,768]{1,0:T(8,128)(2,1)} %slice.162), channel_id=1, source_target_pairs={{0,8},{1,9},{2,10},{3,11},{4,12},{5,13},{6,14},{7,15},{8,0},{9,1},... | collective-permute-start | bytes 2359304 | tf_op jit(solution)/shard_map/ppermute | solution.py:41
  315.8 22.7 %collective-permute-start.47 = (bf16[8,48,1536]{2,1,0:T(8,128)(2,1)}, bf16[8,48,1536]{2,1,0:T(8,128)(2,1)}, u32[]{:S(2)}, u32[]{:S(2)}) collective-permute-start(bf16[8,48,1536]{2,1,0:T(8,128)(2,1)} %get-tuple-element.70), channel_id=1, source_target_pairs={{0,2},{1,5},{2,0},{3,7},{4,6},{5,1},{6,4},{7,3},{8,10},{9,13},{10,... | collective-permute-start | bytes 3538952 | tf_op jit(solution)/shard_map/ppermute | solution.py:41
  320.4 42.5 %collective-permute-start.40 = (bf16[8,48,1664]{2,1,0:T(8,128)(2,1)}, bf16[8,48,1664]{2,1,0:T(8,128)(2,1)S(1)}, u32[]{:S(2)}, u32[]{:S(2)}) collective-permute-start(bf16[8,48,1664]{2,1,0:T(8,128)(2,1)} %get-tuple-element.68), channel_id=1, source_target_pairs={{0,2},{1,5},{2,0},{3,7},{4,6},{5,1},{6,4},{7,3},{8,10},{9,13},{10,... | collective-permute-start | bytes 3833864 | tf_op jit(solution)/shard_map/ppermute | solution.py:41
  334.5 57.1 %collective-permute-start.38 = (bf16[512,768]{1,0:T(8,128)(2,1)S(1)}, bf16[512,768]{1,0:T(8,128)(2,1)S(1)}, u32[]{:S(2)}, u32[]{:S(2)}) collective-permute-start(bf16[512,768]{1,0:T(8,128)(2,1)S(1)} %copy-done.56), channel_id=1, source_target_pairs={{0,8},{1,9},{2,10},{3,11},{4,12},{5,13},{6,14},{7,15},{8,0},{9,1},... | collective-permute-start | bytes 2359304 | tf_op jit(solution)/shard_map/ppermute | solution.py:41
  337.1 29.2 %collective-permute-start.55 = (bf16[4,192,384]{2,1,0:T(8,128)(2,1)S(1)}, bf16[4,192,384]{2,1,0:T(8,128)(2,1)S(1)}, u32[]{:S(2)}, u32[]{:S(2)}) collective-permute-start(bf16[4,192,384]{2,1,0:T(8,128)(2,1)S(1)} %get-tuple-element.126), channel_id=1, source_target_pairs={{0,4},{1,3},{2,6},{3,1},{4,0},{5,7},{6,2},{7,5},{8,12},{9,11},{10,... | collective-permute-start | bytes 1769480 | tf_op jit(solution)/shard_map/ppermute | solution.py:41
  340.2 28.6 %collective-permute-start.48 = (bf16[4,48,1536]{2,1,0:T(8,128)(2,1)S(1)}, bf16[4,48,1536]{2,1,0:T(8,128)(2,1)S(1)}, u32[]{:S(2)}, u32[]{:S(2)}) collective-permute-start(bf16[4,48,1536]{2,1,0:T(8,128)(2,1)S(1)} %get-tuple-element.128), channel_id=1, source_target_pairs={{0,4},{1,3},{2,6},{3,1},{4,0},{5,7},{6,2},{7,5},{8,12},{9,11},{10,... | collective-permute-start | bytes 1769480 | tf_op jit(solution)/shard_map/ppermute | solution.py:41
  363.3 26.6 %collective-permute-start.41 = (bf16[4,48,1664]{2,1,0:T(8,128)(2,1)S(1)}, bf16[4,48,1664]{2,1,0:T(8,128)(2,1)S(1)}, u32[]{:S(2)}, u32[]{:S(2)}) collective-permute-start(bf16[4,48,1664]{2,1,0:T(8,128)(2,1)S(1)} %get-tuple-element.124), channel_id=1, source_target_pairs={{0,4},{1,3},{2,6},{3,1},{4,0},{5,7},{6,2},{7,5},{8,12},{9,11},{10,... | collective-permute-start | bytes 1916936 | tf_op jit(solution)/shard_map/ppermute | solution.py:41
  366.4 13.6 %collective-permute-start.56 = (bf16[192,384]{1,0:T(8,128)(2,1)S(1)}, bf16[192,384]{1,0:T(8,128)(2,1)S(1)}, u32[]{:S(2)}, u32[]{:S(2)}) collective-permute-start(bf16[192,384]{1,0:T(8,128)(2,1)S(1)} %get-tuple-element.140), channel_id=1, source_target_pairs={{0,16},{1,17},{2,18},{3,19},{4,20},{5,21},{6,22},{7,23},{8,24},{9,... | collective-permute-start | bytes 442376 | tf_op jit(solution)/shard_map/ppermute | solution.py:41
  366.5 13.6 %collective-permute-start.57 = (bf16[192,384]{1,0:T(8,128)(2,1)S(1)}, bf16[192,384]{1,0:T(8,128)(2,1)S(1)}, u32[]{:S(2)}, u32[]{:S(2)}) collective-permute-start(bf16[192,384]{1,0:T(8,128)(2,1)S(1)} %get-tuple-element.142), channel_id=1, source_target_pairs={{0,8},{1,9},{2,10},{3,11},{4,12},{5,13},{6,14},{7,15},{8,0},{9,1},... | collective-permute-start | bytes 442376 | tf_op jit(solution)/shard_map/ppermute | solution.py:41
  368.8 13.8 %collective-permute-start.58 = (bf16[192,384]{1,0:T(8,128)(2,1)S(1)}, bf16[192,384]{1,0:T(8,128)(2,1)S(1)}, u32[]{:S(2)}, u32[]{:S(2)}) collective-permute-start(bf16[192,384]{1,0:T(8,128)(2,1)S(1)} %get-tuple-element.141), channel_id=1, source_target_pairs={{0,24},{1,25},{2,26},{3,27},{4,28},{5,29},{6,30},{7,31},{8,16},{9,... | collective-permute-start | bytes 442376 | tf_op jit(solution)/shard_map/ppermute | solution.py:41
  387.4 9.0 %collective-permute-start.59 = (bf16[2,192,384]{2,1,0:T(8,128)(2,1)S(1)}, bf16[2,192,384]{2,1,0:T(8,128)(2,1)S(1)}, u32[]{:S(2)}, u32[]{:S(2)}) collective-permute-start(bf16[2,192,384]{2,1,0:T(8,128)(2,1)S(1)} %get-tuple-element.118), channel_id=1, source_target_pairs={{0,1},{1,0},{2,3},{3,2},{4,5},{5,4},{6,7},{7,6},{8,9},{9,8},{10,11... | collective-permute-start | bytes 884744 | tf_op jit(solution)/shard_map/ppermute | solution.py:41
  390.0 11.3 %collective-permute-start.42 = (bf16[48,1664]{1,0:T(8,128)(2,1)S(1)}, bf16[48,1664]{1,0:T(8,128)(2,1)S(1)}, u32[]{:S(2)}, u32[]{:S(2)}) collective-permute-start(bf16[48,1664]{1,0:T(8,128)(2,1)S(1)} %get-tuple-element.137), channel_id=1, source_target_pairs={{0,16},{1,17},{2,18},{3,19},{4,20},{5,21},{6,22},{7,23},{8,24},{9,... | collective-permute-start | bytes 479240 | tf_op jit(solution)/shard_map/ppermute | solution.py:41
  393.5 12.0 %collective-permute-start.43 = (bf16[48,1664]{1,0:T(8,128)(2,1)S(1)}, bf16[48,1664]{1,0:T(8,128)(2,1)S(1)}, u32[]{:S(2)}, u32[]{:S(2)}) collective-permute-start(bf16[48,1664]{1,0:T(8,128)(2,1)S(1)} %get-tuple-element.139), channel_id=1, source_target_pairs={{0,8},{1,9},{2,10},{3,11},{4,12},{5,13},{6,14},{7,15},{8,0},{9,1},... | collective-permute-start | bytes 479240 | tf_op jit(solution)/shard_map/ppermute | solution.py:41
  394.5 11.0 %collective-permute-start.44 = (bf16[48,1664]{1,0:T(8,128)(2,1)S(1)}, bf16[48,1664]{1,0:T(8,128)(2,1)S(1)}, u32[]{:S(2)}, u32[]{:S(2)}) collective-permute-start(bf16[48,1664]{1,0:T(8,128)(2,1)S(1)} %get-tuple-element.138), channel_id=1, source_target_pairs={{0,24},{1,25},{2,26},{3,27},{4,28},{5,29},{6,30},{7,31},{8,16},{9,... | collective-permute-start | bytes 479240 | tf_op jit(solution)/shard_map/ppermute | solution.py:41
  (75 other events, 596.3 us)

commit v2 on v1

v2 whole, which is shorter than its diff:
```python
from functools import partial

import jax
import jax.numpy as jnp
from jax import lax
from jax.experimental import pallas as pl
from jax.experimental.pallas import tpu as pltpu
from jax.sharding import PartitionSpec as P

AXES = ("dp", "rep")
BF = jnp.bfloat16
F32 = jnp.float32
D = 768
FF = 3072
HEADS = 12
HEAD = 64
PAIRS = HEADS // 2
BLOCK = 128
TILE = 256
EPS = 1e-05
LOSS_WEIGHT = 32.0
MIB = 2**20
AT_OUT = 3 * D
AT_VEC = 4 * D
W_ONE = 4 * D + 256


def smem():
    return pl.BlockSpec(memory_space=pltpu.SMEM)


def vmem():
    return pl.BlockSpec(memory_space=pltpu.VMEM)


def cost(us):
    return pl.CostEstimate(flops=int(us * 1.0e9), transcendentals=0, bytes_accessed=int(us * 3.0e6))


def params(mib):
    return pltpu.CompilerParams(vmem_limit_bytes=mib * MIB)


def still(shape, at=None):
    index = at if at is not None else (0,) * len(shape)
    return pl.BlockSpec(shape, lambda i, *_: index, pipeline_mode=pl.Buffered(1))


def rows_at(width, rows=TILE):
    return pl.BlockSpec((rows, width), lambda i, *_: (i, 0))


def shape(dims, dtype):
    return jax.ShapeDtypeStruct(dims, dtype)


def far(dims, dtype):
    return pltpu.HBM(dims, dtype)


def stay(v):
    return pltpu.with_memory_space_constraint(v, pltpu.HBM)


def after(v, *others):
    return lax.optimization_barrier((v,) + others)[0]


class Order:
    def __init__(self, where):
        self.where = where

    def done(self, out):
        self.where = after(self.where, out)
        return out


def halves(ref_pairs, core, width, source):
    for q, ref in enumerate(ref_pairs):
        at = pl.multiple_of((core ^ q) * width, 128)
        ref[...] = source[:, pl.ds(at, width)]


def send(v, pairs):
    return lax.ppermute(v, AXES, pairs)


class Plan:
    def __init__(self, n, reps):
        self.n, self.reps, self.depth = n, reps, n // 4

    def pairs(self, move):
        return [
            (d * self.reps + r, (d ^ move(r)[0]) * self.reps + (r ^ move(r)[1]))
            for d in range(self.n)
            for r in range(self.reps)
        ]

    def along(self, k):
        return self.pairs(lambda r: (4 * k, 0))

    def first(self):
        return self.pairs(lambda r: (1 + r % 2, 0))

    def second(self):
        return self.pairs(lambda r: (2 - r % 2, 0))

    def sibling(self, q):
        return self.pairs(lambda r: (0, q))


def assemble_kernel(depth, reps, width, where_ref, *refs):
    bufs, out = refs[: 2 * reps], refs[2 * reps]
    me, core = where_ref[0], where_ref[1]
    for q in range(reps):
        owner = core ^ q
        p1 = 1 + owner % 2
        p2 = 2 - owner % 2
        lanes = pl.ds(pl.multiple_of(owner * width, 128), width)
        for b in range(2):
            for f in range(2):
                for k in range(depth):
                    dst = (me ^ (b * p2) ^ (f * p1)) ^ (4 * k)
                    out[pl.ds(dst, 1), :, lanes] = bufs[q * 2 + b][pl.ds(f * depth + k, 1)]


def shards_of(plan, where, shard):
    core, tower = where[1], where[2]
    rows, whole = shard.shape[1:]
    width = whole // plan.reps
    mine = lax.dynamic_slice(shard, (tower, 0, core * width), (1, rows, width))
    other = lax.dynamic_slice(shard, (1 - tower, 0, core * width), (1, rows, width))
    return mine, other


def gather_line(plan, mine, other):
    got = [send(other if k % 2 else mine, plan.along(k)) for k in range(1, plan.depth)]
    return jnp.concatenate([mine] + got, 0)


def gather_steps(plan, both, *others):
    z = both
    k = 2
    while k < plan.depth:
        if others:
            z, others = after(z, *others), ()
        z = jnp.concatenate([z, send(z, plan.along(k))], 0)
        k *= 2
    return z


def gather_plane(plan, z, *others):
    near = jnp.concatenate([z, send(z, plan.first())], 0)
    if others:
        near = after(near, *others)
    return near, send(near, plan.second())


def gather_cores(plan, order, bufs):
    rows, width = bufs[0].shape[1:]
    bufs = list(bufs)
    for q in range(1, plan.reps):
        bufs += [send(b, plan.sibling(q)) for b in bufs[:2]]
    full = pl.pallas_call(
        partial(assemble_kernel, plan.depth, plan.reps, width),
        out_shape=jax.ShapeDtypeStruct((plan.n, rows, width * plan.reps), BF),
        in_specs=[smem()] + [vmem()] * len(bufs),
        out_specs=vmem(),
        compiler_params=params(24),
        name="assemble",
        cost_estimate=cost(2),
    )(order.where, *bufs)
    order.done(full)
    return full.reshape(plan.n * rows, width * plan.reps)


def add_kernel(depth, where_ref, a_hbm, b_ref, s_ref, k_ref, a_ref, sem):
    me, core = where_ref[0], where_ref[1]
    p1 = 1 + core % 2
    p2 = 2 - core % 2
    copies = []
    for j in range(4 * depth):
        at = me ^ ((1 - j // (2 * depth)) * p1) ^ ((1 - j // depth % 2) * p2) ^ (4 * (j % depth))
        copy = pltpu.make_async_copy(a_hbm.at[at], a_ref.at[j], sem.at[j])
        copy.start()
        copies.append((at, copy))
    for j, (at, copy) in enumerate(copies):
        copy.wait()
        o_ref, to = (s_ref, j) if j < 2 * depth else (k_ref, j - 2 * depth)
        o_ref[to] = (a_ref[j].astype(F32) + b_ref[at].astype(F32)).astype(BF)


def two_kernel(where_ref, k_ref, r_ref, s_ref, o_ref):
    q = s_ref.shape[0]
    for j in range(2 * q):
        total = (k_ref[j].astype(F32) + r_ref[j].astype(F32)).astype(BF)
        if j < q:
            s_ref[j] = total
        else:
            o_ref[j - q] = total


def line_kernel(where_ref, k_ref, r_ref, s_ref, o_ref):
    half = o_ref.shape[0]
    for j in range(2 * half):
        total = (k_ref[j].astype(F32) + r_ref[j].astype(F32)).astype(BF)
        if j < half:
            o_ref[j] = total
        else:
            s_ref[j - half] = total


def last_kernel(where_ref, own_ref, got_ref, out):
    tower = where_ref[2]
    out[pl.ds(tower, 1)] = own_ref[...]
    out[pl.ds(1 - tower, 1)] = got_ref[...]


def plus(a, b):
    return (a.astype(F32) + b.astype(F32)).astype(BF)


def in_vmem(kernel, name, us, outs, *args, mib=24):
    return pl.pallas_call(
        kernel,
        out_shape=tuple(shape(*o) for o in outs),
        in_specs=[smem() if a.ndim == 1 else vmem() for a in args],
        out_specs=tuple(vmem() for _ in outs),
        compiler_params=params(mib),
        name=name,
        cost_estimate=cost(us),
    )(*args)


class Scatter:
    def __init__(self, plan, order, parts, rows):
        self.plan, self.order, self.rows = plan, order, rows
        self.width = parts[0].shape[1]
        parts = [p.reshape(plan.n, rows, self.width) for p in parts]
        self.own = parts[0]
        got = [send(parts[q], plan.sibling(q)) for q in range(1, plan.reps)]
        self.rest = got[0]
        for o in got[1:]:
            self.rest = plus(self.rest, o)

    def run(self, kernel, name, us, outs, *args):
        return self.order.done(in_vmem(kernel, name, us, outs, self.order.where, *args))

    def one(self):
        plan = self.plan
        n = plan.n
        whole = (n, self.rows, self.width)
        half = shape((n // 2, self.rows, self.width), BF)
        hs, self.hk = self.order.done(
            pl.pallas_call(
                partial(add_kernel, plan.depth),
                out_shape=(half, half),
                in_specs=[smem(), pl.BlockSpec(memory_space=pl.ANY), vmem()],
                out_specs=(vmem(), vmem()),
                scratch_shapes=[pltpu.VMEM(whole, BF), pltpu.SemaphoreType.DMA((n,))],
                compiler_params=params(24),
                name="pick_add",
                cost_estimate=cost(3),
            )(self.order.where, stay(self.own), self.rest)
        )
        self.r1 = send(hs, plan.first())

    def two(self):
        quarter = ((self.plan.n // 4, self.rows, self.width), BF)
        ks, self.kk = self.run(two_kernel, "add_two", 1, (quarter, quarter), self.hk, self.r1)
        self.r2 = send(ks, self.plan.second())

    def line(self):
        n = self.kk.shape[0] // 2
        half = ((n, self.rows, self.width), BF)
        out, self.kk = self.run(line_kernel, "add_line", 1, (half, half), self.kk, self.r2)
        self.r2 = send(out, self.plan.along(n))
        return out

    def three(self):
        self.line()

    def four(self):
        while self.kk.shape[0] > 1:
            self.out = self.line()

    def last(self):
        plan = self.plan
        outs = (((2, self.rows, self.width), BF),)
        (pair,) = self.run(last_kernel, "add_last", 1, outs, self.kk, self.r2)
        self.ends = [pair] + [send(pair, plan.sibling(q)) for q in range(1, plan.reps)]


def finish_kernel(reps, spans, where_ref, *refs):
    chunks = len(spans)
    ins, outs = refs[: chunks * reps], refs[chunks * reps :]
    core = where_ref[1]
    for c in range(chunks):
        parts = ins[c * reps : (c + 1) * reps]
        width = parts[0].shape[2]
        for q in range(reps):
            for mine in range(reps):

                @pl.when((core ^ q) == mine)
                def copy(q=q, mine=mine):
                    for at, size, out, to in spans[c]:
                        low, high = max(at, mine * width), min(at + size, (mine + 1) * width)
                        if low < high:
                            outs[out][:, :, to + low - at : to + high - at] = parts[q][
                                :, :, low - mine * width : high - mine * width
                            ].astype(F32)


def finish(plan, order, chunks, spans, widths):
    rows = chunks[0].rows
    outs = tuple(((2, rows, w), F32) for w in widths)
    args = [p for c in chunks for p in c.ends]
    return order.done(in_vmem(partial(finish_kernel, plan.reps, spans), "finish", 2, outs, order.where, *args))


def dot(a, b):
    return jnp.dot(a, b, preferred_element_type=F32)


def dot_t(a, b):
    return lax.dot_general(a, b, (((1,), (1,)), ((), ())), preferred_element_type=F32)


def t_dot(a, b):
    return lax.dot_general(a, b, (((0,), (0,)), ((), ())), preferred_element_type=F32)


def normalize(h):
    center = h - jnp.mean(h, -1, keepdims=True)
    rstd = lax.rsqrt(jnp.mean(center * center, -1, keepdims=True) + EPS)
    return center * rstd, rstd


def lane_masks():
    lane = lax.broadcasted_iota(jnp.int32, (1, 2 * HEAD), 1)
    low = (lane < HEAD).astype(F32).astype(BF)
    return low, (1.0 - low.astype(F32)).astype(BF)


def attend_kernel(part, where_ref, x_ref, w_ref, *rest):
    proj_ref, probs_ref, attn_ref, hat_ref, rstd_ref, norm_ref, vec_ref, bias_ref = rest[-8:]

    @pl.when(pl.program_id(0) == 0)
    def prepare():
        vec_ref[...] = jnp.transpose(w_ref[:, AT_VEC : AT_VEC + 128].astype(F32))
        span = where_ref[3]
        row = lax.broadcasted_iota(jnp.int32, (2 * BLOCK, BLOCK), 0) % BLOCK
        col = lax.broadcasted_iota(jnp.int32, (2 * BLOCK, BLOCK), 1)
        bias_ref[...] = jnp.where((row ^ col) < span, 0.0, -1e30)

    x = x_ref[...]
    for j in range(3):
        part = dot(x, w_ref[:, j * D : (j + 1) * D])
        if j != 1:
            part = part + vec_ref[j // 2 : j // 2 + 1, :]
        proj_ref[:, j * D : (j + 1) * D] = part.astype(BF)
    low, high = lane_masks()
    bias = bias_ref[...]
    for blk in range(TILE // BLOCK):
        rows = slice(blk * BLOCK, (blk + 1) * BLOCK)
        for pair in range(PAIRS):
            lanes = slice(pair * 128, (pair + 1) * 128)
            q = proj_ref[rows, lanes]
            k = proj_ref[rows, D + pair * 128 : D + (pair + 1) * 128]
            v = proj_ref[rows, 2 * D + pair * 128 : 2 * D + (pair + 1) * 128]
            s = dot_t(jnp.concatenate([q * low, q * high], 0), k) * HEAD**-0.5 + bias
            e = jnp.exp(s - jnp.max(s, -1, keepdims=True))
            p = (e * (1.0 / jnp.sum(e, -1, keepdims=True))).astype(BF)
            probs_ref[blk, pair] = p
            wide = jnp.concatenate([p[:BLOCK], p[BLOCK:]], 1)
            attn_ref[rows, lanes] = dot(wide, jnp.concatenate([v * low, v * high], 0)).astype(BF)
    hidden = x.astype(F32) + (dot(attn_ref[...], w_ref[:, AT_OUT:AT_VEC]) + vec_ref[2:3, :])
    hat, rstd = normalize(hidden)
    hat_ref[...] = hat
    rstd_ref[...] = rstd
    norm_ref[...] = (hat * vec_ref[10:11, :] + vec_ref[3:4, :]).astype(BF)


def attend(order, x, w_one, part, before=()):
    rows = x.shape[0]
    per = TILE // BLOCK
    steps = rows // TILE // 2
    first = part * steps

    def here(width):
        return pl.BlockSpec((TILE, width), lambda i: (i + first, 0))

    return pl.pallas_call(
        partial(attend_kernel, part),
        grid=(steps,),
        out_shape=(
            far((rows, 3 * D), BF),
            far((rows // BLOCK, PAIRS, 2 * BLOCK, BLOCK), BF),
            far((rows, D), BF),
            far((rows, D), F32),
            far((rows, 1), F32),
            far((rows, D), BF),
            shape((128, D), F32),
        ),
        in_specs=[smem(), here(D), still(w_one.shape)] + [pl.BlockSpec(memory_space=pl.ANY)] * len(before),
        out_specs=[
            here(3 * D),
            pl.BlockSpec((per, PAIRS, 2 * BLOCK, BLOCK), lambda i: (i + first, 0, 0, 0)),
            here(D),
            here(D),
            here(1),
            here(D),
            still((128, D)),
        ],
        scratch_shapes=[pltpu.VMEM((2 * BLOCK, BLOCK), F32)],
        input_output_aliases={3 + j: j for j in range(len(before))},
        compiler_params=params(24),
        name="attend",
        cost_estimate=cost(7),
    )(order.where, x, w_one, *[stay(b) for b in before])


def gelu_pair(u):
    t = 1.0 / (1.0 + (0.3275911 * 2**-0.5) * jnp.abs(u))
    e = jnp.exp(-0.5 * u * u)
    poly = t * (
        0.5 * 0.254829592
        + t * (0.5 * -0.284496736 + t * (0.5 * 1.421413741 + t * (0.5 * -1.453152027 + t * (0.5 * 1.061405429))))
    )
    tail = poly * e
    phi = jnp.where(u < 0, tail, 1.0 - tail)
    return u * phi, phi + u * (e * 0.3989422804014327)


def up_kernel(first, where_ref, norm_ref, w_ref, vec_ref, *rest):
    act_ref, slope_ref = rest[-2:]
    bias = vec_ref[pl.ds(4 + first + pl.program_id(0), 1), :]
    for m in range(0, norm_ref.shape[0], TILE):
        rows = slice(m, m + TILE)
        act, slope = gelu_pair(dot(norm_ref[rows, :], w_ref[...]) + bias)
        act_ref[rows, :] = act.astype(BF)
        slope_ref[rows, :] = slope.astype(BF)


def up(order, norm, w_up, vec, part, before=()):
    rows = norm.shape[0]
    steps = FF // D // 2
    first = part * steps
    col = pl.BlockSpec((rows, D), lambda i: (0, i + first))
    return pl.pallas_call(
        partial(up_kernel, first),
        grid=(steps,),
        out_shape=(far((rows, FF), BF), far((rows, FF), BF)),
        in_specs=[
            smem(),
            still(norm.shape),
            pl.BlockSpec((D, D), lambda i: (0, i + first)),
            still(vec.shape),
        ]
        + [pl.BlockSpec(memory_space=pl.ANY)] * len(before),
        out_specs=[col, col],
        input_output_aliases={4 + j: j for j in range(len(before))},
        compiler_params=params(24),
        name="up",
        cost_estimate=cost(8),
    )(order.where, norm, w_up, vec, *[stay(b) for b in before])


def down_kernel(where_ref, act_ref, w_ref, hat_ref, vec_ref, out_ref, hat2_ref, rstd2_ref, cls_ref):
    normed = hat_ref[...] * vec_ref[10:11, :] + vec_ref[3:4, :]
    second = normed + (dot(act_ref[...], w_ref[...]) + vec_ref[8:9, :])
    hat, rstd = normalize(second)
    hat2_ref[...] = hat
    rstd2_ref[...] = rstd
    out = hat * vec_ref[11:12, :] + vec_ref[9:10, :]
    out_ref[...] = out.astype(BF)
    for j in range(TILE // 32):
        cls_ref[j : j + 1, :] = out[32 * j : 32 * j + 1, :]


def down(order, act, w_down, hat, vec):
    rows = act.shape[0]
    return pl.pallas_call(
        down_kernel,
        grid=(rows // TILE,),
        out_shape=(far((rows, D), BF), far((rows, D), F32), far((rows, 1), F32), shape((rows // 32, D), F32)),
        in_specs=[smem(), rows_at(FF), still(w_down.shape), rows_at(D), still(vec.shape)],
        out_specs=[rows_at(D), rows_at(D), rows_at(1), rows_at(D, TILE // 32)],
        compiler_params=params(24),
        name="down",
        cost_estimate=cost(8),
    )(order.where, stay(act), w_down, hat, vec)


def contrast_kernel(reps, depth, per, where_ref, q_ref, p_ref, loss_ref, grad_ref, acc_ref):
    i = pl.program_id(0)
    me, core, tower = where_ref[0], where_ref[1], where_ref[2]
    pieces = p_ref.shape[0]
    total_p = pieces * per * 2
    cls_q = q_ref[:, :32, :D].reshape(-1, D)
    marks = q_ref[:, :32, D:].reshape(-1, q_ref.shape[2] - D)
    cls_p = p_ref[:, 32:, :D].reshape(-1, D)
    cols = cls_p.shape[0]
    col = lax.broadcasted_iota(jnp.int32, (marks.shape[1], cols), 1)
    row = lax.broadcasted_iota(jnp.int32, (marks.shape[1], cols), 0)
    j, slot = col // 16, col % 16
    line = j % (depth // 2)
    flip = (j // (depth // 2)) % 4
    from_core = core ^ (j // (2 * depth))
    base = (me | 4) ^ (8 * line) ^ flip
    owner = jnp.where(slot < per, base, base ^ 4)
    passage = (owner * reps + from_core) * per + slot % per
    good = slot < 2 * per
    pick = jnp.where((row == passage) & good, 1.0, 0.0).astype(BF)
    marked_cols = dot(marks, pick)
    valid = lax.broadcasted_iota(jnp.int32, (1, cols), 1) % 16 < 2 * per
    raw = jnp.where(valid, dot_t(cls_q, cls_p) * D**-0.5, -1e30)
    e = jnp.exp(raw - jnp.max(raw, -1, keepdims=True))
    total = jnp.sum(e, -1, keepdims=True)
    me_ = marked_cols * e
    marked = jnp.sum(me_, -1, keepdims=True)
    grad = (LOSS_WEIGHT * (e / total - me_ / marked)).astype(BF)
    part = t_dot(grad[:, :128], cls_q) * D**-0.5

    @pl.when(i == 0)
    def first():
        loss_ref[...] = (jnp.log(total) - jnp.log(marked))[:32]
        acc_ref[...] = jnp.zeros_like(acc_ref)
        grad_ref[...] = dot(grad[:32], cls_p) * D**-0.5

    acc_ref[...] += part

    @pl.when((i == pl.num_programs(0) - 1) & (tower == 1))
    def last():
        grad_ref[...] = jnp.zeros_like(grad_ref)
        for s in range(2 * per):
            at = s * (32 // (2 * per))
            grad_ref[at : at + 1, :] = acc_ref[s : s + 1, :]


def contrast(plan, order, cls, positives):
    where = order.where
    tower = where[2]
    queries, passages = positives.shape
    per = queries // 4
    marks = jnp.pad(positives.astype(BF), ((0, 32 - queries), (0, 0)))
    msg = jnp.concatenate([cls.astype(BF), marks], 1)
    got = [msg] + [send(msg, plan.along(k)) for k in range(1, plan.depth)]
    same, other = jnp.stack(got[0::2]), jnp.stack(got[1::2])
    zero = jnp.where(tower == 0, same, other)
    one = jnp.where(tower == 0, other, same)
    marks = jnp.concatenate([zero[:, :queries, D:], one[:, :queries, D:]], 1)
    top = jnp.concatenate([zero[:, :, :D], marks], 2)
    low = jnp.pad(one[:, :: 32 // (2 * per)], ((0, 0), (0, 16 - 2 * per), (0, 0)))
    buf = jnp.concatenate([top, low], 1)
    buf = jnp.concatenate([buf] + [send(buf, plan.pairs(lambda r, m=m: (m, 0))) for m in range(1, 4)], 0)
    buf = jnp.concatenate([buf] + [send(buf, plan.sibling(s)) for s in range(1, plan.reps)], 0)
    pieces = buf.shape[0]
    group = min(16, pieces)
    width = buf.shape[2]
    loss, grad = pl.pallas_call(
        partial(contrast_kernel, plan.reps, plan.depth, per),
        grid=(pieces // group,),
        out_shape=(jax.ShapeDtypeStruct((32, 1), F32), jax.ShapeDtypeStruct((32, D), F32)),
        in_specs=[
            smem(),
            pl.BlockSpec((group, 48, width), lambda i: (i, 0, 0)),
            still(buf.shape),
        ],
        out_specs=[still((32, 1)), still((32, D))],
        scratch_shapes=[pltpu.VMEM((128, D), F32)],
        compiler_params=params(32),
        name="contrast",
        cost_estimate=cost(2),
    )(where, buf, buf)
    loss = lax.dynamic_slice(loss, (tower * queries, 0), (queries, 1))[:, 0]
    return loss, grad


def norm_back(grad, hat, rstd, gain):
    scaled = grad * gain
    a = jnp.mean(scaled, -1, keepdims=True)
    b = jnp.mean(scaled * hat, -1, keepdims=True)
    return rstd * (scaled - a - hat * b)


def col_sum(v):
    return jnp.sum(v, 0, keepdims=True)


def top_kernel(
    reps, where_ref, cot_ref, cls_ref, hat_ref, rstd_ref, vec_ref, act_ref, second_ref, gs_ref, sums_ref, *rest
):
    parts, full_ref = rest[:-1], rest[-1]

    @pl.when(pl.program_id(0) == 0)
    def norm():
        groups = TILE // 32
        at_first = lax.broadcasted_iota(jnp.int32, (groups, 32, D), 1) == 0
        sums_ref[...] = jnp.zeros_like(sums_ref)
        for m in range(0, cot_ref.shape[0], TILE):
            rows = slice(m, m + TILE)
            cls = cls_ref[m // 32 : (m + TILE) // 32, :].reshape(groups, 1, D)
            dout = cot_ref[rows, :].astype(F32) + jnp.where(at_first, cls, 0.0).reshape(TILE, D)
            hat = hat_ref[rows, :]
            grad = norm_back(dout, hat, rstd_ref[rows, :], vec_ref[11:12, :])
            second_ref[rows, :] = grad
            gs = grad.astype(BF)
            gs_ref[rows, :] = gs
            sums_ref[0:1, :] += col_sum(gs.astype(F32))
            sums_ref[1:2, :] += col_sum(dout)
            sums_ref[2:3, :] += col_sum(dout * hat)

    full_ref[...] = t_dot(act_ref[...], gs_ref[...]).astype(BF)
    halves(parts, where_ref[1], D // reps, full_ref)


def top(plan, order, cot, cls_grad, hat2, rstd2, vec, act):
    rows = cot.shape[0]
    part = D // plan.reps
    second, gs, sums, *parts = pl.pallas_call(
        partial(top_kernel, plan.reps),
        grid=(FF // D,),
        out_shape=(far((rows, D), F32), shape((rows, D), BF), shape((8, D), F32))
        + (far((FF, part), BF),) * plan.reps,
        in_specs=[
            smem(),
            still(cot.shape),
            still(cls_grad.shape),
            still(hat2.shape),
            still(rstd2.shape),
            still(vec.shape),
            pl.BlockSpec((rows, D), lambda i: (0, i)),
        ],
        out_specs=[still((rows, D)), still((rows, D)), still((8, D))] + [rows_at(part, D)] * plan.reps,
        scratch_shapes=[pltpu.VMEM((D, D), BF)],
        compiler_params=params(28),
        name="top",
        cost_estimate=cost(11),
    )(order.where, cot, cls_grad, hat2, rstd2, vec, stay(act))
    return second, gs, sums, parts


def gelu_back_kernel(reps, column, where_ref, gs_ref, w_ref, slope_ref, norm_ref, up_ref, acc_ref, sums_ref, *rest):
    parts, gu_ref = rest[:-1], rest[-1]
    i = pl.program_id(0)
    total = jnp.zeros((1, D), F32)
    for m in range(0, gs_ref.shape[0], TILE):
        rows = slice(m, m + TILE)
        gu = (dot_t(gs_ref[rows, :], w_ref[...]) * slope_ref[rows, :].astype(F32)).astype(BF)
        gu_ref[rows, :] = gu
        total = total + col_sum(gu.astype(F32))
    sums_ref[pl.ds(column(i, where_ref), 1), :] = total
    grad = t_dot(norm_ref[...], gu_ref[...]).astype(BF)
    per = (FF // D) // reps
    for q in range(reps):

        @pl.when(i // per == reps - 1 - q)
        def put(q=q):
            parts[q][...] = grad

    @pl.when(i == 0)
    def start():
        acc_ref[...] = dot_t(gu_ref[...], up_ref[...])

    @pl.when(i > 0)
    def add():
        acc_ref[...] += dot_t(gu_ref[...], up_ref[...])


def gelu_back(plan, order, gs, w_down, slope, norm, w_up):
    rows = gs.shape[0]
    reps = plan.reps
    per = (FF // D) // reps

    def column(i, table):
        return (table[1] ^ (reps - 1 - i // per)) * per + i % per

    def held(q):
        return pl.BlockSpec((D, D), lambda i, table: (0, jnp.clip(i - (reps - 1 - q) * per, 0, per - 1)))

    acc, sums, *parts = pl.pallas_call(
        partial(gelu_back_kernel, reps, column),
        out_shape=(shape((rows, D), F32), shape((8, D), F32)) + (far((D, FF // reps), BF),) * reps,
        grid_spec=pltpu.PrefetchScalarGridSpec(
            num_scalar_prefetch=1,
            grid=(FF // D,),
            in_specs=[
                still(gs.shape),
                pl.BlockSpec((D, D), lambda i, table: (column(i, table), 0)),
                pl.BlockSpec((rows, D), lambda i, table: (0, column(i, table))),
                still(norm.shape),
                pl.BlockSpec((D, D), lambda i, table: (0, column(i, table))),
            ],
            out_specs=[still((rows, D)), still((8, D))] + [held(q) for q in range(reps)],
            scratch_shapes=[pltpu.VMEM((rows, D), BF)],
        ),
        compiler_params=params(28),
        name="gelu_back",
        cost_estimate=cost(20),
    )(order.where, gs, stay(w_down), stay(slope), norm, stay(w_up))
    return acc, sums, parts


def hidden_back_kernel(
    where_ref, acc_ref, second_ref, hat_ref, rstd_ref, w_ref, vec_ref, hidden_ref, go_ref, ga_ref, sums_ref
):
    @pl.when(pl.program_id(0) == 0)
    def clear():
        sums_ref[...] = jnp.zeros_like(sums_ref)

    grad = acc_ref[...] + second_ref[...]
    hat = hat_ref[...]
    hidden = norm_back(grad, hat, rstd_ref[...], vec_ref[10:11, :])
    hidden_ref[...] = hidden
    go = hidden.astype(BF)
    go_ref[...] = go
    sums_ref[0:1, :] += col_sum(go.astype(F32))
    sums_ref[1:2, :] += col_sum(grad)
    sums_ref[2:3, :] += col_sum(grad * hat)
    ga_ref[...] = dot_t(go, w_ref[...]).astype(BF)


def hidden_back(order, acc, second, hat, rstd, w_one, vec):
    rows = acc.shape[0]
    return pl.pallas_call(
        hidden_back_kernel,
        grid=(rows // TILE,),
        out_shape=(far((rows, D), F32), shape((rows, D), BF), shape((rows, D), BF), shape((8, D), F32)),
        in_specs=[smem()]
        + [rows_at(D)] * 3
        + [rows_at(1), still((D, D), (0, AT_OUT // D)), still(vec.shape)],
        out_specs=[rows_at(D), rows_at(D), rows_at(D), still((8, D))],
        compiler_params=params(20),
        name="hidden_back",
        cost_estimate=cost(5),
    )(order.where, acc, stay(second), stay(hat), stay(rstd), stay(w_one), vec)


def pair_back(pair, block, rows, ga_ref, proj_ref, probs_ref, low, high):
    q = proj_ref[rows, pair * 128 : (pair + 1) * 128]
    k = proj_ref[rows, D + pair * 128 : D + (pair + 1) * 128]
    v = proj_ref[rows, 2 * D + pair * 128 : 2 * D + (pair + 1) * 128]
    a = ga_ref[rows, pair * 128 : (pair + 1) * 128]
    a2 = jnp.concatenate([a * low, a * high], 0)
    q2 = jnp.concatenate([q * low, q * high], 0)
    k2 = jnp.concatenate([k * low, k * high], 0)
    p = probs_ref[block, pair]
    dp = dot_t(a2, v)
    pf = p.astype(F32)
    ds = (pf * (dp - jnp.sum(pf * dp, -1, keepdims=True)) * HEAD**-0.5).astype(BF)
    wide = jnp.concatenate([ds[:BLOCK], ds[BLOCK:]], 1)
    return dot(wide, k2).astype(BF), t_dot(ds, q2).astype(BF), t_dot(p, a2).astype(BF)


def heads_back(first, count, at, ga_ref, proj_ref, probs_ref, gp_ref):
    low, high = lane_masks()
    for block in range(TILE // BLOCK):
        rows = slice(block * BLOCK, (block + 1) * BLOCK)
        to = pl.ds(pl.multiple_of(at + block * BLOCK, BLOCK), BLOCK)
        for j in range(count):
            three = pair_back(first + j, block, rows, ga_ref, proj_ref, probs_ref, low, high)
            for n, grad in enumerate(three):
                lane = (n * count + j) * 128
                gp_ref[to, lane : lane + 128] = grad


def attend_back_kernel(
    reps, count, where_ref, ga_ref, proj_ref, probs_ref, x_ref, attn_ref, go_ref, gp_ref, sums_ref, *rest
):
    parts, full_ref = rest[:-1], rest[-1]
    i = pl.program_id(0)
    part = count * 128
    heads_back(0, count, i * TILE, ga_ref, proj_ref, probs_ref, gp_ref)

    @pl.when(i == pl.num_programs(0) - 1)
    def weights():
        sums_ref[...] = jnp.zeros_like(sums_ref)
        sums_ref[0:1, :] = col_sum(gp_ref[:, :part].astype(F32))
        sums_ref[1:2, :] = col_sum(gp_ref[:, 2 * part :].astype(F32))
        full_ref[:, :D] = t_dot(attn_ref[...], go_ref[...]).astype(BF)
        full_ref[:, D:] = t_dot(x_ref[...], gp_ref[...]).astype(BF)
        halves(parts, where_ref[1], full_ref.shape[1] // reps, full_ref)


def tile_specs(first):
    per = TILE // BLOCK
    return [
        pl.BlockSpec((TILE, D), lambda i: (i + first, 0)),
        pl.BlockSpec((TILE, 3 * D), lambda i: (i + first, 0)),
        pl.BlockSpec((per, PAIRS, 2 * BLOCK, BLOCK), lambda i: (i + first, 0, 0, 0)),
    ]


def attend_back(plan, order, count, ga, proj, probs, x, attn, go):
    rows = ga.shape[0]
    wide = count * 128
    total = 3 * wide + D
    part = total // plan.reps
    gp, sums, *parts = pl.pallas_call(
        partial(attend_back_kernel, plan.reps, count),
        grid=(rows // TILE,),
        out_shape=(shape((rows, 3 * wide), BF), shape((8, wide), F32)) + (far((D, part), BF),) * plan.reps,
        in_specs=[smem()] + tile_specs(0) + [still(x.shape)] * 3,
        out_specs=[still((rows, 3 * wide)), still((8, wide))] + [still((D, part))] * plan.reps,
        scratch_shapes=[pltpu.VMEM((D, total), BF)],
        compiler_params=params(28),
        name="attend_back",
        cost_estimate=cost(18),
    )(order.where, ga, stay(proj), stay(probs), x, stay(attn), go)
    return gp, sums, parts


def gx_of(count, a_ref, b_ref, w_ref, hidden):
    ca, cb = count * 128, D - count * 128
    for j in range(3):
        hidden = hidden + dot_t(a_ref[:, j * ca : (j + 1) * ca], w_ref[:, j * D : j * D + ca])
        hidden = hidden + dot_t(b_ref[:, j * cb : (j + 1) * cb], w_ref[:, j * D + ca : (j + 1) * D])
    return hidden


def far_back_kernel(count, where_ref, ga_ref, proj_ref, probs_ref, a_ref, w_ref, hidden_ref, gp_ref, far_ref):
    heads_back(count, PAIRS - count, 0, ga_ref, proj_ref, probs_ref, gp_ref)
    far_ref[...] = gx_of(count, a_ref, gp_ref, w_ref, hidden_ref[...]).astype(BF)


def far_back(order, count, ga, proj, probs, gp, w_one, hidden):
    rows = ga.shape[0] // 2
    steps = rows // TILE
    wide = 3 * (D - count * 128)
    return pl.pallas_call(
        partial(far_back_kernel, count),
        grid=(steps,),
        out_shape=(shape((rows, wide), BF), shape((rows, D), BF)),
        in_specs=[smem()]
        + tile_specs(steps)
        + [
            pl.BlockSpec((TILE, gp.shape[1]), lambda i: (i + steps, 0)),
            still((D, 3 * D)),
            pl.BlockSpec((TILE, D), lambda i: (i + steps, 0)),
        ],
        out_specs=[rows_at(wide), rows_at(D)],
        compiler_params=params(24),
        name="far_back",
        cost_estimate=cost(9),
    )(order.where, ga, stay(proj), stay(probs), gp, stay(w_one), stay(hidden))


def near_back_kernel(
    reps, count, where_ref, ga_ref, proj_ref, probs_ref, x_ref, far_ref, lines_ref, sums_ref, gp_ref, *rest
):
    parts, full_ref = rest[:-1], rest[-1]
    i = pl.program_id(0)
    heads_back(count, PAIRS - count, i * TILE, ga_ref, proj_ref, probs_ref, gp_ref)

    @pl.when(i == pl.num_programs(0) - 1)
    def weights():
        part = D - count * 128
        split = count * 128
        half = gp_ref.shape[0]
        full_ref[:, : 3 * part] = (t_dot(x_ref[:half, :], gp_ref[...]) + t_dot(x_ref[half:, :], far_ref[...])).astype(BF)
        lines = lines_ref[...]
        row = lax.broadcasted_iota(jnp.int32, lines.shape, 0)
        for n, at in ((0, 0), (1, 2 * part)):
            rest_of = col_sum(gp_ref[:, at : at + part].astype(F32)) + col_sum(far_ref[:, at : at + part].astype(F32))
            line = jnp.concatenate([sums_ref[n : n + 1, :], rest_of], 1)
            lines = jnp.where(row == n, line, lines)
        full_ref[:, 3 * part : 3 * part + 128] = jnp.transpose(lines).astype(BF)
        full_ref[:, 3 * part + 128 :] = jnp.zeros((D, full_ref.shape[1] - 3 * part - 128), BF)
        halves(parts, where_ref[1], full_ref.shape[1] // reps, full_ref)


def near_back(plan, order, count, ga, proj, probs, x, gp_far, lines, sums):
    rows = ga.shape[0] // 2
    wide = 3 * (D - count * 128)
    total = wide + W_ONE - AT_VEC
    part = total // plan.reps
    gp, *parts = pl.pallas_call(
        partial(near_back_kernel, plan.reps, count),
        grid=(rows // TILE,),
        out_shape=(shape((rows, wide), BF),) + (far((D, part), BF),) * plan.reps,
        in_specs=[smem()] + tile_specs(0) + [still(x.shape), still(gp_far.shape), still(lines.shape), still(sums.shape)],
        out_specs=[still((rows, wide))] + [still((D, part))] * plan.reps,
        scratch_shapes=[pltpu.VMEM((D, total), BF)],
        compiler_params=params(24),
        name="near_back",
        cost_estimate=cost(7),
    )(order.where, ga, stay(proj), stay(probs), x, gp_far, lines, sums)
    return gp, parts


def token_back_kernel(count, where_ref, a_ref, b_ref, w_ref, hidden_ref, own_ref):
    own_ref[...] = gx_of(count, a_ref, b_ref, w_ref, hidden_ref[...])


def token_back(order, count, ga, gb, w_one, hidden):
    rows = gb.shape[0]
    return pl.pallas_call(
        partial(token_back_kernel, count),
        grid=(rows // TILE,),
        out_shape=shape((rows, D), F32),
        in_specs=[smem(), rows_at(ga.shape[1]), rows_at(gb.shape[1]), still((D, 3 * D)), rows_at(D)],
        out_specs=rows_at(D),
        compiler_params=params(24),
        name="token_back",
        cost_estimate=cost(4),
    )(order.where, ga, gb, stay(w_one), stay(hidden))


def on_device(
    plan, query_tokens, passage_tokens, query_cot, passage_cot, positives, w_qkv, w_out, w_up, w_down, biases, gains
):
    me = lax.axis_index("dp")
    core = lax.axis_index("rep")
    tower = (me >> 2) & 1
    span = jnp.where(tower == 0, query_tokens.shape[1], passage_tokens.shape[1])
    where = jnp.stack([me, core, tower, span]).astype(jnp.int32)
    swap = plan.along(1)

    def exchange(a, b):
        a, b = a.reshape(-1, D), b.reshape(-1, D)
        return jnp.concatenate([jnp.where(tower == 0, a, b), send(jnp.where(tower == 0, b, a), swap)], 0)

    def merged(own, back):
        a = jnp.where(tower == 0, own, back)
        b = jnp.where(tower == 0, back, own)
        return a.reshape(query_tokens.shape), b.reshape(passage_tokens.shape)

    vecs = jnp.swapaxes(jnp.concatenate([biases, gains], 1), 1, 2)
    one = jnp.concatenate([w_qkv, w_out, jnp.pad(vecs, ((0, 0), (0, 0), (0, W_ONE - AT_VEC - vecs.shape[2])))], 2)
    mine, other = shards_of(plan, where, one)
    mine2, other2 = shards_of(plan, where, w_up)
    mine3, other3 = shards_of(plan, where, w_down)
    z1 = gather_line(plan, mine, other)
    x = exchange(query_tokens, passage_tokens)
    both2 = jnp.concatenate([mine2, send(other2, swap)], 0)
    z2 = gather_steps(plan, both2, z1)
    p1 = gather_plane(plan, z1, x, both2)
    both3 = jnp.concatenate([mine3, send(after(other3, x), swap)], 0)
    p1 = tuple(after(b, z2, both3) for b in p1)
    order = Order(where)
    w_one = gather_cores(plan, order, p1)
    p2 = gather_plane(plan, z2)
    z3 = gather_steps(plan, both3, z2)
    p3 = gather_plane(plan, after(z3, p2[0]))

    order.done(p2[0])
    first = order.done(attend(order, x, w_one, 0))
    proj, probs, attn, hat1, rstd1, norm, vec = order.done(attend(order, x, w_one, 1, first[:6]))
    w_two = gather_cores(plan, order, tuple(after(b, first[6]) for b in p2))
    half_up = order.done(up(order, norm, w_two, vec, 0))
    act, slope = order.done(up(order, norm, w_two, vec, 1, half_up))
    w_three = gather_cores(plan, order, tuple(after(b, half_up[0]) for b in p3))
    cot = exchange(after(query_cot, p3[0]), after(passage_cot, p3[0]))
    out, hat2, rstd2, cls = order.done(down(order, act, w_three, hat1, vec))
    query_loss, cls_grad = order.done(contrast(plan, order, cls, positives))

    second, gs, sums_top, g_down = order.done(top(plan, order, cot, cls_grad, hat2, rstd2, vec, act))
    half = out.shape[0] // 2
    out_back = send(after(out[half:], gs), swap)
    down_part = Scatter(plan, order, g_down, w_down.shape[1])
    acc, sums_up, g_up = order.done(gelu_back(plan, order, gs, w_three, slope, norm, w_two))
    up_part = Scatter(plan, order, g_up, w_up.shape[1])
    down_part.one()
    hidden, go, ga, sums = order.done(hidden_back(order, acc, second, hat1, rstd1, w_one, vec))
    up_part.one()
    down_part.two()
    order.done(out_back)
    split = 4
    gp_a, sums_a, g_a = order.done(attend_back(plan, order, split, ga, proj, probs, x, attn, go))
    a_part = Scatter(plan, order, g_a, w_qkv.shape[1])
    down_part.three()
    up_part.two()
    lines = jnp.concatenate(
        [jnp.zeros((2, D), F32), sums[0:2], sums_up[0:4], sums_top[0:2], sums[2:3], sums_top[2:3], jnp.zeros((116, D), F32)],
        0,
    )
    gp_far, gx_far = order.done(far_back(order, split, ga, proj, probs, gp_a, w_one, hidden))
    gx_back = send(gx_far, swap)
    a_part.one()
    down_part.four()
    up_part.three()
    gp_near, g_b = order.done(near_back(plan, order, split, ga, proj, probs, x, gp_far, lines, sums_a))
    b_part = Scatter(plan, order, g_b, w_qkv.shape[1])
    a_part.two()
    down_part.last()
    b_part.one()
    up_part.four()
    gx_own = order.done(token_back(order, split, gp_a, gp_near, w_one, hidden))
    a_part.three()
    b_part.two()
    up_part.last()
    a_part.four()
    b_part.three()
    (grad_down,) = finish(plan, order, [down_part], [[(0, D, 0, 0)]], [D])
    (grad_up,) = finish(plan, order, [up_part], [[(0, FF, 0, 0)]], [FF])
    b_part.four()
    query_out, passage_out = merged(out[:half], after(out_back, b_part.out))
    query_grad, passage_grad = merged(gx_own, after(gx_back, b_part.out).astype(F32))
    a_part.last()
    b_part.last()
    qa, qb = split * 128, D - split * 128
    spans_a = [(0, D, 1, 0)] + [(D + j * qa, qa, 0, j * D) for j in range(3)]
    spans_b = [(j * qb, qb, 0, j * D + qa) for j in range(3)] + [(3 * qb, 128, 2, 0)]
    grad_qkv, grad_out, grad_vecs = finish(plan, order, [a_part, b_part], [spans_a, spans_b], [3 * D, D, 128])
    grad_vecs = jnp.swapaxes(grad_vecs[:, :, :12], 1, 2)
    return (
        query_out,
        passage_out,
        query_grad,
        passage_grad,
        query_loss,
        grad_qkv,
        grad_out,
        grad_up,
        grad_down,
        grad_vecs[:, :10],
        grad_vecs[:, 10:],
    )


def solution(mesh):
    plan = Plan(mesh.shape["dp"], mesh.shape["rep"])
    rows = P(("dp", "rep"), None, None)
    shards = P(None, "dp", None)
    lanes = P(None, None, "dp")
    return jax.shard_map(
        partial(on_device, plan),
        mesh=mesh,
        in_specs=(rows,) * 4 + (P(("dp", "rep"), None),) + (shards,) * 4 + (lanes,) * 2,
        out_specs=(rows,) * 4 + (P(("dp", "rep")),) + (shards,) * 4 + (lanes,) * 2,
        check_vma=False,
    )
```

time: 416 us -> 346 us (0.83)
  waiting for transfers between devices: 144 us -> 98 us
  Pallas kernels: 114 us -> 159 us
  local copies, waits for them, and re-layouts: 50.5 us -> 18 us
  matrix products: 27.2 us -> 0 us
  other arithmetic: 24 us -> 10.9 us
    pallas_call x12 -> x38, Pallas kernels: 110 us -> 158 us  [the longest x1 21.9 us: gelu_back(): pl.pallas_call(partial(gelu_back_kernel, reps, column), out_shape=(shape(...]
    ppermute x60 -> x54, waiting for transfers between devices: 144 us -> 98 us  [send(): return lax.ppermute(v, AXES, pairs)]
    dot_general x4 -> x0, matrix products: 27.2 us -> none  [t_dot(): lax.dot_general(a, b, (((0,), (0,)), ((), ())), preferred_element_type=F32)]
    unnamed x129 -> x78, local copies, waits for them, and re-layouts: 30.5 us -> 10 us
    dynamic_slice x6 -> x2, local copies, waits for them, and re-layouts: 10.3 us -> 1.03 us  [shards_of(): mine = lax.dynamic_slice(shard, (tower, 0, core * width), (1, rows, width))]
    convert_element_type x14 -> x2, other arithmetic: 4.33 us -> 0.01 us  [the longest x1 0.01 us: contrast(): msg = jnp.concatenate([cls.astype(BF), marks], 1)]
    ppermute x60 -> x54, starting transfers between devices: 49.8 us -> 53.4 us  [send(): return lax.ppermute(v, AXES, pairs)]
  transfers between devices with their start and end apart: 60 -> 54, of which waited for: 22 -> 21; matrix products, arithmetic and copies ran while one was open for 11% -> 5% of each run, Pallas kernels for 3% -> 42%
where the time goes in v2:
time: 346 us; the launch traced here: 342 us
  Pallas kernels  159 us (46%)
  waiting for transfers between devices  98 us (28%)
  starting transfers between devices  53.4 us (15%)
  local copies, waits for them, and re-layouts  18 us (5%)
  other arithmetic  10.9 us (3%)
    ppermute x54, waiting for transfers between devices, send(): return lax.ppermute(v, AXES, pairs)  98 us
    ppermute x54, starting transfers between devices, send(): return lax.ppermute(v, AXES, pairs)  53.4 us
    pallas_call x1, Pallas kernels, gelu_back(): pl.pallas_call(partial(gelu_back_kernel, reps, column), out_shape=(shape(...  21.9 us
    pallas_call x2, Pallas kernels, up(): pl.pallas_call(partial(up_kernel, first), grid=(steps,), out_shape=(far((...  19.4 us
    pallas_call x1, Pallas kernels, attend_back(): pl.pallas_call(partial(attend_back_kernel, plan.reps, count), grid=(rows...  18.9 us
    pallas_call x2, Pallas kernels, attend(): pl.pallas_call(partial(attend_kernel, part), grid=(steps,), out_shape=(fa...  16.7 us
    pallas_call x19, Pallas kernels, in_vmem(): pl.pallas_call(kernel, out_shape=tuple((shape(*o) for o in outs)), in_spe...  16.1 us
    pallas_call x1, Pallas kernels, top(): pl.pallas_call(partial(top_kernel, plan.reps), grid=(FF // D,), out_shape...  11.6 us
  transfers between devices with their start and end apart: 54, of which 21 were waited for; matrix products, arithmetic and copies ran while one was open for 5% of the time, Pallas kernels for 42%

profile of v2, /device:TPU:0, one launch (start us, length us, event | category | flops | bytes accessed | tf_op | source)
XLA Modules:
  0.0 342.4 jit_solution(5486029005445251077)
XLA Ops:
  3.6 3.1 collective-permute-start
  6.7 2.5 collective-permute-start.2
  10.3 1.9 collective-permute-start.5
  13.7 7.5 %collective-permute-done.5 = bf16[1,48,1536]{2,1,0:T(8,128)(2,1)S(1)} collective-permute-done((bf16[1,48,1536]{2,1,0:T(8,128)(2,1)S(1)}, bf16[1,48,1536]{2,1,0:T(8,128)(2,1)S(1)}, u32[]{:S(2)}, u32[]{:S(2)}) %collective-permute-start.5) | collective-permute-done | bytes 147488 | tf_op jit(solution)/shard_map/ppermute | solution.py:85
  21.3 2.2 collective-permute-done.1
  25.2 13.6 %collective-permute-done.4 = bf16[512,768]{1,0:T(8,128)(2,1)S(1)} collective-permute-done((bf16[512,768]{1,0:T(8,128)(2,1)S(1)}, bf16[512,768]{1,0:T(8,128)(2,1)S(1)}, u32[]{:S(2)}, u32[]{:S(2)}) %collective-permute-start.4) | collective-permute-done | bytes 786464 | tf_op jit(solution)/shard_map/ppermute | solution.py:85
  45.0 12.1 %collective-permute-done.6 = bf16[2,48,1536]{2,1,0:T(8,128)(2,1)S(1)} collective-permute-done((bf16[2,48,1536]{2,1,0:T(8,128)(2,1)S(1)}, bf16[2,48,1536]{2,1,0:T(8,128)(2,1)S(1)}, u32[]{:S(2)}, u32[]{:S(2)}) %collective-permute-start.6) | collective-permute-done | bytes 294944 | tf_op jit(solution)/shard_map/ppermute | solution.py:85
  60.7 7.0 %collective-permute-done.11 = bf16[4,48,1536]{2,1,0:T(8,128)(2,1)S(1)} collective-permute-done((bf16[4,48,1536]{2,1,0:T(8,128)(2,1)S(1)}, bf16[4,48,1536]{2,1,0:T(8,128)(2,1)S(1)}, u32[]{:S(2)}, u32[]{:S(2)}) %collective-permute-start.11) | collective-permute-done | bytes 589856 | tf_op jit(solution)/shard_map/ppermute | solution.py:85
  69.4 6.1 %collective-permute-done.15 = bf16[2,192,384]{2,1,0:T(8,128)(2,1)S(1)} collective-permute-done((bf16[2,192,384]{2,1,0:T(8,128)(2,1)S(1)}, bf16[2,192,384]{2,1,0:T(8,128)(2,1)S(1)}, u32[]{:S(2)}, u32[]{:S(2)}) %collective-permute-start.15) | collective-permute-done | bytes 294944 | tf_op jit(solution)/shard_map/ppermute | solution.py:85
  76.9 2.5 assemble.3
  79.4 8.8 %attend.2 = (bf16[1024,2304]{1,0:T(8,128)(2,1)}, bf16[8,6,256,128]{3,2,1,0:T(8,128)(2,1)}, bf16[1024,768]{1,0:T(8,128)(2,1)}, f32[1024,768]{1,0:T(8,128)}, f32[1...) custom-call(s32[4]{0:T(128)S(1)} %pad_add_fusion.where_ref, bf16[1024,768]{1,0:T(8,128)(2,1)S(1)} %copy-done.3, ...), custom_call_target="tpu_custom_call" | custom-call | flops 7000000000 | bytes 21000000 | tf_op jit(solution)/shard_map/attend/pallas_call | solution.py:393
  90.5 2.2 collective-permute-start.17
  92.7 8.0 %attend.3 = (bf16[1024,2304]{1,0:T(8,128)(2,1)}, bf16[8,6,256,128]{3,2,1,0:T(8,128)(2,1)}, bf16[1024,768]{1,0:T(8,128)(2,1)}, f32[1024,768]{1,0:T(8,128)}, f32[1...) custom-call(s32[4]{0:T(128)S(1)} %pad_add_fusion.where_ref, ...), custom_call_target="tpu_custom_call", output_to_operand_aliasing={{0}: (3, {}), {1}: (4, {}), {2}: (5, {}), {3}: (6, {}), {4}... | custom-call | flops 7000000000 | bytes 21000000 | tf_op jit(solution)/shard_map/attend/pallas_call | solution.py:393
  100.7 1.8 assemble.4
  102.5 9.5 %up.2 = (bf16[1024,3072]{1,0:T(8,128)(2,1)}, bf16[1024,3072]{1,0:T(8,128)(2,1)}) custom-call(s32[4]{0:T(128)S(1)} %pad_add_fusion.where_ref, bf16[1024,768]{1,0:T(8,128)(2,1)S(1)} %copy-done.14, bf16[768,3072]{1,0:T(8,128)(2,1)S(1)} %bitcast.48, f32[128,768]{1,0:T(8,128)S(1)} %get-tuple-element.169.vec_ref), custom_call_target="tpu_custom_call" | custom-call | flops 8000000000 | bytes 24000000 | tf_op jit(solution)/shard_map/up/pallas_call | solution.py:450
  114.0 9.9 %up.3 = (bf16[1024,3072]{1,0:T(8,128)(2,1)}, bf16[1024,3072]{1,0:T(8,128)(2,1)}) custom-call(s32[4]{0:T(128)S(1)} %pad_add_fusion.where_ref, bf16[1024,768]{1,0:T(8,128)(2,1)S(1)} %copy-done.14, bf16[768,3072]{1,0:T(8,128)(2,1)S(1)} %bitcast.49, f32[128,768]{1,0:T(8,128)S(1)} %get-tuple-element.169.vec_ref, ...), custom_call_target="tpu_custom_call", output_to_operand_aliasing={{0}: (4, {}), {1}: (5, {})} | custom-call | flops 8000000000 | bytes 24000000 | tf_op jit(solution)/shard_map/up/pallas_call | solution.py:450
  125.8 10.2 %down.1 = (bf16[1024,768]{1,0:T(8,128)(2,1)}, f32[1024,768]{1,0:T(8,128)}, f32[1024,1]{1,0:T(8,128)}, f32[32,768]{1,0:T(8,128)S(1)}) custom-call(s32[4]{0:T(128)S(1)} %pad_add_fusion.where_ref, bf16[1024,3072]{1,0:T(8,128)(2,1)} %get-tuple-element.177.act_ref, bf16[3072,768]{1,0:T(8,128)(2,1)S(1)} %bitcast.51, f32[1024,768]{1,0:T(8,128)S(1)} %copy-done.9, ...), custom_call_target="tpu_custom_call" | custom-call | flops 8000000000 | bytes 24000000 | tf_op jit(solution)/shard_map/down/pallas_call | solution.py:483
  136.0 2.6 collective-permute-start.20
  142.8 2.2 collective-permute-done.22
  148.8 3.3 collective-permute-done.23
  152.2 2.5 collective-permute-done.24
  161.8 1.7 contrast.1
  164.2 11.6 %top.1 = (f32[1024,768]{1,0:T(8,128)}, bf16[1024,768]{1,0:T(8,128)(2,1)S(1)}, f32[8,768]{1,0:T(8,128)S(1)}, bf16[3072,384]{1,0:T(8,128)(2,1)}, bf16[3072,384]{1,0:T(8,128)(2,1)}) custom-call(s32[4]{0:T(128)S(1)} %pad_add_fusion.where_ref, bf16[1024,768]{1,0:T(8,128)(2,1)S(1)} %pad_maximum_fusion.1.cot_ref, f32[32,768]{1,0:T(8,128)S(1)} %get-tuple-element.191.cls_ref, ...), custom_call_target="tpu_custom_call" | custom-call | flops 11000000512 | bytes 33000000 | tf_op jit(solution)/shard_map/top/pallas_call | solution.py:621
  176.3 21.9 %gelu_back.1 = (f32[1024,768]{1,0:T(8,128)S(1)}, f32[8,768]{1,0:T(8,128)S(1)}, bf16[768,1536]{1,0:T(8,128)(2,1)}, bf16[768,1536]{1,0:T(8,128)(2,1)}) custom-call(s32[4]{0:T(128)S(1)} %pad_add_fusion.where_ref, bf16[1024,768]{1,0:T(8,128)(2,1)S(1)} %get-tuple-element.195.gs_ref, bf16[3072,768]{1,0:T(8,128)(2,1)} %bitcast.52, ...), custom_call_target="tpu_custom_call" | custom-call | flops 20000000000 | bytes 60000000 | tf_op jit(solution)/shard_map/gelu_back/pallas_call | solution.py:682
  198.2 2.4 pick_add.4
  201.9 6.9 %hidden_back.1 = (f32[1024,768]{1,0:T(8,128)}, bf16[1024,768]{1,0:T(8,128)(2,1)S(1)}, bf16[1024,768]{1,0:T(8,128)(2,1)S(1)}, f32[8,768]{1,0:T(8,128)S(1)}) custom-call(s32[4]{0:T(128)S(1)} %pad_add_fusion.where_ref, f32[1024,768]{1,0:T(8,128)S(1)} %get-tuple-element.202.acc_ref, f32[1024,768]{1,0:T(8,128)} %get-tuple-element.197.second_ref, ...), custom_call_target="tpu_custom_call" | custom-call | flops 5000000000 | bytes 15000000 | tf_op jit(solution)/shard_map/hidden_back/pallas_call | solution.py:726
  208.8 3.4 pick_add.5
  213.3 3.6 %collective-permute-done.31.r_ref = bf16[8,192,384]{2,1,0:T(8,128)(2,1)S(1)} collective-permute-done((bf16[8,192,384]{2,1,0:T(8,128)(2,1)S(1)}, bf16[8,192,384]{2,1,0:T(8,128)(2,1)S(1)}, u32[]{:S(2)}, u32[]{:S(2)}) %collective-permute-start.31) | collective-permute-done | bytes 1179680 | tf_op jit(solution)/shard_map/ppermute | solution.py:85
  217.8 3.8 %collective-permute-done.28 = bf16[512,768]{1,0:T(8,128)(2,1)S(1)} collective-permute-done((bf16[512,768]{1,0:T(8,128)(2,1)S(1)}, bf16[512,768]{1,0:T(8,128)(2,1)S(1)}, u32[]{:S(2)}, u32[]{:S(2)}) %collective-permute-start.28) | collective-permute-done | bytes 786464 | tf_op jit(solution)/shard_map/ppermute | solution.py:85
  221.6 18.9 %attend_back.1 = (bf16[1024,1536]{1,0:T(8,128)(2,1)S(1)}, f32[8,512]{1,0:T(8,128)S(1)}, bf16[768,1152]{1,0:T(8,128)(2,1)}, bf16[768,1152]{1,0:T(8,128)(2,1)}) custom-call(s32[4]{0:T(128)S(1)} %pad_add_fusion.where_ref, bf16[1024,768]{1,0:T(8,128)(2,1)S(1)} %get-tuple-element.212.ga_ref, bf16[1024,2304]{1,0:T(8,128)(2,1)} %get-tuple-element.163.proj_ref, ...), custom_call_target="tpu_custom_call" | custom-call | flops 17999998976 | bytes 54000000 | tf_op jit(solution)/shard_map/attend_back/pallas_call | solution.py:800
  245.5 1.8 concatenate.78.lines_ref
  247.3 4.8 %collective-permute-done.32.r_ref = bf16[4,192,384]{2,1,0:T(8,128)(2,1)S(1)} collective-permute-done((bf16[4,192,384]{2,1,0:T(8,128)(2,1)S(1)}, bf16[4,192,384]{2,1,0:T(8,128)(2,1)S(1)}, u32[]{:S(2)}, u32[]{:S(2)}) %collective-permute-start.32) | collective-permute-done | bytes 589856 | tf_op jit(solution)/shard_map/ppermute | solution.py:85
  257.2 1.8 collective-permute-start.36
  259.0 7.9 %far_back.1 = (bf16[512,768]{1,0:T(8,128)(2,1)S(1)}, bf16[512,768]{1,0:T(8,128)(2,1)S(1)}) custom-call(s32[4]{0:T(128)S(1)} %pad_add_fusion.where_ref, bf16[1024,768]{1,0:T(8,128)(2,1)S(1)} %copy-done.13, bf16[1024,2304]{1,0:T(8,128)(2,1)} %get-tuple-element.163.proj_ref, bf16[8,6,256,128]{3,2,1,0:T(8,128)(2,1)} %get-tuple-element.164.probs_ref, ...), custom_call_target="tpu_custom_call" | custom-call | flops 8999999488 | bytes 27000000 | tf_op jit(solution)/shard_map/far_back/pallas_call | solution.py:831
  266.9 3.2 pick_add.6
  272.0 7.1 %near_back.1 = (bf16[512,768]{1,0:T(8,128)(2,1)S(1)}, bf16[768,512]{1,0:T(8,128)(2,1)}, bf16[768,512]{1,0:T(8,128)(2,1)}) custom-call(s32[4]{0:T(128)S(1)} %pad_add_fusion.where_ref, bf16[1024,768]{1,0:T(8,128)(2,1)S(1)} %copy-done.13, bf16[1024,2304]{1,0:T(8,128)(2,1)} %get-tuple-element.163.proj_ref, ...), custom_call_target="tpu_custom_call" | custom-call | flops 7000000000 | bytes 21000000 | tf_op jit(solution)/shard_map/near_back/pallas_call | solution.py:878
  280.5 2.7 collective-permute-done.37.r_ref
  284.5 2.9 collective-permute-done.38.got_ref
  288.0 1.8 pick_add.7
  289.9 1.7 collective-permute-start.42
  291.6 4.6 %collective-permute-done.40.r_ref = bf16[2,48,1536]{2,1,0:T(8,128)(2,1)S(1)} collective-permute-done((bf16[2,48,1536]{2,1,0:T(8,128)(2,1)S(1)}, bf16[2,48,1536]{2,1,0:T(8,128)(2,1)S(1)}, u32[]{:S(2)}, u32[]{:S(2)}) %collective-permute-start.40) | collective-permute-done | bytes 294944 | tf_op jit(solution)/shard_map/ppermute | solution.py:85
  296.9 4.8 %token_back.1 = f32[512,768]{1,0:T(8,128)S(1)} custom-call(s32[4]{0:T(128)S(1)} %pad_add_fusion.where_ref, bf16[1024,1536]{1,0:T(8,128)(2,1)S(1)} %copy-done.6, bf16[512,768]{1,0:T(8,128)(2,1)S(1)} %get-tuple-element.245.b_ref, bf16[768,3328]{1,0:T(8,128)(2,1)} %bitcast.47, f32[1024,768]{1,0:T(8,128)} %get-tuple-element.210.hidden_ref), custom_call_target="tpu_custom_call" | custom-call | flops 4000000000 | bytes 12000000 | tf_op jit(solution)/shard_map/token_back/pallas_call | solution.py:898
  302.4 2.1 collective-permute-start.44
  307.4 7.5 %collective-permute-done.44.r_ref = bf16[2,48,1152]{2,1,0:T(8,128)(2,1)S(1)} collective-permute-done((bf16[2,48,1152]{2,1,0:T(8,128)(2,1)S(1)}, bf16[2,48,1152]{2,1,0:T(8,128)(2,1)S(1)}, u32[]{:S(2)}, u32[]{:S(2)}) %collective-permute-start.44) | collective-permute-done | bytes 221216 | tf_op jit(solution)/shard_map/ppermute | solution.py:85
  316.2 2.1 collective-permute-start.48
  321.6 8.2 %collective-permute-done.48.r_ref = bf16[2,48,512]{2,1,0:T(8,128)(2,1)S(1)} collective-permute-done((bf16[2,48,512]{2,1,0:T(8,128)(2,1)S(1)}, bf16[2,48,512]{2,1,0:T(8,128)(2,1)S(1)}, u32[]{:S(2)}, u32[]{:S(2)}) %collective-permute-start.48) | collective-permute-done | bytes 98336 | tf_op jit(solution)/shard_map/ppermute | solution.py:85
  330.4 3.4 %collective-permute-start.51 = (bf16[1,48,512]{2,1,0:T(8,128)(2,1)S(1)}, bf16[1,48,512]{2,1,0:T(8,128)(2,1)S(1)}, u32[]{:S(2)}, u32[]{:S(2)}) collective-permute-start(bf16[1,48,512]{2,1,0:T(8,128)(2,1)S(1)} %get-tuple-element.275), channel_id=1, source_target_pairs={{0,8},{1,9},{2,10},{3,11},{4,12},{5,13},{6,14},{7,15},{8,0},{9,1},... | collective-permute-start | bytes 147464 | tf_op jit(solution)/shard_map/ppermute | solution.py:85
  333.8 1.9 convert_select_fusion
  (220 shorter events, 75.6 us)
Async XLA Ops:
  3.6 17.7 %collective-permute-start = (bf16[1,48,1664]{2,1,0:T(8,128)(2,1)S(1)}, bf16[1,48,1664]{2,1,0:T(8,128)(2,1)S(1)}, u32[]{:S(2)}, u32[]{:S(2)}) collective-permute-start(bf16[1,48,1664]{2,1,0:T(8,128)(2,1)S(1)} %get-tuple-element.339), channel_id=1, source_target_pairs={{0,8},{1,9},{2,10},{3,11},{4,12},{5,13},{6,14},{7,15},{8,0},{9,1},... | collective-permute-start | bytes 479240 | tf_op jit(solution)/shard_map/ppermute | solution.py:85
  6.7 16.8 %collective-permute-start.2 = (bf16[1,48,1664]{2,1,0:T(8,128)(2,1)S(1)}, bf16[1,48,1664]{2,1,0:T(8,128)(2,1)S(1)}, u32[]{:S(2)}, u32[]{:S(2)}) collective-permute-start(bf16[1,48,1664]{2,1,0:T(8,128)(2,1)S(1)} %get-tuple-element.339), channel_id=1, source_target_pairs={{0,24},{1,25},{2,26},{3,27},{4,28},{5,29},{6,30},{7,31},{8,16},{9,... | collective-permute-start | bytes 479240 | tf_op jit(solution)/shard_map/ppermute | solution.py:85
  9.1 14.3 %collective-permute-start.1 = (bf16[1,48,1664]{2,1,0:T(8,128)(2,1)S(1)}, bf16[1,48,1664]{2,1,0:T(8,128)(2,1)S(1)}, u32[]{:S(2)}, u32[]{:S(2)}) collective-permute-start(bf16[1,48,1664]{2,1,0:T(8,128)(2,1)S(1)} %get-tuple-element.330), channel_id=1, source_target_pairs={{0,16},{1,17},{2,18},{3,19},{4,20},{5,21},{6,22},{7,23},{8,24},{9,... | collective-permute-start | bytes 479240 | tf_op jit(solution)/shard_map/ppermute | solution.py:85
  10.3 11.0 %collective-permute-start.5 = (bf16[1,48,1536]{2,1,0:T(8,128)(2,1)S(1)}, bf16[1,48,1536]{2,1,0:T(8,128)(2,1)S(1)}, u32[]{:S(2)}, u32[]{:S(2)}) collective-permute-start(bf16[1,48,1536]{2,1,0:T(8,128)(2,1)S(1)} %get-tuple-element.343), channel_id=1, source_target_pairs={{0,8},{1,9},{2,10},{3,11},{4,12},{5,13},{6,14},{7,15},{8,0},{9,1},... | collective-permute-start | bytes 442376 | tf_op jit(solution)/shard_map/ppermute | solution.py:85
  13.4 25.4 %collective-permute-start.4 = (bf16[512,768]{1,0:T(8,128)(2,1)S(1)}, bf16[512,768]{1,0:T(8,128)(2,1)S(1)}, u32[]{:S(2)}, u32[]{:S(2)}) collective-permute-start(bf16[512,768]{1,0:T(8,128)(2,1)S(1)} %get-tuple-element.338), channel_id=1, source_target_pairs={{0,8},{1,9},{2,10},{3,11},{4,12},{5,13},{6,14},{7,15},{8,0},{9,1},... | collective-permute-start | bytes 2359304 | tf_op jit(solution)/shard_map/ppermute | solution.py:85
  23.6 16.5 %collective-permute-start.3 = (bf16[4,48,1664]{2,1,0:T(8,128)(2,1)S(1)}, bf16[4,48,1664]{2,1,0:T(8,128)(2,1)S(1)}, u32[]{:S(2)}, u32[]{:S(2)}) collective-permute-start(bf16[4,48,1664]{2,1,0:T(8,128)(2,1)S(1)} %pad_maximum_fusion.3), channel_id=1, source_target_pairs={{0,2},{1,5},{2,0},{3,7},{4,6},{5,1},{6,4},{7,3},{8,10},{9,13},{10,... | collective-permute-start | bytes 1916936 | tf_op jit(solution)/shard_map/ppermute | solution.py:85
  40.2 17.4 %collective-permute-start.8 = (bf16[8,48,1664]{2,1,0:T(8,128)(2,1)S(1)}, bf16[8,48,1664]{2,1,0:T(8,128)(2,1)}, u32[]{:S(2)}, u32[]{:S(2)}) collective-permute-start(bf16[8,48,1664]{2,1,0:T(8,128)(2,1)S(1)} %constant_dynamic-update-slice_fusion.refs_0_), channel_id=1, source_target_pairs={{0,4},{1,3},{2,6},{3,1},{4,0},{5,7},{6,2},{7,5},{8,12},{9,11},{10,... | collective-permute-start | bytes 3833864 | tf_op jit(solution)/shard_map/ppermute | solution.py:85
  41.7 15.4 %collective-permute-start.6 = (bf16[2,48,1536]{2,1,0:T(8,128)(2,1)S(1)}, bf16[2,48,1536]{2,1,0:T(8,128)(2,1)S(1)}, u32[]{:S(2)}, u32[]{:S(2)}) collective-permute-start(bf16[2,48,1536]{2,1,0:T(8,128)(2,1)S(1)} %pad_maximum_fusion.5), channel_id=1, source_target_pairs={{0,16},{1,17},{2,18},{3,19},{4,20},{5,21},{6,22},{7,23},{8,24},{9,... | collective-permute-start | bytes 884744 | tf_op jit(solution)/shard_map/ppermute | solution.py:85
  43.4 13.8 %collective-permute-start.7 = (bf16[1,192,384]{2,1,0:T(8,128)(2,1)S(1)}, bf16[1,192,384]{2,1,0:T(8,128)(2,1)S(1)}, u32[]{:S(2)}, u32[]{:S(2)}) collective-permute-start(bf16[1,192,384]{2,1,0:T(8,128)(2,1)S(1)} %get-tuple-element.150), channel_id=1, source_target_pairs={{0,8},{1,9},{2,10},{3,11},{4,12},{5,13},{6,14},{7,15},{8,0},{9,1},... | collective-permute-start | bytes 442376 | tf_op jit(solution)/shard_map/ppermute | solution.py:85
  57.2 19.7 %collective-permute-start.9 = (bf16[8,48,1664]{2,1,0:T(8,128)(2,1)S(1)}, bf16[8,48,1664]{2,1,0:T(8,128)(2,1)}, u32[]{:S(2)}, u32[]{:S(2)}) collective-permute-start(bf16[8,48,1664]{2,1,0:T(8,128)(2,1)S(1)} %constant_dynamic-update-slice_fusion.refs_0_), channel_id=1, source_target_pairs={{0,1},{1,0},{2,3},{3,2},{4,5},{5,4},{6,7},{7,6},{8,9},{9,8},{10,11... | collective-permute-start | bytes 3833864 | tf_op jit(solution)/shard_map/ppermute | solution.py:85
  57.6 19.3 %collective-permute-start.10 = (bf16[8,48,1664]{2,1,0:T(8,128)(2,1)}, bf16[8,48,1664]{2,1,0:T(8,128)(2,1)}, u32[]{:S(2)}, u32[]{:S(2)}) collective-permute-start(bf16[8,48,1664]{2,1,0:T(8,128)(2,1)} %collective-permute-done.8.refs_1_), channel_id=1, source_target_pairs={{0,1},{1,0},{2,3},{3,2},{4,5},{5,4},{6,7},{7,6},{8,9},{9,8},{10,11... | collective-permute-start | bytes 3833864 | tf_op jit(solution)/shard_map/ppermute | solution.py:85
  57.8 9.9 %collective-permute-start.11 = (bf16[4,48,1536]{2,1,0:T(8,128)(2,1)S(1)}, bf16[4,48,1536]{2,1,0:T(8,128)(2,1)S(1)}, u32[]{:S(2)}, u32[]{:S(2)}) collective-permute-start(bf16[4,48,1536]{2,1,0:T(8,128)(2,1)S(1)} %get-tuple-element.345), channel_id=1, source_target_pairs={{0,2},{1,5},{2,0},{3,7},{4,6},{5,1},{6,4},{7,3},{8,10},{9,13},{10,... | collective-permute-start | bytes 1769480 | tf_op jit(solution)/shard_map/ppermute | solution.py:85
  59.1 16.4 %collective-permute-start.15 = (bf16[2,192,384]{2,1,0:T(8,128)(2,1)S(1)}, bf16[2,192,384]{2,1,0:T(8,128)(2,1)S(1)}, u32[]{:S(2)}, u32[]{:S(2)}) collective-permute-start(bf16[2,192,384]{2,1,0:T(8,128)(2,1)S(1)} %pad_maximum_fusion.6), channel_id=1, source_target_pairs={{0,16},{1,17},{2,18},{3,19},{4,20},{5,21},{6,22},{7,23},{8,24},{9,... | collective-permute-start | bytes 884744 | tf_op jit(solution)/shard_map/ppermute | solution.py:85
  67.7 22.1 %collective-permute-start.12 = (bf16[8,48,1536]{2,1,0:T(8,128)(2,1)S(1)}, bf16[8,48,1536]{2,1,0:T(8,128)(2,1)}, u32[]{:S(2)}, u32[]{:S(2)}) collective-permute-start(bf16[8,48,1536]{2,1,0:T(8,128)(2,1)S(1)} %constant_dynamic-update-slice_fusion.7.refs_0_), channel_id=1, source_target_pairs={{0,4},{1,3},{2,6},{3,1},{4,0},{5,7},{6,2},{7,5},{8,12},{9,11},{10,... | collective-permute-start | bytes 3538952 | tf_op jit(solution)/shard_map/ppermute | solution.py:85
  75.5 14.9 %collective-permute-start.16 = (bf16[4,192,384]{2,1,0:T(8,128)(2,1)S(1)}, bf16[4,192,384]{2,1,0:T(8,128)(2,1)S(1)}, u32[]{:S(2)}, u32[]{:S(2)}) collective-permute-start(bf16[4,192,384]{2,1,0:T(8,128)(2,1)S(1)} %pad_maximum_fusion.4), channel_id=1, source_target_pairs={{0,2},{1,5},{2,0},{3,7},{4,6},{5,1},{6,4},{7,3},{8,10},{9,13},{10,... | collective-permute-start | bytes 1769480 | tf_op jit(solution)/shard_map/ppermute | solution.py:85
  89.9 10.8 %collective-permute-start.14 = (bf16[8,48,1536]{2,1,0:T(8,128)(2,1)}, bf16[8,48,1536]{2,1,0:T(8,128)(2,1)S(1)}, u32[]{:S(2)}, u32[]{:S(2)}) collective-permute-start(bf16[8,48,1536]{2,1,0:T(8,128)(2,1)} %collective-permute-done.12.refs_1_), channel_id=1, source_target_pairs={{0,1},{1,0},{2,3},{3,2},{4,5},{5,4},{6,7},{7,6},{8,9},{9,8},{10,11... | collective-permute-start | bytes 3538952 | tf_op jit(solution)/shard_map/ppermute | solution.py:85
  89.9 10.8 %collective-permute-start.13 = (bf16[8,48,1536]{2,1,0:T(8,128)(2,1)S(1)}, bf16[8,48,1536]{2,1,0:T(8,128)(2,1)S(1)}, u32[]{:S(2)}, u32[]{:S(2)}) collective-permute-start(bf16[8,48,1536]{2,1,0:T(8,128)(2,1)S(1)} %constant_dynamic-update-slice_fusion.7.refs_0_), channel_id=1, source_target_pairs={{0,1},{1,0},{2,3},{3,2},{4,5},{5,4},{6,7},{7,6},{8,9},{9,8},{10,11... | collective-permute-start | bytes 3538952 | tf_op jit(solution)/shard_map/ppermute | solution.py:85
  90.5 21.5 %collective-permute-start.17 = (bf16[8,192,384]{2,1,0:T(8,128)(2,1)S(1)}, bf16[8,192,384]{2,1,0:T(8,128)(2,1)S(1)}, u32[]{:S(2)}, u32[]{:S(2)}) collective-permute-start(bf16[8,192,384]{2,1,0:T(8,128)(2,1)S(1)} %constant_dynamic-update-slice_fusion.10.refs_0_), channel_id=1, source_target_pairs={{0,4},{1,3},{2,6},{3,1},{4,0},{5,7},{6,2},{7,5},{8,12},{9,11},{10,... | collective-permute-start | bytes 3538952 | tf_op jit(solution)/shard_map/ppermute | solution.py:85
  112.0 11.9 %collective-permute-start.18 = (bf16[8,192,384]{2,1,0:T(8,128)(2,1)S(1)}, bf16[8,192,384]{2,1,0:T(8,128)(2,1)S(1)}, u32[]{:S(2)}, u32[]{:S(2)}) collective-permute-start(bf16[8,192,384]{2,1,0:T(8,128)(2,1)S(1)} %constant_dynamic-update-slice_fusion.10.refs_0_), channel_id=1, source_target_pairs={{0,1},{1,0},{2,3},{3,2},{4,5},{5,4},{6,7},{7,6},{8,9},{9,8},{10,11... | collective-permute-start | bytes 3538952 | tf_op jit(solution)/shard_map/ppermute | solution.py:85
  112.1 11.9 %collective-permute-start.19 = (bf16[8,192,384]{2,1,0:T(8,128)(2,1)S(1)}, bf16[8,192,384]{2,1,0:T(8,128)(2,1)S(1)}, u32[]{:S(2)}, u32[]{:S(2)}) collective-permute-start(bf16[8,192,384]{2,1,0:T(8,128)(2,1)S(1)} %collective-permute-done.17.refs_1_), channel_id=1, source_target_pairs={{0,1},{1,0},{2,3},{3,2},{4,5},{5,4},{6,7},{7,6},{8,9},{9,8},{10,11... | collective-permute-start | bytes 3538952 | tf_op jit(solution)/shard_map/ppermute | solution.py:85
  113.7 42.0 %collective-permute-start.27 = (bf16[512,768]{1,0:T(8,128)(2,1)S(1)}, bf16[512,768]{1,0:T(8,128)(2,1)S(1)}, u32[]{:S(2)}, u32[]{:S(2)}) collective-permute-start(bf16[512,768]{1,0:T(8,128)(2,1)S(1)} %get-tuple-element.336), channel_id=1, source_target_pairs={{0,8},{1,9},{2,10},{3,11},{4,12},{5,13},{6,14},{7,15},{8,0},{9,1},... | collective-permute-start | bytes 2359304 | tf_op jit(solution)/shard_map/ppermute | solution.py:85
  145.3 6.9 %collective-permute-start.23 = (bf16[2,48,896]{2,1,0:T(8,128)(2,1)S(1)}, bf16[2,48,896]{2,1,0:T(8,128)(2,1)S(1)}, u32[]{:S(2)}, u32[]{:S(2)}) collective-permute-start(bf16[2,48,896]{2,1,0:T(8,128)(2,1)S(1)} %get-tuple-element.350), channel_id=1, source_target_pairs={{0,2},{1,3},{2,0},{3,1},{4,6},{5,7},{6,4},{7,5},{8,10},{9,11},{10,... | collective-permute-start | bytes 516104 | tf_op jit(solution)/shard_map/ppermute | solution.py:85
  146.8 7.8 %collective-permute-start.24 = (bf16[2,48,896]{2,1,0:T(8,128)(2,1)S(1)}, bf16[2,48,896]{2,1,0:T(8,128)(2,1)S(1)}, u32[]{:S(2)}, u32[]{:S(2)}) collective-permute-start(bf16[2,48,896]{2,1,0:T(8,128)(2,1)S(1)} %get-tuple-element.350), channel_id=1, source_target_pairs={{0,4},{1,5},{2,6},{3,7},{4,0},{5,1},{6,2},{7,3},{8,12},{9,13},{10,... | collective-permute-start | bytes 516104 | tf_op jit(solution)/shard_map/ppermute | solution.py:85
  147.3 7.3 %collective-permute-start.25 = (bf16[2,48,896]{2,1,0:T(8,128)(2,1)S(1)}, bf16[2,48,896]{2,1,0:T(8,128)(2,1)S(1)}, u32[]{:S(2)}, u32[]{:S(2)}) collective-permute-start(bf16[2,48,896]{2,1,0:T(8,128)(2,1)S(1)} %get-tuple-element.350), channel_id=1, source_target_pairs={{0,6},{1,7},{2,4},{3,5},{4,2},{5,3},{6,0},{7,1},{8,14},{9,15},{10,... | collective-permute-start | bytes 516104 | tf_op jit(solution)/shard_map/ppermute | solution.py:85
  175.8 22.4 %collective-permute-start.29 = (bf16[16,192,384]{2,1,0:T(8,128)(2,1)}, bf16[16,192,384]{2,1,0:T(8,128)(2,1)S(1)}, u32[]{:S(2)}, u32[]{:S(2)}) collective-permute-start(bf16[16,192,384]{2,1,0:T(8,128)(2,1)} %bitcast.62), channel_id=1, source_target_pairs={{0,1},{1,0},{2,3},{3,2},{4,5},{5,4},{6,7},{7,6},{8,9},{9,8},{10,11... | collective-permute-start | bytes 7077896 | tf_op jit(solution)/shard_map/ppermute | solution.py:85
  198.2 10.6 %collective-permute-start.30 = (bf16[16,48,1536]{2,1,0:T(8,128)(2,1)}, bf16[16,48,1536]{2,1,0:T(8,128)(2,1)S(1)}, u32[]{:S(2)}, u32[]{:S(2)}) collective-permute-start(bf16[16,48,1536]{2,1,0:T(8,128)(2,1)} %bitcast.61), channel_id=1, source_target_pairs={{0,1},{1,0},{2,3},{3,2},{4,5},{5,4},{6,7},{7,6},{8,9},{9,8},{10,11... | collective-permute-start | bytes 7077896 | tf_op jit(solution)/shard_map/ppermute | solution.py:85
  200.7 16.3 %collective-permute-start.31 = (bf16[8,192,384]{2,1,0:T(8,128)(2,1)S(1)}, bf16[8,192,384]{2,1,0:T(8,128)(2,1)S(1)}, u32[]{:S(2)}, u32[]{:S(2)}) collective-permute-start(bf16[8,192,384]{2,1,0:T(8,128)(2,1)S(1)} %get-tuple-element.207), channel_id=1, source_target_pairs={{0,2},{1,5},{2,0},{3,7},{4,6},{5,1},{6,4},{7,3},{8,10},{9,13},{10,... | collective-permute-start | bytes 3538952 | tf_op jit(solution)/shard_map/ppermute | solution.py:85
  201.5 20.1 %collective-permute-start.28 = (bf16[512,768]{1,0:T(8,128)(2,1)S(1)}, bf16[512,768]{1,0:T(8,128)(2,1)S(1)}, u32[]{:S(2)}, u32[]{:S(2)}) collective-permute-start(bf16[512,768]{1,0:T(8,128)(2,1)S(1)} %slice.46), channel_id=1, source_target_pairs={{0,8},{1,9},{2,10},{3,11},{4,12},{5,13},{6,14},{7,15},{8,0},{9,1},... | collective-permute-start | bytes 2359304 | tf_op jit(solution)/shard_map/ppermute | solution.py:85
  212.2 43.3 %collective-permute-start.33 = (bf16[8,48,1536]{2,1,0:T(8,128)(2,1)}, bf16[8,48,1536]{2,1,0:T(8,128)(2,1)}, u32[]{:S(2)}, u32[]{:S(2)}) collective-permute-start(bf16[8,48,1536]{2,1,0:T(8,128)(2,1)} %get-tuple-element.215), channel_id=1, source_target_pairs={{0,2},{1,5},{2,0},{3,7},{4,6},{5,1},{6,4},{7,3},{8,10},{9,13},{10,... | collective-permute-start | bytes 3538952 | tf_op jit(solution)/shard_map/ppermute | solution.py:85
  242.2 24.7 %collective-permute-start.34 = (bf16[16,48,1152]{2,1,0:T(8,128)(2,1)}, bf16[16,48,1152]{2,1,0:T(8,128)(2,1)}, u32[]{:S(2)}, u32[]{:S(2)}) collective-permute-start(bf16[16,48,1152]{2,1,0:T(8,128)(2,1)} %bitcast.63), channel_id=1, source_target_pairs={{0,1},{1,0},{2,3},{3,2},{4,5},{5,4},{6,7},{7,6},{8,9},{9,8},{10,11... | collective-permute-start | bytes 5308424 | tf_op jit(solution)/shard_map/ppermute | solution.py:85
  242.2 9.9 %collective-permute-start.32 = (bf16[4,192,384]{2,1,0:T(8,128)(2,1)S(1)}, bf16[4,192,384]{2,1,0:T(8,128)(2,1)S(1)}, u32[]{:S(2)}, u32[]{:S(2)}) collective-permute-start(bf16[4,192,384]{2,1,0:T(8,128)(2,1)S(1)} %get-tuple-element.218), channel_id=1, source_target_pairs={{0,4},{1,3},{2,6},{3,1},{4,0},{5,7},{6,2},{7,5},{8,12},{9,11},{10,... | collective-permute-start | bytes 1769480 | tf_op jit(solution)/shard_map/ppermute | solution.py:85
  253.9 16.9 %collective-permute-start.35 = (bf16[2,192,384]{2,1,0:T(8,128)(2,1)S(1)}, bf16[2,192,384]{2,1,0:T(8,128)(2,1)S(1)}, u32[]{:S(2)}, u32[]{:S(2)}) collective-permute-start(bf16[2,192,384]{2,1,0:T(8,128)(2,1)S(1)} %get-tuple-element.227), channel_id=1, source_target_pairs={{0,16},{1,17},{2,18},{3,19},{4,20},{5,21},{6,22},{7,23},{8,24},{9,... | collective-permute-start | bytes 884744 | tf_op jit(solution)/shard_map/ppermute | solution.py:85
  257.2 14.1 %collective-permute-start.36 = (bf16[4,48,1536]{2,1,0:T(8,128)(2,1)S(1)}, bf16[4,48,1536]{2,1,0:T(8,128)(2,1)S(1)}, u32[]{:S(2)}, u32[]{:S(2)}) collective-permute-start(bf16[4,48,1536]{2,1,0:T(8,128)(2,1)S(1)} %get-tuple-element.230), channel_id=1, source_target_pairs={{0,4},{1,3},{2,6},{3,1},{4,0},{5,7},{6,2},{7,5},{8,12},{9,11},{10,... | collective-permute-start | bytes 1769480 | tf_op jit(solution)/shard_map/ppermute | solution.py:85
  270.1 13.1 %collective-permute-start.37 = (bf16[8,48,1152]{2,1,0:T(8,128)(2,1)S(1)}, bf16[8,48,1152]{2,1,0:T(8,128)(2,1)S(1)}, u32[]{:S(2)}, u32[]{:S(2)}) collective-permute-start(bf16[8,48,1152]{2,1,0:T(8,128)(2,1)S(1)} %get-tuple-element.236), channel_id=1, source_target_pairs={{0,2},{1,5},{2,0},{3,7},{4,6},{5,1},{6,4},{7,3},{8,10},{9,13},{10,... | collective-permute-start | bytes 2654216 | tf_op jit(solution)/shard_map/ppermute | solution.py:85
  279.1 8.9 %collective-permute-start.39 = (bf16[16,48,512]{2,1,0:T(8,128)(2,1)}, bf16[16,48,512]{2,1,0:T(8,128)(2,1)S(1)}, u32[]{:S(2)}, u32[]{:S(2)}) collective-permute-start(bf16[16,48,512]{2,1,0:T(8,128)(2,1)} %bitcast.64), channel_id=1, source_target_pairs={{0,1},{1,0},{2,3},{3,2},{4,5},{5,4},{6,7},{7,6},{8,9},{9,8},{10,11... | collective-permute-start | bytes 2359304 | tf_op jit(solution)/shard_map/ppermute | solution.py:85
  279.1 8.3 %collective-permute-start.38 = (bf16[1,192,384]{2,1,0:T(8,128)(2,1)S(1)}, bf16[1,192,384]{2,1,0:T(8,128)(2,1)S(1)}, u32[]{:S(2)}, u32[]{:S(2)}) collective-permute-start(bf16[1,192,384]{2,1,0:T(8,128)(2,1)S(1)} %get-tuple-element.239), channel_id=1, source_target_pairs={{0,8},{1,9},{2,10},{3,11},{4,12},{5,13},{6,14},{7,15},{8,0},{9,1},... | collective-permute-start | bytes 442376 | tf_op jit(solution)/shard_map/ppermute | solution.py:85
  279.8 16.4 %collective-permute-start.40 = (bf16[2,48,1536]{2,1,0:T(8,128)(2,1)S(1)}, bf16[2,48,1536]{2,1,0:T(8,128)(2,1)S(1)}, u32[]{:S(2)}, u32[]{:S(2)}) collective-permute-start(bf16[2,48,1536]{2,1,0:T(8,128)(2,1)S(1)} %get-tuple-element.242), channel_id=1, source_target_pairs={{0,16},{1,17},{2,18},{3,19},{4,20},{5,21},{6,22},{7,23},{8,24},{9,... | collective-permute-start | bytes 884744 | tf_op jit(solution)/shard_map/ppermute | solution.py:85
  284.0 17.7 %collective-permute-start.41 = (bf16[4,48,1152]{2,1,0:T(8,128)(2,1)S(1)}, bf16[4,48,1152]{2,1,0:T(8,128)(2,1)S(1)}, u32[]{:S(2)}, u32[]{:S(2)}) collective-permute-start(bf16[4,48,1152]{2,1,0:T(8,128)(2,1)S(1)} %get-tuple-element.249), channel_id=1, source_target_pairs={{0,4},{1,3},{2,6},{3,1},{4,0},{5,7},{6,2},{7,5},{8,12},{9,11},{10,... | collective-permute-start | bytes 1327112 | tf_op jit(solution)/shard_map/ppermute | solution.py:85
  289.9 14.7 %collective-permute-start.42 = (bf16[8,48,512]{2,1,0:T(8,128)(2,1)S(1)}, bf16[8,48,512]{2,1,0:T(8,128)(2,1)S(1)}, u32[]{:S(2)}, u32[]{:S(2)}) collective-permute-start(bf16[8,48,512]{2,1,0:T(8,128)(2,1)S(1)} %get-tuple-element.253), channel_id=1, source_target_pairs={{0,2},{1,5},{2,0},{3,7},{4,6},{5,1},{6,4},{7,3},{8,10},{9,13},{10,... | collective-permute-start | bytes 1179656 | tf_op jit(solution)/shard_map/ppermute | solution.py:85
  296.8 9.3 %collective-permute-start.43 = (bf16[1,48,1536]{2,1,0:T(8,128)(2,1)S(1)}, bf16[1,48,1536]{2,1,0:T(8,128)(2,1)S(1)}, u32[]{:S(2)}, u32[]{:S(2)}) collective-permute-start(bf16[1,48,1536]{2,1,0:T(8,128)(2,1)S(1)} %get-tuple-element.256), channel_id=1, source_target_pairs={{0,8},{1,9},{2,10},{3,11},{4,12},{5,13},{6,14},{7,15},{8,0},{9,1},... | collective-permute-start | bytes 442376 | tf_op jit(solution)/shard_map/ppermute | solution.py:85
  302.4 12.5 %collective-permute-start.44 = (bf16[2,48,1152]{2,1,0:T(8,128)(2,1)S(1)}, bf16[2,48,1152]{2,1,0:T(8,128)(2,1)S(1)}, u32[]{:S(2)}, u32[]{:S(2)}) collective-permute-start(bf16[2,48,1152]{2,1,0:T(8,128)(2,1)S(1)} %get-tuple-element.260), channel_id=1, source_target_pairs={{0,16},{1,17},{2,18},{3,19},{4,20},{5,21},{6,22},{7,23},{8,24},{9,... | collective-permute-start | bytes 663560 | tf_op jit(solution)/shard_map/ppermute | solution.py:85
  304.5 29.3 %collective-permute-start.49 = (bf16[512,768]{1,0:T(8,128)(2,1)S(1)}, bf16[512,768]{1,0:T(8,128)(2,1)S(1)}, u32[]{:S(2)}, u32[]{:S(2)}) collective-permute-start(bf16[512,768]{1,0:T(8,128)(2,1)S(1)} %get-tuple-element.234), channel_id=1, source_target_pairs={{0,8},{1,9},{2,10},{3,11},{4,12},{5,13},{6,14},{7,15},{8,0},{9,1},... | collective-permute-start | bytes 2359304 | tf_op jit(solution)/shard_map/ppermute | solution.py:85
  304.5 13.8 %collective-permute-start.46 = (bf16[2,192,384]{2,1,0:T(8,128)(2,1)S(1)}, bf16[2,192,384]{2,1,0:T(8,128)(2,1)S(1)}, u32[]{:S(2)}, u32[]{:S(2)}) collective-permute-start(bf16[2,192,384]{2,1,0:T(8,128)(2,1)S(1)} %add_last.4.refs_0_), channel_id=1, source_target_pairs={{0,1},{1,0},{2,3},{3,2},{4,5},{5,4},{6,7},{7,6},{8,9},{9,8},{10,11... | collective-permute-start | bytes 884744 | tf_op jit(solution)/shard_map/ppermute | solution.py:85
  305.2 10.4 %collective-permute-start.45 = (bf16[4,48,512]{2,1,0:T(8,128)(2,1)S(1)}, bf16[4,48,512]{2,1,0:T(8,128)(2,1)S(1)}, u32[]{:S(2)}, u32[]{:S(2)}) collective-permute-start(bf16[4,48,512]{2,1,0:T(8,128)(2,1)S(1)} %get-tuple-element.263), channel_id=1, source_target_pairs={{0,4},{1,3},{2,6},{3,1},{4,0},{5,7},{6,2},{7,5},{8,12},{9,11},{10,... | collective-permute-start | bytes 589832 | tf_op jit(solution)/shard_map/ppermute | solution.py:85
  306.7 13.2 %collective-permute-start.47 = (bf16[2,48,1536]{2,1,0:T(8,128)(2,1)S(1)}, bf16[2,48,1536]{2,1,0:T(8,128)(2,1)S(1)}, u32[]{:S(2)}, u32[]{:S(2)}) collective-permute-start(bf16[2,48,1536]{2,1,0:T(8,128)(2,1)S(1)} %add_last.5.refs_0_), channel_id=1, source_target_pairs={{0,1},{1,0},{2,3},{3,2},{4,5},{5,4},{6,7},{7,6},{8,9},{9,8},{10,11... | collective-permute-start | bytes 884744 | tf_op jit(solution)/shard_map/ppermute | solution.py:85
  315.5 20.2 %collective-permute-start.50 = (bf16[1,48,1152]{2,1,0:T(8,128)(2,1)S(1)}, bf16[1,48,1152]{2,1,0:T(8,128)(2,1)S(1)}, u32[]{:S(2)}, u32[]{:S(2)}) collective-permute-start(bf16[1,48,1152]{2,1,0:T(8,128)(2,1)S(1)} %get-tuple-element.267), channel_id=1, source_target_pairs={{0,8},{1,9},{2,10},{3,11},{4,12},{5,13},{6,14},{7,15},{8,0},{9,1},... | collective-permute-start | bytes 331784 | tf_op jit(solution)/shard_map/ppermute | solution.py:85
  316.2 13.6 %collective-permute-start.48 = (bf16[2,48,512]{2,1,0:T(8,128)(2,1)S(1)}, bf16[2,48,512]{2,1,0:T(8,128)(2,1)S(1)}, u32[]{:S(2)}, u32[]{:S(2)}) collective-permute-start(bf16[2,48,512]{2,1,0:T(8,128)(2,1)S(1)} %get-tuple-element.270), channel_id=1, source_target_pairs={{0,16},{1,17},{2,18},{3,19},{4,20},{5,21},{6,22},{7,23},{8,24},{9,... | collective-permute-start | bytes 294920 | tf_op jit(solution)/shard_map/ppermute | solution.py:85
  330.4 6.0 %collective-permute-start.51 = (bf16[1,48,512]{2,1,0:T(8,128)(2,1)S(1)}, bf16[1,48,512]{2,1,0:T(8,128)(2,1)S(1)}, u32[]{:S(2)}, u32[]{:S(2)}) collective-permute-start(bf16[1,48,512]{2,1,0:T(8,128)(2,1)S(1)} %get-tuple-element.275), channel_id=1, source_target_pairs={{0,8},{1,9},{2,10},{3,11},{4,12},{5,13},{6,14},{7,15},{8,0},{9,1},... | collective-permute-start | bytes 147464 | tf_op jit(solution)/shard_map/ppermute | solution.py:85
  (38 other events, 233.1 us)

commit v3 on v2

--- a/solution.py
+++ b/solution.py
@@ -22,7 +22,6 @@
 MIB = 2**20
 AT_OUT = 3 * D
 AT_VEC = 4 * D
-W_ONE = 4 * D + 256
 
 
 def smem():
@@ -35,6 +34,10 @@
 
 def cost(us):
     return pl.CostEstimate(flops=int(us * 1.0e9), transcendentals=0, bytes_accessed=int(us * 3.0e6))
+
+
+def behind(us):
+    return cost(4 * us)
 
 
 def params(mib):
@@ -75,10 +78,42 @@
         return out
 
 
-def halves(ref_pairs, core, width, source):
-    for q, ref in enumerate(ref_pairs):
-        at = pl.multiple_of((core ^ q) * width, 128)
-        ref[...] = source[:, pl.ds(at, width)]
+def in_vmem(kernel, name, us, outs, *args, mib=24):
+    return pl.pallas_call(
+        kernel,
+        out_shape=tuple(shape(*o) for o in outs),
+        in_specs=[smem() if a.ndim == 1 else vmem() for a in args],
+        out_specs=tuple(vmem() for _ in outs),
+        compiler_params=params(mib),
+        name=name,
+        cost_estimate=cost(us),
+    )(*args)
+
+
+def wide(width, reps):
+    unit = 128 * reps
+    return -(-width // unit) * unit
+
+
+def by_core(core, reps, width, move):
+    if width % 128 == 0:
+        move(pl.ds(pl.multiple_of(core * width, 128), width))
+        return
+    for c in range(reps):
+
+        @pl.when(core == c)
+        def one(c=c):
+            move(slice(c * width, (c + 1) * width))
+
+
+def halves(refs, core, source):
+    width = refs[0].shape[1]
+    for q, ref in enumerate(refs):
+
+        def move(lanes, ref=ref):
+            ref[...] = source[:, lanes]
+
+        by_core(core ^ q, len(refs), width, move)
 
 
 def send(v, pairs):
@@ -116,21 +151,75 @@
         owner = core ^ q
         p1 = 1 + owner % 2
         p2 = 2 - owner % 2
-        lanes = pl.ds(pl.multiple_of(owner * width, 128), width)
-        for b in range(2):
-            for f in range(2):
-                for k in range(depth):
-                    dst = (me ^ (b * p2) ^ (f * p1)) ^ (4 * k)
-                    out[pl.ds(dst, 1), :, lanes] = bufs[q * 2 + b][pl.ds(f * depth + k, 1)]
-
-
-def shards_of(plan, where, shard):
-    core, tower = where[1], where[2]
-    rows, whole = shard.shape[1:]
-    width = whole // plan.reps
-    mine = lax.dynamic_slice(shard, (tower, 0, core * width), (1, rows, width))
-    other = lax.dynamic_slice(shard, (1 - tower, 0, core * width), (1, rows, width))
-    return mine, other
+
+        def move(lanes, q=q, p1=p1, p2=p2):
+            for b in range(2):
+                for f in range(2):
+                    for k in range(depth):
+                        dst = (me ^ (b * p2) ^ (f * p1)) ^ (4 * k)
+                        out[pl.ds(dst, 1), :, lanes] = bufs[q * 2 + b][pl.ds(f * depth + k, 1)]
+
+        by_core(owner, reps, width, move)
+
+
+def shards_kernel(reps, where_ref, qkv_ref, out_ref, bias_ref, gain_ref, up_ref, down_ref, *rest):
+    outs, full_ref = rest[:-1], rest[-1]
+    core, tower = where_ref[1], where_ref[2]
+    spare = full_ref.shape[2] - AT_VEC
+
+    def turned(ref, t, at):
+        rows = ref[t][0].astype(F32)
+        i = lax.broadcasted_iota(jnp.int32, (rows.shape[0], spare), 0)
+        j = lax.broadcasted_iota(jnp.int32, (rows.shape[0], spare), 1)
+        return t_dot(rows.astype(BF), jnp.where(i + at == j, 1.0, 0.0).astype(BF))
+
+    for n in range(2):
+        t = pl.ds(tower if n == 0 else 1 - tower, 1)
+        full_ref[:, :, :AT_OUT] = qkv_ref[t]
+        full_ref[:, :, AT_OUT:AT_VEC] = out_ref[t]
+        full_ref[0, :, AT_VEC:] = (turned(bias_ref, t, 0) + turned(gain_ref, t, bias_ref.shape[1])).astype(BF)
+        for c, ref in enumerate((full_ref, up_ref, down_ref)):
+            put = outs[2 * c + n]
+
+            def move(lanes, ref=ref, put=put, t=t):
+                put[...] = ref[:, :, lanes] if ref is full_ref else ref[t, :, lanes]
+
+            by_core(core, reps, put.shape[2], move)
+
+
+def shards_of(plan, order, w_qkv, w_out, biases, gains, w_up, w_down):
+    reps = plan.reps
+    one = wide(AT_VEC + 128, reps)
+    outs = []
+    for rows, width in ((w_qkv.shape[1], one), (w_up.shape[1], FF), (w_down.shape[1], D)):
+        outs += [shape((1, rows, width // reps), BF)] * 2
+    args = (w_qkv, w_out, biases, gains, w_up, w_down)
+    got = pl.pallas_call(
+        partial(shards_kernel, reps),
+        grid=(1,),
+        out_shape=tuple(outs),
+        in_specs=[smem()] + [still(a.shape) for a in args],
+        out_specs=[still(o.shape) for o in outs],
+        scratch_shapes=[pltpu.VMEM((1, w_qkv.shape[1], one), BF)],
+        compiler_params=params(24),
+        name="shards",
+        cost_estimate=cost(2),
+    )(order.where, *[stay(a) for a in args])
+    return order.done(got)
+
+
+def join_kernel(where_ref, *refs):
+    ins, out_ref = refs[:-1], refs[-1]
+    at = 0
+    for ref in ins:
+        out_ref[at : at + ref.shape[0]] = ref[...]
+        at += ref.shape[0]
+
+
+def join(order, *bufs):
+    total = sum(b.shape[0] for b in bufs)
+    outs = (((total,) + bufs[0].shape[1:], bufs[0].dtype),)
+    return order.done(in_vmem(join_kernel, "join", 0.5, outs, order.where, *bufs))[0]
 
 
 def gather_line(plan, mine, other):
@@ -220,18 +309,6 @@
     return (a.astype(F32) + b.astype(F32)).astype(BF)
 
 
-def in_vmem(kernel, name, us, outs, *args, mib=24):
-    return pl.pallas_call(
-        kernel,
-        out_shape=tuple(shape(*o) for o in outs),
-        in_specs=[smem() if a.ndim == 1 else vmem() for a in args],
-        out_specs=tuple(vmem() for _ in outs),
-        compiler_params=params(mib),
-        name=name,
-        cost_estimate=cost(us),
-    )(*args)
-
-
 class Scatter:
     def __init__(self, plan, order, parts, rows):
         self.plan, self.order, self.rows = plan, order, rows
@@ -260,7 +337,7 @@
                 scratch_shapes=[pltpu.VMEM(whole, BF), pltpu.SemaphoreType.DMA((n,))],
                 compiler_params=params(24),
                 name="pick_add",
-                cost_estimate=cost(3),
+                cost_estimate=behind(3),
             )(self.order.where, stay(self.own), self.rest)
         )
         self.r1 = send(hs, plan.first())
@@ -343,14 +420,14 @@
 
 
 def attend_kernel(part, where_ref, x_ref, w_ref, *rest):
-    proj_ref, probs_ref, attn_ref, hat_ref, rstd_ref, norm_ref, vec_ref, bias_ref = rest[-8:]
+    proj_ref, probs_ref, attn_ref, hat_ref, rstd_ref, norm_ref, vec_ref, cls_ref, bias_ref = rest[-9:]
 
     @pl.when(pl.program_id(0) == 0)
     def prepare():
         vec_ref[...] = jnp.transpose(w_ref[:, AT_VEC : AT_VEC + 128].astype(F32))
         span = where_ref[3]
-        row = lax.broadcasted_iota(jnp.int32, (2 * BLOCK, BLOCK), 0) % BLOCK
-        col = lax.broadcasted_iota(jnp.int32, (2 * BLOCK, BLOCK), 1)
+        row = lax.broadcasted_iota(jnp.int32, (BLOCK, 2 * BLOCK), 0)
+        col = lax.broadcasted_iota(jnp.int32, (BLOCK, 2 * BLOCK), 1) % BLOCK
         bias_ref[...] = jnp.where((row ^ col) < span, 0.0, -1e30)
 
     x = x_ref[...]
@@ -368,17 +445,20 @@
             q = proj_ref[rows, lanes]
             k = proj_ref[rows, D + pair * 128 : D + (pair + 1) * 128]
             v = proj_ref[rows, 2 * D + pair * 128 : 2 * D + (pair + 1) * 128]
-            s = dot_t(jnp.concatenate([q * low, q * high], 0), k) * HEAD**-0.5 + bias
-            e = jnp.exp(s - jnp.max(s, -1, keepdims=True))
-            p = (e * (1.0 / jnp.sum(e, -1, keepdims=True))).astype(BF)
+            s = dot_t(k, jnp.concatenate([q * low, q * high], 0)) * HEAD**-0.5 + bias
+            e = jnp.exp(s - jnp.max(s, 0, keepdims=True))
+            p = (e * (1.0 / jnp.sum(e, 0, keepdims=True))).astype(BF)
             probs_ref[blk, pair] = p
-            wide = jnp.concatenate([p[:BLOCK], p[BLOCK:]], 1)
-            attn_ref[rows, lanes] = dot(wide, jnp.concatenate([v * low, v * high], 0)).astype(BF)
+            tall = jnp.concatenate([p[:, :BLOCK], p[:, BLOCK:]], 0)
+            attn_ref[rows, lanes] = t_dot(tall, jnp.concatenate([v * low, v * high], 0)).astype(BF)
     hidden = x.astype(F32) + (dot(attn_ref[...], w_ref[:, AT_OUT:AT_VEC]) + vec_ref[2:3, :])
     hat, rstd = normalize(hidden)
     hat_ref[...] = hat
     rstd_ref[...] = rstd
-    norm_ref[...] = (hat * vec_ref[10:11, :] + vec_ref[3:4, :]).astype(BF)
+    norm = hat * vec_ref[10:11, :] + vec_ref[3:4, :]
+    norm_ref[...] = norm.astype(BF)
+    for j in range(TILE // 32):
+        cls_ref[j : j + 1, :] = norm[32 * j : 32 * j + 1, :]
 
 
 def attend(order, x, w_one, part, before=()):
@@ -395,24 +475,26 @@
         grid=(steps,),
         out_shape=(
             far((rows, 3 * D), BF),
-            far((rows // BLOCK, PAIRS, 2 * BLOCK, BLOCK), BF),
+            far((rows // BLOCK, PAIRS, BLOCK, 2 * BLOCK), BF),
             far((rows, D), BF),
             far((rows, D), F32),
             far((rows, 1), F32),
             far((rows, D), BF),
             shape((128, D), F32),
+            shape((rows // 64, D), F32),
         ),
-        in_specs=[smem(), here(D), still(w_one.shape)] + [pl.BlockSpec(memory_space=pl.ANY)] * len(before),
+        in_specs=[smem(), here(D), vmem()] + [pl.BlockSpec(memory_space=pl.ANY)] * len(before),
         out_specs=[
             here(3 * D),
-            pl.BlockSpec((per, PAIRS, 2 * BLOCK, BLOCK), lambda i: (i + first, 0, 0, 0)),
+            pl.BlockSpec((per, PAIRS, BLOCK, 2 * BLOCK), lambda i: (i + first, 0, 0, 0)),
             here(D),
             here(D),
             here(1),
             here(D),
             still((128, D)),
+            rows_at(D, TILE // 32),
         ],
-        scratch_shapes=[pltpu.VMEM((2 * BLOCK, BLOCK), F32)],
+        scratch_shapes=[pltpu.VMEM((BLOCK, 2 * BLOCK), F32)],
         input_output_aliases={3 + j: j for j in range(len(before))},
         compiler_params=params(24),
         name="attend",
@@ -421,15 +503,8 @@
 
 
 def gelu_pair(u):
-    t = 1.0 / (1.0 + (0.3275911 * 2**-0.5) * jnp.abs(u))
-    e = jnp.exp(-0.5 * u * u)
-    poly = t * (
-        0.5 * 0.254829592
-        + t * (0.5 * -0.284496736 + t * (0.5 * 1.421413741 + t * (0.5 * -1.453152027 + t * (0.5 * 1.061405429))))
-    )
-    tail = poly * e
-    phi = jnp.where(u < 0, tail, 1.0 - tail)
-    return u * phi, phi + u * (e * 0.3989422804014327)
+    phi = 0.5 + 0.5 * lax.erf(u * 2**-0.5)
+    return u * phi, phi + u * (jnp.exp(-0.5 * u * u) * (2 * jnp.pi) ** -0.5)
 
 
 def up_kernel(first, where_ref, norm_ref, w_ref, vec_ref, *rest):
@@ -466,115 +541,152 @@
     )(order.where, norm, w_up, vec, *[stay(b) for b in before])
 
 
-def down_kernel(where_ref, act_ref, w_ref, hat_ref, vec_ref, out_ref, hat2_ref, rstd2_ref, cls_ref):
+def down_kernel(where_ref, act_ref, w_ref, hat_ref, vec_ref, own_ref, far_ref, hat2_ref, rstd2_ref):
     normed = hat_ref[...] * vec_ref[10:11, :] + vec_ref[3:4, :]
     second = normed + (dot(act_ref[...], w_ref[...]) + vec_ref[8:9, :])
     hat, rstd = normalize(second)
     hat2_ref[...] = hat
     rstd2_ref[...] = rstd
-    out = hat * vec_ref[11:12, :] + vec_ref[9:10, :]
-    out_ref[...] = out.astype(BF)
-    for j in range(TILE // 32):
-        cls_ref[j : j + 1, :] = out[32 * j : 32 * j + 1, :]
+    out = (hat * vec_ref[11:12, :] + vec_ref[9:10, :]).astype(BF)
+    half = pl.num_programs(0) // 2
+
+    @pl.when(pl.program_id(0) < half)
+    def near():
+        own_ref[...] = out
+
+    @pl.when(pl.program_id(0) >= half)
+    def away():
+        far_ref[...] = out
 
 
 def down(order, act, w_down, hat, vec):
     rows = act.shape[0]
+    half = rows // TILE // 2
+    near = pl.BlockSpec((TILE, D), lambda i: (jnp.minimum(i, half - 1), 0))
+    away = pl.BlockSpec((TILE, D), lambda i: (jnp.maximum(i - half, 0), 0))
     return pl.pallas_call(
         down_kernel,
         grid=(rows // TILE,),
-        out_shape=(far((rows, D), BF), far((rows, D), F32), far((rows, 1), F32), shape((rows // 32, D), F32)),
-        in_specs=[smem(), rows_at(FF), still(w_down.shape), rows_at(D), still(vec.shape)],
-        out_specs=[rows_at(D), rows_at(D), rows_at(1), rows_at(D, TILE // 32)],
+        out_shape=(far((rows // 2, D), BF), shape((rows // 2, D), BF), far((rows, D), F32), far((rows, 1), F32)),
+        in_specs=[smem(), rows_at(FF), vmem(), rows_at(D), still(vec.shape)],
+        out_specs=[near, away, rows_at(D), rows_at(1)],
         compiler_params=params(24),
         name="down",
         cost_estimate=cost(8),
-    )(order.where, stay(act), w_down, hat, vec)
-
-
-def contrast_kernel(reps, depth, per, where_ref, q_ref, p_ref, loss_ref, grad_ref, acc_ref):
-    i = pl.program_id(0)
+    )(order.where, stay(act), w_down, stay(hat), vec)
+
+
+def first_kernel(where_ref, a_ref, b_ref, up_ref, down_ref, vec_ref, marks_ref, msg_ref):
+    norm = jnp.concatenate([a_ref[...], b_ref[...]], 0)
+    second = norm + vec_ref[8:9, :]
+    wide = norm.astype(BF)
+    for j in range(FF // D):
+        u = dot(wide, up_ref[:, j * D : (j + 1) * D]) + vec_ref[4 + j : 5 + j, :]
+        second = second + dot(gelu_pair(u)[0].astype(BF), down_ref[j * D : (j + 1) * D, :])
+    hat, _ = normalize(second)
+    msg_ref[:, :D] = (hat * vec_ref[11:12, :] + vec_ref[9:10, :]).astype(BF)
+    marks = marks_ref[...].astype(F32)
+    pad = jnp.zeros((32 - marks.shape[0], marks.shape[1]), F32)
+    msg_ref[:, D:] = jnp.concatenate([marks, pad], 0).astype(BF)
+
+
+def first_rows(order, a, b, w_up, w_down, vec, positives):
+    outs = (((32, D + positives.shape[1]), BF),)
+    return order.done(in_vmem(first_kernel, "first_rows", 4, outs, order.where, a, b, w_up, w_down, vec, positives))[0]
+
+
+def pack_kernel(per, where_ref, *refs):
+    msgs, out_ref = refs[:-1], refs[-1]
+    queries = per * 4
+    pick_row = lax.broadcasted_iota(jnp.int32, (16, 32), 0)
+    pick_col = lax.broadcasted_iota(jnp.int32, (16, 32), 1)
+    pick = jnp.where((pick_col == pick_row * (32 // (2 * per))) & (pick_row < 2 * per), 1.0, 0.0).astype(BF)
+    for n in range(len(msgs) // 2):
+        for tower in range(2):
+
+            @pl.when(where_ref[2] == tower)
+            def put(n=n, tower=tower):
+                zero, one = msgs[2 * n + tower], msgs[2 * n + 1 - tower]
+                out_ref[n, :32, :D] = zero[:, :D]
+                out_ref[n, :queries, D:] = zero[:queries, D:]
+                out_ref[n, queries:32, D:] = one[:queries, D:]
+                out_ref[n, 32:, :D] = dot(pick, one[:, :D]).astype(BF)
+                out_ref[n, 32:, D:] = jnp.zeros((16, out_ref.shape[2] - D), BF)
+
+
+def contrast_kernel(reps, depth, per, where_ref, *refs):
+    parts, loss_ref, grad_ref, acc_ref = refs[:reps], refs[reps], refs[reps + 1], refs[reps + 2]
     me, core, tower = where_ref[0], where_ref[1], where_ref[2]
-    pieces = p_ref.shape[0]
-    total_p = pieces * per * 2
-    cls_q = q_ref[:, :32, :D].reshape(-1, D)
-    marks = q_ref[:, :32, D:].reshape(-1, q_ref.shape[2] - D)
-    cls_p = p_ref[:, 32:, :D].reshape(-1, D)
+    pieces = parts[0].shape[0]
+    passages = parts[0].shape[2] - D
+    cls_p = jnp.concatenate([part[:, 32:, :D].reshape(pieces * 16, D) for part in parts], 0)
     cols = cls_p.shape[0]
-    col = lax.broadcasted_iota(jnp.int32, (marks.shape[1], cols), 1)
-    row = lax.broadcasted_iota(jnp.int32, (marks.shape[1], cols), 0)
+    col = lax.broadcasted_iota(jnp.int32, (passages, cols), 1)
+    row = lax.broadcasted_iota(jnp.int32, (passages, cols), 0)
     j, slot = col // 16, col % 16
-    line = j % (depth // 2)
-    flip = (j // (depth // 2)) % 4
-    from_core = core ^ (j // (2 * depth))
-    base = (me | 4) ^ (8 * line) ^ flip
+    base = (me | 4) ^ (8 * (j % (depth // 2))) ^ ((j // (depth // 2)) % 4)
     owner = jnp.where(slot < per, base, base ^ 4)
-    passage = (owner * reps + from_core) * per + slot % per
-    good = slot < 2 * per
-    pick = jnp.where((row == passage) & good, 1.0, 0.0).astype(BF)
-    marked_cols = dot(marks, pick)
+    passage = (owner * reps + (core ^ (j // (2 * depth)))) * per + slot % per
+    pick = jnp.where((row == passage) & (slot < 2 * per), 1.0, 0.0).astype(BF)
     valid = lax.broadcasted_iota(jnp.int32, (1, cols), 1) % 16 < 2 * per
-    raw = jnp.where(valid, dot_t(cls_q, cls_p) * D**-0.5, -1e30)
-    e = jnp.exp(raw - jnp.max(raw, -1, keepdims=True))
-    total = jnp.sum(e, -1, keepdims=True)
-    me_ = marked_cols * e
-    marked = jnp.sum(me_, -1, keepdims=True)
-    grad = (LOSS_WEIGHT * (e / total - me_ / marked)).astype(BF)
-    part = t_dot(grad[:, :128], cls_q) * D**-0.5
-
-    @pl.when(i == 0)
-    def first():
-        loss_ref[...] = (jnp.log(total) - jnp.log(marked))[:32]
-        acc_ref[...] = jnp.zeros_like(acc_ref)
-        grad_ref[...] = dot(grad[:32], cls_p) * D**-0.5
-
-    acc_ref[...] += part
-
-    @pl.when((i == pl.num_programs(0) - 1) & (tower == 1))
-    def last():
+    acc_ref[...] = jnp.zeros_like(acc_ref)
+    group = min(8, pieces)
+    for q, part in enumerate(parts):
+        for at in range(0, pieces, group):
+            cls_q = part[at : at + group, :32, :D].reshape(group * 32, D)
+            marks = dot(part[at : at + group, :32, D:].reshape(group * 32, passages), pick)
+            raw = jnp.where(valid, dot_t(cls_q, cls_p) * D**-0.5, -1e30)
+            e = jnp.exp(raw - jnp.max(raw, -1, keepdims=True))
+            total = jnp.sum(e, -1, keepdims=True)
+            me_ = marks * e
+            marked = jnp.sum(me_, -1, keepdims=True)
+            grad = (LOSS_WEIGHT * (e / total - me_ / marked)).astype(BF)
+            acc_ref[...] += t_dot(grad[:, :128], cls_q)[:16] * D**-0.5
+            if q == 0 and at == 0:
+                loss_ref[...] = (jnp.log(total) - jnp.log(marked))[:32]
+                grad_ref[...] = dot(grad[:32], cls_p) * D**-0.5
+
+    @pl.when(tower == 1)
+    def passages_own():
         grad_ref[...] = jnp.zeros_like(grad_ref)
         for s in range(2 * per):
             at = s * (32 // (2 * per))
             grad_ref[at : at + 1, :] = acc_ref[s : s + 1, :]
 
 
-def contrast(plan, order, cls, positives):
-    where = order.where
-    tower = where[2]
-    queries, passages = positives.shape
-    per = queries // 4
-    marks = jnp.pad(positives.astype(BF), ((0, 32 - queries), (0, 0)))
-    msg = jnp.concatenate([cls.astype(BF), marks], 1)
-    got = [msg] + [send(msg, plan.along(k)) for k in range(1, plan.depth)]
-    same, other = jnp.stack(got[0::2]), jnp.stack(got[1::2])
-    zero = jnp.where(tower == 0, same, other)
-    one = jnp.where(tower == 0, other, same)
-    marks = jnp.concatenate([zero[:, :queries, D:], one[:, :queries, D:]], 1)
-    top = jnp.concatenate([zero[:, :, :D], marks], 2)
-    low = jnp.pad(one[:, :: 32 // (2 * per)], ((0, 0), (0, 16 - 2 * per), (0, 0)))
-    buf = jnp.concatenate([top, low], 1)
-    buf = jnp.concatenate([buf] + [send(buf, plan.pairs(lambda r, m=m: (m, 0))) for m in range(1, 4)], 0)
-    buf = jnp.concatenate([buf] + [send(buf, plan.sibling(s)) for s in range(1, plan.reps)], 0)
-    pieces = buf.shape[0]
-    group = min(16, pieces)
-    width = buf.shape[2]
-    loss, grad = pl.pallas_call(
-        partial(contrast_kernel, plan.reps, plan.depth, per),
-        grid=(pieces // group,),
-        out_shape=(jax.ShapeDtypeStruct((32, 1), F32), jax.ShapeDtypeStruct((32, D), F32)),
-        in_specs=[
-            smem(),
-            pl.BlockSpec((group, 48, width), lambda i: (i, 0, 0)),
-            still(buf.shape),
-        ],
-        out_specs=[still((32, 1)), still((32, D))],
-        scratch_shapes=[pltpu.VMEM((128, D), F32)],
-        compiler_params=params(32),
-        name="contrast",
-        cost_estimate=cost(2),
-    )(where, buf, buf)
-    loss = lax.dynamic_slice(loss, (tower * queries, 0), (queries, 1))[:, 0]
-    return loss, grad
+class Contrast:
+    def __init__(self, plan, order, msg, queries):
+        self.plan, self.order, self.queries = plan, order, queries
+        self.msgs = [msg] + [send(msg, plan.along(k)) for k in range(1, plan.depth)]
+
+    def pack(self):
+        plan = self.plan
+        outs = (((plan.depth // 2, 48, self.msgs[0].shape[1]), BF),)
+        kernel = partial(pack_kernel, self.queries // 4)
+        (buf,) = self.order.done(in_vmem(kernel, "pack", 1, outs, self.order.where, *self.msgs))
+        self.bufs = [buf] + [send(buf, plan.pairs(lambda r, m=m: (m, 0))) for m in range(1, 4)]
+
+    def join(self):
+        plan = self.plan
+        buf = join(self.order, *self.bufs)
+        self.parts = [buf] + [send(buf, plan.sibling(s)) for s in range(1, plan.reps)]
+
+    def loss(self):
+        plan, order = self.plan, self.order
+        loss, grad = order.done(
+            pl.pallas_call(
+                partial(contrast_kernel, plan.reps, plan.depth, self.queries // 4),
+                out_shape=(shape((32, 1), F32), shape((32, D), F32)),
+                in_specs=[smem()] + [vmem()] * plan.reps,
+                out_specs=(vmem(), vmem()),
+                scratch_shapes=[pltpu.VMEM((16, D), F32)],
+                compiler_params=params(40),
+                name="contrast",
+                cost_estimate=cost(2),
+            )(order.where, *self.parts)
+        )
+        at = order.where[2] * self.queries
+        return lax.dynamic_slice(loss, (at, 0), (self.queries, 1))[:, 0], grad
 
 
 def norm_back(grad, hat, rstd, gain):
@@ -589,7 +701,7 @@
 
 
 def top_kernel(
-    reps, where_ref, cot_ref, cls_ref, hat_ref, rstd_ref, vec_ref, act_ref, second_ref, gs_ref, sums_ref, *rest
+    where_ref, cot_ref, cls_ref, hat_ref, rstd_ref, vec_ref, act_ref, second_ref, gs_ref, sums_ref, *rest
 ):
     parts, full_ref = rest[:-1], rest[-1]
 
@@ -612,14 +724,14 @@
             sums_ref[2:3, :] += col_sum(dout * hat)
 
     full_ref[...] = t_dot(act_ref[...], gs_ref[...]).astype(BF)
-    halves(parts, where_ref[1], D // reps, full_ref)
+    halves(parts, where_ref[1], full_ref)
 
 
 def top(plan, order, cot, cls_grad, hat2, rstd2, vec, act):
     rows = cot.shape[0]
     part = D // plan.reps
     second, gs, sums, *parts = pl.pallas_call(
-        partial(top_kernel, plan.reps),
+        top_kernel,
         grid=(FF // D,),
         out_shape=(far((rows, D), F32), shape((rows, D), BF), shape((8, D), F32))
         + (far((FF, part), BF),) * plan.reps,
@@ -636,7 +748,7 @@
         scratch_shapes=[pltpu.VMEM((D, D), BF)],
         compiler_params=params(28),
         name="top",
-        cost_estimate=cost(11),
+        cost_estimate=behind(11),
     )(order.where, cot, cls_grad, hat2, rstd2, vec, stay(act))
     return second, gs, sums, parts
 
@@ -697,7 +809,7 @@
         ),
         compiler_params=params(28),
         name="gelu_back",
-        cost_estimate=cost(20),
+        cost_estimate=behind(20),
     )(order.where, gs, stay(w_down), stay(slope), norm, stay(w_up))
     return acc, sums, parts
 
@@ -733,7 +845,7 @@
         out_specs=[rows_at(D), rows_at(D), rows_at(D), still((8, D))],
         compiler_params=params(20),
         name="hidden_back",
-        cost_estimate=cost(5),
+        cost_estimate=behind(5),
     )(order.where, acc, stay(second), stay(hat), stay(rstd), stay(w_one), vec)
 
 
@@ -746,11 +858,11 @@
     q2 = jnp.concatenate([q * low, q * high], 0)
     k2 = jnp.concatenate([k * low, k * high], 0)
     p = probs_ref[block, pair]
-    dp = dot_t(a2, v)
+    dp = dot_t(v, a2)
     pf = p.astype(F32)
-    ds = (pf * (dp - jnp.sum(pf * dp, -1, keepdims=True)) * HEAD**-0.5).astype(BF)
-    wide = jnp.concatenate([ds[:BLOCK], ds[BLOCK:]], 1)
-    return dot(wide, k2).astype(BF), t_dot(ds, q2).astype(BF), t_dot(p, a2).astype(BF)
+    ds = (pf * (dp - jnp.sum(pf * dp, 0, keepdims=True)) * HEAD**-0.5).astype(BF)
+    tall = jnp.concatenate([ds[:, :BLOCK], ds[:, BLOCK:]], 0)
+    return t_dot(tall, k2).astype(BF), dot(ds, q2).astype(BF), dot(p, a2).astype(BF)
 
 
 def heads_back(first, count, at, ga_ref, proj_ref, probs_ref, gp_ref):
@@ -765,22 +877,8 @@
                 gp_ref[to, lane : lane + 128] = grad
 
 
-def attend_back_kernel(
-    reps, count, where_ref, ga_ref, proj_ref, probs_ref, x_ref, attn_ref, go_ref, gp_ref, sums_ref, *rest
-):
-    parts, full_ref = rest[:-1], rest[-1]
-    i = pl.program_id(0)
-    part = count * 128
-    heads_back(0, count, i * TILE, ga_ref, proj_ref, probs_ref, gp_ref)
-
-    @pl.when(i == pl.num_programs(0) - 1)
-    def weights():
-        sums_ref[...] = jnp.zeros_like(sums_ref)
-        sums_ref[0:1, :] = col_sum(gp_ref[:, :part].astype(F32))
-        sums_ref[1:2, :] = col_sum(gp_ref[:, 2 * part :].astype(F32))
-        full_ref[:, :D] = t_dot(attn_ref[...], go_ref[...]).astype(BF)
-        full_ref[:, D:] = t_dot(x_ref[...], gp_ref[...]).astype(BF)
-        halves(parts, where_ref[1], full_ref.shape[1] // reps, full_ref)
+def attend_back_kernel(first, count, where_ref, ga_ref, proj_ref, probs_ref, gp_ref):
+    heads_back(first, count, 0, ga_ref, proj_ref, probs_ref, gp_ref)
 
 
 def tile_specs(first):
@@ -788,27 +886,78 @@
     return [
         pl.BlockSpec((TILE, D), lambda i: (i + first, 0)),
         pl.BlockSpec((TILE, 3 * D), lambda i: (i + first, 0)),
-        pl.BlockSpec((per, PAIRS, 2 * BLOCK, BLOCK), lambda i: (i + first, 0, 0, 0)),
+        pl.BlockSpec((per, PAIRS, BLOCK, 2 * BLOCK), lambda i: (i + first, 0, 0, 0)),
     ]
 
 
-def attend_back(plan, order, count, ga, proj, probs, x, attn, go):
-    rows = ga.shape[0]
+def attend_back(order, first, count, ga, proj, probs, rows):
+    wide = 3 * count * 128
+    return pl.pallas_call(
+        partial(attend_back_kernel, first, count),
+        grid=(rows // TILE,),
+        out_shape=shape((rows, wide), BF),
+        in_specs=[smem()] + tile_specs(0),
+        out_specs=rows_at(wide),
+        compiler_params=params(20),
+        name="attend_back",
+        cost_estimate=behind(10 * count * rows // 4096),
+    )(order.where, ga, stay(proj), stay(probs))
+
+
+def both_rows(x_ref, near_ref, far_ref):
+    half = near_ref.shape[0]
+    return (t_dot(x_ref[:half, :], near_ref[...]) + t_dot(x_ref[half:, :], far_ref[...])).astype(BF)
+
+
+def first_weights_kernel(where_ref, x_ref, near_ref, far_ref, attn_ref, go_ref, *rest):
+    parts, full_ref = rest[:-1], rest[-1]
+    full_ref[:, :D] = t_dot(attn_ref[...], go_ref[...]).astype(BF)
+    end = D + near_ref.shape[1]
+    full_ref[:, D:end] = both_rows(x_ref, near_ref, far_ref)
+    if end < full_ref.shape[1]:
+        full_ref[:, end:] = jnp.zeros((D, full_ref.shape[1] - end), BF)
+    halves(parts, where_ref[1], full_ref)
+
+
+def last_weights_kernel(
+    count, where_ref, x_ref, near_ref, far_ref, first_near_ref, first_far_ref, up_ref, top_ref, hidden_ref, *rest
+):
+    parts, full_ref, lines_ref = rest[:-2], rest[-2], rest[-1]
+    part = D - count * 128
     wide = count * 128
-    total = 3 * wide + D
+    full_ref[:, : 3 * part] = both_rows(x_ref, near_ref, far_ref)
+
+    def sums(j, width, a_ref, b_ref):
+        lanes = slice(j * width, (j + 1) * width)
+        return col_sum(a_ref[:, lanes].astype(F32)) + col_sum(b_ref[:, lanes].astype(F32))
+
+    lines_ref[...] = jnp.zeros_like(lines_ref)
+    for n, j in ((0, 0), (1, 2)):
+        lines_ref[n : n + 1, :wide] = sums(j, wide, first_near_ref, first_far_ref)
+        lines_ref[n : n + 1, wide:] = sums(j, part, near_ref, far_ref)
+    lines_ref[2:4, :] = hidden_ref[0:2, :]
+    lines_ref[4:8, :] = up_ref[0:4, :]
+    lines_ref[8:10, :] = top_ref[0:2, :]
+    lines_ref[10:11, :] = hidden_ref[2:3, :]
+    lines_ref[11:12, :] = top_ref[2:3, :]
+    full_ref[:, 3 * part : 3 * part + 128] = jnp.transpose(lines_ref[...]).astype(BF)
+    full_ref[:, 3 * part + 128 :] = jnp.zeros((D, full_ref.shape[1] - 3 * part - 128), BF)
+    halves(parts, where_ref[1], full_ref)
+
+
+def weights(plan, order, kernel, name, us, total, scratch, *args):
     part = total // plan.reps
-    gp, sums, *parts = pl.pallas_call(
-        partial(attend_back_kernel, plan.reps, count),
-        grid=(rows // TILE,),
-        out_shape=(shape((rows, 3 * wide), BF), shape((8, wide), F32)) + (far((D, part), BF),) * plan.reps,
-        in_specs=[smem()] + tile_specs(0) + [still(x.shape)] * 3,
-        out_specs=[still((rows, 3 * wide)), still((8, wide))] + [still((D, part))] * plan.reps,
-        scratch_shapes=[pltpu.VMEM((D, total), BF)],
+    return pl.pallas_call(
+        kernel,
+        grid=(1,),
+        out_shape=(far((D, part), BF),) * plan.reps,
+        in_specs=[smem()] + [still(a.shape) for a in args],
+        out_specs=[still((D, part))] * plan.reps,
+        scratch_shapes=[pltpu.VMEM((D, total), BF)] + scratch,
         compiler_params=params(28),
-        name="attend_back",
-        cost_estimate=cost(18),
-    )(order.where, ga, stay(proj), stay(probs), x, stay(attn), go)
-    return gp, sums, parts
+        name=name,
+        cost_estimate=behind(us),
+    )(order.where, *args)
 
 
 def gx_of(count, a_ref, b_ref, w_ref, hidden):
@@ -819,74 +968,28 @@
     return hidden
 
 
-def far_back_kernel(count, where_ref, ga_ref, proj_ref, probs_ref, a_ref, w_ref, hidden_ref, gp_ref, far_ref):
-    heads_back(count, PAIRS - count, 0, ga_ref, proj_ref, probs_ref, gp_ref)
-    far_ref[...] = gx_of(count, a_ref, gp_ref, w_ref, hidden_ref[...]).astype(BF)
-
-
-def far_back(order, count, ga, proj, probs, gp, w_one, hidden):
+def far_back_kernel(count, where_ref, ga_ref, proj_ref, probs_ref, w_ref, hidden_ref, a_ref, b_ref, far_ref):
+    heads_back(0, count, 0, ga_ref, proj_ref, probs_ref, a_ref)
+    heads_back(count, PAIRS - count, 0, ga_ref, proj_ref, probs_ref, b_ref)
+    far_ref[...] = gx_of(count, a_ref, b_ref, w_ref, hidden_ref[...]).astype(BF)
+
+
+def far_back(order, count, ga, proj, probs, w_one, hidden):
     rows = ga.shape[0] // 2
     steps = rows // TILE
-    wide = 3 * (D - count * 128)
+    wide = 3 * count * 128
     return pl.pallas_call(
         partial(far_back_kernel, count),
         grid=(steps,),
-        out_shape=(shape((rows, wide), BF), shape((rows, D), BF)),
+        out_shape=(shape((rows, wide), BF), shape((rows, 3 * D - wide), BF), shape((rows, D), BF)),
         in_specs=[smem()]
         + tile_specs(steps)
-        + [
-            pl.BlockSpec((TILE, gp.shape[1]), lambda i: (i + steps, 0)),
-            still((D, 3 * D)),
-            pl.BlockSpec((TILE, D), lambda i: (i + steps, 0)),
-        ],
-        out_specs=[rows_at(wide), rows_at(D)],
+        + [still((D, 3 * D)), pl.BlockSpec((TILE, D), lambda i: (i + steps, 0))],
+        out_specs=[rows_at(wide), rows_at(3 * D - wide), rows_at(D)],
         compiler_params=params(24),
         name="far_back",
-        cost_estimate=cost(9),
-    )(order.where, ga, stay(proj), stay(probs), gp, stay(w_one), stay(hidden))
-
-
-def near_back_kernel(
-    reps, count, where_ref, ga_ref, proj_ref, probs_ref, x_ref, far_ref, lines_ref, sums_ref, gp_ref, *rest
-):
-    parts, full_ref = rest[:-1], rest[-1]
-    i = pl.program_id(0)
-    heads_back(count, PAIRS - count, i * TILE, ga_ref, proj_ref, probs_ref, gp_ref)
-
-    @pl.when(i == pl.num_programs(0) - 1)
-    def weights():
-        part = D - count * 128
-        split = count * 128
-        half = gp_ref.shape[0]
-        full_ref[:, : 3 * part] = (t_dot(x_ref[:half, :], gp_ref[...]) + t_dot(x_ref[half:, :], far_ref[...])).astype(BF)
-        lines = lines_ref[...]
-        row = lax.broadcasted_iota(jnp.int32, lines.shape, 0)
-        for n, at in ((0, 0), (1, 2 * part)):
-            rest_of = col_sum(gp_ref[:, at : at + part].astype(F32)) + col_sum(far_ref[:, at : at + part].astype(F32))
-            line = jnp.concatenate([sums_ref[n : n + 1, :], rest_of], 1)
-            lines = jnp.where(row == n, line, lines)
-        full_ref[:, 3 * part : 3 * part + 128] = jnp.transpose(lines).astype(BF)
-        full_ref[:, 3 * part + 128 :] = jnp.zeros((D, full_ref.shape[1] - 3 * part - 128), BF)
-        halves(parts, where_ref[1], full_ref.shape[1] // reps, full_ref)
-
-
-def near_back(plan, order, count, ga, proj, probs, x, gp_far, lines, sums):
-    rows = ga.shape[0] // 2
-    wide = 3 * (D - count * 128)
-    total = wide + W_ONE - AT_VEC
-    part = total // plan.reps
-    gp, *parts = pl.pallas_call(
-        partial(near_back_kernel, plan.reps, count),
-        grid=(rows // TILE,),
-        out_shape=(shape((rows, wide), BF),) + (far((D, part), BF),) * plan.reps,
-        in_specs=[smem()] + tile_specs(0) + [still(x.shape), still(gp_far.shape), still(lines.shape), still(sums.shape)],
-        out_specs=[still((rows, wide))] + [still((D, part))] * plan.reps,
-        scratch_shapes=[pltpu.VMEM((D, total), BF)],
-        compiler_params=params(24),
-        name="near_back",
-        cost_estimate=cost(7),
-    )(order.where, ga, stay(proj), stay(probs), x, gp_far, lines, sums)
-    return gp, parts
+        cost_estimate=behind(11),
+    )(order.where, ga, stay(proj), stay(probs), stay(w_one), stay(hidden))
 
 
 def token_back_kernel(count, where_ref, a_ref, b_ref, w_ref, hidden_ref, own_ref):
@@ -903,7 +1006,7 @@
         out_specs=rows_at(D),
         compiler_params=params(24),
         name="token_back",
-        cost_estimate=cost(4),
+        cost_estimate=behind(4),
     )(order.where, ga, gb, stay(w_one), stay(hidden))
 
 
@@ -917,28 +1020,26 @@
     where = jnp.stack([me, core, tower, span]).astype(jnp.int32)
     swap = plan.along(1)
 
-    def exchange(a, b):
+    def exchange(a, b, *others):
         a, b = a.reshape(-1, D), b.reshape(-1, D)
-        return jnp.concatenate([jnp.where(tower == 0, a, b), send(jnp.where(tower == 0, b, a), swap)], 0)
+        away = jnp.where(tower == 0, b, a)
+        return jnp.where(tower == 0, a, b), send(after(away, *others) if others else away, swap)
 
     def merged(own, back):
         a = jnp.where(tower == 0, own, back)
         b = jnp.where(tower == 0, back, own)
         return a.reshape(query_tokens.shape), b.reshape(passage_tokens.shape)
 
-    vecs = jnp.swapaxes(jnp.concatenate([biases, gains], 1), 1, 2)
-    one = jnp.concatenate([w_qkv, w_out, jnp.pad(vecs, ((0, 0), (0, 0), (0, W_ONE - AT_VEC - vecs.shape[2])))], 2)
-    mine, other = shards_of(plan, where, one)
-    mine2, other2 = shards_of(plan, where, w_up)
-    mine3, other3 = shards_of(plan, where, w_down)
+    order = Order(where)
+    mine, other, mine2, other2, mine3, other3 = shards_of(plan, order, w_qkv, w_out, biases, gains, w_up, w_down)
     z1 = gather_line(plan, mine, other)
-    x = exchange(query_tokens, passage_tokens)
+    x_mine, x_got = exchange(query_tokens, passage_tokens)
     both2 = jnp.concatenate([mine2, send(other2, swap)], 0)
     z2 = gather_steps(plan, both2, z1)
-    p1 = gather_plane(plan, z1, x, both2)
+    p1 = gather_plane(plan, z1, both2)
+    x = jnp.concatenate([x_mine, x_got], 0)
     both3 = jnp.concatenate([mine3, send(after(other3, x), swap)], 0)
     p1 = tuple(after(b, z2, both3) for b in p1)
-    order = Order(where)
     w_one = gather_cores(plan, order, p1)
     p2 = gather_plane(plan, z2)
     z3 = gather_steps(plan, both3, z2)
@@ -946,56 +1047,67 @@
 
     order.done(p2[0])
     first = order.done(attend(order, x, w_one, 0))
-    proj, probs, attn, hat1, rstd1, norm, vec = order.done(attend(order, x, w_one, 1, first[:6]))
+    proj, probs, attn, hat1, rstd1, norm, vec, cls_b = order.done(attend(order, x, w_one, 1, first[:6]))
     w_two = gather_cores(plan, order, tuple(after(b, first[6]) for b in p2))
+    cot_mine, cot_got = exchange(query_cot, passage_cot, z3)
     half_up = order.done(up(order, norm, w_two, vec, 0))
     act, slope = order.done(up(order, norm, w_two, vec, 1, half_up))
+    cot = jnp.concatenate([cot_mine, cot_got], 0)
     w_three = gather_cores(plan, order, tuple(after(b, half_up[0]) for b in p3))
-    cot = exchange(after(query_cot, p3[0]), after(passage_cot, p3[0]))
-    out, hat2, rstd2, cls = order.done(down(order, act, w_three, hat1, vec))
-    query_loss, cls_grad = order.done(contrast(plan, order, cls, positives))
+    msg = first_rows(order, first[7], cls_b, w_two, w_three, vec, positives)
+    loss = Contrast(plan, order, msg, positives.shape[0])
+    out_own, out_far, hat2, rstd2 = order.done(down(order, act, w_three, hat1, vec))
+    out_back = send(out_far, swap)
+    loss.pack()
+    order.done(cot)
+    loss.join()
+    query_loss, cls_grad = loss.loss()
 
     second, gs, sums_top, g_down = order.done(top(plan, order, cot, cls_grad, hat2, rstd2, vec, act))
-    half = out.shape[0] // 2
-    out_back = send(after(out[half:], gs), swap)
     down_part = Scatter(plan, order, g_down, w_down.shape[1])
     acc, sums_up, g_up = order.done(gelu_back(plan, order, gs, w_three, slope, norm, w_two))
     up_part = Scatter(plan, order, g_up, w_up.shape[1])
+    order.done(out_back)
     down_part.one()
     hidden, go, ga, sums = order.done(hidden_back(order, acc, second, hat1, rstd1, w_one, vec))
     up_part.one()
+    split = 4
+    half = ga.shape[0] // 2
+    far_a, far_b, gx_far = order.done(far_back(order, split, ga, proj, probs, w_one, hidden))
+    gx_back = send(gx_far, swap)
+    near_a = order.done(attend_back(order, 0, split, ga, proj, probs, half))
+    total = wide(3 * split * 128 + D, plan.reps)
+    kernel = first_weights_kernel
+    g_a = order.done(weights(plan, order, kernel, "first_weights", 5, total, [], x, near_a, far_a, stay(attn), go))
+    a_part = Scatter(plan, order, g_a, w_qkv.shape[1])
+    order.done(gx_back)
     down_part.two()
-    order.done(out_back)
-    split = 4
-    gp_a, sums_a, g_a = order.done(attend_back(plan, order, split, ga, proj, probs, x, attn, go))
-    a_part = Scatter(plan, order, g_a, w_qkv.shape[1])
+    up_part.two()
+    near_b = order.done(attend_back(order, split, PAIRS - split, ga, proj, probs, half))
     down_part.three()
-    up_part.two()
-    lines = jnp.concatenate(
-        [jnp.zeros((2, D), F32), sums[0:2], sums_up[0:4], sums_top[0:2], sums[2:3], sums_top[2:3], jnp.zeros((116, D), F32)],
-        0,
-    )
-    gp_far, gx_far = order.done(far_back(order, split, ga, proj, probs, gp_a, w_one, hidden))
-    gx_back = send(gx_far, swap)
     a_part.one()
+    up_part.three()
+    total = wide(3 * (D - split * 128) + 128, plan.reps)
+    kernel = partial(last_weights_kernel, split)
+    scratch = [pltpu.VMEM((128, D), F32)]
+    args = (x, near_b, far_b, near_a, far_a, sums_up, sums_top, sums)
+    g_b = order.done(weights(plan, order, kernel, "last_weights", 4, total, scratch, *args))
+    b_part = Scatter(plan, order, g_b, w_qkv.shape[1])
+    gx_own = order.done(token_back(order, split, near_a, near_b, w_one, hidden))
+    a_part.two()
+    b_part.one()
     down_part.four()
-    up_part.three()
-    gp_near, g_b = order.done(near_back(plan, order, split, ga, proj, probs, x, gp_far, lines, sums_a))
-    b_part = Scatter(plan, order, g_b, w_qkv.shape[1])
-    a_part.two()
-    down_part.last()
-    b_part.one()
     up_part.four()
-    gx_own = order.done(token_back(order, split, gp_a, gp_near, w_one, hidden))
     a_part.three()
     b_part.two()
+    down_part.last()
     up_part.last()
     a_part.four()
     b_part.three()
     (grad_down,) = finish(plan, order, [down_part], [[(0, D, 0, 0)]], [D])
     (grad_up,) = finish(plan, order, [up_part], [[(0, FF, 0, 0)]], [FF])
     b_part.four()
-    query_out, passage_out = merged(out[:half], after(out_back, b_part.out))
+    query_out, passage_out = merged(out_own, after(out_back, b_part.out))
     query_grad, passage_grad = merged(gx_own, after(gx_back, b_part.out).astype(F32))
     a_part.last()
     b_part.last()

time: 346 us -> 300 us (0.87)
  waiting for transfers between devices: 98 us -> 82.4 us
  local copies, waits for them, and re-layouts: 18 us -> 6.28 us
  Pallas kernels: 159 us -> 150 us
  other arithmetic: 10.9 us -> 3.81 us
    ppermute x54, waiting for transfers between devices: 98 us -> 82.4 us  [send(): return lax.ppermute(v, AXES, pairs)]
    pallas_call x2, Pallas kernels: 19.4 us -> 13.6 us  [up(): pl.pallas_call(partial(up_kernel, first), grid=(steps,), out_shape=(far((...]
    unnamed x78 -> x56, local copies, waits for them, and re-layouts: 10 us -> 4.67 us
    concatenate x9 -> x2, other arithmetic: 5.15 us -> 0.2 us  [the longest x1 0.1 us: on_device(): cot = jnp.concatenate([cot_mine, cot_got], 0)]
    pallas_call x5 -> x8, Pallas kernels: 49.5 us -> 44.9 us  [the longest x1 11.1 us: top(): pl.pallas_call(top_kernel, grid=(FF // D,), out_shape=(far((rows, D), F32...]
    pallas_call x19 -> x22, Pallas kernels: 16.1 us -> 19.2 us  [in_vmem(): pl.pallas_call(kernel, out_shape=tuple((shape(*o) for o in outs)), in_spe...]
  transfers between devices with their start and end apart: 54 -> 54, of which waited for: 21 -> 19; matrix products, arithmetic and copies ran while one was open for 5% -> 2% of each run, Pallas kernels for 42% -> 49%
where the time goes in v3:
time: 300 us; the launch traced here: 297 us
  Pallas kernels  150 us (50%)
  waiting for transfers between devices  82.4 us (27%)
  starting transfers between devices  52.3 us (17%)
  local copies, waits for them, and re-layouts  6.28 us (2%)
  other arithmetic  3.81 us (1%)
    ppermute x54, waiting for transfers between devices, send(): return lax.ppermute(v, AXES, pairs)  82.4 us
    ppermute x54, starting transfers between devices, send(): return lax.ppermute(v, AXES, pairs)  52.3 us
    pallas_call x1, Pallas kernels, gelu_back(): pl.pallas_call(partial(gelu_back_kernel, reps, column), out_shape=(shape(...  21.8 us
    pallas_call x22, Pallas kernels, in_vmem(): pl.pallas_call(kernel, out_shape=tuple((shape(*o) for o in outs)), in_spe...  19.2 us
    pallas_call x2, Pallas kernels, attend(): pl.pallas_call(partial(attend_kernel, part), grid=(steps,), out_shape=(fa...  16.2 us
    pallas_call x2, Pallas kernels, up(): pl.pallas_call(partial(up_kernel, first), grid=(steps,), out_shape=(far((...  13.6 us
    pallas_call x1, Pallas kernels, top(): pl.pallas_call(top_kernel, grid=(FF // D,), out_shape=(far((rows, D), F32...  11.1 us
    pallas_call x1, Pallas kernels, far_back(): pl.pallas_call(partial(far_back_kernel, count), grid=(steps,), out_shape=...  10.9 us
  transfers between devices with their start and end apart: 54, of which 19 were waited for; matrix products, arithmetic and copies ran while one was open for 2% of the time, Pallas kernels for 49%

profile of v3, /device:TPU:0, one launch (start us, length us, event | category | flops | bytes accessed | tf_op | source)
XLA Modules:
  0.0 296.7 jit_solution(3162064085310178334)
XLA Ops:
  2.0 1.8 shards.1
  3.8 3.1 %collective-permute-start = (bf16[1,48,1664]{2,1,0:T(8,128)(2,1)S(1)}, bf16[1,48,1664]{2,1,0:T(8,128)(2,1)S(1)}, u32[]{:S(2)}, u32[]{:S(2)}) collective-permute-start(bf16[1,48,1664]{2,1,0:T(8,128)(2,1)S(1)} %get-tuple-element.161), channel_id=1, source_target_pairs={{0,8},{1,9},{2,10},{3,11},{4,12},{5,13},{6,14},{7,15},{8,0},{9,1},... | collective-permute-start | bytes 479240 | tf_op jit(solution)/shard_map/ppermute | solution.py:120
  6.9 2.5 collective-permute-start.2
  9.5 1.8 collective-permute-start.4
  11.5 12.1 %collective-permute-done.1 = bf16[1,48,1664]{2,1,0:T(8,128)(2,1)S(1)} collective-permute-done((bf16[1,48,1664]{2,1,0:T(8,128)(2,1)S(1)}, bf16[1,48,1664]{2,1,0:T(8,128)(2,1)S(1)}, u32[]{:S(2)}, u32[]{:S(2)}) %collective-permute-start.1) | collective-permute-done | bytes 159776 | tf_op jit(solution)/shard_map/ppermute | solution.py:120
  25.6 8.6 %collective-permute-done.3 = bf16[4,48,1664]{2,1,0:T(8,128)(2,1)S(1)} collective-permute-done((bf16[4,48,1664]{2,1,0:T(8,128)(2,1)S(1)}, bf16[4,48,1664]{2,1,0:T(8,128)(2,1)S(1)}, u32[]{:S(2)}, u32[]{:S(2)}) %collective-permute-start.3) | collective-permute-done | bytes 639008 | tf_op jit(solution)/shard_map/ppermute | solution.py:120
  36.0 14.0 %collective-permute-done.6 = bf16[512,768]{1,0:T(8,128)(2,1)S(1)} collective-permute-done((bf16[512,768]{1,0:T(8,128)(2,1)S(1)}, bf16[512,768]{1,0:T(8,128)(2,1)S(1)}, u32[]{:S(2)}, u32[]{:S(2)}) %collective-permute-start.6) | collective-permute-done | bytes 786464 | tf_op jit(solution)/shard_map/ppermute | solution.py:120
  50.3 5.1 %collective-permute-done.7 = bf16[1,192,384]{2,1,0:T(8,128)(2,1)S(1)} collective-permute-done((bf16[1,192,384]{2,1,0:T(8,128)(2,1)S(1)}, bf16[1,192,384]{2,1,0:T(8,128)(2,1)S(1)}, u32[]{:S(2)}, u32[]{:S(2)}) %collective-permute-start.7) | collective-permute-done | bytes 147488 | tf_op jit(solution)/shard_map/ppermute | solution.py:120
  58.2 7.6 %collective-permute-done.11 = bf16[4,48,1536]{2,1,0:T(8,128)(2,1)S(1)} collective-permute-done((bf16[4,48,1536]{2,1,0:T(8,128)(2,1)S(1)}, bf16[4,48,1536]{2,1,0:T(8,128)(2,1)S(1)}, u32[]{:S(2)}, u32[]{:S(2)}) %collective-permute-start.11) | collective-permute-done | bytes 589856 | tf_op jit(solution)/shard_map/ppermute | solution.py:120
  65.9 2.0 collective-permute-start.12
  67.9 5.9 %collective-permute-done.15 = bf16[2,192,384]{2,1,0:T(8,128)(2,1)S(1)} collective-permute-done((bf16[2,192,384]{2,1,0:T(8,128)(2,1)S(1)}, bf16[2,192,384]{2,1,0:T(8,128)(2,1)S(1)}, u32[]{:S(2)}, u32[]{:S(2)}) %collective-permute-start.15) | collective-permute-done | bytes 294944 | tf_op jit(solution)/shard_map/ppermute | solution.py:120
  75.0 8.5 %attend.2 = (bf16[1024,2304]{1,0:T(8,128)(2,1)}, bf16[8,6,128,256]{3,2,1,0:T(8,128)(2,1)}, bf16[1024,768]{1,0:T(8,128)(2,1)}, f32[1024,768]{1,0:T(8,128)}, f32[1...) custom-call(s32[4]{0:T(128)S(1)} %pad_add_fusion.where_ref, ...), custom_call_target="tpu_custom_call" | custom-call | flops 7000000000 | bytes 21000000 | tf_op jit(solution)/shard_map/attend/pallas_call | solution.py:473
  83.5 4.5 %collective-permute-done.12.refs_1_ = bf16[8,48,1536]{2,1,0:T(8,128)(2,1)S(1)} collective-permute-done((bf16[8,48,1536]{2,1,0:T(8,128)(2,1)S(1)}, bf16[8,48,1536]{2,1,0:T(8,128)(2,1)S(1)}, u32[]{:S(2)}, u32[]{:S(2)}) %collective-permute-start.12) | collective-permute-done | bytes 1179680 | tf_op jit(solution)/shard_map/ppermute | solution.py:120
  88.6 2.5 collective-permute-start.17
  91.2 7.7 %attend.3 = (bf16[1024,2304]{1,0:T(8,128)(2,1)}, bf16[8,6,128,256]{3,2,1,0:T(8,128)(2,1)}, bf16[1024,768]{1,0:T(8,128)(2,1)}, f32[1024,768]{1,0:T(8,128)}, f32[1...) custom-call(s32[4]{0:T(128)S(1)} %pad_add_fusion.where_ref, ...), custom_call_target="tpu_custom_call", output_to_operand_aliasing={{0}: (3, {}), {1}: (4, {}), {2}: (5, {}), {3}: (6, {}), {4}... | custom-call | flops 7000000000 | bytes 21000000 | tf_op jit(solution)/shard_map/attend/pallas_call | solution.py:473
  100.3 6.7 %up.2 = (bf16[1024,3072]{1,0:T(8,128)(2,1)}, bf16[1024,3072]{1,0:T(8,128)(2,1)}) custom-call(s32[4]{0:T(128)S(1)} %pad_add_fusion.where_ref, bf16[1024,768]{1,0:T(8,128)(2,1)S(1)} %copy-done.6, bf16[768,3072]{1,0:T(8,128)(2,1)S(1)} %bitcast.40, f32[128,768]{1,0:T(8,128)S(1)} %get-tuple-element.189.vec_ref), custom_call_target="tpu_custom_call" | custom-call | flops 8000000000 | bytes 24000000 | tf_op jit(solution)/shard_map/up/pallas_call | solution.py:525
  107.7 6.9 %up.3 = (bf16[1024,3072]{1,0:T(8,128)(2,1)}, bf16[1024,3072]{1,0:T(8,128)(2,1)}) custom-call(s32[4]{0:T(128)S(1)} %pad_add_fusion.where_ref, bf16[1024,768]{1,0:T(8,128)(2,1)S(1)} %copy-done.6, bf16[768,3072]{1,0:T(8,128)(2,1)S(1)} %bitcast.41, f32[128,768]{1,0:T(8,128)S(1)} %get-tuple-element.189.vec_ref, ...), custom_call_target="tpu_custom_call", output_to_operand_aliasing={{0}: (4, {}), {1}: (5, {})} | custom-call | flops 8000000000 | bytes 24000000 | tf_op jit(solution)/shard_map/up/pallas_call | solution.py:525
  115.7 2.6 first_rows.1.refs_0_
  118.4 2.1 collective-permute-start.21
  123.1 9.9 %down.1 = (bf16[512,768]{1,0:T(8,128)(2,1)}, bf16[512,768]{1,0:T(8,128)(2,1)S(1)}, f32[1024,768]{1,0:T(8,128)}, f32[1024,1]{1,0:T(8,128)}) custom-call(s32[4]{0:T(128)S(1)} %pad_add_fusion.where_ref, bf16[1024,3072]{1,0:T(8,128)(2,1)} %get-tuple-element.198.act_ref, bf16[3072,768]{1,0:T(8,128)(2,1)S(1)} %bitcast.45, f32[1024,768]{1,0:T(8,128)} %get-tuple-element.186.hat_ref, ...), custom_call_target="tpu_custom_call" | custom-call | flops 8000000000 | bytes 24000000 | tf_op jit(solution)/shard_map/down/pallas_call | solution.py:567
  135.2 2.2 collective-permute-start.27
  137.5 3.7 %collective-permute-done.25.refs_1_ = bf16[2,48,896]{2,1,0:T(8,128)(2,1)S(1)} collective-permute-done((bf16[2,48,896]{2,1,0:T(8,128)(2,1)S(1)}, bf16[2,48,896]{2,1,0:T(8,128)(2,1)S(1)}, u32[]{:S(2)}, u32[]{:S(2)}) %collective-permute-start.25) | collective-permute-done | bytes 172064 | tf_op jit(solution)/shard_map/ppermute | solution.py:120
  141.2 2.0 collective-permute-done.26.refs_2_
  146.0 1.9 contrast.1
  147.9 11.1 %top.1 = (f32[1024,768]{1,0:T(8,128)}, bf16[1024,768]{1,0:T(8,128)(2,1)S(1)}, f32[8,768]{1,0:T(8,128)S(1)}, bf16[3072,384]{1,0:T(8,128)(2,1)}, bf16[3072,384]{1,0:T(8,128)(2,1)}) custom-call(s32[4]{0:T(128)S(1)} %pad_add_fusion.where_ref, bf16[1024,768]{1,0:T(8,128)(2,1)S(1)} %pad_maximum_fusion.1.cot_ref, f32[32,768]{1,0:T(8,128)S(1)} %get-tuple-element.217.cls_ref, ...), custom_call_target="tpu_custom_call" | custom-call | flops 44000002048 | bytes 132000000 | tf_op jit(solution)/shard_map/top/pallas_call | solution.py:733
  159.1 21.8 %gelu_back.1 = (f32[1024,768]{1,0:T(8,128)S(1)}, f32[8,768]{1,0:T(8,128)S(1)}, bf16[768,1536]{1,0:T(8,128)(2,1)}, bf16[768,1536]{1,0:T(8,128)(2,1)}) custom-call(s32[4]{0:T(128)S(1)} %pad_add_fusion.where_ref, bf16[1024,768]{1,0:T(8,128)(2,1)S(1)} %get-tuple-element.220.gs_ref, bf16[3072,768]{1,0:T(8,128)(2,1)} %bitcast.46, ...), custom_call_target="tpu_custom_call" | custom-call | flops 80000000000 | bytes 240000000 | tf_op jit(solution)/shard_map/gelu_back/pallas_call | solution.py:794
  181.3 2.4 pick_add.4
  183.8 1.7 collective-permute-start.32
  185.5 6.8 %hidden_back.1 = (f32[1024,768]{1,0:T(8,128)}, bf16[1024,768]{1,0:T(8,128)(2,1)S(1)}, bf16[1024,768]{1,0:T(8,128)(2,1)S(1)}, f32[8,768]{1,0:T(8,128)S(1)}) custom-call(s32[4]{0:T(128)S(1)} %pad_add_fusion.where_ref, f32[1024,768]{1,0:T(8,128)S(1)} %get-tuple-element.225.acc_ref, f32[1024,768]{1,0:T(8,128)} %get-tuple-element.219.second_ref, ...), custom_call_target="tpu_custom_call" | custom-call | flops 20000000000 | bytes 60000000 | tf_op jit(solution)/shard_map/hidden_back/pallas_call | solution.py:838
  192.4 2.4 pick_add.5
  195.2 10.9 %far_back.1 = (bf16[512,1536]{1,0:T(8,128)(2,1)S(1)}, bf16[512,768]{1,0:T(8,128)(2,1)S(1)}, bf16[512,768]{1,0:T(8,128)(2,1)S(1)}) custom-call(s32[4]{0:T(128)S(1)} %pad_add_fusion.where_ref, bf16[1024,768]{1,0:T(8,128)(2,1)S(1)} %get-tuple-element.236.ga_ref, bf16[1024,2304]{1,0:T(8,128)(2,1)} %get-tuple-element.183.proj_ref, ...), custom_call_target="tpu_custom_call" | custom-call | flops 44000002048 | bytes 132000000 | tf_op jit(solution)/shard_map/far_back/pallas_call | solution.py:981
  206.9 5.4 %attend_back.2.near_ref.first_near_ref.a_ref = bf16[512,1536]{1,0:T(8,128)(2,1)S(1)} custom-call(s32[4]{0:T(128)S(1)} %pad_add_fusion.where_ref, bf16[1024,768]{1,0:T(8,128)(2,1)S(1)} %get-tuple-element.236.ga_ref, bf16[1024,2304]{1,0:T(8,128)(2,1)} %get-tuple-element.183.proj_ref, bf16[8,6,128,256]{3,2,1,0:T(8,128)(2,1)} %get-tuple-element.184.probs_ref), custom_call_target="tpu_custom_call" | custom-call | flops 20000000000 | bytes 60000000 | tf_op jit(solution)/shard_map/attend_back/pallas_call | solution.py:895
  212.3 7.3 %first_weights.1 = (bf16[768,1152]{1,0:T(8,128)(2,1)}, bf16[768,1152]{1,0:T(8,128)(2,1)}) custom-call(s32[4]{0:T(128)S(1)} %pad_add_fusion.where_ref, bf16[1024,768]{1,0:T(8,128)(2,1)S(1)} %copy-done.4, bf16[512,1536]{1,0:T(8,128)(2,1)S(1)} %attend_back.2.near_ref.first_near_ref.a_ref, bf16[512,1536]{1,0:T(8,128)(2,1)S(1)} %get-tuple-element.242.far_ref.first_far_ref, ...), custom_call_target="tpu_custom_call" | custom-call | flops 20000000000 | bytes 60000000 | tf_op jit(solution)/shard_map/first_weights/pallas_call | solution.py:950
  219.6 5.6 %collective-permute-done.31 = bf16[512,768]{1,0:T(8,128)(2,1)S(1)} collective-permute-done((bf16[512,768]{1,0:T(8,128)(2,1)S(1)}, bf16[512,768]{1,0:T(8,128)(2,1)S(1)}, u32[]{:S(2)}, u32[]{:S(2)}) %collective-permute-start.31) | collective-permute-done | bytes 786464 | tf_op jit(solution)/shard_map/ppermute | solution.py:120
  229.0 3.9 %attend_back.3.near_ref.b_ref = bf16[512,768]{1,0:T(8,128)(2,1)S(1)} custom-call(s32[4]{0:T(128)S(1)} %pad_add_fusion.where_ref, bf16[1024,768]{1,0:T(8,128)(2,1)S(1)} %get-tuple-element.236.ga_ref, bf16[1024,2304]{1,0:T(8,128)(2,1)} %get-tuple-element.183.proj_ref, bf16[8,6,128,256]{3,2,1,0:T(8,128)(2,1)} %get-tuple-element.184.probs_ref), custom_call_target="tpu_custom_call" | custom-call | flops 8000000000 | bytes 24000000 | tf_op jit(solution)/shard_map/attend_back/pallas_call | solution.py:895
  233.0 3.0 %collective-permute-done.34.r_ref = bf16[4,192,384]{2,1,0:T(8,128)(2,1)S(1)} collective-permute-done((bf16[4,192,384]{2,1,0:T(8,128)(2,1)S(1)}, bf16[4,192,384]{2,1,0:T(8,128)(2,1)S(1)}, u32[]{:S(2)}, u32[]{:S(2)}) %collective-permute-start.34) | collective-permute-done | bytes 589856 | tf_op jit(solution)/shard_map/ppermute | solution.py:120
  236.7 1.9 collective-permute-start.39
  238.7 2.2 pick_add.6
  244.2 2.8 collective-permute-start.40
  247.0 3.6 %last_weights.1 = (bf16[768,512]{1,0:T(8,128)(2,1)}, bf16[768,512]{1,0:T(8,128)(2,1)}) custom-call(s32[4]{0:T(128)S(1)} %pad_add_fusion.where_ref, bf16[1024,768]{1,0:T(8,128)(2,1)S(1)} %copy-done.4, bf16[512,768]{1,0:T(8,128)(2,1)S(1)} %attend_back.3.near_ref.b_ref, bf16[512,768]{1,0:T(8,128)(2,1)S(1)} %get-tuple-element.243.far_ref, ...), custom_call_target="tpu_custom_call" | custom-call | flops 16000000000 | bytes 48000000 | tf_op jit(solution)/shard_map/last_weights/pallas_call | solution.py:950
  250.5 4.5 %token_back.1 = f32[512,768]{1,0:T(8,128)S(1)} custom-call(s32[4]{0:T(128)S(1)} %pad_add_fusion.where_ref, bf16[512,1536]{1,0:T(8,128)(2,1)S(1)} %attend_back.2.near_ref.first_near_ref.a_ref, bf16[512,768]{1,0:T(8,128)(2,1)S(1)} %attend_back.3.near_ref.b_ref, bf16[768,3328]{1,0:T(8,128)(2,1)} %bitcast.39, f32[1024,768]{1,0:T(8,128)} %get-tuple-element.234.hidden_ref), custom_call_target="tpu_custom_call" | custom-call | flops 16000000000 | bytes 48000000 | tf_op jit(solution)/shard_map/token_back/pallas_call | solution.py:1001
  257.1 1.8 pick_add.7
  264.1 2.2 collective-permute-done.41.r_ref
  275.2 3.6 %collective-permute-done.45.r_ref = bf16[2,48,1152]{2,1,0:T(8,128)(2,1)S(1)} collective-permute-done((bf16[2,48,1152]{2,1,0:T(8,128)(2,1)S(1)}, bf16[2,48,1152]{2,1,0:T(8,128)(2,1)S(1)}, u32[]{:S(2)}, u32[]{:S(2)}) %collective-permute-start.45) | collective-permute-done | bytes 221216 | tf_op jit(solution)/shard_map/ppermute | solution.py:120
  280.1 1.9 collective-permute-start.49
  286.5 1.8 collective-permute-start.51
  288.3 1.9 convert_select_fusion
  293.4 1.7 finish.5
  (179 shorter events, 56.4 us)
Async XLA Ops:
  3.8 7.6 %collective-permute-start = (bf16[1,48,1664]{2,1,0:T(8,128)(2,1)S(1)}, bf16[1,48,1664]{2,1,0:T(8,128)(2,1)S(1)}, u32[]{:S(2)}, u32[]{:S(2)}) collective-permute-start(bf16[1,48,1664]{2,1,0:T(8,128)(2,1)S(1)} %get-tuple-element.161), channel_id=1, source_target_pairs={{0,8},{1,9},{2,10},{3,11},{4,12},{5,13},{6,14},{7,15},{8,0},{9,1},... | collective-permute-start | bytes 479240 | tf_op jit(solution)/shard_map/ppermute | solution.py:120
  6.9 16.7 %collective-permute-start.2 = (bf16[1,48,1664]{2,1,0:T(8,128)(2,1)S(1)}, bf16[1,48,1664]{2,1,0:T(8,128)(2,1)S(1)}, u32[]{:S(2)}, u32[]{:S(2)}) collective-permute-start(bf16[1,48,1664]{2,1,0:T(8,128)(2,1)S(1)} %get-tuple-element.161), channel_id=1, source_target_pairs={{0,24},{1,25},{2,26},{3,27},{4,28},{5,29},{6,30},{7,31},{8,16},{9,... | collective-permute-start | bytes 479240 | tf_op jit(solution)/shard_map/ppermute | solution.py:120
  9.4 14.2 %collective-permute-start.1 = (bf16[1,48,1664]{2,1,0:T(8,128)(2,1)S(1)}, bf16[1,48,1664]{2,1,0:T(8,128)(2,1)S(1)}, u32[]{:S(2)}, u32[]{:S(2)}) collective-permute-start(bf16[1,48,1664]{2,1,0:T(8,128)(2,1)S(1)} %get-tuple-element.160), channel_id=1, source_target_pairs={{0,16},{1,17},{2,18},{3,19},{4,20},{5,21},{6,22},{7,23},{8,24},{9,... | collective-permute-start | bytes 479240 | tf_op jit(solution)/shard_map/ppermute | solution.py:120
  9.5 16.1 %collective-permute-start.4 = (bf16[1,48,1536]{2,1,0:T(8,128)(2,1)S(1)}, bf16[1,48,1536]{2,1,0:T(8,128)(2,1)S(1)}, u32[]{:S(2)}, u32[]{:S(2)}) collective-permute-start(bf16[1,48,1536]{2,1,0:T(8,128)(2,1)S(1)} %get-tuple-element.163), channel_id=1, source_target_pairs={{0,8},{1,9},{2,10},{3,11},{4,12},{5,13},{6,14},{7,15},{8,0},{9,1},... | collective-permute-start | bytes 442376 | tf_op jit(solution)/shard_map/ppermute | solution.py:120
  23.7 10.5 %collective-permute-start.3 = (bf16[4,48,1664]{2,1,0:T(8,128)(2,1)S(1)}, bf16[4,48,1664]{2,1,0:T(8,128)(2,1)S(1)}, u32[]{:S(2)}, u32[]{:S(2)}) collective-permute-start(bf16[4,48,1664]{2,1,0:T(8,128)(2,1)S(1)} %get-tuple-element.343), channel_id=1, source_target_pairs={{0,2},{1,5},{2,0},{3,7},{4,6},{5,1},{6,4},{7,3},{8,10},{9,13},{10,... | collective-permute-start | bytes 1916936 | tf_op jit(solution)/shard_map/ppermute | solution.py:120
  25.5 24.5 %collective-permute-start.6 = (bf16[512,768]{1,0:T(8,128)(2,1)S(1)}, bf16[512,768]{1,0:T(8,128)(2,1)S(1)}, u32[]{:S(2)}, u32[]{:S(2)}) collective-permute-start(bf16[512,768]{1,0:T(8,128)(2,1)S(1)} %get-tuple-element.338), channel_id=1, source_target_pairs={{0,8},{1,9},{2,10},{3,11},{4,12},{5,13},{6,14},{7,15},{8,0},{9,1},... | collective-permute-start | bytes 2359304 | tf_op jit(solution)/shard_map/ppermute | solution.py:120
  34.2 21.2 %collective-permute-start.8 = (bf16[8,48,1664]{2,1,0:T(8,128)(2,1)S(1)}, bf16[8,48,1664]{2,1,0:T(8,128)(2,1)S(1)}, u32[]{:S(2)}, u32[]{:S(2)}) collective-permute-start(bf16[8,48,1664]{2,1,0:T(8,128)(2,1)S(1)} %constant_dynamic-update-slice_fusion.4.refs_0_), channel_id=1, source_target_pairs={{0,4},{1,3},{2,6},{3,1},{4,0},{5,7},{6,2},{7,5},{8,12},{9,11},{10,... | collective-permute-start | bytes 3833864 | tf_op jit(solution)/shard_map/ppermute | solution.py:120
  35.8 14.4 %collective-permute-start.5 = (bf16[2,48,1536]{2,1,0:T(8,128)(2,1)S(1)}, bf16[2,48,1536]{2,1,0:T(8,128)(2,1)S(1)}, u32[]{:S(2)}, u32[]{:S(2)}) collective-permute-start(bf16[2,48,1536]{2,1,0:T(8,128)(2,1)S(1)} %constant_dynamic-update-slice_fusion.9), channel_id=1, source_target_pairs={{0,16},{1,17},{2,18},{3,19},{4,20},{5,21},{6,22},{7,23},{8,24},{9,... | collective-permute-start | bytes 884744 | tf_op jit(solution)/shard_map/ppermute | solution.py:120
  55.4 18.6 %collective-permute-start.9 = (bf16[8,48,1664]{2,1,0:T(8,128)(2,1)S(1)}, bf16[8,48,1664]{2,1,0:T(8,128)(2,1)S(1)}, u32[]{:S(2)}, u32[]{:S(2)}) collective-permute-start(bf16[8,48,1664]{2,1,0:T(8,128)(2,1)S(1)} %constant_dynamic-update-slice_fusion.4.refs_0_), channel_id=1, source_target_pairs={{0,1},{1,0},{2,3},{3,2},{4,5},{5,4},{6,7},{7,6},{8,9},{9,8},{10,11... | collective-permute-start | bytes 3833864 | tf_op jit(solution)/shard_map/ppermute | solution.py:120
  55.5 18.5 %collective-permute-start.10 = (bf16[8,48,1664]{2,1,0:T(8,128)(2,1)S(1)}, bf16[8,48,1664]{2,1,0:T(8,128)(2,1)S(1)}, u32[]{:S(2)}, u32[]{:S(2)}) collective-permute-start(bf16[8,48,1664]{2,1,0:T(8,128)(2,1)S(1)} %collective-permute-done.8.refs_1_), channel_id=1, source_target_pairs={{0,1},{1,0},{2,3},{3,2},{4,5},{5,4},{6,7},{7,6},{8,9},{9,8},{10,11... | collective-permute-start | bytes 3833864 | tf_op jit(solution)/shard_map/ppermute | solution.py:120
  55.9 9.9 %collective-permute-start.11 = (bf16[4,48,1536]{2,1,0:T(8,128)(2,1)S(1)}, bf16[4,48,1536]{2,1,0:T(8,128)(2,1)S(1)}, u32[]{:S(2)}, u32[]{:S(2)}) collective-permute-start(bf16[4,48,1536]{2,1,0:T(8,128)(2,1)S(1)} %get-tuple-element.340), channel_id=1, source_target_pairs={{0,2},{1,5},{2,0},{3,7},{4,6},{5,1},{6,4},{7,3},{8,10},{9,13},{10,... | collective-permute-start | bytes 1769480 | tf_op jit(solution)/shard_map/ppermute | solution.py:120
  57.4 16.4 %collective-permute-start.15 = (bf16[2,192,384]{2,1,0:T(8,128)(2,1)S(1)}, bf16[2,192,384]{2,1,0:T(8,128)(2,1)S(1)}, u32[]{:S(2)}, u32[]{:S(2)}) collective-permute-start(bf16[2,192,384]{2,1,0:T(8,128)(2,1)S(1)} %constant_dynamic-update-slice_fusion.13), channel_id=1, source_target_pairs={{0,16},{1,17},{2,18},{3,19},{4,20},{5,21},{6,22},{7,23},{8,24},{9,... | collective-permute-start | bytes 884744 | tf_op jit(solution)/shard_map/ppermute | solution.py:120
  65.9 22.1 %collective-permute-start.12 = (bf16[8,48,1536]{2,1,0:T(8,128)(2,1)S(1)}, bf16[8,48,1536]{2,1,0:T(8,128)(2,1)S(1)}, u32[]{:S(2)}, u32[]{:S(2)}) collective-permute-start(bf16[8,48,1536]{2,1,0:T(8,128)(2,1)S(1)} %constant_dynamic-update-slice_fusion.15.refs_0_), channel_id=1, source_target_pairs={{0,4},{1,3},{2,6},{3,1},{4,0},{5,7},{6,2},{7,5},{8,12},{9,11},{10,... | collective-permute-start | bytes 3538952 | tf_op jit(solution)/shard_map/ppermute | solution.py:120
  73.9 14.6 %collective-permute-start.16 = (bf16[4,192,384]{2,1,0:T(8,128)(2,1)S(1)}, bf16[4,192,384]{2,1,0:T(8,128)(2,1)S(1)}, u32[]{:S(2)}, u32[]{:S(2)}) collective-permute-start(bf16[4,192,384]{2,1,0:T(8,128)(2,1)S(1)} %constant_dynamic-update-slice_fusion.18), channel_id=1, source_target_pairs={{0,2},{1,5},{2,0},{3,7},{4,6},{5,1},{6,4},{7,3},{8,10},{9,13},{10,... | collective-permute-start | bytes 1769480 | tf_op jit(solution)/shard_map/ppermute | solution.py:120
  87.9 10.9 %collective-permute-start.14 = (bf16[8,48,1536]{2,1,0:T(8,128)(2,1)S(1)}, bf16[8,48,1536]{2,1,0:T(8,128)(2,1)S(1)}, u32[]{:S(2)}, u32[]{:S(2)}) collective-permute-start(bf16[8,48,1536]{2,1,0:T(8,128)(2,1)S(1)} %collective-permute-done.12.refs_1_), channel_id=1, source_target_pairs={{0,1},{1,0},{2,3},{3,2},{4,5},{5,4},{6,7},{7,6},{8,9},{9,8},{10,11... | collective-permute-start | bytes 3538952 | tf_op jit(solution)/shard_map/ppermute | solution.py:120
  87.9 10.9 %collective-permute-start.13 = (bf16[8,48,1536]{2,1,0:T(8,128)(2,1)S(1)}, bf16[8,48,1536]{2,1,0:T(8,128)(2,1)S(1)}, u32[]{:S(2)}, u32[]{:S(2)}) collective-permute-start(bf16[8,48,1536]{2,1,0:T(8,128)(2,1)S(1)} %constant_dynamic-update-slice_fusion.15.refs_0_), channel_id=1, source_target_pairs={{0,1},{1,0},{2,3},{3,2},{4,5},{5,4},{6,7},{7,6},{8,9},{9,8},{10,11... | collective-permute-start | bytes 3538952 | tf_op jit(solution)/shard_map/ppermute | solution.py:120
  88.6 18.3 %collective-permute-start.17 = (bf16[8,192,384]{2,1,0:T(8,128)(2,1)S(1)}, bf16[8,192,384]{2,1,0:T(8,128)(2,1)S(1)}, u32[]{:S(2)}, u32[]{:S(2)}) collective-permute-start(bf16[8,192,384]{2,1,0:T(8,128)(2,1)S(1)} %constant_dynamic-update-slice_fusion.20.refs_0_), channel_id=1, source_target_pairs={{0,4},{1,3},{2,6},{3,1},{4,0},{5,7},{6,2},{7,5},{8,12},{9,11},{10,... | collective-permute-start | bytes 3538952 | tf_op jit(solution)/shard_map/ppermute | solution.py:120
  106.9 7.7 %collective-permute-start.18 = (bf16[8,192,384]{2,1,0:T(8,128)(2,1)S(1)}, bf16[8,192,384]{2,1,0:T(8,128)(2,1)S(1)}, u32[]{:S(2)}, u32[]{:S(2)}) collective-permute-start(bf16[8,192,384]{2,1,0:T(8,128)(2,1)S(1)} %constant_dynamic-update-slice_fusion.20.refs_0_), channel_id=1, source_target_pairs={{0,1},{1,0},{2,3},{3,2},{4,5},{5,4},{6,7},{7,6},{8,9},{9,8},{10,11... | collective-permute-start | bytes 3538952 | tf_op jit(solution)/shard_map/ppermute | solution.py:120
  106.9 7.7 %collective-permute-start.19 = (bf16[8,192,384]{2,1,0:T(8,128)(2,1)S(1)}, bf16[8,192,384]{2,1,0:T(8,128)(2,1)S(1)}, u32[]{:S(2)}, u32[]{:S(2)}) collective-permute-start(bf16[8,192,384]{2,1,0:T(8,128)(2,1)S(1)} %collective-permute-done.17.refs_1_), channel_id=1, source_target_pairs={{0,1},{1,0},{2,3},{3,2},{4,5},{5,4},{6,7},{7,6},{8,9},{9,8},{10,11... | collective-permute-start | bytes 3538952 | tf_op jit(solution)/shard_map/ppermute | solution.py:120
  107.7 29.7 %collective-permute-start.24 = (bf16[512,768]{1,0:T(8,128)(2,1)S(1)}, bf16[512,768]{1,0:T(8,128)(2,1)S(1)}, u32[]{:S(2)}, u32[]{:S(2)}) collective-permute-start(bf16[512,768]{1,0:T(8,128)(2,1)S(1)} %get-tuple-element.213), channel_id=1, source_target_pairs={{0,8},{1,9},{2,10},{3,11},{4,12},{5,13},{6,14},{7,15},{8,0},{9,1},... | collective-permute-start | bytes 2359304 | tf_op jit(solution)/shard_map/ppermute | solution.py:120
  118.4 14.7 %collective-permute-start.21 = (bf16[32,896]{1,0:T(8,128)(2,1)S(1)}, bf16[32,896]{1,0:T(8,128)(2,1)S(1)}, u32[]{:S(2)}, u32[]{:S(2)}) collective-permute-start(bf16[32,896]{1,0:T(8,128)(2,1)S(1)} %first_rows.1.refs_0_), channel_id=1, source_target_pairs={{0,8},{1,9},{2,10},{3,11},{4,12},{5,13},{6,14},{7,15},{8,0},{9,1},... | collective-permute-start | bytes 172040 | tf_op jit(solution)/shard_map/ppermute | solution.py:120
  120.4 12.6 %collective-permute-start.22 = (bf16[32,896]{1,0:T(8,128)(2,1)S(1)}, bf16[32,896]{1,0:T(8,128)(2,1)S(1)}, u32[]{:S(2)}, u32[]{:S(2)}) collective-permute-start(bf16[32,896]{1,0:T(8,128)(2,1)S(1)} %first_rows.1.refs_0_), channel_id=1, source_target_pairs={{0,16},{1,17},{2,18},{3,19},{4,20},{5,21},{6,22},{7,23},{8,24},{9,... | collective-permute-start | bytes 172040 | tf_op jit(solution)/shard_map/ppermute | solution.py:120
  121.8 11.3 %collective-permute-start.23 = (bf16[32,896]{1,0:T(8,128)(2,1)S(1)}, bf16[32,896]{1,0:T(8,128)(2,1)S(1)}, u32[]{:S(2)}, u32[]{:S(2)}) collective-permute-start(bf16[32,896]{1,0:T(8,128)(2,1)S(1)} %first_rows.1.refs_0_), channel_id=1, source_target_pairs={{0,24},{1,25},{2,26},{3,27},{4,28},{5,29},{6,30},{7,31},{8,16},{9,... | collective-permute-start | bytes 172040 | tf_op jit(solution)/shard_map/ppermute | solution.py:120
  133.9 7.3 %collective-permute-start.25 = (bf16[2,48,896]{2,1,0:T(8,128)(2,1)S(1)}, bf16[2,48,896]{2,1,0:T(8,128)(2,1)S(1)}, u32[]{:S(2)}, u32[]{:S(2)}) collective-permute-start(bf16[2,48,896]{2,1,0:T(8,128)(2,1)S(1)} %pack.1.refs_0_), channel_id=1, source_target_pairs={{0,2},{1,3},{2,0},{3,1},{4,6},{5,7},{6,4},{7,5},{8,10},{9,11},{10,... | collective-permute-start | bytes 516104 | tf_op jit(solution)/shard_map/ppermute | solution.py:120
  133.9 9.3 %collective-permute-start.26 = (bf16[2,48,896]{2,1,0:T(8,128)(2,1)S(1)}, bf16[2,48,896]{2,1,0:T(8,128)(2,1)S(1)}, u32[]{:S(2)}, u32[]{:S(2)}) collective-permute-start(bf16[2,48,896]{2,1,0:T(8,128)(2,1)S(1)} %pack.1.refs_0_), channel_id=1, source_target_pairs={{0,4},{1,5},{2,6},{3,7},{4,0},{5,1},{6,2},{7,3},{8,12},{9,13},{10,... | collective-permute-start | bytes 516104 | tf_op jit(solution)/shard_map/ppermute | solution.py:120
  135.2 8.0 %collective-permute-start.27 = (bf16[2,48,896]{2,1,0:T(8,128)(2,1)S(1)}, bf16[2,48,896]{2,1,0:T(8,128)(2,1)S(1)}, u32[]{:S(2)}, u32[]{:S(2)}) collective-permute-start(bf16[2,48,896]{2,1,0:T(8,128)(2,1)S(1)} %pack.1.refs_0_), channel_id=1, source_target_pairs={{0,6},{1,7},{2,4},{3,5},{4,2},{5,3},{6,0},{7,1},{8,14},{9,15},{10,... | collective-permute-start | bytes 516104 | tf_op jit(solution)/shard_map/ppermute | solution.py:120
  143.9 37.0 %collective-permute-start.20 = (bf16[512,768]{1,0:T(8,128)(2,1)S(1)}, bf16[512,768]{1,0:T(8,128)(2,1)S(1)}, u32[]{:S(2)}, u32[]{:S(2)}) collective-permute-start(bf16[512,768]{1,0:T(8,128)(2,1)S(1)} %get-tuple-element.208), channel_id=1, source_target_pairs={{0,8},{1,9},{2,10},{3,11},{4,12},{5,13},{6,14},{7,15},{8,0},{9,1},... | collective-permute-start | bytes 2359304 | tf_op jit(solution)/shard_map/ppermute | solution.py:120
  159.0 22.3 %collective-permute-start.29 = (bf16[16,192,384]{2,1,0:T(8,128)(2,1)}, bf16[16,192,384]{2,1,0:T(8,128)(2,1)S(1)}, u32[]{:S(2)}, u32[]{:S(2)}) collective-permute-start(bf16[16,192,384]{2,1,0:T(8,128)(2,1)} %bitcast.53), channel_id=1, source_target_pairs={{0,1},{1,0},{2,3},{3,2},{4,5},{5,4},{6,7},{7,6},{8,9},{9,8},{10,11... | collective-permute-start | bytes 7077896 | tf_op jit(solution)/shard_map/ppermute | solution.py:120
  180.9 11.5 %collective-permute-start.30 = (bf16[16,48,1536]{2,1,0:T(8,128)(2,1)}, bf16[16,48,1536]{2,1,0:T(8,128)(2,1)S(1)}, u32[]{:S(2)}, u32[]{:S(2)}) collective-permute-start(bf16[16,48,1536]{2,1,0:T(8,128)(2,1)} %bitcast.52), channel_id=1, source_target_pairs={{0,1},{1,0},{2,3},{3,2},{4,5},{5,4},{6,7},{7,6},{8,9},{9,8},{10,11... | collective-permute-start | bytes 7077896 | tf_op jit(solution)/shard_map/ppermute | solution.py:120
  183.8 41.4 %collective-permute-start.32 = (bf16[8,192,384]{2,1,0:T(8,128)(2,1)S(1)}, bf16[8,192,384]{2,1,0:T(8,128)(2,1)S(1)}, u32[]{:S(2)}, u32[]{:S(2)}) collective-permute-start(bf16[8,192,384]{2,1,0:T(8,128)(2,1)S(1)} %get-tuple-element.231), channel_id=1, source_target_pairs={{0,2},{1,5},{2,0},{3,7},{4,6},{5,1},{6,4},{7,3},{8,10},{9,13},{10,... | collective-permute-start | bytes 3538952 | tf_op jit(solution)/shard_map/ppermute | solution.py:120
  194.8 32.7 %collective-permute-start.33 = (bf16[8,48,1536]{2,1,0:T(8,128)(2,1)S(1)}, bf16[8,48,1536]{2,1,0:T(8,128)(2,1)S(1)}, u32[]{:S(2)}, u32[]{:S(2)}) collective-permute-start(bf16[8,48,1536]{2,1,0:T(8,128)(2,1)S(1)} %get-tuple-element.239), channel_id=1, source_target_pairs={{0,2},{1,5},{2,0},{3,7},{4,6},{5,1},{6,4},{7,3},{8,10},{9,13},{10,... | collective-permute-start | bytes 3538952 | tf_op jit(solution)/shard_map/ppermute | solution.py:120
  206.1 19.1 %collective-permute-start.31 = (bf16[512,768]{1,0:T(8,128)(2,1)S(1)}, bf16[512,768]{1,0:T(8,128)(2,1)S(1)}, u32[]{:S(2)}, u32[]{:S(2)}) collective-permute-start(bf16[512,768]{1,0:T(8,128)(2,1)S(1)} %get-tuple-element.244), channel_id=1, source_target_pairs={{0,8},{1,9},{2,10},{3,11},{4,12},{5,13},{6,14},{7,15},{8,0},{9,1},... | collective-permute-start | bytes 2359304 | tf_op jit(solution)/shard_map/ppermute | solution.py:120
  219.6 19.0 %collective-permute-start.35 = (bf16[16,48,1152]{2,1,0:T(8,128)(2,1)}, bf16[16,48,1152]{2,1,0:T(8,128)(2,1)S(1)}, u32[]{:S(2)}, u32[]{:S(2)}) collective-permute-start(bf16[16,48,1152]{2,1,0:T(8,128)(2,1)} %bitcast.54), channel_id=1, source_target_pairs={{0,1},{1,0},{2,3},{3,2},{4,5},{5,4},{6,7},{7,6},{8,9},{9,8},{10,11... | collective-permute-start | bytes 5308424 | tf_op jit(solution)/shard_map/ppermute | solution.py:120
  226.1 9.9 %collective-permute-start.34 = (bf16[4,192,384]{2,1,0:T(8,128)(2,1)S(1)}, bf16[4,192,384]{2,1,0:T(8,128)(2,1)S(1)}, u32[]{:S(2)}, u32[]{:S(2)}) collective-permute-start(bf16[4,192,384]{2,1,0:T(8,128)(2,1)S(1)} %get-tuple-element.251), channel_id=1, source_target_pairs={{0,4},{1,3},{2,6},{3,1},{4,0},{5,7},{6,2},{7,5},{8,12},{9,11},{10,... | collective-permute-start | bytes 1769480 | tf_op jit(solution)/shard_map/ppermute | solution.py:120
  228.3 15.2 %collective-permute-start.36 = (bf16[4,48,1536]{2,1,0:T(8,128)(2,1)S(1)}, bf16[4,48,1536]{2,1,0:T(8,128)(2,1)S(1)}, u32[]{:S(2)}, u32[]{:S(2)}) collective-permute-start(bf16[4,48,1536]{2,1,0:T(8,128)(2,1)S(1)} %get-tuple-element.254), channel_id=1, source_target_pairs={{0,4},{1,3},{2,6},{3,1},{4,0},{5,7},{6,2},{7,5},{8,12},{9,11},{10,... | collective-permute-start | bytes 1769480 | tf_op jit(solution)/shard_map/ppermute | solution.py:120
  236.7 23.6 %collective-permute-start.39 = (bf16[2,192,384]{2,1,0:T(8,128)(2,1)S(1)}, bf16[2,192,384]{2,1,0:T(8,128)(2,1)S(1)}, u32[]{:S(2)}, u32[]{:S(2)}) collective-permute-start(bf16[2,192,384]{2,1,0:T(8,128)(2,1)S(1)} %get-tuple-element.258), channel_id=1, source_target_pairs={{0,16},{1,17},{2,18},{3,19},{4,20},{5,21},{6,22},{7,23},{8,24},{9,... | collective-permute-start | bytes 884744 | tf_op jit(solution)/shard_map/ppermute | solution.py:120
  240.9 14.2 %collective-permute-start.37 = (bf16[8,48,1152]{2,1,0:T(8,128)(2,1)S(1)}, bf16[8,48,1152]{2,1,0:T(8,128)(2,1)S(1)}, u32[]{:S(2)}, u32[]{:S(2)}) collective-permute-start(bf16[8,48,1152]{2,1,0:T(8,128)(2,1)S(1)} %get-tuple-element.261), channel_id=1, source_target_pairs={{0,2},{1,5},{2,0},{3,7},{4,6},{5,1},{6,4},{7,3},{8,10},{9,13},{10,... | collective-permute-start | bytes 2654216 | tf_op jit(solution)/shard_map/ppermute | solution.py:120
  244.2 19.2 %collective-permute-start.40 = (bf16[2,48,1536]{2,1,0:T(8,128)(2,1)S(1)}, bf16[2,48,1536]{2,1,0:T(8,128)(2,1)S(1)}, u32[]{:S(2)}, u32[]{:S(2)}) collective-permute-start(bf16[2,48,1536]{2,1,0:T(8,128)(2,1)S(1)} %get-tuple-element.264), channel_id=1, source_target_pairs={{0,16},{1,17},{2,18},{3,19},{4,20},{5,21},{6,22},{7,23},{8,24},{9,... | collective-permute-start | bytes 884744 | tf_op jit(solution)/shard_map/ppermute | solution.py:120
  250.5 6.5 %collective-permute-start.38 = (bf16[16,48,512]{2,1,0:T(8,128)(2,1)}, bf16[16,48,512]{2,1,0:T(8,128)(2,1)S(1)}, u32[]{:S(2)}, u32[]{:S(2)}) collective-permute-start(bf16[16,48,512]{2,1,0:T(8,128)(2,1)} %bitcast.55), channel_id=1, source_target_pairs={{0,1},{1,0},{2,3},{3,2},{4,5},{5,4},{6,7},{7,6},{8,9},{9,8},{10,11... | collective-permute-start | bytes 2359304 | tf_op jit(solution)/shard_map/ppermute | solution.py:120
  255.9 10.5 %collective-permute-start.41 = (bf16[4,48,1152]{2,1,0:T(8,128)(2,1)S(1)}, bf16[4,48,1152]{2,1,0:T(8,128)(2,1)S(1)}, u32[]{:S(2)}, u32[]{:S(2)}) collective-permute-start(bf16[4,48,1152]{2,1,0:T(8,128)(2,1)S(1)} %get-tuple-element.271), channel_id=1, source_target_pairs={{0,4},{1,3},{2,6},{3,1},{4,0},{5,7},{6,2},{7,5},{8,12},{9,11},{10,... | collective-permute-start | bytes 1327112 | tf_op jit(solution)/shard_map/ppermute | solution.py:120
  258.9 9.1 %collective-permute-start.42 = (bf16[8,48,512]{2,1,0:T(8,128)(2,1)S(1)}, bf16[8,48,512]{2,1,0:T(8,128)(2,1)S(1)}, u32[]{:S(2)}, u32[]{:S(2)}) collective-permute-start(bf16[8,48,512]{2,1,0:T(8,128)(2,1)S(1)} %get-tuple-element.274), channel_id=1, source_target_pairs={{0,2},{1,5},{2,0},{3,7},{4,6},{5,1},{6,4},{7,3},{8,10},{9,13},{10,... | collective-permute-start | bytes 1179656 | tf_op jit(solution)/shard_map/ppermute | solution.py:120
  260.9 7.7 %collective-permute-start.43 = (bf16[1,192,384]{2,1,0:T(8,128)(2,1)S(1)}, bf16[1,192,384]{2,1,0:T(8,128)(2,1)S(1)}, u32[]{:S(2)}, u32[]{:S(2)}) collective-permute-start(bf16[1,192,384]{2,1,0:T(8,128)(2,1)S(1)} %get-tuple-element.277), channel_id=1, source_target_pairs={{0,8},{1,9},{2,10},{3,11},{4,12},{5,13},{6,14},{7,15},{8,0},{9,1},... | collective-permute-start | bytes 442376 | tf_op jit(solution)/shard_map/ppermute | solution.py:120
  264.0 8.9 %collective-permute-start.44 = (bf16[1,48,1536]{2,1,0:T(8,128)(2,1)S(1)}, bf16[1,48,1536]{2,1,0:T(8,128)(2,1)S(1)}, u32[]{:S(2)}, u32[]{:S(2)}) collective-permute-start(bf16[1,48,1536]{2,1,0:T(8,128)(2,1)S(1)} %get-tuple-element.280), channel_id=1, source_target_pairs={{0,8},{1,9},{2,10},{3,11},{4,12},{5,13},{6,14},{7,15},{8,0},{9,1},... | collective-permute-start | bytes 442376 | tf_op jit(solution)/shard_map/ppermute | solution.py:120
  267.0 11.8 %collective-permute-start.45 = (bf16[2,48,1152]{2,1,0:T(8,128)(2,1)S(1)}, bf16[2,48,1152]{2,1,0:T(8,128)(2,1)S(1)}, u32[]{:S(2)}, u32[]{:S(2)}) collective-permute-start(bf16[2,48,1152]{2,1,0:T(8,128)(2,1)S(1)} %get-tuple-element.283), channel_id=1, source_target_pairs={{0,16},{1,17},{2,18},{3,19},{4,20},{5,21},{6,22},{7,23},{8,24},{9,... | collective-permute-start | bytes 663560 | tf_op jit(solution)/shard_map/ppermute | solution.py:120
  269.3 12.7 %collective-permute-start.47 = (bf16[2,192,384]{2,1,0:T(8,128)(2,1)S(1)}, bf16[2,192,384]{2,1,0:T(8,128)(2,1)S(1)}, u32[]{:S(2)}, u32[]{:S(2)}) collective-permute-start(bf16[2,192,384]{2,1,0:T(8,128)(2,1)S(1)} %add_last.4.refs_0_), channel_id=1, source_target_pairs={{0,1},{1,0},{2,3},{3,2},{4,5},{5,4},{6,7},{7,6},{8,9},{9,8},{10,11... | collective-permute-start | bytes 884744 | tf_op jit(solution)/shard_map/ppermute | solution.py:120
  269.9 9.6 %collective-permute-start.46 = (bf16[4,48,512]{2,1,0:T(8,128)(2,1)S(1)}, bf16[4,48,512]{2,1,0:T(8,128)(2,1)S(1)}, u32[]{:S(2)}, u32[]{:S(2)}) collective-permute-start(bf16[4,48,512]{2,1,0:T(8,128)(2,1)S(1)} %get-tuple-element.286), channel_id=1, source_target_pairs={{0,4},{1,3},{2,6},{3,1},{4,0},{5,7},{6,2},{7,5},{8,12},{9,11},{10,... | collective-permute-start | bytes 589832 | tf_op jit(solution)/shard_map/ppermute | solution.py:120
  274.4 9.3 %collective-permute-start.48 = (bf16[2,48,1536]{2,1,0:T(8,128)(2,1)S(1)}, bf16[2,48,1536]{2,1,0:T(8,128)(2,1)S(1)}, u32[]{:S(2)}, u32[]{:S(2)}) collective-permute-start(bf16[2,48,1536]{2,1,0:T(8,128)(2,1)S(1)} %add_last.5.refs_0_), channel_id=1, source_target_pairs={{0,1},{1,0},{2,3},{3,2},{4,5},{5,4},{6,7},{7,6},{8,9},{9,8},{10,11... | collective-permute-start | bytes 884744 | tf_op jit(solution)/shard_map/ppermute | solution.py:120
  279.4 10.8 %collective-permute-start.50 = (bf16[1,48,1152]{2,1,0:T(8,128)(2,1)S(1)}, bf16[1,48,1152]{2,1,0:T(8,128)(2,1)S(1)}, u32[]{:S(2)}, u32[]{:S(2)}) collective-permute-start(bf16[1,48,1152]{2,1,0:T(8,128)(2,1)S(1)} %get-tuple-element.291), channel_id=1, source_target_pairs={{0,8},{1,9},{2,10},{3,11},{4,12},{5,13},{6,14},{7,15},{8,0},{9,1},... | collective-permute-start | bytes 331784 | tf_op jit(solution)/shard_map/ppermute | solution.py:120
  (28 other events, 195.3 us)

commit v4 on v3

--- a/solution.py
+++ b/solution.py
@@ -20,6 +20,28 @@
 EPS = 1e-05
 LOSS_WEIGHT = 32.0
 MIB = 2**20
+O_NEAR1 = "z2,both3"
+O_NEAR3 = "p2"
+O_X = 'z3'
+O_D2 = "first"
+O_D3 = "norm"
+O_P2 = True
+O_FCOST = 1.0
+O_COT = 'norm'
+O_COTD = "loss"
+O_SPLIT = 4
+O_GELU = 1
+O_GX = 'u3'
+O_BCOST = 4.0
+O_TAIL = 0
+O_OUT = "pick"
+O_D2DN = 1
+O_V1 = True
+O_V2 = True
+O_V3 = True
+O_V4 = 0
+O_V5 = True
+O_V6 = False
 AT_OUT = 3 * D
 AT_VEC = 4 * D
 
@@ -37,7 +59,7 @@
 
 
 def behind(us):
-    return cost(4 * us)
+    return cost(O_BCOST * us)
 
 
 def params(mib):
@@ -55,6 +77,10 @@
 
 def shape(dims, dtype):
     return jax.ShapeDtypeStruct(dims, dtype)
+
+
+def later(dims, dtype):
+    return shape(dims, dtype) if O_V2 else far(dims, dtype)
 
 
 def far(dims, dtype):
@@ -257,7 +283,7 @@
         out_specs=vmem(),
         compiler_params=params(24),
         name="assemble",
-        cost_estimate=cost(2),
+        cost_estimate=cost(2 * O_FCOST),
     )(order.where, *bufs)
     order.done(full)
     return full.reshape(plan.n * rows, width * plan.reps)
@@ -279,6 +305,16 @@
         o_ref[to] = (a_ref[j].astype(F32) + b_ref[at].astype(F32)).astype(BF)
 
 
+def add_kernel2(depth, where_ref, a_ref, b_ref, s_ref, k_ref):
+    me, core = where_ref[0], where_ref[1]
+    p1 = 1 + core % 2
+    p2 = 2 - core % 2
+    for j in range(4 * depth):
+        at = me ^ ((1 - j // (2 * depth)) * p1) ^ ((1 - j // depth % 2) * p2) ^ (4 * (j % depth))
+        o_ref, to = (s_ref, j) if j < 2 * depth else (k_ref, j - 2 * depth)
+        o_ref[to] = (a_ref[at].astype(F32) + b_ref[at].astype(F32)).astype(BF)
+
+
 def two_kernel(where_ref, k_ref, r_ref, s_ref, o_ref):
     q = s_ref.shape[0]
     for j in range(2 * q):
@@ -309,13 +345,20 @@
     return (a.astype(F32) + b.astype(F32)).astype(BF)
 
 
+def send_cut(v, pairs):
+    if O_D2DN == 1:
+        return send(v, pairs)
+    n = v.shape[0] // O_D2DN
+    return jnp.concatenate([send(v[i * n : (i + 1) * n], pairs) for i in range(O_D2DN)], 0)
+
+
 class Scatter:
     def __init__(self, plan, order, parts, rows):
         self.plan, self.order, self.rows = plan, order, rows
         self.width = parts[0].shape[1]
         parts = [p.reshape(plan.n, rows, self.width) for p in parts]
         self.own = parts[0]
-        got = [send(parts[q], plan.sibling(q)) for q in range(1, plan.reps)]
+        got = [send_cut(parts[q], plan.sibling(q)) for q in range(1, plan.reps)]
         self.rest = got[0]
         for o in got[1:]:
             self.rest = plus(self.rest, o)
@@ -328,6 +371,20 @@
         n = plan.n
         whole = (n, self.rows, self.width)
         half = shape((n // 2, self.rows, self.width), BF)
+        if O_V2:
+            hs, self.hk = self.order.done(
+                pl.pallas_call(
+                    partial(add_kernel2, plan.depth),
+                    out_shape=(half, half),
+                    in_specs=[smem(), vmem(), vmem()],
+                    out_specs=(vmem(), vmem()),
+                    compiler_params=params(24),
+                    name="pick_add",
+                    cost_estimate=behind(3),
+                )(self.order.where, self.own, self.rest)
+            )
+            self.r1 = send(hs, plan.first())
+            return
         hs, self.hk = self.order.done(
             pl.pallas_call(
                 partial(add_kernel, plan.depth),
@@ -368,7 +425,7 @@
         self.ends = [pair] + [send(pair, plan.sibling(q)) for q in range(1, plan.reps)]
 
 
-def finish_kernel(reps, spans, where_ref, *refs):
+def finish_kernel(reps, spans, vec, where_ref, *refs):
     chunks = len(spans)
     ins, outs = refs[: chunks * reps], refs[chunks * reps :]
     core = where_ref[1]
@@ -379,20 +436,33 @@
             for mine in range(reps):
 
                 @pl.when((core ^ q) == mine)
-                def copy(q=q, mine=mine):
+                def copy(c=c, parts=parts, q=q, mine=mine):
                     for at, size, out, to in spans[c]:
                         low, high = max(at, mine * width), min(at + size, (mine + 1) * width)
-                        if low < high:
-                            outs[out][:, :, to + low - at : to + high - at] = parts[q][
-                                :, :, low - mine * width : high - mine * width
-                            ].astype(F32)
-
-
-def finish(plan, order, chunks, spans, widths):
-    rows = chunks[0].rows
-    outs = tuple(((2, rows, w), F32) for w in widths)
+                        if low >= high:
+                            continue
+                        lanes = slice(low - mine * width, high - mine * width)
+                        if out == vec:
+                            turn(parts[q], lanes, low - at, outs[out], outs[out + 1])
+                        else:
+                            outs[out][:, :, to + low - at : to + high - at] = parts[q][:, :, lanes].astype(F32)
+
+
+def turn(part_ref, lanes, at, bias_ref, gain_ref):
+    for t in range(2):
+        columns = part_ref[t, :, lanes]
+        for ref, start in ((bias_ref, 0), (gain_ref, bias_ref.shape[1])):
+            n = ref.shape[1]
+            i = lax.broadcasted_iota(jnp.int32, (n, columns.shape[1]), 0)
+            j = lax.broadcasted_iota(jnp.int32, (n, columns.shape[1]), 1)
+            ref[t] = dot_t(jnp.where(i + start == j + at, 1.0, 0.0).astype(BF), columns)
+
+
+def finish(plan, order, chunks, spans, shapes, vec=-1):
+    outs = tuple((s, F32) for s in shapes)
     args = [p for c in chunks for p in c.ends]
-    return order.done(in_vmem(partial(finish_kernel, plan.reps, spans), "finish", 2, outs, order.where, *args))
+    kernel = partial(finish_kernel, plan.reps, spans, vec)
+    return order.done(in_vmem(kernel, "finish", 2, outs, order.where, *args))
 
 
 def dot(a, b):
@@ -462,7 +532,7 @@
 
 
 def attend(order, x, w_one, part, before=()):
-    rows = x.shape[0]
+    rows = 2 * x.shape[0]
     per = TILE // BLOCK
     steps = rows // TILE // 2
     first = part * steps
@@ -483,7 +553,7 @@
             shape((128, D), F32),
             shape((rows // 64, D), F32),
         ),
-        in_specs=[smem(), here(D), vmem()] + [pl.BlockSpec(memory_space=pl.ANY)] * len(before),
+        in_specs=[smem(), rows_at(D), vmem()] + [pl.BlockSpec(memory_space=pl.ANY)] * len(before),
         out_specs=[
             here(3 * D),
             pl.BlockSpec((per, PAIRS, BLOCK, 2 * BLOCK), lambda i: (i + first, 0, 0, 0)),
@@ -498,12 +568,17 @@
         input_output_aliases={3 + j: j for j in range(len(before))},
         compiler_params=params(24),
         name="attend",
-        cost_estimate=cost(7),
+        cost_estimate=cost(7 * O_FCOST),
     )(order.where, x, w_one, *[stay(b) for b in before])
 
 
 def gelu_pair(u):
     phi = 0.5 + 0.5 * lax.erf(u * 2**-0.5)
+    if O_V4 == 1:
+        return u * phi, phi + u * jnp.exp2(u * u * (-0.5 / 0.6931471805599453) - 1.3257480647361595)
+    if O_V4 == 2:
+        v = u.astype(BF)
+        return u * phi, phi.astype(BF) + v * jnp.exp((v * v) * jnp.asarray(-0.5, BF)) * jnp.asarray((2 * jnp.pi) ** -0.5, BF)
     return u * phi, phi + u * (jnp.exp(-0.5 * u * u) * (2 * jnp.pi) ** -0.5)
 
 
@@ -537,7 +612,7 @@
         input_output_aliases={4 + j: j for j in range(len(before))},
         compiler_params=params(24),
         name="up",
-        cost_estimate=cost(8),
+        cost_estimate=cost(8 * O_FCOST),
     )(order.where, norm, w_up, vec, *[stay(b) for b in before])
 
 
@@ -567,12 +642,12 @@
     return pl.pallas_call(
         down_kernel,
         grid=(rows // TILE,),
-        out_shape=(far((rows // 2, D), BF), shape((rows // 2, D), BF), far((rows, D), F32), far((rows, 1), F32)),
+        out_shape=(far((rows // 2, D), BF), shape((rows // 2, D), BF), shape((rows, D), F32), shape((rows, 1), F32)),
         in_specs=[smem(), rows_at(FF), vmem(), rows_at(D), still(vec.shape)],
         out_specs=[near, away, rows_at(D), rows_at(1)],
         compiler_params=params(24),
         name="down",
-        cost_estimate=cost(8),
+        cost_estimate=cost(8 * O_FCOST),
     )(order.where, stay(act), w_down, stay(hat), vec)
 
 
@@ -733,14 +808,14 @@
     second, gs, sums, *parts = pl.pallas_call(
         top_kernel,
         grid=(FF // D,),
-        out_shape=(far((rows, D), F32), shape((rows, D), BF), shape((8, D), F32))
-        + (far((FF, part), BF),) * plan.reps,
+        out_shape=(shape((rows, D), F32) if O_V6 else far((rows, D), F32), shape((rows, D), BF), shape((8, D), F32))
+        + (later((FF, part), BF),) * plan.reps,
         in_specs=[
             smem(),
-            still(cot.shape),
+            vmem(),
             still(cls_grad.shape),
-            still(hat2.shape),
-            still(rstd2.shape),
+            vmem(),
+            vmem(),
             still(vec.shape),
             pl.BlockSpec((rows, D), lambda i: (0, i)),
         ],
@@ -793,15 +868,15 @@
 
     acc, sums, *parts = pl.pallas_call(
         partial(gelu_back_kernel, reps, column),
-        out_shape=(shape((rows, D), F32), shape((8, D), F32)) + (far((D, FF // reps), BF),) * reps,
+        out_shape=(shape((rows, D), F32), shape((8, D), F32)) + (later((D, FF // reps), BF),) * reps,
         grid_spec=pltpu.PrefetchScalarGridSpec(
             num_scalar_prefetch=1,
             grid=(FF // D,),
             in_specs=[
-                still(gs.shape),
+                vmem() if O_V5 else still(gs.shape),
                 pl.BlockSpec((D, D), lambda i, table: (column(i, table), 0)),
                 pl.BlockSpec((rows, D), lambda i, table: (0, column(i, table))),
-                still(norm.shape),
+                vmem() if O_V5 else still(norm.shape),
                 pl.BlockSpec((D, D), lambda i, table: (0, column(i, table))),
             ],
             out_specs=[still((rows, D)), still((8, D))] + [held(q) for q in range(reps)],
@@ -824,7 +899,8 @@
     grad = acc_ref[...] + second_ref[...]
     hat = hat_ref[...]
     hidden = norm_back(grad, hat, rstd_ref[...], vec_ref[10:11, :])
-    hidden_ref[...] = hidden
+    if not O_V3:
+        hidden_ref[...] = hidden
     go = hidden.astype(BF)
     go_ref[...] = go
     sums_ref[0:1, :] += col_sum(go.astype(F32))
@@ -838,15 +914,102 @@
     return pl.pallas_call(
         hidden_back_kernel,
         grid=(rows // TILE,),
-        out_shape=(far((rows, D), F32), shape((rows, D), BF), shape((rows, D), BF), shape((8, D), F32)),
+        out_shape=((shape((8, D), F32) if O_V3 else far((rows, D), F32)), shape((rows, D), BF), shape((rows, D), BF), shape((8, D), F32)),
         in_specs=[smem()]
         + [rows_at(D)] * 3
         + [rows_at(1), still((D, D), (0, AT_OUT // D)), still(vec.shape)],
-        out_specs=[rows_at(D), rows_at(D), rows_at(D), still((8, D))],
+        out_specs=[still((8, D)) if O_V3 else rows_at(D), rows_at(D), rows_at(D), still((8, D))],
         compiler_params=params(20),
         name="hidden_back",
         cost_estimate=behind(5),
-    )(order.where, acc, stay(second), stay(hat), stay(rstd), stay(w_one), vec)
+    )(order.where, acc, second if O_V6 else stay(second), stay(hat), stay(rstd), stay(w_one), vec)
+
+
+def gelu_back2_kernel(reps, column, where_ref, gs_ref, w_ref, slope_ref, norm_ref, gu_ref, sums_ref, *parts):
+    i = pl.program_id(0)
+    total = jnp.zeros((1, D), F32)
+    for m in range(0, gs_ref.shape[0], TILE):
+        rows = slice(m, m + TILE)
+        gu = (dot_t(gs_ref[rows, :], w_ref[...]) * slope_ref[rows, :].astype(F32)).astype(BF)
+        gu_ref[rows, :] = gu
+        total = total + col_sum(gu.astype(F32))
+    sums_ref[pl.ds(column(i, where_ref), 1), :] = total
+    grad = t_dot(norm_ref[...], gu_ref[...]).astype(BF)
+    per = (FF // D) // reps
+    for q in range(reps):
+
+        @pl.when(i // per == reps - 1 - q)
+        def put(q=q):
+            parts[q][...] = grad
+
+
+def gelu_back2(plan, order, gs, w_down, slope, norm):
+    rows = gs.shape[0]
+    reps = plan.reps
+    per = (FF // D) // reps
+
+    def column(i, table):
+        return (table[1] ^ (reps - 1 - i // per)) * per + i % per
+
+    def held(q):
+        return pl.BlockSpec((D, D), lambda i, table: (0, jnp.clip(i - (reps - 1 - q) * per, 0, per - 1)))
+
+    col = pl.BlockSpec((rows, D), lambda i, table: (0, column(i, table)))
+    gu, sums, *parts = pl.pallas_call(
+        partial(gelu_back2_kernel, reps, column),
+        out_shape=(shape((rows, FF), BF), shape((8, D), F32)) + (later((D, FF // reps), BF),) * reps,
+        grid_spec=pltpu.PrefetchScalarGridSpec(
+            num_scalar_prefetch=1,
+            grid=(FF // D,),
+            in_specs=[
+                still(gs.shape),
+                pl.BlockSpec((D, D), lambda i, table: (column(i, table), 0)),
+                col,
+                still(norm.shape),
+            ],
+            out_specs=[col, still((8, D))] + [held(q) for q in range(reps)],
+        ),
+        compiler_params=params(28),
+        name="gelu_back",
+        cost_estimate=behind(14),
+    )(order.where, gs, stay(w_down), stay(slope), norm)
+    return gu, sums, parts
+
+
+def hidden_back2_kernel(
+    where_ref, gu_ref, up_ref, second_ref, hat_ref, rstd_ref, w_ref, vec_ref, hidden_ref, go_ref, ga_ref, sums_ref
+):
+    @pl.when(pl.program_id(0) == 0)
+    def clear():
+        sums_ref[...] = jnp.zeros_like(sums_ref)
+
+    grad = dot_t(gu_ref[...], up_ref[...]) + second_ref[...]
+    hat = hat_ref[...]
+    hidden = norm_back(grad, hat, rstd_ref[...], vec_ref[10:11, :])
+    if not O_V3:
+        hidden_ref[...] = hidden
+    go = hidden.astype(BF)
+    go_ref[...] = go
+    sums_ref[0:1, :] += col_sum(go.astype(F32))
+    sums_ref[1:2, :] += col_sum(grad)
+    sums_ref[2:3, :] += col_sum(grad * hat)
+    ga_ref[...] = dot_t(go, w_ref[...]).astype(BF)
+
+
+def hidden_back2(order, gu, w_up, second, hat, rstd, w_one, vec):
+    rows = gu.shape[0]
+    return pl.pallas_call(
+        hidden_back2_kernel,
+        grid=(rows // TILE,),
+        out_shape=((shape((8, D), F32) if O_V3 else far((rows, D), F32)), shape((rows, D), BF), shape((rows, D), BF), shape((8, D), F32)),
+        in_specs=[smem(), rows_at(FF), vmem()]
+        + [rows_at(D)] * 2
+        + [rows_at(1), still((D, D), (0, AT_OUT // D)), still(vec.shape)],
+        out_specs=[still((8, D)) if O_V3 else rows_at(D), rows_at(D), rows_at(D), still((8, D))],
+        compiler_params=params(24),
+        name="hidden_back",
+        cost_estimate=behind(11),
+    )(order.where, gu, w_up, stay(second), stay(hat), stay(rstd), stay(w_one), vec)
 
 
 def pair_back(pair, block, rows, ga_ref, proj_ref, probs_ref, low, high):
@@ -904,28 +1067,27 @@
     )(order.where, ga, stay(proj), stay(probs))
 
 
-def both_rows(x_ref, near_ref, far_ref):
-    half = near_ref.shape[0]
-    return (t_dot(x_ref[:half, :], near_ref[...]) + t_dot(x_ref[half:, :], far_ref[...])).astype(BF)
-
-
-def first_weights_kernel(where_ref, x_ref, near_ref, far_ref, attn_ref, go_ref, *rest):
+def both_rows(x_ref, y_ref, near_ref, far_ref):
+    return (t_dot(x_ref[...], near_ref[...]) + t_dot(y_ref[...], far_ref[...])).astype(BF)
+
+
+def first_weights_kernel(where_ref, x_ref, y_ref, near_ref, far_ref, attn_ref, go_ref, *rest):
     parts, full_ref = rest[:-1], rest[-1]
     full_ref[:, :D] = t_dot(attn_ref[...], go_ref[...]).astype(BF)
     end = D + near_ref.shape[1]
-    full_ref[:, D:end] = both_rows(x_ref, near_ref, far_ref)
+    full_ref[:, D:end] = both_rows(x_ref, y_ref, near_ref, far_ref)
     if end < full_ref.shape[1]:
         full_ref[:, end:] = jnp.zeros((D, full_ref.shape[1] - end), BF)
     halves(parts, where_ref[1], full_ref)
 
 
 def last_weights_kernel(
-    count, where_ref, x_ref, near_ref, far_ref, first_near_ref, first_far_ref, up_ref, top_ref, hidden_ref, *rest
+    count, where_ref, x_ref, y_ref, near_ref, far_ref, first_near_ref, first_far_ref, up_ref, top_ref, hidden_ref, *rest
 ):
     parts, full_ref, lines_ref = rest[:-2], rest[-2], rest[-1]
     part = D - count * 128
     wide = count * 128
-    full_ref[:, : 3 * part] = both_rows(x_ref, near_ref, far_ref)
+    full_ref[:, : 3 * part] = both_rows(x_ref, y_ref, near_ref, far_ref)
 
     def sums(j, width, a_ref, b_ref):
         lanes = slice(j * width, (j + 1) * width)
@@ -941,7 +1103,8 @@
     lines_ref[10:11, :] = hidden_ref[2:3, :]
     lines_ref[11:12, :] = top_ref[2:3, :]
     full_ref[:, 3 * part : 3 * part + 128] = jnp.transpose(lines_ref[...]).astype(BF)
-    full_ref[:, 3 * part + 128 :] = jnp.zeros((D, full_ref.shape[1] - 3 * part - 128), BF)
+    if 3 * part + 128 < full_ref.shape[1]:
+        full_ref[:, 3 * part + 128 :] = jnp.zeros((D, full_ref.shape[1] - 3 * part - 128), BF)
     halves(parts, where_ref[1], full_ref)
 
 
@@ -950,8 +1113,8 @@
     return pl.pallas_call(
         kernel,
         grid=(1,),
-        out_shape=(far((D, part), BF),) * plan.reps,
-        in_specs=[smem()] + [still(a.shape) for a in args],
+        out_shape=(later((D, part), BF),) * plan.reps,
+        in_specs=[smem()] + [vmem() if O_V1 else still(a.shape) for a in args],
         out_specs=[still((D, part))] * plan.reps,
         scratch_shapes=[pltpu.VMEM((D, total), BF)] + scratch,
         compiler_params=params(28),
@@ -961,6 +1124,7 @@
 
 
 def gx_of(count, a_ref, b_ref, w_ref, hidden):
+    hidden = hidden.astype(F32)
     ca, cb = count * 128, D - count * 128
     for j in range(3):
         hidden = hidden + dot_t(a_ref[:, j * ca : (j + 1) * ca], w_ref[:, j * D : j * D + ca])
@@ -1033,101 +1197,150 @@
     order = Order(where)
     mine, other, mine2, other2, mine3, other3 = shards_of(plan, order, w_qkv, w_out, biases, gains, w_up, w_down)
     z1 = gather_line(plan, mine, other)
-    x_mine, x_got = exchange(query_tokens, passage_tokens)
     both2 = jnp.concatenate([mine2, send(other2, swap)], 0)
+    both3 = jnp.concatenate([mine3, send(other3, swap)], 0)
     z2 = gather_steps(plan, both2, z1)
-    p1 = gather_plane(plan, z1, both2)
-    x = jnp.concatenate([x_mine, x_got], 0)
-    both3 = jnp.concatenate([mine3, send(after(other3, x), swap)], 0)
-    p1 = tuple(after(b, z2, both3) for b in p1)
+    env = {"z1": z1, "z2": z2, "both2": both2, "both3": both3}
+
+    def deps(names):
+        return [env[n] for n in names.split(",") if n]
+
+    p1 = gather_plane(plan, z1, *deps(O_NEAR1))
+    z3 = gather_steps(plan, both3, z2)
+    env["z3"] = z3
+    x_mine, x_got = exchange(query_tokens, passage_tokens, *deps(O_X))
     w_one = gather_cores(plan, order, p1)
     p2 = gather_plane(plan, z2)
-    z3 = gather_steps(plan, both3, z2)
-    p3 = gather_plane(plan, after(z3, p2[0]))
-
-    order.done(p2[0])
-    first = order.done(attend(order, x, w_one, 0))
-    proj, probs, attn, hat1, rstd1, norm, vec, cls_b = order.done(attend(order, x, w_one, 1, first[:6]))
-    w_two = gather_cores(plan, order, tuple(after(b, first[6]) for b in p2))
-    cot_mine, cot_got = exchange(query_cot, passage_cot, z3)
+    env["p2"] = p2[0]
+    if O_NEAR3 != "first" and O_NEAR3 != "join":
+        p3 = gather_plane(plan, after(z3, *deps(O_NEAR3)) if O_NEAR3 else z3)
+    if O_P2:
+        order.done(p2[0])
+    first = order.done(attend(order, x_mine, w_one, 0))
+    if O_NEAR3 == "first":
+        p3 = gather_plane(plan, z3, first[6])
+    if O_NEAR3 == "join":
+        step3 = send(z3, plan.first())
+        near3 = join(order, z3, step3)
+        p3 = near3, send(near3, plan.second())
+    proj, probs, attn, hat1, rstd1, norm, vec, cls_b = order.done(attend(order, x_got, w_one, 1, first[:6]))
+    env["first"], env["norm"] = first[6], norm
+    w_two = gather_cores(plan, order, tuple(after(b, *deps(O_D2)) for b in p2) if O_D2 else p2)
     half_up = order.done(up(order, norm, w_two, vec, 0))
+    env["up"] = half_up[0]
+    w_three = gather_cores(plan, order, tuple(after(b, *deps(O_D3)) for b in p3) if O_D3 else p3)
+    msg = first_rows(order, first[7], cls_b, w_two, w_three, vec, positives)
+    env["msg"] = msg
+    if O_COT != "pack":
+        cot_mine, cot_got = exchange(query_cot, passage_cot, *deps(O_COT))
+    loss = Contrast(plan, order, msg, positives.shape[0])
     act, slope = order.done(up(order, norm, w_two, vec, 1, half_up))
+    loss.pack()
+    if O_COT == "pack":
+        cot_mine, cot_got = exchange(query_cot, passage_cot, loss.bufs[0])
     cot = jnp.concatenate([cot_mine, cot_got], 0)
-    w_three = gather_cores(plan, order, tuple(after(b, half_up[0]) for b in p3))
-    msg = first_rows(order, first[7], cls_b, w_two, w_three, vec, positives)
-    loss = Contrast(plan, order, msg, positives.shape[0])
+    if O_COTD == "down":
+        order.done(cot)
     out_own, out_far, hat2, rstd2 = order.done(down(order, act, w_three, hat1, vec))
     out_back = send(out_far, swap)
-    loss.pack()
-    order.done(cot)
     loss.join()
+    if O_COTD == "loss":
+        order.done(cot)
+    if O_OUT == "loss":
+        order.done(out_back)
     query_loss, cls_grad = loss.loss()
 
     second, gs, sums_top, g_down = order.done(top(plan, order, cot, cls_grad, hat2, rstd2, vec, act))
     down_part = Scatter(plan, order, g_down, w_down.shape[1])
-    acc, sums_up, g_up = order.done(gelu_back(plan, order, gs, w_three, slope, norm, w_two))
+    if O_GELU == 1:
+        acc, sums_up, g_up = order.done(gelu_back(plan, order, gs, w_three, slope, norm, w_two))
+    else:
+        gu, sums_up, g_up = order.done(gelu_back2(plan, order, gs, w_three, slope, norm))
     up_part = Scatter(plan, order, g_up, w_up.shape[1])
-    order.done(out_back)
+    if O_OUT == "pick":
+        order.done(out_back)
     down_part.one()
-    hidden, go, ga, sums = order.done(hidden_back(order, acc, second, hat1, rstd1, w_one, vec))
+    if O_OUT == "hidden":
+        order.done(out_back)
+    if O_GELU == 1:
+        hidden, go, ga, sums = order.done(hidden_back(order, acc, second, hat1, rstd1, w_one, vec))
+    else:
+        hidden, go, ga, sums = order.done(hidden_back2(order, gu, w_two, second, hat1, rstd1, w_one, vec))
+    if O_OUT == "pick5":
+        order.done(out_back)
     up_part.one()
-    split = 4
+    split = O_SPLIT
     half = ga.shape[0] // 2
+    if O_V3:
+        hidden = go
     far_a, far_b, gx_far = order.done(far_back(order, split, ga, proj, probs, w_one, hidden))
     gx_back = send(gx_far, swap)
     near_a = order.done(attend_back(order, 0, split, ga, proj, probs, half))
     total = wide(3 * split * 128 + D, plan.reps)
     kernel = first_weights_kernel
-    g_a = order.done(weights(plan, order, kernel, "first_weights", 5, total, [], x, near_a, far_a, stay(attn), go))
+    g_a = order.done(weights(plan, order, kernel, "first_weights", 5, total, [], x_mine, x_got, near_a, far_a, stay(attn), go))
     a_part = Scatter(plan, order, g_a, w_qkv.shape[1])
-    order.done(gx_back)
+    if O_GX == "fw":
+        order.done(gx_back)
     down_part.two()
+    if O_GX == "two":
+        order.done(gx_back)
     up_part.two()
     near_b = order.done(attend_back(order, split, PAIRS - split, ga, proj, probs, half))
+    if O_GX == "nb":
+        order.done(gx_back)
     down_part.three()
     a_part.one()
+    if O_GX == "a1":
+        order.done(gx_back)
     up_part.three()
+    if O_GX == "u3":
+        order.done(gx_back)
     total = wide(3 * (D - split * 128) + 128, plan.reps)
     kernel = partial(last_weights_kernel, split)
     scratch = [pltpu.VMEM((128, D), F32)]
-    args = (x, near_b, far_b, near_a, far_a, sums_up, sums_top, sums)
+    args = (x_mine, x_got, near_b, far_b, near_a, far_a, sums_up, sums_top, sums)
     g_b = order.done(weights(plan, order, kernel, "last_weights", 4, total, scratch, *args))
     b_part = Scatter(plan, order, g_b, w_qkv.shape[1])
     gx_own = order.done(token_back(order, split, near_a, near_b, w_one, hidden))
-    a_part.two()
-    b_part.one()
-    down_part.four()
-    up_part.four()
-    a_part.three()
-    b_part.two()
-    down_part.last()
-    up_part.last()
-    a_part.four()
-    b_part.three()
-    (grad_down,) = finish(plan, order, [down_part], [[(0, D, 0, 0)]], [D])
-    (grad_up,) = finish(plan, order, [up_part], [[(0, FF, 0, 0)]], [FF])
-    b_part.four()
+    steps = {
+        "a2": a_part.two, "b1": b_part.one, "d4": down_part.four, "u4": up_part.four, "a3": a_part.three,
+        "b2": b_part.two, "dl": down_part.last, "ul": up_part.last, "a4": a_part.four, "b3": b_part.three,
+        "b4": b_part.four, "al": a_part.last, "bl": b_part.last,
+        "fd": lambda: outs.append(finish(plan, order, [down_part], [[(0, D, 0, 0)]], [w_down.shape])[0]),
+        "fu": lambda: outs.append(finish(plan, order, [up_part], [[(0, FF, 0, 0)]], [w_up.shape])[0]),
+    }
+    outs = []
+    tails = [
+        "a2 b1 d4 u4 a3 b2 dl ul a4 b3 fd fu b4 al bl",
+        "b1 a2 d4 u4 b2 a3 dl b3 ul a4 fd b4 fu bl al",
+        "a2 b1 d4 b2 u4 a3 b3 dl ul a4 b4 fd fu al bl",
+        "a2 d4 b1 u4 a3 dl b2 ul b3 a4 fd fu b4 al bl",
+        "b1 a2 d4 u4 a3 b2 dl ul b3 a4 fd fu b4 al bl",
+        "a2 b1 d4 u4 a3 b2 b3 dl ul a4 b4 fd fu al bl",
+    ]
+    for step in tails[O_TAIL].split():
+        steps[step]()
+    grad_down, grad_up = outs
     query_out, passage_out = merged(out_own, after(out_back, b_part.out))
     query_grad, passage_grad = merged(gx_own, after(gx_back, b_part.out).astype(F32))
-    a_part.last()
-    b_part.last()
     qa, qb = split * 128, D - split * 128
     spans_a = [(0, D, 1, 0)] + [(D + j * qa, qa, 0, j * D) for j in range(3)]
     spans_b = [(j * qb, qb, 0, j * D + qa) for j in range(3)] + [(3 * qb, 128, 2, 0)]
-    grad_qkv, grad_out, grad_vecs = finish(plan, order, [a_part, b_part], [spans_a, spans_b], [3 * D, D, 128])
-    grad_vecs = jnp.swapaxes(grad_vecs[:, :, :12], 1, 2)
+    shapes = [w_qkv.shape, w_out.shape, biases.shape, gains.shape]
+    grads = finish(plan, order, [a_part, b_part], [spans_a, spans_b], shapes, 2)
     return (
         query_out,
         passage_out,
         query_grad,
         passage_grad,
         query_loss,
-        grad_qkv,
-        grad_out,
+        grads[0],
+        grads[1],
         grad_up,
         grad_down,
-        grad_vecs[:, :10],
-        grad_vecs[:, 10:],
+        grads[2],
+        grads[3],
     )
 
 

time: 300 us -> 287 us (0.957)
  starting transfers between devices: 52.3 us -> 41.9 us
  Pallas kernels: 150 us -> 141 us
  waiting for transfers between devices: 82.4 us -> 87.5 us
    ppermute x54, starting transfers between devices: 52.3 us -> 41.9 us  [send(): return lax.ppermute(v, AXES, pairs)]
    pallas_call x8, Pallas kernels: 37.7 us -> 30.1 us  [the longest x1 11.6 us: top(): pl.pallas_call(top_kernel, grid=(FF // D,), out_shape=(shape((rows, D), F...]
    ppermute x54, waiting for transfers between devices: 82.4 us -> 87.5 us  [send(): return lax.ppermute(v, AXES, pairs)]
  transfers between devices with their start and end apart: 54 -> 54, of which waited for: 19 -> 14; matrix products, arithmetic and copies ran while one was open for 2% -> 2% of each run, Pallas kernels for 49% -> 48%
where the time goes in v4:
time: 287 us; the launch traced here: 283 us
  Pallas kernels  141 us (49%)
  waiting for transfers between devices  87.5 us (30%)
  starting transfers between devices  41.9 us (15%)
  local copies, waits for them, and re-layouts  6.92 us (2%)
  other arithmetic  3.75 us (1%)
    ppermute x54, waiting for transfers between devices, send(): return lax.ppermute(v, AXES, pairs)  87.5 us
    ppermute x54, starting transfers between devices, send(): return lax.ppermute(v, AXES, pairs)  41.9 us
    pallas_call x1, Pallas kernels, gelu_back(): pl.pallas_call(partial(gelu_back_kernel, reps, column), out_shape=(shape(...  20.7 us
    pallas_call x22, Pallas kernels, in_vmem(): pl.pallas_call(kernel, out_shape=tuple((shape(*o) for o in outs)), in_spe...  19.4 us
    pallas_call x2, Pallas kernels, attend(): pl.pallas_call(partial(attend_kernel, part), grid=(steps,), out_shape=(fa...  16.2 us
    pallas_call x2, Pallas kernels, up(): pl.pallas_call(partial(up_kernel, first), grid=(steps,), out_shape=(far((...  13.9 us
    pallas_call x1, Pallas kernels, top(): pl.pallas_call(top_kernel, grid=(FF // D,), out_shape=(shape((rows, D), F...  11.6 us
    pallas_call x1, Pallas kernels, far_back(): pl.pallas_call(partial(far_back_kernel, count), grid=(steps,), out_shape=...  10.8 us
  transfers between devices with their start and end apart: 54, of which 14 were waited for; matrix products, arithmetic and copies ran while one was open for 2% of the time, Pallas kernels for 48%

profile of v4, /device:TPU:0, one launch (start us, length us, event | category | flops | bytes accessed | tf_op | source)
XLA Modules:
  0.0 283.1 jit_solution(12695431088580149496)
XLA Ops:
  2.0 1.8 shards.1
  3.8 3.1 %collective-permute-start = (bf16[1,48,1664]{2,1,0:T(8,128)(2,1)S(1)}, bf16[1,48,1664]{2,1,0:T(8,128)(2,1)S(1)}, u32[]{:S(2)}, u32[]{:S(2)}) collective-permute-start(bf16[1,48,1664]{2,1,0:T(8,128)(2,1)S(1)} %get-tuple-element.159), channel_id=1, source_target_pairs={{0,8},{1,9},{2,10},{3,11},{4,12},{5,13},{6,14},{7,15},{8,0},{9,1},... | collective-permute-start | bytes 479240 | tf_op jit(solution)/shard_map/ppermute | solution.py:146
  6.9 2.5 collective-permute-start.2
  9.5 1.8 collective-permute-start.4
  11.6 12.1 %collective-permute-done.1 = bf16[1,48,1664]{2,1,0:T(8,128)(2,1)S(1)} collective-permute-done((bf16[1,48,1664]{2,1,0:T(8,128)(2,1)S(1)}, bf16[1,48,1664]{2,1,0:T(8,128)(2,1)S(1)}, u32[]{:S(2)}, u32[]{:S(2)}) %collective-permute-start.1) | collective-permute-done | bytes 159776 | tf_op jit(solution)/shard_map/ppermute | solution.py:146
  23.8 1.6 collective-permute-start.3
  25.5 14.6 %collective-permute-done.5 = bf16[2,48,1536]{2,1,0:T(8,128)(2,1)S(1)} collective-permute-done((bf16[2,48,1536]{2,1,0:T(8,128)(2,1)S(1)}, bf16[2,48,1536]{2,1,0:T(8,128)(2,1)S(1)}, u32[]{:S(2)}, u32[]{:S(2)}) %collective-permute-start.5) | collective-permute-done | bytes 294944 | tf_op jit(solution)/shard_map/ppermute | solution.py:146
  40.9 1.5 collective-permute-start.10
  42.4 21.6 %collective-permute-done.7.refs_1_ = bf16[8,48,1664]{2,1,0:T(8,128)(2,1)S(1)} collective-permute-done((bf16[8,48,1664]{2,1,0:T(8,128)(2,1)S(1)}, bf16[8,48,1664]{2,1,0:T(8,128)(2,1)S(1)}, u32[]{:S(2)}, u32[]{:S(2)}) %collective-permute-start.7) | collective-permute-done | bytes 1277984 | tf_op jit(solution)/shard_map/ppermute | solution.py:146
  65.9 14.5 %collective-permute-done.16 = bf16[4,192,384]{2,1,0:T(8,128)(2,1)S(1)} collective-permute-done((bf16[4,192,384]{2,1,0:T(8,128)(2,1)S(1)}, bf16[4,192,384]{2,1,0:T(8,128)(2,1)S(1)}, u32[]{:S(2)}, u32[]{:S(2)}) %collective-permute-start.16) | collective-permute-done | bytes 589856 | tf_op jit(solution)/shard_map/ppermute | solution.py:146
  81.6 8.5 %attend.2 = (bf16[1024,2304]{1,0:T(8,128)(2,1)}, bf16[8,6,128,256]{3,2,1,0:T(8,128)(2,1)}, bf16[1024,768]{1,0:T(8,128)(2,1)}, f32[1024,768]{1,0:T(8,128)}, f32[1...) custom-call(s32[4]{0:T(128)S(1)} %pad_add_fusion.where_ref, ...), custom_call_target="tpu_custom_call" | custom-call | flops 7000000000 | bytes 21000000 | tf_op jit(solution)/shard_map/attend/pallas_call | solution.py:543
  90.7 7.7 %attend.3 = (bf16[1024,2304]{1,0:T(8,128)(2,1)}, bf16[8,6,128,256]{3,2,1,0:T(8,128)(2,1)}, bf16[1024,768]{1,0:T(8,128)(2,1)}, f32[1024,768]{1,0:T(8,128)}, f32[1...) custom-call(s32[4]{0:T(128)S(1)} %pad_add_fusion.where_ref, ...), custom_call_target="tpu_custom_call", output_to_operand_aliasing={{0}: (3, {}), {1}: (4, {}), {2}: (5, {}), {3}: (6, {}), {4}... | custom-call | flops 7000000000 | bytes 21000000 | tf_op jit(solution)/shard_map/attend/pallas_call | solution.py:543
  101.0 6.7 %up.2 = (bf16[1024,3072]{1,0:T(8,128)(2,1)}, bf16[1024,3072]{1,0:T(8,128)(2,1)}) custom-call(s32[4]{0:T(128)S(1)} %pad_add_fusion.where_ref, bf16[1024,768]{1,0:T(8,128)(2,1)S(1)} %copy-done.8, bf16[768,3072]{1,0:T(8,128)(2,1)S(1)} %bitcast.37, f32[128,768]{1,0:T(8,128)S(1)} %get-tuple-element.186.vec_ref), custom_call_target="tpu_custom_call" | custom-call | flops 8000000000 | bytes 24000000 | tf_op jit(solution)/shard_map/up/pallas_call | solution.py:600
  108.8 2.6 first_rows.1.refs_0_
  111.5 1.7 collective-permute-start.20
  113.4 2.6 collective-permute-start.22
  115.9 7.1 %up.3 = (bf16[1024,3072]{1,0:T(8,128)(2,1)}, bf16[1024,3072]{1,0:T(8,128)(2,1)}) custom-call(s32[4]{0:T(128)S(1)} %pad_add_fusion.where_ref, bf16[1024,768]{1,0:T(8,128)(2,1)S(1)} %copy-done.8, bf16[768,3072]{1,0:T(8,128)(2,1)S(1)} %bitcast.39, f32[128,768]{1,0:T(8,128)S(1)} %get-tuple-element.186.vec_ref, ...), custom_call_target="tpu_custom_call", output_to_operand_aliasing={{0}: (4, {}), {1}: (5, {})} | custom-call | flops 8000000000 | bytes 24000000 | tf_op jit(solution)/shard_map/up/pallas_call | solution.py:600
  124.7 1.6 collective-permute-start.25
  127.4 9.3 %down.1 = (bf16[512,768]{1,0:T(8,128)(2,1)}, bf16[512,768]{1,0:T(8,128)(2,1)S(1)}, f32[1024,768]{1,0:T(8,128)S(1)}, f32[1024,1]{1,0:T(8,128)S(1)}) custom-call(s32[4]{0:T(128)S(1)} %pad_add_fusion.where_ref, bf16[1024,3072]{1,0:T(8,128)(2,1)} %get-tuple-element.200.act_ref, bf16[3072,768]{1,0:T(8,128)(2,1)S(1)} %bitcast.42, ...), custom_call_target="tpu_custom_call" | custom-call | flops 8000000000 | bytes 24000000 | tf_op jit(solution)/shard_map/down/pallas_call | solution.py:642
  139.5 1.8 contrast.1
  141.3 11.6 %top.1 = (f32[1024,768]{1,0:T(8,128)}, bf16[1024,768]{1,0:T(8,128)(2,1)S(1)}, f32[8,768]{1,0:T(8,128)S(1)}, bf16[3072,384]{1,0:T(8,128)(2,1)S(1)}, bf16[3072,384]{1,0:T(8,128)(2,1)S(1)}) custom-call(s32[4]{0:T(128)S(1)} %pad_add_fusion.where_ref, bf16[1024,768]{1,0:T(8,128)(2,1)S(1)} %pad_maximum_fusion.cot_ref, f32[32,768]{1,0:T(8,128)S(1)} %get-tuple-element.213.cls_ref, ...), custom_call_target="tpu_custom_call" | custom-call | flops 44000002048 | bytes 132000000 | tf_op jit(solution)/shard_map/top/pallas_call | solution.py:808
  153.0 20.7 %gelu_back.1 = (f32[1024,768]{1,0:T(8,128)S(1)}, f32[8,768]{1,0:T(8,128)S(1)}, bf16[768,1536]{1,0:T(8,128)(2,1)S(1)}, bf16[768,1536]{1,0:T(8,128)(2,1)S(1)}) custom-call(s32[4]{0:T(128)S(1)} %pad_add_fusion.where_ref, bf16[1024,768]{1,0:T(8,128)(2,1)S(1)} %get-tuple-element.216.gs_ref, bf16[3072,768]{1,0:T(8,128)(2,1)} %bitcast.43, ...), custom_call_target="tpu_custom_call" | custom-call | flops 80000000000 | bytes 240000000 | tf_op jit(solution)/shard_map/gelu_back/pallas_call | solution.py:869
  176.2 6.6 %hidden_back.1 = (f32[8,768]{1,0:T(8,128)}, bf16[1024,768]{1,0:T(8,128)(2,1)S(1)}, bf16[1024,768]{1,0:T(8,128)(2,1)S(1)}, f32[8,768]{1,0:T(8,128)S(1)}) custom-call(s32[4]{0:T(128)S(1)} %pad_add_fusion.where_ref, f32[1024,768]{1,0:T(8,128)S(1)} %get-tuple-element.221.acc_ref, f32[1024,768]{1,0:T(8,128)} %get-tuple-element.215.second_ref, ...), custom_call_target="tpu_custom_call" | custom-call | flops 20000000000 | bytes 60000000 | tf_op jit(solution)/shard_map/hidden_back/pallas_call | solution.py:914
  185.0 1.3 collective-permute-start.32
  186.3 10.8 %far_back.1 = (bf16[512,1536]{1,0:T(8,128)(2,1)S(1)}, bf16[512,768]{1,0:T(8,128)(2,1)S(1)}, bf16[512,768]{1,0:T(8,128)(2,1)S(1)}) custom-call(s32[4]{0:T(128)S(1)} %pad_add_fusion.where_ref, bf16[1024,768]{1,0:T(8,128)(2,1)S(1)} %get-tuple-element.231.ga_ref, bf16[1024,2304]{1,0:T(8,128)(2,1)} %get-tuple-element.180.proj_ref, ...), custom_call_target="tpu_custom_call" | custom-call | flops 44000002048 | bytes 132000000 | tf_op jit(solution)/shard_map/far_back/pallas_call | solution.py:1145
  197.2 5.5 %attend_back.2.near_ref.first_near_ref.a_ref = bf16[512,1536]{1,0:T(8,128)(2,1)S(1)} custom-call(s32[4]{0:T(128)S(1)} %pad_add_fusion.where_ref, bf16[1024,768]{1,0:T(8,128)(2,1)S(1)} %get-tuple-element.231.ga_ref, bf16[1024,2304]{1,0:T(8,128)(2,1)} %get-tuple-element.180.proj_ref, bf16[8,6,128,256]{3,2,1,0:T(8,128)(2,1)} %get-tuple-element.181.probs_ref), custom_call_target="tpu_custom_call" | custom-call | flops 20000000000 | bytes 60000000 | tf_op jit(solution)/shard_map/attend_back/pallas_call | solution.py:1058
  202.7 5.6 %first_weights.1 = (bf16[768,1152]{1,0:T(8,128)(2,1)S(1)}, bf16[768,1152]{1,0:T(8,128)(2,1)S(1)}) custom-call(s32[4]{0:T(128)S(1)} %pad_add_fusion.where_ref, bf16[512,768]{1,0:T(8,128)(2,1)S(1)} %copy-done.4, bf16[512,768]{1,0:T(8,128)(2,1)S(1)} %copy-done.6, bf16[512,1536]{1,0:T(8,128)(2,1)S(1)} %attend_back.2.near_ref.first_near_ref.a_ref, ...), custom_call_target="tpu_custom_call" | custom-call | flops 20000000000 | bytes 60000000 | tf_op jit(solution)/shard_map/first_weights/pallas_call | solution.py:1113
  210.0 1.6 collective-permute-start.33
  213.0 3.9 %attend_back.3.near_ref.b_ref = bf16[512,768]{1,0:T(8,128)(2,1)S(1)} custom-call(s32[4]{0:T(128)S(1)} %pad_add_fusion.where_ref, bf16[1024,768]{1,0:T(8,128)(2,1)S(1)} %get-tuple-element.231.ga_ref, bf16[1024,2304]{1,0:T(8,128)(2,1)} %get-tuple-element.180.proj_ref, bf16[8,6,128,256]{3,2,1,0:T(8,128)(2,1)} %get-tuple-element.181.probs_ref), custom_call_target="tpu_custom_call" | custom-call | flops 8000000000 | bytes 24000000 | tf_op jit(solution)/shard_map/attend_back/pallas_call | solution.py:1058
  217.0 3.0 %collective-permute-done.33.r_ref = bf16[4,192,384]{2,1,0:T(8,128)(2,1)S(1)} collective-permute-done((bf16[4,192,384]{2,1,0:T(8,128)(2,1)S(1)}, bf16[4,192,384]{2,1,0:T(8,128)(2,1)S(1)}, u32[]{:S(2)}, u32[]{:S(2)}) %collective-permute-start.33) | collective-permute-done | bytes 589856 | tf_op jit(solution)/shard_map/ppermute | solution.py:146
  220.7 1.8 collective-permute-start.39
  224.3 3.0 %collective-permute-done.35.r_ref = bf16[4,48,1536]{2,1,0:T(8,128)(2,1)S(1)} collective-permute-done((bf16[4,48,1536]{2,1,0:T(8,128)(2,1)S(1)}, bf16[4,48,1536]{2,1,0:T(8,128)(2,1)S(1)}, u32[]{:S(2)}, u32[]{:S(2)}) %collective-permute-start.35) | collective-permute-done | bytes 589856 | tf_op jit(solution)/shard_map/ppermute | solution.py:146
  228.0 2.5 collective-permute-start.40
  230.5 2.9 %collective-permute-done.36 = bf16[512,768]{1,0:T(8,128)(2,1)S(1)} collective-permute-done((bf16[512,768]{1,0:T(8,128)(2,1)S(1)}, bf16[512,768]{1,0:T(8,128)(2,1)S(1)}, u32[]{:S(2)}, u32[]{:S(2)}) %collective-permute-start.36) | collective-permute-done | bytes 786464 | tf_op jit(solution)/shard_map/ppermute | solution.py:146
  233.4 2.5 last_weights.1
  236.0 4.4 %token_back.1 = f32[512,768]{1,0:T(8,128)S(1)} custom-call(s32[4]{0:T(128)S(1)} %pad_add_fusion.where_ref, bf16[512,1536]{1,0:T(8,128)(2,1)S(1)} %attend_back.2.near_ref.first_near_ref.a_ref, bf16[512,768]{1,0:T(8,128)(2,1)S(1)} %attend_back.3.near_ref.b_ref, bf16[768,3328]{1,0:T(8,128)(2,1)} %bitcast.36, bf16[1024,768]{1,0:T(8,128)(2,1)} %copy-done.13), custom_call_target="tpu_custom_call" | custom-call | flops 16000000000 | bytes 48000000 | tf_op jit(solution)/shard_map/token_back/pallas_call | solution.py:1165
  241.2 1.6 collective-permute-start.41
  245.1 3.9 %collective-permute-done.40.r_ref = bf16[2,48,1536]{2,1,0:T(8,128)(2,1)S(1)} collective-permute-done((bf16[2,48,1536]{2,1,0:T(8,128)(2,1)S(1)}, bf16[2,48,1536]{2,1,0:T(8,128)(2,1)S(1)}, u32[]{:S(2)}, u32[]{:S(2)}) %collective-permute-start.40) | collective-permute-done | bytes 294944 | tf_op jit(solution)/shard_map/ppermute | solution.py:146
  249.7 3.8 %collective-permute-done.41.r_ref = bf16[4,48,1152]{2,1,0:T(8,128)(2,1)S(1)} collective-permute-done((bf16[4,48,1152]{2,1,0:T(8,128)(2,1)S(1)}, bf16[4,48,1152]{2,1,0:T(8,128)(2,1)S(1)}, u32[]{:S(2)}, u32[]{:S(2)}) %collective-permute-start.41) | collective-permute-done | bytes 442400 | tf_op jit(solution)/shard_map/ppermute | solution.py:146
  257.1 1.6 collective-permute-start.46
  262.1 2.6 collective-permute-done.45.r_ref
  266.0 2.4 collective-permute-start.49
  268.4 1.6 finish.3
  270.1 1.6 finish.4
  271.7 2.2 collective-permute-done.49.r_ref
  274.5 1.9 convert_select_fusion
  277.1 1.5 collective-permute-done.51.got_ref
  280.5 1.8 finish.5
  (178 shorter events, 41.9 us)
Async XLA Ops:
  6.9 16.8 %collective-permute-start.2 = (bf16[1,48,1664]{2,1,0:T(8,128)(2,1)S(1)}, bf16[1,48,1664]{2,1,0:T(8,128)(2,1)S(1)}, u32[]{:S(2)}, u32[]{:S(2)}) collective-permute-start(bf16[1,48,1664]{2,1,0:T(8,128)(2,1)S(1)} %get-tuple-element.159), channel_id=1, source_target_pairs={{0,24},{1,25},{2,26},{3,27},{4,28},{5,29},{6,30},{7,31},{8,16},{9,... | collective-permute-start | bytes 479240 | tf_op jit(solution)/shard_map/ppermute | solution.py:146
  9.4 14.3 %collective-permute-start.1 = (bf16[1,48,1664]{2,1,0:T(8,128)(2,1)S(1)}, bf16[1,48,1664]{2,1,0:T(8,128)(2,1)S(1)}, u32[]{:S(2)}, u32[]{:S(2)}) collective-permute-start(bf16[1,48,1664]{2,1,0:T(8,128)(2,1)S(1)} %get-tuple-element.158), channel_id=1, source_target_pairs={{0,16},{1,17},{2,18},{3,19},{4,20},{5,21},{6,22},{7,23},{8,24},{9,... | collective-permute-start | bytes 479240 | tf_op jit(solution)/shard_map/ppermute | solution.py:146
  9.5 15.8 %collective-permute-start.4 = (bf16[1,48,1536]{2,1,0:T(8,128)(2,1)S(1)}, bf16[1,48,1536]{2,1,0:T(8,128)(2,1)S(1)}, u32[]{:S(2)}, u32[]{:S(2)}) collective-permute-start(bf16[1,48,1536]{2,1,0:T(8,128)(2,1)S(1)} %get-tuple-element.161), channel_id=1, source_target_pairs={{0,8},{1,9},{2,10},{3,11},{4,12},{5,13},{6,14},{7,15},{8,0},{9,1},... | collective-permute-start | bytes 442376 | tf_op jit(solution)/shard_map/ppermute | solution.py:146
  11.3 14.2 %collective-permute-start.6 = (bf16[1,192,384]{2,1,0:T(8,128)(2,1)S(1)}, bf16[1,192,384]{2,1,0:T(8,128)(2,1)S(1)}, u32[]{:S(2)}, u32[]{:S(2)}) collective-permute-start(bf16[1,192,384]{2,1,0:T(8,128)(2,1)S(1)} %get-tuple-element.163), channel_id=1, source_target_pairs={{0,8},{1,9},{2,10},{3,11},{4,12},{5,13},{6,14},{7,15},{8,0},{9,1},... | collective-permute-start | bytes 442376 | tf_op jit(solution)/shard_map/ppermute | solution.py:146
  23.8 16.4 %collective-permute-start.3 = (bf16[4,48,1664]{2,1,0:T(8,128)(2,1)S(1)}, bf16[4,48,1664]{2,1,0:T(8,128)(2,1)S(1)}, u32[]{:S(2)}, u32[]{:S(2)}) collective-permute-start(bf16[4,48,1664]{2,1,0:T(8,128)(2,1)S(1)} %get-tuple-element.339), channel_id=1, source_target_pairs={{0,2},{1,5},{2,0},{3,7},{4,6},{5,1},{6,4},{7,3},{8,10},{9,13},{10,... | collective-permute-start | bytes 1916936 | tf_op jit(solution)/shard_map/ppermute | solution.py:146
  25.4 14.8 %collective-permute-start.5 = (bf16[2,48,1536]{2,1,0:T(8,128)(2,1)S(1)}, bf16[2,48,1536]{2,1,0:T(8,128)(2,1)S(1)}, u32[]{:S(2)}, u32[]{:S(2)}) collective-permute-start(bf16[2,48,1536]{2,1,0:T(8,128)(2,1)S(1)} %pad_maximum_fusion.1), channel_id=1, source_target_pairs={{0,16},{1,17},{2,18},{3,19},{4,20},{5,21},{6,22},{7,23},{8,24},{9,... | collective-permute-start | bytes 884744 | tf_op jit(solution)/shard_map/ppermute | solution.py:146
  40.3 23.6 %collective-permute-start.7 = (bf16[8,48,1664]{2,1,0:T(8,128)(2,1)S(1)}, bf16[8,48,1664]{2,1,0:T(8,128)(2,1)S(1)}, u32[]{:S(2)}, u32[]{:S(2)}) collective-permute-start(bf16[8,48,1664]{2,1,0:T(8,128)(2,1)S(1)} %constant_dynamic-update-slice_fusion.4.refs_0_), channel_id=1, source_target_pairs={{0,4},{1,3},{2,6},{3,1},{4,0},{5,7},{6,2},{7,5},{8,12},{9,11},{10,... | collective-permute-start | bytes 3833864 | tf_op jit(solution)/shard_map/ppermute | solution.py:146
  40.9 23.2 %collective-permute-start.10 = (bf16[4,48,1536]{2,1,0:T(8,128)(2,1)S(1)}, bf16[4,48,1536]{2,1,0:T(8,128)(2,1)S(1)}, u32[]{:S(2)}, u32[]{:S(2)}) collective-permute-start(bf16[4,48,1536]{2,1,0:T(8,128)(2,1)S(1)} %get-tuple-element.336), channel_id=1, source_target_pairs={{0,2},{1,5},{2,0},{3,7},{4,6},{5,1},{6,4},{7,3},{8,10},{9,13},{10,... | collective-permute-start | bytes 1769480 | tf_op jit(solution)/shard_map/ppermute | solution.py:146
  42.4 21.6 %collective-permute-start.11 = (bf16[2,192,384]{2,1,0:T(8,128)(2,1)S(1)}, bf16[2,192,384]{2,1,0:T(8,128)(2,1)S(1)}, u32[]{:S(2)}, u32[]{:S(2)}) collective-permute-start(bf16[2,192,384]{2,1,0:T(8,128)(2,1)S(1)} %constant_dynamic-update-slice_fusion.11), channel_id=1, source_target_pairs={{0,16},{1,17},{2,18},{3,19},{4,20},{5,21},{6,22},{7,23},{8,24},{9,... | collective-permute-start | bytes 884744 | tf_op jit(solution)/shard_map/ppermute | solution.py:146
  42.4 38.2 %collective-permute-start.8 = (bf16[8,48,1664]{2,1,0:T(8,128)(2,1)S(1)}, bf16[8,48,1664]{2,1,0:T(8,128)(2,1)S(1)}, u32[]{:S(2)}, u32[]{:S(2)}) collective-permute-start(bf16[8,48,1664]{2,1,0:T(8,128)(2,1)S(1)} %constant_dynamic-update-slice_fusion.4.refs_0_), channel_id=1, source_target_pairs={{0,1},{1,0},{2,3},{3,2},{4,5},{5,4},{6,7},{7,6},{8,9},{9,8},{10,11... | collective-permute-start | bytes 3833864 | tf_op jit(solution)/shard_map/ppermute | solution.py:146
  64.0 16.6 %collective-permute-start.9 = (bf16[8,48,1664]{2,1,0:T(8,128)(2,1)S(1)}, bf16[8,48,1664]{2,1,0:T(8,128)(2,1)S(1)}, u32[]{:S(2)}, u32[]{:S(2)}) collective-permute-start(bf16[8,48,1664]{2,1,0:T(8,128)(2,1)S(1)} %collective-permute-done.7.refs_1_), channel_id=1, source_target_pairs={{0,1},{1,0},{2,3},{3,2},{4,5},{5,4},{6,7},{7,6},{8,9},{9,8},{10,11... | collective-permute-start | bytes 3833864 | tf_op jit(solution)/shard_map/ppermute | solution.py:146
  64.1 16.3 %collective-permute-start.16 = (bf16[4,192,384]{2,1,0:T(8,128)(2,1)S(1)}, bf16[4,192,384]{2,1,0:T(8,128)(2,1)S(1)}, u32[]{:S(2)}, u32[]{:S(2)}) collective-permute-start(bf16[4,192,384]{2,1,0:T(8,128)(2,1)S(1)} %constant_dynamic-update-slice_fusion.16), channel_id=1, source_target_pairs={{0,2},{1,5},{2,0},{3,7},{4,6},{5,1},{6,4},{7,3},{8,10},{9,13},{10,... | collective-permute-start | bytes 1769480 | tf_op jit(solution)/shard_map/ppermute | solution.py:146
  65.0 25.1 %collective-permute-start.13 = (bf16[8,48,1536]{2,1,0:T(8,128)(2,1)S(1)}, bf16[8,48,1536]{2,1,0:T(8,128)(2,1)S(1)}, u32[]{:S(2)}, u32[]{:S(2)}) collective-permute-start(bf16[8,48,1536]{2,1,0:T(8,128)(2,1)S(1)} %constant_dynamic-update-slice_fusion.13.refs_0_), channel_id=1, source_target_pairs={{0,4},{1,3},{2,6},{3,1},{4,0},{5,7},{6,2},{7,5},{8,12},{9,11},{10,... | collective-permute-start | bytes 3538952 | tf_op jit(solution)/shard_map/ppermute | solution.py:146
  65.7 25.0 %collective-permute-start.12 = (bf16[512,768]{1,0:T(8,128)(2,1)S(1)}, bf16[512,768]{1,0:T(8,128)(2,1)S(1)}, u32[]{:S(2)}, u32[]{:S(2)}) collective-permute-start(bf16[512,768]{1,0:T(8,128)(2,1)S(1)} %get-tuple-element.179), channel_id=1, source_target_pairs={{0,8},{1,9},{2,10},{3,11},{4,12},{5,13},{6,14},{7,15},{8,0},{9,1},... | collective-permute-start | bytes 2359304 | tf_op jit(solution)/shard_map/ppermute | solution.py:146
  80.5 18.4 %collective-permute-start.17 = (bf16[8,192,384]{2,1,0:T(8,128)(2,1)S(1)}, bf16[8,192,384]{2,1,0:T(8,128)(2,1)S(1)}, u32[]{:S(2)}, u32[]{:S(2)}) collective-permute-start(bf16[8,192,384]{2,1,0:T(8,128)(2,1)S(1)} %constant_dynamic-update-slice_fusion.18.refs_0_), channel_id=1, source_target_pairs={{0,4},{1,3},{2,6},{3,1},{4,0},{5,7},{6,2},{7,5},{8,12},{9,11},{10,... | collective-permute-start | bytes 3538952 | tf_op jit(solution)/shard_map/ppermute | solution.py:146
  90.1 9.6 %collective-permute-start.15 = (bf16[8,48,1536]{2,1,0:T(8,128)(2,1)S(1)}, bf16[8,48,1536]{2,1,0:T(8,128)(2,1)S(1)}, u32[]{:S(2)}, u32[]{:S(2)}) collective-permute-start(bf16[8,48,1536]{2,1,0:T(8,128)(2,1)S(1)} %collective-permute-done.13.refs_1_), channel_id=1, source_target_pairs={{0,1},{1,0},{2,3},{3,2},{4,5},{5,4},{6,7},{7,6},{8,9},{9,8},{10,11... | collective-permute-start | bytes 3538952 | tf_op jit(solution)/shard_map/ppermute | solution.py:146
  90.2 9.6 %collective-permute-start.14 = (bf16[8,48,1536]{2,1,0:T(8,128)(2,1)S(1)}, bf16[8,48,1536]{2,1,0:T(8,128)(2,1)S(1)}, u32[]{:S(2)}, u32[]{:S(2)}) collective-permute-start(bf16[8,48,1536]{2,1,0:T(8,128)(2,1)S(1)} %constant_dynamic-update-slice_fusion.13.refs_0_), channel_id=1, source_target_pairs={{0,1},{1,0},{2,3},{3,2},{4,5},{5,4},{6,7},{7,6},{8,9},{9,8},{10,11... | collective-permute-start | bytes 3538952 | tf_op jit(solution)/shard_map/ppermute | solution.py:146
  98.9 8.9 %collective-permute-start.19 = (bf16[8,192,384]{2,1,0:T(8,128)(2,1)S(1)}, bf16[8,192,384]{2,1,0:T(8,128)(2,1)S(1)}, u32[]{:S(2)}, u32[]{:S(2)}) collective-permute-start(bf16[8,192,384]{2,1,0:T(8,128)(2,1)S(1)} %collective-permute-done.17.refs_1_), channel_id=1, source_target_pairs={{0,1},{1,0},{2,3},{3,2},{4,5},{5,4},{6,7},{7,6},{8,9},{9,8},{10,11... | collective-permute-start | bytes 3538952 | tf_op jit(solution)/shard_map/ppermute | solution.py:146
  99.0 8.8 %collective-permute-start.18 = (bf16[8,192,384]{2,1,0:T(8,128)(2,1)S(1)}, bf16[8,192,384]{2,1,0:T(8,128)(2,1)S(1)}, u32[]{:S(2)}, u32[]{:S(2)}) collective-permute-start(bf16[8,192,384]{2,1,0:T(8,128)(2,1)S(1)} %constant_dynamic-update-slice_fusion.18.refs_0_), channel_id=1, source_target_pairs={{0,1},{1,0},{2,3},{3,2},{4,5},{5,4},{6,7},{7,6},{8,9},{9,8},{10,11... | collective-permute-start | bytes 3538952 | tf_op jit(solution)/shard_map/ppermute | solution.py:146
  99.6 37.7 %collective-permute-start.27 = (bf16[512,768]{1,0:T(8,128)(2,1)S(1)}, bf16[512,768]{1,0:T(8,128)(2,1)S(1)}, u32[]{:S(2)}, u32[]{:S(2)}) collective-permute-start(bf16[512,768]{1,0:T(8,128)(2,1)S(1)} %get-tuple-element.210), channel_id=1, source_target_pairs={{0,8},{1,9},{2,10},{3,11},{4,12},{5,13},{6,14},{7,15},{8,0},{9,1},... | collective-permute-start | bytes 2359304 | tf_op jit(solution)/shard_map/ppermute | solution.py:146
  111.5 11.6 %collective-permute-start.20 = (bf16[32,896]{1,0:T(8,128)(2,1)S(1)}, bf16[32,896]{1,0:T(8,128)(2,1)S(1)}, u32[]{:S(2)}, u32[]{:S(2)}) collective-permute-start(bf16[32,896]{1,0:T(8,128)(2,1)S(1)} %first_rows.1.refs_0_), channel_id=1, source_target_pairs={{0,8},{1,9},{2,10},{3,11},{4,12},{5,13},{6,14},{7,15},{8,0},{9,1},... | collective-permute-start | bytes 172040 | tf_op jit(solution)/shard_map/ppermute | solution.py:146
  113.2 9.9 %collective-permute-start.21 = (bf16[32,896]{1,0:T(8,128)(2,1)S(1)}, bf16[32,896]{1,0:T(8,128)(2,1)S(1)}, u32[]{:S(2)}, u32[]{:S(2)}) collective-permute-start(bf16[32,896]{1,0:T(8,128)(2,1)S(1)} %first_rows.1.refs_0_), channel_id=1, source_target_pairs={{0,16},{1,17},{2,18},{3,19},{4,20},{5,21},{6,22},{7,23},{8,24},{9,... | collective-permute-start | bytes 172040 | tf_op jit(solution)/shard_map/ppermute | solution.py:146
  113.4 9.7 %collective-permute-start.22 = (bf16[32,896]{1,0:T(8,128)(2,1)S(1)}, bf16[32,896]{1,0:T(8,128)(2,1)S(1)}, u32[]{:S(2)}, u32[]{:S(2)}) collective-permute-start(bf16[32,896]{1,0:T(8,128)(2,1)S(1)} %first_rows.1.refs_0_), channel_id=1, source_target_pairs={{0,24},{1,25},{2,26},{3,27},{4,28},{5,29},{6,30},{7,31},{8,16},{9,... | collective-permute-start | bytes 172040 | tf_op jit(solution)/shard_map/ppermute | solution.py:146
  123.9 12.8 %collective-permute-start.24 = (bf16[2,48,896]{2,1,0:T(8,128)(2,1)S(1)}, bf16[2,48,896]{2,1,0:T(8,128)(2,1)S(1)}, u32[]{:S(2)}, u32[]{:S(2)}) collective-permute-start(bf16[2,48,896]{2,1,0:T(8,128)(2,1)S(1)} %pack.1.refs_0_), channel_id=1, source_target_pairs={{0,2},{1,3},{2,0},{3,1},{4,6},{5,7},{6,4},{7,5},{8,10},{9,11},{10,... | collective-permute-start | bytes 516104 | tf_op jit(solution)/shard_map/ppermute | solution.py:146
  124.7 12.0 %collective-permute-start.25 = (bf16[2,48,896]{2,1,0:T(8,128)(2,1)S(1)}, bf16[2,48,896]{2,1,0:T(8,128)(2,1)S(1)}, u32[]{:S(2)}, u32[]{:S(2)}) collective-permute-start(bf16[2,48,896]{2,1,0:T(8,128)(2,1)S(1)} %pack.1.refs_0_), channel_id=1, source_target_pairs={{0,4},{1,5},{2,6},{3,7},{4,0},{5,1},{6,2},{7,3},{8,12},{9,13},{10,... | collective-permute-start | bytes 516104 | tf_op jit(solution)/shard_map/ppermute | solution.py:146
  126.2 10.4 %collective-permute-start.26 = (bf16[2,48,896]{2,1,0:T(8,128)(2,1)S(1)}, bf16[2,48,896]{2,1,0:T(8,128)(2,1)S(1)}, u32[]{:S(2)}, u32[]{:S(2)}) collective-permute-start(bf16[2,48,896]{2,1,0:T(8,128)(2,1)S(1)} %pack.1.refs_0_), channel_id=1, source_target_pairs={{0,6},{1,7},{2,4},{3,5},{4,2},{5,3},{6,0},{7,1},{8,14},{9,15},{10,... | collective-permute-start | bytes 516104 | tf_op jit(solution)/shard_map/ppermute | solution.py:146
  137.5 36.3 %collective-permute-start.23 = (bf16[512,768]{1,0:T(8,128)(2,1)S(1)}, bf16[512,768]{1,0:T(8,128)(2,1)S(1)}, u32[]{:S(2)}, u32[]{:S(2)}) collective-permute-start(bf16[512,768]{1,0:T(8,128)(2,1)S(1)} %get-tuple-element.205), channel_id=1, source_target_pairs={{0,8},{1,9},{2,10},{3,11},{4,12},{5,13},{6,14},{7,15},{8,0},{9,1},... | collective-permute-start | bytes 2359304 | tf_op jit(solution)/shard_map/ppermute | solution.py:146
  152.9 21.3 %collective-permute-start.29 = (bf16[16,192,384]{2,1,0:T(8,128)(2,1)S(1)}, bf16[16,192,384]{2,1,0:T(8,128)(2,1)S(1)}, u32[]{:S(2)}, u32[]{:S(2)}) collective-permute-start(bf16[16,192,384]{2,1,0:T(8,128)(2,1)S(1)} %bitcast.45), channel_id=1, source_target_pairs={{0,1},{1,0},{2,3},{3,2},{4,5},{5,4},{6,7},{7,6},{8,9},{9,8},{10,11... | collective-permute-start | bytes 7077896 | tf_op jit(solution)/shard_map/ppermute | solution.py:146
  173.8 10.2 %collective-permute-start.30 = (bf16[16,48,1536]{2,1,0:T(8,128)(2,1)S(1)}, bf16[16,48,1536]{2,1,0:T(8,128)(2,1)S(1)}, u32[]{:S(2)}, u32[]{:S(2)}) collective-permute-start(bf16[16,48,1536]{2,1,0:T(8,128)(2,1)S(1)} %bitcast.44), channel_id=1, source_target_pairs={{0,1},{1,0},{2,3},{3,2},{4,5},{5,4},{6,7},{7,6},{8,9},{9,8},{10,11... | collective-permute-start | bytes 7077896 | tf_op jit(solution)/shard_map/ppermute | solution.py:146
  175.4 33.8 %collective-permute-start.31 = (bf16[8,192,384]{2,1,0:T(8,128)(2,1)S(1)}, bf16[8,192,384]{2,1,0:T(8,128)(2,1)S(1)}, u32[]{:S(2)}, u32[]{:S(2)}) collective-permute-start(bf16[8,192,384]{2,1,0:T(8,128)(2,1)S(1)} %get-tuple-element.227), channel_id=1, source_target_pairs={{0,2},{1,5},{2,0},{3,7},{4,6},{5,1},{6,4},{7,3},{8,10},{9,13},{10,... | collective-permute-start | bytes 3538952 | tf_op jit(solution)/shard_map/ppermute | solution.py:146
  185.0 26.6 %collective-permute-start.32 = (bf16[8,48,1536]{2,1,0:T(8,128)(2,1)S(1)}, bf16[8,48,1536]{2,1,0:T(8,128)(2,1)S(1)}, u32[]{:S(2)}, u32[]{:S(2)}) collective-permute-start(bf16[8,48,1536]{2,1,0:T(8,128)(2,1)S(1)} %get-tuple-element.234), channel_id=1, source_target_pairs={{0,2},{1,5},{2,0},{3,7},{4,6},{5,1},{6,4},{7,3},{8,10},{9,13},{10,... | collective-permute-start | bytes 3538952 | tf_op jit(solution)/shard_map/ppermute | solution.py:146
  208.3 14.2 %collective-permute-start.34 = (bf16[16,48,1152]{2,1,0:T(8,128)(2,1)S(1)}, bf16[16,48,1152]{2,1,0:T(8,128)(2,1)S(1)}, u32[]{:S(2)}, u32[]{:S(2)}) collective-permute-start(bf16[16,48,1152]{2,1,0:T(8,128)(2,1)S(1)} %bitcast.46), channel_id=1, source_target_pairs={{0,1},{1,0},{2,3},{3,2},{4,5},{5,4},{6,7},{7,6},{8,9},{9,8},{10,11... | collective-permute-start | bytes 5308424 | tf_op jit(solution)/shard_map/ppermute | solution.py:146
  208.4 25.0 %collective-permute-start.36 = (bf16[512,768]{1,0:T(8,128)(2,1)S(1)}, bf16[512,768]{1,0:T(8,128)(2,1)S(1)}, u32[]{:S(2)}, u32[]{:S(2)}) collective-permute-start(bf16[512,768]{1,0:T(8,128)(2,1)S(1)} %get-tuple-element.239), channel_id=1, source_target_pairs={{0,8},{1,9},{2,10},{3,11},{4,12},{5,13},{6,14},{7,15},{8,0},{9,1},... | collective-permute-start | bytes 2359304 | tf_op jit(solution)/shard_map/ppermute | solution.py:146
  210.0 9.9 %collective-permute-start.33 = (bf16[4,192,384]{2,1,0:T(8,128)(2,1)S(1)}, bf16[4,192,384]{2,1,0:T(8,128)(2,1)S(1)}, u32[]{:S(2)}, u32[]{:S(2)}) collective-permute-start(bf16[4,192,384]{2,1,0:T(8,128)(2,1)S(1)} %get-tuple-element.245), channel_id=1, source_target_pairs={{0,4},{1,3},{2,6},{3,1},{4,0},{5,7},{6,2},{7,5},{8,12},{9,11},{10,... | collective-permute-start | bytes 1769480 | tf_op jit(solution)/shard_map/ppermute | solution.py:146
  212.4 14.9 %collective-permute-start.35 = (bf16[4,48,1536]{2,1,0:T(8,128)(2,1)S(1)}, bf16[4,48,1536]{2,1,0:T(8,128)(2,1)S(1)}, u32[]{:S(2)}, u32[]{:S(2)}) collective-permute-start(bf16[4,48,1536]{2,1,0:T(8,128)(2,1)S(1)} %get-tuple-element.248), channel_id=1, source_target_pairs={{0,4},{1,3},{2,6},{3,1},{4,0},{5,7},{6,2},{7,5},{8,12},{9,11},{10,... | collective-permute-start | bytes 1769480 | tf_op jit(solution)/shard_map/ppermute | solution.py:146
  220.7 23.7 %collective-permute-start.39 = (bf16[2,192,384]{2,1,0:T(8,128)(2,1)S(1)}, bf16[2,192,384]{2,1,0:T(8,128)(2,1)S(1)}, u32[]{:S(2)}, u32[]{:S(2)}) collective-permute-start(bf16[2,192,384]{2,1,0:T(8,128)(2,1)S(1)} %get-tuple-element.252), channel_id=1, source_target_pairs={{0,16},{1,17},{2,18},{3,19},{4,20},{5,21},{6,22},{7,23},{8,24},{9,... | collective-permute-start | bytes 884744 | tf_op jit(solution)/shard_map/ppermute | solution.py:146
  223.5 16.9 %collective-permute-start.37 = (bf16[8,48,1152]{2,1,0:T(8,128)(2,1)S(1)}, bf16[8,48,1152]{2,1,0:T(8,128)(2,1)S(1)}, u32[]{:S(2)}, u32[]{:S(2)}) collective-permute-start(bf16[8,48,1152]{2,1,0:T(8,128)(2,1)S(1)} %get-tuple-element.255), channel_id=1, source_target_pairs={{0,2},{1,5},{2,0},{3,7},{4,6},{5,1},{6,4},{7,3},{8,10},{9,13},{10,... | collective-permute-start | bytes 2654216 | tf_op jit(solution)/shard_map/ppermute | solution.py:146
  228.0 20.9 %collective-permute-start.40 = (bf16[2,48,1536]{2,1,0:T(8,128)(2,1)S(1)}, bf16[2,48,1536]{2,1,0:T(8,128)(2,1)S(1)}, u32[]{:S(2)}, u32[]{:S(2)}) collective-permute-start(bf16[2,48,1536]{2,1,0:T(8,128)(2,1)S(1)} %get-tuple-element.258), channel_id=1, source_target_pairs={{0,16},{1,17},{2,18},{3,19},{4,20},{5,21},{6,22},{7,23},{8,24},{9,... | collective-permute-start | bytes 884744 | tf_op jit(solution)/shard_map/ppermute | solution.py:146
  241.2 12.3 %collective-permute-start.41 = (bf16[4,48,1152]{2,1,0:T(8,128)(2,1)S(1)}, bf16[4,48,1152]{2,1,0:T(8,128)(2,1)S(1)}, u32[]{:S(2)}, u32[]{:S(2)}) collective-permute-start(bf16[4,48,1152]{2,1,0:T(8,128)(2,1)S(1)} %get-tuple-element.266), channel_id=1, source_target_pairs={{0,4},{1,3},{2,6},{3,1},{4,0},{5,7},{6,2},{7,5},{8,12},{9,11},{10,... | collective-permute-start | bytes 1327112 | tf_op jit(solution)/shard_map/ppermute | solution.py:146
  243.5 11.6 %collective-permute-start.42 = (bf16[8,48,512]{2,1,0:T(8,128)(2,1)S(1)}, bf16[8,48,512]{2,1,0:T(8,128)(2,1)S(1)}, u32[]{:S(2)}, u32[]{:S(2)}) collective-permute-start(bf16[8,48,512]{2,1,0:T(8,128)(2,1)S(1)} %get-tuple-element.269), channel_id=1, source_target_pairs={{0,2},{1,5},{2,0},{3,7},{4,6},{5,1},{6,4},{7,3},{8,10},{9,13},{10,... | collective-permute-start | bytes 1179656 | tf_op jit(solution)/shard_map/ppermute | solution.py:146
  245.0 11.4 %collective-permute-start.43 = (bf16[1,192,384]{2,1,0:T(8,128)(2,1)S(1)}, bf16[1,192,384]{2,1,0:T(8,128)(2,1)S(1)}, u32[]{:S(2)}, u32[]{:S(2)}) collective-permute-start(bf16[1,192,384]{2,1,0:T(8,128)(2,1)S(1)} %get-tuple-element.272), channel_id=1, source_target_pairs={{0,8},{1,9},{2,10},{3,11},{4,12},{5,13},{6,14},{7,15},{8,0},{9,1},... | collective-permute-start | bytes 442376 | tf_op jit(solution)/shard_map/ppermute | solution.py:146
  249.6 11.0 %collective-permute-start.44 = (bf16[1,48,1536]{2,1,0:T(8,128)(2,1)S(1)}, bf16[1,48,1536]{2,1,0:T(8,128)(2,1)S(1)}, u32[]{:S(2)}, u32[]{:S(2)}) collective-permute-start(bf16[1,48,1536]{2,1,0:T(8,128)(2,1)S(1)} %get-tuple-element.275), channel_id=1, source_target_pairs={{0,8},{1,9},{2,10},{3,11},{4,12},{5,13},{6,14},{7,15},{8,0},{9,1},... | collective-permute-start | bytes 442376 | tf_op jit(solution)/shard_map/ppermute | solution.py:146
  254.1 10.6 %collective-permute-start.45 = (bf16[2,48,1152]{2,1,0:T(8,128)(2,1)S(1)}, bf16[2,48,1152]{2,1,0:T(8,128)(2,1)S(1)}, u32[]{:S(2)}, u32[]{:S(2)}) collective-permute-start(bf16[2,48,1152]{2,1,0:T(8,128)(2,1)S(1)} %get-tuple-element.278), channel_id=1, source_target_pairs={{0,16},{1,17},{2,18},{3,19},{4,20},{5,21},{6,22},{7,23},{8,24},{9,... | collective-permute-start | bytes 663560 | tf_op jit(solution)/shard_map/ppermute | solution.py:146
  257.0 11.4 %collective-permute-start.47 = (bf16[2,192,384]{2,1,0:T(8,128)(2,1)S(1)}, bf16[2,192,384]{2,1,0:T(8,128)(2,1)S(1)}, u32[]{:S(2)}, u32[]{:S(2)}) collective-permute-start(bf16[2,192,384]{2,1,0:T(8,128)(2,1)S(1)} %add_last.4.refs_0_), channel_id=1, source_target_pairs={{0,1},{1,0},{2,3},{3,2},{4,5},{5,4},{6,7},{7,6},{8,9},{9,8},{10,11... | collective-permute-start | bytes 884744 | tf_op jit(solution)/shard_map/ppermute | solution.py:146
  257.1 8.3 %collective-permute-start.46 = (bf16[4,48,512]{2,1,0:T(8,128)(2,1)S(1)}, bf16[4,48,512]{2,1,0:T(8,128)(2,1)S(1)}, u32[]{:S(2)}, u32[]{:S(2)}) collective-permute-start(bf16[4,48,512]{2,1,0:T(8,128)(2,1)S(1)} %get-tuple-element.281), channel_id=1, source_target_pairs={{0,4},{1,3},{2,6},{3,1},{4,0},{5,7},{6,2},{7,5},{8,12},{9,11},{10,... | collective-permute-start | bytes 589832 | tf_op jit(solution)/shard_map/ppermute | solution.py:146
  262.1 8.0 %collective-permute-start.48 = (bf16[2,48,1536]{2,1,0:T(8,128)(2,1)S(1)}, bf16[2,48,1536]{2,1,0:T(8,128)(2,1)S(1)}, u32[]{:S(2)}, u32[]{:S(2)}) collective-permute-start(bf16[2,48,1536]{2,1,0:T(8,128)(2,1)S(1)} %add_last.5.refs_0_), channel_id=1, source_target_pairs={{0,1},{1,0},{2,3},{3,2},{4,5},{5,4},{6,7},{7,6},{8,9},{9,8},{10,11... | collective-permute-start | bytes 884744 | tf_op jit(solution)/shard_map/ppermute | solution.py:146
  265.3 11.1 %collective-permute-start.50 = (bf16[1,48,1152]{2,1,0:T(8,128)(2,1)S(1)}, bf16[1,48,1152]{2,1,0:T(8,128)(2,1)S(1)}, u32[]{:S(2)}, u32[]{:S(2)}) collective-permute-start(bf16[1,48,1152]{2,1,0:T(8,128)(2,1)S(1)} %get-tuple-element.286), channel_id=1, source_target_pairs={{0,8},{1,9},{2,10},{3,11},{4,12},{5,13},{6,14},{7,15},{8,0},{9,1},... | collective-permute-start | bytes 331784 | tf_op jit(solution)/shard_map/ppermute | solution.py:146
  266.0 7.8 %collective-permute-start.49 = (bf16[2,48,512]{2,1,0:T(8,128)(2,1)S(1)}, bf16[2,48,512]{2,1,0:T(8,128)(2,1)S(1)}, u32[]{:S(2)}, u32[]{:S(2)}) collective-permute-start(bf16[2,48,512]{2,1,0:T(8,128)(2,1)S(1)} %get-tuple-element.289), channel_id=1, source_target_pairs={{0,16},{1,17},{2,18},{3,19},{4,20},{5,21},{6,22},{7,23},{8,24},{9,... | collective-permute-start | bytes 294920 | tf_op jit(solution)/shard_map/ppermute | solution.py:146
  (30 other events, 201.5 us)

commit v5 on v3

v5 whole, which is shorter than its diff:
```python
from functools import partial
import jax
import jax.numpy as jnp
from jax import lax
from jax.experimental import pallas as pl
from jax.experimental.pallas import tpu as pltpu
from jax.sharding import PartitionSpec as P
AXES = ('dp', 'rep')
BF = jnp.bfloat16
F32 = jnp.float32
D = 768
FF = 3072
HEADS = 12
HEAD = 64
PAIRS = HEADS // 2
BLOCK = 128
TILE = 256
EPS = 1e-05
LOSS_WEIGHT = 32.0
MIB = 2 ** 20
AT_OUT = 3 * D
AT_VEC = 4 * D


def smem():
    return pl.BlockSpec(memory_space=pltpu.SMEM)


def vmem():
    return pl.BlockSpec(memory_space=pltpu.VMEM)


def cost(us):
    return pl.CostEstimate(flops=int(us * 1000000000.0), transcendentals=0, bytes_accessed=int(us * 3000000.0))


def behind(us):
    return cost(4.0 * us)


def params(mib):
    return pltpu.CompilerParams(vmem_limit_bytes=int(mib) * MIB)


def still(shape, at=None):
    index = at if at is not None else (0,) * len(shape)
    return pl.BlockSpec(shape, lambda i, *_: index, pipeline_mode=pl.Buffered(1))


def rows_at(width, rows=TILE):
    return pl.BlockSpec((rows, width), lambda i, *_: (i, 0))


def shape(dims, dtype):
    return jax.ShapeDtypeStruct(dims, dtype)


def far(dims, dtype):
    return pltpu.HBM(dims, dtype)


def stay(v):
    return pltpu.with_memory_space_constraint(v, pltpu.HBM)


def after(v, *others):
    return lax.optimization_barrier((v,) + others)[0]


class Order:
    def __init__(self, where):
        self.where = where

    def done(self, out):
        self.where = after(self.where, out)
        return out


def in_vmem(kernel, name, us, outs, *args, mib=24):
    return pl.pallas_call(kernel, out_shape=tuple((shape(*o) for o in outs)), in_specs=[smem() if a.ndim == 1 else vmem() for a in args], out_specs=tuple((vmem() for _ in outs)), compiler_params=params(mib), name=name, cost_estimate=cost(us))(*args)


def wide(width, reps):
    unit = 128 * reps
    return -(-width // unit) * unit


def by_core(core, reps, width, move):
    if width % 128 == 0:
        move(pl.ds(pl.multiple_of(core * width, 128), width))
        return
    for c in range(reps):

        @pl.when(core == c)
        def one(c=c):
            move(slice(c * width, (c + 1) * width))


def halves(refs, core, source):
    width = refs[0].shape[1]
    for q, ref in enumerate(refs):

        def move(lanes, ref=ref):
            ref[...] = source[:, lanes]
        by_core(core ^ q, len(refs), width, move)


def send(v, pairs):
    return lax.ppermute(v, AXES, pairs)


class Plan:
    def __init__(self, n, reps):
        self.n, self.reps, self.depth = (n, reps, n // 4)

    def pairs(self, move):
        return [(d * self.reps + r, (d ^ move(r)[0]) * self.reps + (r ^ move(r)[1])) for d in range(self.n) for r in range(self.reps)]

    def along(self, k):
        return self.pairs(lambda r: (4 * k, 0))

    def first(self):
        return self.pairs(lambda r: (1 + r % 2, 0))

    def second(self):
        return self.pairs(lambda r: (2 - r % 2, 0))

    def sibling(self, q):
        return self.pairs(lambda r: (0, q))


def assemble_kernel(depth, reps, width, where_ref, *refs):
    bufs, out = (refs[:2 * reps], refs[2 * reps])
    me, core = (where_ref[0], where_ref[1])
    for q in range(reps):
        owner = core ^ q
        p1 = 1 + owner % 2
        p2 = 2 - owner % 2

        def move(lanes, q=q, p1=p1, p2=p2):
            for b in range(2):
                for f in range(2):
                    for k in range(depth):
                        dst = me ^ b * p2 ^ f * p1 ^ 4 * k
                        out[pl.ds(dst, 1), :, lanes] = bufs[q * 2 + b][pl.ds(f * depth + k, 1)]
        by_core(owner, reps, width, move)


def shards_kernel(reps, where_ref, qkv_ref, out_ref, bias_ref, gain_ref, up_ref, down_ref, *rest):
    outs, full_ref = (rest[:-1], rest[-1])
    core, tower = (where_ref[1], where_ref[2])
    spare = full_ref.shape[2] - AT_VEC

    def turned(ref, t, at):
        rows = ref[t][0].astype(F32)
        i = lax.broadcasted_iota(jnp.int32, (rows.shape[0], spare), 0)
        j = lax.broadcasted_iota(jnp.int32, (rows.shape[0], spare), 1)
        return t_dot(rows.astype(BF), jnp.where(i + at == j, 1.0, 0.0).astype(BF))
    for n in range(2):
        t = pl.ds(tower if n == 0 else 1 - tower, 1)
        full_ref[:, :, :AT_OUT] = qkv_ref[t]
        full_ref[:, :, AT_OUT:AT_VEC] = out_ref[t]
        full_ref[0, :, AT_VEC:] = (turned(bias_ref, t, 0) + turned(gain_ref, t, bias_ref.shape[1])).astype(BF)
        for c, ref in enumerate((full_ref, up_ref, down_ref)):
            put = outs[2 * c + n]

            def move(lanes, ref=ref, put=put, t=t):
                put[...] = ref[:, :, lanes] if ref is full_ref else ref[t, :, lanes]
            by_core(core, reps, put.shape[2], move)


def shards_of(plan, order, w_qkv, w_out, biases, gains, w_up, w_down):
    reps = plan.reps
    one = wide(AT_VEC + 128, reps)
    outs = []
    for rows, width in ((w_qkv.shape[1], one), (w_up.shape[1], FF), (w_down.shape[1], D)):
        outs += [shape((1, rows, width // reps), BF)] * 2
    args = (w_qkv, w_out, biases, gains, w_up, w_down)
    got = pl.pallas_call(partial(shards_kernel, reps), grid=(1,), out_shape=tuple(outs), in_specs=[smem()] + [still(a.shape) for a in args], out_specs=[still(o.shape) for o in outs], scratch_shapes=[pltpu.VMEM((1, w_qkv.shape[1], one), BF)], compiler_params=params(24), name='shards', cost_estimate=cost(2))(order.where, *[stay(a) for a in args])
    return order.done(got)


def join_kernel(where_ref, *refs):
    ins, out_ref = (refs[:-1], refs[-1])
    at = 0
    for ref in ins:
        out_ref[at:at + ref.shape[0]] = ref[...]
        at += ref.shape[0]


def join(order, *bufs):
    total = sum((b.shape[0] for b in bufs))
    outs = (((total,) + bufs[0].shape[1:], bufs[0].dtype),)
    return order.done(in_vmem(join_kernel, 'join', 0.5, outs, order.where, *bufs))[0]


def gather_line(plan, mine, other):
    got = [send(other if k % 2 else mine, plan.along(k)) for k in range(1, plan.depth)]
    return jnp.concatenate([mine] + got, 0)


def gather_steps(plan, both, *others):
    z = both
    k = 2
    while k < plan.depth:
        if others:
            z, others = (after(z, *others), ())
        z = jnp.concatenate([z, send(z, plan.along(k))], 0)
        k *= 2
    return z


def gather_plane(plan, z, *others):
    near = jnp.concatenate([z, send(z, plan.first())], 0)
    if others:
        near = after(near, *others)
    return (near, send(near, plan.second()))


def gather_cores(plan, order, bufs):
    rows, width = bufs[0].shape[1:]
    bufs = list(bufs)
    for q in range(1, plan.reps):
        bufs += [send(b, plan.sibling(q)) for b in bufs[:2]]
    full = pl.pallas_call(partial(assemble_kernel, plan.depth, plan.reps, width), out_shape=jax.ShapeDtypeStruct((plan.n, rows, width * plan.reps), BF), in_specs=[smem()] + [vmem()] * len(bufs), out_specs=vmem(), compiler_params=params(24), name='assemble', cost_estimate=cost(2))(order.where, *bufs)
    order.done(full)
    return full.reshape(plan.n * rows, width * plan.reps)


def add_kernel(depth, where_ref, a_ref, b_ref, s_ref, k_ref):
    me, core = (where_ref[0], where_ref[1])
    p1 = 1 + core % 2
    p2 = 2 - core % 2
    for j in range(4 * depth):
        at = me ^ (1 - j // (2 * depth)) * p1 ^ (1 - j // depth % 2) * p2 ^ 4 * (j % depth)
        o_ref, to = (s_ref, j) if j < 2 * depth else (k_ref, j - 2 * depth)
        o_ref[to] = (a_ref[at].astype(F32) + b_ref[at].astype(F32)).astype(BF)


def two_kernel(where_ref, k_ref, r_ref, s_ref, o_ref):
    q = s_ref.shape[0]
    for j in range(2 * q):
        total = (k_ref[j].astype(F32) + r_ref[j].astype(F32)).astype(BF)
        if j < q:
            s_ref[j] = total
        else:
            o_ref[j - q] = total


def line_kernel(where_ref, k_ref, r_ref, s_ref, o_ref):
    half = o_ref.shape[0]
    for j in range(2 * half):
        total = (k_ref[j].astype(F32) + r_ref[j].astype(F32)).astype(BF)
        if j < half:
            o_ref[j] = total
        else:
            s_ref[j - half] = total


def last_kernel(where_ref, own_ref, got_ref, out):
    tower = where_ref[2]
    out[pl.ds(tower, 1)] = own_ref[...]
    out[pl.ds(1 - tower, 1)] = got_ref[...]


def plus(a, b):
    return (a.astype(F32) + b.astype(F32)).astype(BF)


class Scatter:
    def __init__(self, plan, order, parts, rows):
        self.plan, self.order, self.rows = (plan, order, rows)
        self.width = parts[0].shape[1]
        parts = [p.reshape(plan.n, rows, self.width) for p in parts]
        self.own = parts[0]
        got = [send(parts[q], plan.sibling(q)) for q in range(1, plan.reps)]
        self.rest = got[0]
        for o in got[1:]:
            self.rest = plus(self.rest, o)

    def run(self, kernel, name, us, outs, *args):
        return self.order.done(in_vmem(kernel, name, us, outs, self.order.where, *args))

    def one(self):
        plan = self.plan
        n = plan.n
        whole = (n, self.rows, self.width)
        half = shape((n // 2, self.rows, self.width), BF)
        hs, self.hk = self.order.done(pl.pallas_call(partial(add_kernel, plan.depth), out_shape=(half, half), in_specs=[smem(), vmem(), vmem()], out_specs=(vmem(), vmem()), compiler_params=params(24), name='pick_add', cost_estimate=behind(3))(self.order.where, self.own, self.rest))
        self.r1 = send(hs, plan.first())
        return

    def two(self):
        quarter = ((self.plan.n // 4, self.rows, self.width), BF)
        ks, self.kk = self.run(two_kernel, 'add_two', 1, (quarter, quarter), self.hk, self.r1)
        self.r2 = send(ks, self.plan.second())

    def line(self):
        n = self.kk.shape[0] // 2
        half = ((n, self.rows, self.width), BF)
        out, self.kk = self.run(line_kernel, 'add_line', 1, (half, half), self.kk, self.r2)
        self.r2 = send(out, self.plan.along(n))
        return out

    def three(self):
        self.line()

    def four(self):
        while self.kk.shape[0] > 1:
            self.out = self.line()

    def last(self):
        plan = self.plan
        outs = (((2, self.rows, self.width), BF),)
        pair, = self.run(last_kernel, 'add_last', 1, outs, self.kk, self.r2)
        self.ends = [pair] + [send(pair, plan.sibling(q)) for q in range(1, plan.reps)]


def finish_kernel(reps, spans, vec, where_ref, *refs):
    chunks = len(spans)
    ins, outs = (refs[:chunks * reps], refs[chunks * reps:])
    core = where_ref[1]
    for c in range(chunks):
        parts = ins[c * reps:(c + 1) * reps]
        width = parts[0].shape[2]
        for q in range(reps):
            for mine in range(reps):

                @pl.when(core ^ q == mine)
                def copy(c=c, parts=parts, q=q, mine=mine):
                    for at, size, out, to in spans[c]:
                        low, high = (max(at, mine * width), min(at + size, (mine + 1) * width))
                        if low >= high:
                            continue
                        lanes = slice(low - mine * width, high - mine * width)
                        if out == vec:
                            turn(parts[q], lanes, low - at, outs[out], outs[out + 1])
                        else:
                            outs[out][:, :, to + low - at:to + high - at] = parts[q][:, :, lanes].astype(F32)


def turn(part_ref, lanes, at, bias_ref, gain_ref):
    for t in range(2):
        columns = part_ref[t, :, lanes]
        for ref, start in ((bias_ref, 0), (gain_ref, bias_ref.shape[1])):
            n = ref.shape[1]
            i = lax.broadcasted_iota(jnp.int32, (n, columns.shape[1]), 0)
            j = lax.broadcasted_iota(jnp.int32, (n, columns.shape[1]), 1)
            ref[t] = dot_t(jnp.where(i + start == j + at, 1.0, 0.0).astype(BF), columns)


def finish(plan, order, chunks, spans, shapes, vec=-1):
    outs = tuple(((s, F32) for s in shapes))
    args = [p for c in chunks for p in c.ends]
    kernel = partial(finish_kernel, plan.reps, spans, vec)
    return order.done(in_vmem(kernel, 'finish', 2, outs, order.where, *args))


def dot(a, b):
    return jnp.dot(a, b, preferred_element_type=F32)


def dot_t(a, b):
    return lax.dot_general(a, b, (((1,), (1,)), ((), ())), preferred_element_type=F32)


def t_dot(a, b):
    return lax.dot_general(a, b, (((0,), (0,)), ((), ())), preferred_element_type=F32)


def normalize(h):
    center = h - jnp.mean(h, -1, keepdims=True)
    rstd = lax.rsqrt(jnp.mean(center * center, -1, keepdims=True) + EPS)
    return (center * rstd, rstd)


def lane_masks():
    lane = lax.broadcasted_iota(jnp.int32, (1, 2 * HEAD), 1)
    low = (lane < HEAD).astype(F32).astype(BF)
    return (low, (1.0 - low.astype(F32)).astype(BF))


def attend_kernel(part, where_ref, x_ref, w_ref, *rest):
    proj_ref, probs_ref, attn_ref, hat_ref, rstd_ref, norm_ref, vec_ref, cls_ref, bias_ref = rest[-9:]

    @pl.when(pl.program_id(0) == 0)
    def prepare():
        vec_ref[...] = jnp.transpose(w_ref[:, AT_VEC:AT_VEC + 128].astype(F32))
        span = where_ref[3]
        row = lax.broadcasted_iota(jnp.int32, (BLOCK, 2 * BLOCK), 0)
        col = lax.broadcasted_iota(jnp.int32, (BLOCK, 2 * BLOCK), 1) % BLOCK
        bias_ref[...] = jnp.where(row ^ col < span, 0.0, -1e+30)
    x = x_ref[...]
    for j in range(3):
        part = dot(x, w_ref[:, j * D:(j + 1) * D])
        if j != 1:
            part = part + vec_ref[j // 2:j // 2 + 1, :]
        proj_ref[:, j * D:(j + 1) * D] = part.astype(BF)
    low, high = lane_masks()
    bias = bias_ref[...]
    for blk in range(256 // BLOCK):
        rows = slice(blk * BLOCK, (blk + 1) * BLOCK)
        for pair in range(PAIRS):
            lanes = slice(pair * 128, (pair + 1) * 128)
            q = proj_ref[rows, lanes]
            k = proj_ref[rows, D + pair * 128:D + (pair + 1) * 128]
            v = proj_ref[rows, 2 * D + pair * 128:2 * D + (pair + 1) * 128]
            s = dot_t(k, jnp.concatenate([q * low, q * high], 0)) * HEAD ** (-0.5) + bias
            e = jnp.exp(s - jnp.max(s, 0, keepdims=True))
            p = (e * (1.0 / jnp.sum(e, 0, keepdims=True))).astype(BF)
            probs_ref[blk, pair] = p
            tall = jnp.concatenate([p[:, :BLOCK], p[:, BLOCK:]], 0)
            attn_ref[rows, lanes] = t_dot(tall, jnp.concatenate([v * low, v * high], 0)).astype(BF)
    hidden = x.astype(F32) + (dot(attn_ref[...], w_ref[:, AT_OUT:AT_VEC]) + vec_ref[2:3, :])
    hat, rstd = normalize(hidden)
    hat_ref[...] = hat
    rstd_ref[...] = rstd
    norm = hat * vec_ref[10:11, :] + vec_ref[3:4, :]
    norm_ref[...] = norm.astype(BF)
    for j in range(8):
        cls_ref[j:j + 1, :] = norm[32 * j:32 * j + 1, :]


def attend(order, x, w_one, part, before=()):
    rows = 2 * x.shape[0]
    per = 256 // BLOCK
    steps = rows // 256 // 2
    first = part * steps

    def here(width):
        return pl.BlockSpec((256, width), lambda i: (i + first, 0))
    return pl.pallas_call(partial(attend_kernel, part), grid=(steps,), out_shape=(far((rows, 3 * D), BF), far((rows // BLOCK, PAIRS, BLOCK, 2 * BLOCK), BF), far((rows, D), BF), far((rows, D), F32), far((rows, 1), F32), far((rows, D), BF), shape((128, D), F32), shape((rows // 64, D), F32)), in_specs=[smem(), rows_at(D, 256), vmem()] + [pl.BlockSpec(memory_space=pl.ANY)] * len(before), out_specs=[here(3 * D), pl.BlockSpec((per, PAIRS, BLOCK, 2 * BLOCK), lambda i: (i + first, 0, 0, 0)), here(D), here(D), here(1), here(D), still((128, D)), rows_at(D, 8)], scratch_shapes=[pltpu.VMEM((BLOCK, 2 * BLOCK), F32)], input_output_aliases={3 + j: j for j in range(len(before))}, compiler_params=params(24), name='attend', cost_estimate=cost(7))(order.where, x, w_one, *[b for b in before])


def gelu_pair(u):
    phi = 0.5 + 0.5 * lax.erf(u * 2 ** (-0.5))
    return (u * phi, phi + u * (jnp.exp(-0.5 * u * u) * (2 * jnp.pi) ** (-0.5)))


def up_kernel(first, where_ref, norm_ref, w_ref, vec_ref, *rest):
    act_ref, slope_ref = rest[-2:]
    bias = vec_ref[pl.ds(4 + first + pl.program_id(0), 1), :]
    for m in range(0, norm_ref.shape[0], 256):
        rows = slice(m, m + 256)
        act, slope = gelu_pair(dot(norm_ref[rows, :], w_ref[...]) + bias)
        act_ref[rows, :] = act.astype(BF)
        slope_ref[rows, :] = slope.astype(BF)


def up(order, norm, w_up, vec, part, before=()):
    rows = norm.shape[0]
    steps = FF // D // 2
    first = part * steps
    col = pl.BlockSpec((rows, D), lambda i: (0, i + first))
    return pl.pallas_call(partial(up_kernel, first), grid=(steps,), out_shape=(shape((rows, FF), BF), far((rows, FF), BF)), in_specs=[smem(), still(norm.shape), pl.BlockSpec((D, D), lambda i: (0, i + first)), still(vec.shape)] + [pl.BlockSpec(memory_space=pl.ANY)] * len(before), out_specs=[col, col], input_output_aliases={4 + j: j for j in range(len(before))}, compiler_params=params(24), name='up', cost_estimate=cost(8))(order.where, norm, w_up, vec, *[b for b in before])


def down_kernel(where_ref, act_ref, w_ref, hat_ref, vec_ref, own_ref, far_ref, hat2_ref, rstd2_ref):
    normed = hat_ref[...] * vec_ref[10:11, :] + vec_ref[3:4, :]
    second = normed + (dot(act_ref[...], w_ref[...]) + vec_ref[8:9, :])
    hat, rstd = normalize(second)
    hat2_ref[...] = hat
    rstd2_ref[...] = rstd
    out = (hat * vec_ref[11:12, :] + vec_ref[9:10, :]).astype(BF)
    half = pl.num_programs(0) // 2

    @pl.when(pl.program_id(0) < half)
    def near():
        own_ref[...] = out

    @pl.when(pl.program_id(0) >= half)
    def away():
        far_ref[...] = out


def down(order, act, w_down, hat, vec):
    rows = act.shape[0]
    half = rows // 256 // 2
    near = pl.BlockSpec((256, D), lambda i: (jnp.minimum(i, half - 1), 0))
    away = pl.BlockSpec((256, D), lambda i: (jnp.maximum(i - half, 0), 0))
    return pl.pallas_call(down_kernel, grid=(rows // 256,), out_shape=(far((rows // 2, D), BF), shape((rows // 2, D), BF), shape((rows, D), F32), shape((rows, 1), F32)), in_specs=[smem(), rows_at(FF, 256), vmem(), rows_at(D, 256), still(vec.shape)], out_specs=[near, away, rows_at(D, 256), rows_at(1, 256)], compiler_params=params(24), name='down', cost_estimate=cost(8))(order.where, act, w_down, stay(hat), vec)


def first_kernel(where_ref, a_ref, b_ref, up_ref, down_ref, vec_ref, marks_ref, msg_ref):
    norm = jnp.concatenate([a_ref[...], b_ref[...]], 0)
    second = norm + vec_ref[8:9, :]
    wide = norm.astype(BF)
    for j in range(FF // D):
        u = dot(wide, up_ref[:, j * D:(j + 1) * D]) + vec_ref[4 + j:5 + j, :]
        second = second + dot(gelu_pair(u)[0].astype(BF), down_ref[j * D:(j + 1) * D, :])
    hat, _ = normalize(second)
    msg_ref[:, :D] = (hat * vec_ref[11:12, :] + vec_ref[9:10, :]).astype(BF)
    marks = marks_ref[...].astype(F32)
    pad = jnp.zeros((32 - marks.shape[0], marks.shape[1]), F32)
    msg_ref[:, D:] = jnp.concatenate([marks, pad], 0).astype(BF)


def first_rows(order, a, b, w_up, w_down, vec, positives):
    outs = (((32, D + positives.shape[1]), BF),)
    return order.done(in_vmem(first_kernel, 'first_rows', 4, outs, order.where, a, b, w_up, w_down, vec, positives))[0]


def pack_kernel(per, where_ref, *refs):
    msgs, out_ref = (refs[:-1], refs[-1])
    queries = per * 4
    pick_row = lax.broadcasted_iota(jnp.int32, (16, 32), 0)
    pick_col = lax.broadcasted_iota(jnp.int32, (16, 32), 1)
    pick = jnp.where((pick_col == pick_row * (32 // (2 * per))) & (pick_row < 2 * per), 1.0, 0.0).astype(BF)
    for n in range(len(msgs) // 2):
        for tower in range(2):

            @pl.when(where_ref[2] == tower)
            def put(n=n, tower=tower):
                zero, one = (msgs[2 * n + tower], msgs[2 * n + 1 - tower])
                out_ref[n, :32, :D] = zero[:, :D]
                out_ref[n, :queries, D:] = zero[:queries, D:]
                out_ref[n, queries:32, D:] = one[:queries, D:]
                out_ref[n, 32:, :D] = dot(pick, one[:, :D]).astype(BF)
                out_ref[n, 32:, D:] = jnp.zeros((16, out_ref.shape[2] - D), BF)


def contrast_kernel(reps, depth, per, where_ref, *refs):
    parts, loss_ref, grad_ref, acc_ref = (refs[:reps], refs[reps], refs[reps + 1], refs[reps + 2])
    me, core, tower = (where_ref[0], where_ref[1], where_ref[2])
    pieces = parts[0].shape[0]
    passages = parts[0].shape[2] - D
    cls_p = jnp.concatenate([part[:, 32:, :D].reshape(pieces * 16, D) for part in parts], 0)
    cols = cls_p.shape[0]
    col = lax.broadcasted_iota(jnp.int32, (passages, cols), 1)
    row = lax.broadcasted_iota(jnp.int32, (passages, cols), 0)
    j, slot = (col // 16, col % 16)
    base = (me | 4) ^ 8 * (j % (depth // 2)) ^ j // (depth // 2) % 4
    owner = jnp.where(slot < per, base, base ^ 4)
    passage = (owner * reps + (core ^ j // (2 * depth))) * per + slot % per
    pick = jnp.where((row == passage) & (slot < 2 * per), 1.0, 0.0).astype(BF)
    valid = lax.broadcasted_iota(jnp.int32, (1, cols), 1) % 16 < 2 * per
    acc_ref[...] = jnp.zeros_like(acc_ref)
    group = min(8, pieces)
    for q, part in enumerate(parts):
        for at in range(0, pieces, group):
            cls_q = part[at:at + group, :32, :D].reshape(group * 32, D)
            marks = dot(part[at:at + group, :32, D:].reshape(group * 32, passages), pick)
            raw = jnp.where(valid, dot_t(cls_q, cls_p) * D ** (-0.5), -1e+30)
            e = jnp.exp(raw - jnp.max(raw, -1, keepdims=True))
            total = jnp.sum(e, -1, keepdims=True)
            me_ = marks * e
            marked = jnp.sum(me_, -1, keepdims=True)
            grad = (LOSS_WEIGHT * (e / total - me_ / marked)).astype(BF)
            acc_ref[...] += t_dot(grad[:, :128], cls_q)[:16] * D ** (-0.5)
            if q == 0 and at == 0:
                loss_ref[...] = (jnp.log(total) - jnp.log(marked))[:32]
                grad_ref[...] = dot(grad[:32], cls_p) * D ** (-0.5)

    @pl.when(tower == 1)
    def passages_own():
        grad_ref[...] = jnp.zeros_like(grad_ref)
        for s in range(2 * per):
            at = s * (32 // (2 * per))
            grad_ref[at:at + 1, :] = acc_ref[s:s + 1, :]


class Contrast:

    def __init__(self, plan, order, msg, queries):
        self.plan, self.order, self.queries = (plan, order, queries)
        self.msgs = [msg] + [send(msg, plan.along(k)) for k in range(1, plan.depth)]

    def pack(self):
        plan = self.plan
        outs = (((plan.depth // 2, 48, self.msgs[0].shape[1]), BF),)
        kernel = partial(pack_kernel, self.queries // 4)
        buf, = self.order.done(in_vmem(kernel, 'pack', 1, outs, self.order.where, *self.msgs))
        self.bufs = [buf] + [send(buf, plan.pairs(lambda r, m=m: (m, 0))) for m in range(1, 4)]

    def join(self):
        plan = self.plan
        buf = join(self.order, *self.bufs)
        self.parts = [buf] + [send(buf, plan.sibling(s)) for s in range(1, plan.reps)]

    def loss(self):
        plan, order = (self.plan, self.order)
        loss, grad = order.done(pl.pallas_call(partial(contrast_kernel, plan.reps, plan.depth, self.queries // 4), out_shape=(shape((32, 1), F32), shape((32, D), F32)), in_specs=[smem()] + [vmem()] * plan.reps, out_specs=(vmem(), vmem()), scratch_shapes=[pltpu.VMEM((16, D), F32)], compiler_params=params(40), name='contrast', cost_estimate=cost(2))(order.where, *self.parts))
        at = order.where[2] * self.queries
        return (lax.dynamic_slice(loss, (at, 0), (self.queries, 1))[:, 0], grad)


def norm_back(grad, hat, rstd, gain):
    scaled = grad * gain
    a = jnp.mean(scaled, -1, keepdims=True)
    b = jnp.mean(scaled * hat, -1, keepdims=True)
    return rstd * (scaled - a - hat * b)


def col_sum(v):
    return jnp.sum(v, 0, keepdims=True)


def top_kernel(where_ref, cot_ref, cls_ref, hat_ref, rstd_ref, vec_ref, act_ref, second_ref, gs_ref, sums_ref, *rest):
    parts, full_ref = (rest[:-1], rest[-1])

    @pl.when(pl.program_id(0) == 0)
    def norm():
        groups = TILE // 32
        at_first = lax.broadcasted_iota(jnp.int32, (groups, 32, D), 1) == 0
        sums_ref[...] = jnp.zeros_like(sums_ref)
        for m in range(0, cot_ref.shape[0], TILE):
            rows = slice(m, m + TILE)
            cls = cls_ref[m // 32:(m + TILE) // 32, :].reshape(groups, 1, D)
            dout = cot_ref[rows, :].astype(F32) + jnp.where(at_first, cls, 0.0).reshape(TILE, D)
            hat = hat_ref[rows, :]
            grad = norm_back(dout, hat, rstd_ref[rows, :], vec_ref[11:12, :])
            second_ref[rows, :] = grad
            gs = grad.astype(BF)
            gs_ref[rows, :] = gs
            sums_ref[0:1, :] += col_sum(gs.astype(F32))
            sums_ref[1:2, :] += col_sum(dout)
            sums_ref[2:3, :] += col_sum(dout * hat)
    full_ref[...] = t_dot(act_ref[...], gs_ref[...]).astype(BF)
    halves(parts, where_ref[1], full_ref)


def top(plan, order, cot, cls_grad, hat2, rstd2, vec, act):
    rows = cot.shape[0]
    part = D // plan.reps
    second, gs, sums, *parts = pl.pallas_call(top_kernel, grid=(FF // D,), out_shape=(far((rows, D), F32), shape((rows, D), BF), shape((8, D), F32)) + (shape((FF, part), BF),) * plan.reps, in_specs=[smem(), vmem(), still(cls_grad.shape), vmem(), vmem(), still(vec.shape), pl.BlockSpec((rows, D), lambda i: (0, i))], out_specs=[still((rows, D)), still((rows, D)), still((8, D))] + [rows_at(part, D)] * plan.reps, scratch_shapes=[pltpu.VMEM((D, D), BF)], compiler_params=params(28), name='top', cost_estimate=behind(11))(order.where, cot, cls_grad, hat2, rstd2, vec, act)
    return (second, gs, sums, parts)


def gelu_back_kernel(reps, column, where_ref, gs_ref, w_ref, slope_ref, norm_ref, up_ref, acc_ref, sums_ref, *rest):
    parts, gu_ref = (rest[:-1], rest[-1])
    i = pl.program_id(0)
    total = jnp.zeros((1, D), F32)
    for m in range(0, gs_ref.shape[0], TILE):
        rows = slice(m, m + TILE)
        gu = (dot_t(gs_ref[rows, :], w_ref[...]) * slope_ref[rows, :].astype(F32)).astype(BF)
        gu_ref[rows, :] = gu
        total = total + col_sum(gu.astype(F32))
    sums_ref[pl.ds(column(i, where_ref), 1), :] = total
    for m in range(0, gs_ref.shape[0], TILE):
        rows = slice(m, m + TILE)
        before = jnp.where(i == 0, 0.0, acc_ref[rows, :])
        acc_ref[rows, :] = before + dot_t(gu_ref[rows, :], up_ref[...])
    grad = t_dot(norm_ref[...], gu_ref[...]).astype(BF)
    per = FF // D // reps
    for q in range(reps):

        @pl.when(i // per == reps - 1 - q)
        def put(q=q):
            parts[q][...] = grad


def gelu_back(plan, order, gs, w_down, slope, norm, w_up):
    rows = gs.shape[0]
    reps = plan.reps
    per = FF // D // reps

    def column(i, table):
        return (table[1] ^ reps - 1 - i // per) * per + i % per

    def held(q):
        return pl.BlockSpec((D, D), lambda i, table: (0, jnp.clip(i - (reps - 1 - q) * per, 0, per - 1)))
    acc, sums, *parts = pl.pallas_call(partial(gelu_back_kernel, reps, column), out_shape=(shape((rows, D), F32), shape((8, D), F32)) + (shape((D, FF // reps), BF),) * reps, grid_spec=pltpu.PrefetchScalarGridSpec(num_scalar_prefetch=1, grid=(FF // D,), in_specs=[vmem(), pl.BlockSpec((D, D), lambda i, table: (column(i, table), 0)), pl.BlockSpec((rows, D), lambda i, table: (0, column(i, table))), vmem(), pl.BlockSpec((D, D), lambda i, table: (0, column(i, table)))], out_specs=[still((rows, D)), still((8, D))] + [held(q) for q in range(reps)], scratch_shapes=[pltpu.VMEM((rows, D), BF)]), compiler_params=params(28), name='gelu_back', cost_estimate=behind(20))(order.where, gs, stay(w_down), stay(slope), norm, stay(w_up))
    return (acc, sums, parts)


def hidden_back_kernel(where_ref, acc_ref, second_ref, hat_ref, rstd_ref, w_ref, vec_ref, go_ref, ga_ref, sums_ref):

    @pl.when(pl.program_id(0) == 0)
    def clear():
        sums_ref[...] = jnp.zeros_like(sums_ref)
    grad = acc_ref[...] + second_ref[...]
    hat = hat_ref[...]
    hidden = norm_back(grad, hat, rstd_ref[...], vec_ref[10:11, :])
    go = hidden.astype(BF)
    go_ref[...] = go
    sums_ref[0:1, :] += col_sum(go.astype(F32))
    sums_ref[1:2, :] += col_sum(grad)
    sums_ref[2:3, :] += col_sum(grad * hat)
    ga_ref[...] = dot_t(go, w_ref[...]).astype(BF)


def hidden_back(order, acc, second, hat, rstd, w_one, vec):
    rows = acc.shape[0]
    return pl.pallas_call(hidden_back_kernel, grid=(rows // TILE,), out_shape=(shape((rows, D), BF), shape((rows, D), BF), shape((8, D), F32)), in_specs=[smem()] + [rows_at(D)] * 3 + [rows_at(1), still((D, D), (0, AT_OUT // D)), still(vec.shape)], out_specs=[rows_at(D), rows_at(D), still((8, D))], compiler_params=params(20), name='hidden_back', cost_estimate=behind(5))(order.where, acc, stay(second), stay(hat), stay(rstd), stay(w_one), vec)


def pair_back(pair, block, rows, ga_ref, proj_ref, probs_ref, low, high):
    q = proj_ref[rows, pair * 128:(pair + 1) * 128]
    k = proj_ref[rows, D + pair * 128:D + (pair + 1) * 128]
    v = proj_ref[rows, 2 * D + pair * 128:2 * D + (pair + 1) * 128]
    a = ga_ref[rows, pair * 128:(pair + 1) * 128]
    a2 = jnp.concatenate([a * low, a * high], 0)
    q2 = jnp.concatenate([q * low, q * high], 0)
    k2 = jnp.concatenate([k * low, k * high], 0)
    p = probs_ref[block, pair]
    dp = dot_t(v, a2)
    pf = p.astype(F32)
    ds = (pf * (dp - jnp.sum(pf * dp, 0, keepdims=True)) * HEAD ** (-0.5)).astype(BF)
    tall = jnp.concatenate([ds[:, :BLOCK], ds[:, BLOCK:]], 0)
    return (t_dot(tall, k2).astype(BF), dot(ds, q2).astype(BF), dot(p, a2).astype(BF))


def heads_back(first, count, at, ga_ref, proj_ref, probs_ref, gp_ref):
    low, high = lane_masks()
    for block in range(256 // BLOCK):
        rows = slice(block * BLOCK, (block + 1) * BLOCK)
        to = pl.ds(pl.multiple_of(at + block * BLOCK, BLOCK), BLOCK)
        for j in range(count):
            three = pair_back(first + j, block, rows, ga_ref, proj_ref, probs_ref, low, high)
            for n, grad in enumerate(three):
                lane = (n * count + j) * 128
                gp_ref[to, lane:lane + 128] = grad


def attend_back_kernel(first, count, where_ref, ga_ref, proj_ref, probs_ref, gp_ref):
    heads_back(first, count, 0, ga_ref, proj_ref, probs_ref, gp_ref)


def tile_specs(first):
    per = 256 // BLOCK
    return [pl.BlockSpec((256, D), lambda i: (i + first, 0)), pl.BlockSpec((256, 3 * D), lambda i: (i + first, 0)), pl.BlockSpec((per, PAIRS, BLOCK, 2 * BLOCK), lambda i: (i + first, 0, 0, 0))]


def attend_back(order, first, count, ga, proj, probs, rows, weight=1.0):
    wide = 3 * count * 128
    return pl.pallas_call(partial(attend_back_kernel, first, count), grid=(rows // 256,), out_shape=shape((rows, wide), BF), in_specs=[smem()] + tile_specs(0), out_specs=rows_at(wide, 256), compiler_params=params(20), name='attend_back', cost_estimate=behind(10 * count * rows / 4096 * weight))(order.where, ga, stay(proj), stay(probs))


def both_rows(x_ref, y_ref, near_ref, far_ref):
    return (t_dot(x_ref[...], near_ref[...]) + t_dot(y_ref[...], far_ref[...])).astype(BF)


def first_weights_kernel(where_ref, x_ref, y_ref, near_ref, far_ref, attn_ref, go_ref, *rest):
    parts, full_ref = (rest[:-1], rest[-1])
    full_ref[:, :D] = t_dot(attn_ref[...], go_ref[...]).astype(BF)
    end = D + near_ref.shape[1]
    full_ref[:, D:end] = both_rows(x_ref, y_ref, near_ref, far_ref)
    if end < full_ref.shape[1]:
        full_ref[:, end:] = jnp.zeros((D, full_ref.shape[1] - end), BF)
    halves(parts, where_ref[1], full_ref)


def last_weights_kernel(count, where_ref, x_ref, y_ref, near_ref, far_ref, first_near_ref, first_far_ref, up_ref, top_ref, hidden_ref, *rest):
    parts, full_ref, lines_ref = (rest[:-2], rest[-2], rest[-1])
    part = D - count * 128
    wide = count * 128
    full_ref[:, :3 * part] = both_rows(x_ref, y_ref, near_ref, far_ref)

    def sums(j, width, a_ref, b_ref):
        lanes = slice(j * width, (j + 1) * width)
        return col_sum(a_ref[:, lanes].astype(F32)) + col_sum(b_ref[:, lanes].astype(F32))
    lines_ref[...] = jnp.zeros_like(lines_ref)
    for n, j in ((0, 0), (1, 2)):
        lines_ref[n:n + 1, :wide] = sums(j, wide, first_near_ref, first_far_ref)
        lines_ref[n:n + 1, wide:] = sums(j, part, near_ref, far_ref)
    lines_ref[2:4, :] = hidden_ref[0:2, :]
    lines_ref[4:8, :] = up_ref[0:4, :]
    lines_ref[8:10, :] = top_ref[0:2, :]
    lines_ref[10:11, :] = hidden_ref[2:3, :]
    lines_ref[11:12, :] = top_ref[2:3, :]
    full_ref[:, 3 * part:3 * part + 128] = jnp.transpose(lines_ref[...]).astype(BF)
    if 3 * part + 128 < full_ref.shape[1]:
        full_ref[:, 3 * part + 128:] = jnp.zeros((D, full_ref.shape[1] - 3 * part - 128), BF)
    halves(parts, where_ref[1], full_ref)


def weights(plan, order, kernel, name, us, total, scratch, *args):
    part = total // plan.reps
    return pl.pallas_call(kernel, grid=(1,), out_shape=(shape((D, part), BF),) * plan.reps, in_specs=[smem()] + [vmem() for a in args], out_specs=[still((D, part))] * plan.reps, scratch_shapes=[pltpu.VMEM((D, total), BF)] + scratch, compiler_params=params(28), name=name, cost_estimate=behind(us))(order.where, *args)


def gx_of(count, a_ref, b_ref, w_ref, hidden):
    hidden = hidden.astype(F32)
    ca, cb = (count * 128, D - count * 128)
    for j in range(3):
        hidden = hidden + dot_t(a_ref[:, j * ca:(j + 1) * ca], w_ref[:, j * D:j * D + ca])
        hidden = hidden + dot_t(b_ref[:, j * cb:(j + 1) * cb], w_ref[:, j * D + ca:(j + 1) * D])
    return hidden


def far_back_kernel(count, where_ref, ga_ref, proj_ref, probs_ref, w_ref, hidden_ref, a_ref, b_ref, far_ref):
    heads_back(0, count, 0, ga_ref, proj_ref, probs_ref, a_ref)
    heads_back(count, PAIRS - count, 0, ga_ref, proj_ref, probs_ref, b_ref)
    far_ref[...] = gx_of(count, a_ref, b_ref, w_ref, hidden_ref[...]).astype(BF)


def far_back(order, count, ga, proj, probs, w_one, hidden):
    rows = ga.shape[0] // 2
    steps = rows // 256
    wide = 3 * count * 128
    return pl.pallas_call(partial(far_back_kernel, count), grid=(steps,), out_shape=(shape((rows, wide), BF), shape((rows, 3 * D - wide), BF), shape((rows, D), BF)), in_specs=[smem()] + tile_specs(steps) + [still((D, 3 * D)), pl.BlockSpec((256, D), lambda i: (i + steps, 0))], out_specs=[rows_at(wide, 256), rows_at(3 * D - wide, 256), rows_at(D, 256)], compiler_params=params(24), name='far_back', cost_estimate=behind(11))(order.where, ga, stay(proj), stay(probs), stay(w_one), stay(hidden))


def token_back_kernel(count, where_ref, a_ref, b_ref, w_ref, hidden_ref, own_ref):
    own_ref[...] = gx_of(count, a_ref, b_ref, w_ref, hidden_ref[...])


def token_back(order, count, ga, gb, w_one, hidden):
    rows = gb.shape[0]
    return pl.pallas_call(partial(token_back_kernel, count), grid=(rows // TILE,), out_shape=shape((rows, D), F32), in_specs=[smem(), rows_at(ga.shape[1]), rows_at(gb.shape[1]), still((D, 3 * D)), rows_at(D)], out_specs=rows_at(D), compiler_params=params(24), name='token_back', cost_estimate=behind(4))(order.where, ga, gb, stay(w_one), stay(hidden))


def on_device(plan, query_tokens, passage_tokens, query_cot, passage_cot, positives, w_qkv, w_out, w_up, w_down, biases, gains):
    me = lax.axis_index('dp')
    core = lax.axis_index('rep')
    tower = me >> 2 & 1
    span = jnp.where(tower == 0, query_tokens.shape[1], passage_tokens.shape[1])
    where = jnp.stack([me, core, tower, span]).astype(jnp.int32)
    swap = plan.along(1)

    def exchange(a, b, *others):
        a, b = (a.reshape(-1, D), b.reshape(-1, D))
        away = jnp.where(tower == 0, b, a)
        return (jnp.where(tower == 0, a, b), send(after(away, *others) if others else away, swap))

    def merged(own, back):
        a = jnp.where(tower == 0, own, back)
        b = jnp.where(tower == 0, back, own)
        return (a.reshape(query_tokens.shape), b.reshape(passage_tokens.shape))
    order = Order(where)
    mine, other, mine2, other2, mine3, other3 = shards_of(plan, order, w_qkv, w_out, biases, gains, w_up, w_down)
    z1 = gather_line(plan, mine, other)
    both2 = jnp.concatenate([mine2, send(other2, swap)], 0)
    both3 = jnp.concatenate([mine3, send(other3, swap)], 0)
    z2 = gather_steps(plan, both2, z1)
    p1 = gather_plane(plan, z1, z2, both3)
    z3 = gather_steps(plan, both3, z2)
    x_mine, x_got = exchange(query_tokens, passage_tokens, z3)
    w_one = gather_cores(plan, order, p1)
    p2 = gather_plane(plan, z2)
    p3 = gather_plane(plan, after(z3, p2[0]))
    order.done(p2[0])
    first = order.done(attend(order, x_mine, w_one, 0))
    proj, probs, attn, hat1, rstd1, norm, vec, cls_b = order.done(attend(order, x_got, w_one, 1, first[:6]))
    w_two = gather_cores(plan, order, tuple((after(b, first[6]) for b in p2)))
    half_up = order.done(up(order, norm, w_two, vec, 0))
    w_three = gather_cores(plan, order, tuple((after(b, norm) for b in p3)))
    msg = first_rows(order, first[7], cls_b, w_two, w_three, vec, positives)
    cot_mine, cot_got = exchange(query_cot, passage_cot, norm)
    loss = Contrast(plan, order, msg, positives.shape[0])
    act, slope = order.done(up(order, norm, w_two, vec, 1, half_up))
    loss.pack()
    cot = jnp.concatenate([cot_mine, cot_got], 0)
    out_own, out_far, hat2, rstd2 = order.done(down(order, act, w_three, hat1, vec))
    out_back = send(out_far, swap)
    loss.join()
    order.done(cot)
    query_loss, cls_grad = loss.loss()
    second, gs, sums_top, g_down = order.done(top(plan, order, cot, cls_grad, hat2, rstd2, vec, act))
    down_part = Scatter(plan, order, g_down, w_down.shape[1])
    acc, sums_up, g_up = order.done(gelu_back(plan, order, gs, w_three, slope, norm, w_two))
    up_part = Scatter(plan, order, g_up, w_up.shape[1])
    order.done(out_back)
    down_part.one()
    go, ga, sums = order.done(hidden_back(order, acc, second, hat1, rstd1, w_one, vec))
    up_part.one()
    split = 4
    half = ga.shape[0] // 2
    hidden = go
    far_a, far_b, gx_far = order.done(far_back(order, split, ga, proj, probs, w_one, go))
    gx_back = send(gx_far, swap)
    near_a = order.done(attend_back(order, 0, split, ga, proj, probs, half))
    total = wide(3 * split * 128 + D, plan.reps)
    args = (x_mine, x_got, near_a, far_a, stay(attn), go)
    g_a = order.done(weights(plan, order, first_weights_kernel, 'first_weights', 5, total, [], *args))
    a_part = Scatter(plan, order, g_a, w_qkv.shape[1])
    down_part.two()
    up_part.two()
    order.done(gx_back)
    near_b = order.done(attend_back(order, split, PAIRS - split, ga, proj, probs, half))
    down_part.three()
    a_part.one()
    up_part.three()
    total = wide(3 * (D - split * 128) + 128, plan.reps)
    scratch = [pltpu.VMEM((128, D), F32)]
    args = (x_mine, x_got, near_b, far_b, near_a, far_a, sums_up, sums_top, sums)
    kernel = partial(last_weights_kernel, split)
    g_b = order.done(weights(plan, order, kernel, 'last_weights', 4, total, scratch, *args))
    b_part = Scatter(plan, order, g_b, w_qkv.shape[1])
    gx_own = order.done(token_back(order, split, near_a, near_b, w_one, go))
    a_part.two()
    b_part.one()
    down_part.four()
    up_part.four()
    a_part.three()
    b_part.two()
    down_part.last()
    up_part.last()
    a_part.four()
    b_part.three()
    grad_down, = finish(plan, order, [down_part], [[(0, D, 0, 0)]], [w_down.shape])
    grad_up, = finish(plan, order, [up_part], [[(0, FF, 0, 0)]], [w_up.shape])
    b_part.four()
    a_part.last()
    b_part.last()
    query_out, passage_out = merged(out_own, after(out_back, b_part.out))
    query_grad, passage_grad = merged(gx_own, after(gx_back, b_part.out).astype(F32))
    qa, qb = (split * 128, D - split * 128)
    spans_a = [(0, D, 1, 0)] + [(D + j * qa, qa, 0, j * D) for j in range(3)]
    spans_b = [(j * qb, qb, 0, j * D + qa) for j in range(3)] + [(3 * qb, 128, 2, 0)]
    shapes = [w_qkv.shape, w_out.shape, biases.shape, gains.shape]
    grads = finish(plan, order, [a_part, b_part], [spans_a, spans_b], shapes, 2)
    return (query_out, passage_out, query_grad, passage_grad, query_loss, grads[0], grads[1], grad_up, grad_down, grads[2], grads[3])


def solution(mesh):
    plan = Plan(mesh.shape['dp'], mesh.shape['rep'])
    rows = P(('dp', 'rep'), None, None)
    shards = P(None, 'dp', None)
    lanes = P(None, None, 'dp')
    return jax.shard_map(partial(on_device, plan), mesh=mesh, in_specs=(rows,) * 4 + (P(('dp', 'rep'), None),) + (shards,) * 4 + (lanes,) * 2, out_specs=(rows,) * 4 + (P(('dp', 'rep')),) + (shards,) * 4 + (lanes,) * 2, check_vma=False)
```

time: 300 us -> 282 us (0.940)
  Pallas kernels: 150 us -> 137 us
  starting transfers between devices: 52.3 us -> 44.4 us
    ppermute x54, starting transfers between devices: 52.3 us -> 44.4 us  [send(): return lax.ppermute(v, AXES, pairs)]
    pallas_call x8, Pallas kernels: 50.6 us -> 45.5 us  [the longest x2 13.1 us: up(): pl.pallas_call(partial(up_kernel, first), grid=(steps,), out_shape=(shape...]
    pallas_call x4, Pallas kernels: 8.9 us -> 3.89 us  [one(): pl.pallas_call(partial(add_kernel, plan.depth), out_shape=(half, half), i...]
    unnamed x56 -> x58, local copies, waits for them, and re-layouts: 4.67 us -> 6.05 us
  transfers between devices with their start and end apart: 54 -> 54, of which waited for: 19 -> 14; matrix products, arithmetic and copies ran while one was open for 2% -> 2% of each run, Pallas kernels for 49% -> 48%
where the time goes in v5:
time: 282 us; the launch traced here: 278 us
  Pallas kernels  137 us (49%)
  waiting for transfers between devices  81.9 us (29%)
  starting transfers between devices  44.4 us (16%)
  local copies, waits for them, and re-layouts  7.58 us (3%)
  other arithmetic  4.87 us (2%)
    ppermute x54, waiting for transfers between devices, send(): return lax.ppermute(v, AXES, pairs)  81.9 us
    ppermute x54, starting transfers between devices, send(): return lax.ppermute(v, AXES, pairs)  44.4 us
    pallas_call x1, Pallas kernels, gelu_back(): pl.pallas_call(partial(gelu_back_kernel, reps, column), out_shape=(shape(...  19.5 us
    pallas_call x22, Pallas kernels, in_vmem(): pl.pallas_call(kernel, out_shape=tuple((shape(*o) for o in outs)), in_spe...  19.4 us
    pallas_call x2, Pallas kernels, attend(): pl.pallas_call(partial(attend_kernel, part), grid=(steps,), out_shape=(fa...  16.2 us
    pallas_call x2, Pallas kernels, up(): pl.pallas_call(partial(up_kernel, first), grid=(steps,), out_shape=(shape...  13.1 us
    pallas_call x1, Pallas kernels, top(): pl.pallas_call(top_kernel, grid=(FF // D,), out_shape=(far((rows, D), F32...  11 us
    pallas_call x1, Pallas kernels, far_back(): pl.pallas_call(partial(far_back_kernel, count), grid=(steps,), out_shape=...  10.8 us
  transfers between devices with their start and end apart: 54, of which 14 were waited for; matrix products, arithmetic and copies ran while one was open for 2% of the time, Pallas kernels for 48%

profile of v5, /device:TPU:0, one launch (start us, length us, event | category | flops | bytes accessed | tf_op | source)
XLA Modules:
  0.0 278.4 jit_solution(4978578675462327822)
XLA Ops:
  0.6 1.3 copy.32.bias_ref
  2.0 1.8 shards.1
  3.8 3.1 %collective-permute-start = (bf16[1,48,1664]{2,1,0:T(8,128)(2,1)S(1)}, bf16[1,48,1664]{2,1,0:T(8,128)(2,1)S(1)}, u32[]{:S(2)}, u32[]{:S(2)}) collective-permute-start(bf16[1,48,1664]{2,1,0:T(8,128)(2,1)S(1)} %get-tuple-element.159), channel_id=1, source_target_pairs={{0,8},{1,9},{2,10},{3,11},{4,12},{5,13},{6,14},{7,15},{8,0},{9,1},... | collective-permute-start | bytes 479240 | tf_op jit(solution)/shard_map/ppermute | solution.py:109
  6.9 2.5 collective-permute-start.2
  9.5 1.8 collective-permute-start.4
  11.6 12.1 %collective-permute-done.1 = bf16[1,48,1664]{2,1,0:T(8,128)(2,1)S(1)} collective-permute-done((bf16[1,48,1664]{2,1,0:T(8,128)(2,1)S(1)}, bf16[1,48,1664]{2,1,0:T(8,128)(2,1)S(1)}, u32[]{:S(2)}, u32[]{:S(2)}) %collective-permute-start.1) | collective-permute-done | bytes 159776 | tf_op jit(solution)/shard_map/ppermute | solution.py:109
  23.8 1.6 collective-permute-start.3
  25.5 14.6 %collective-permute-done.5 = bf16[2,48,1536]{2,1,0:T(8,128)(2,1)S(1)} collective-permute-done((bf16[2,48,1536]{2,1,0:T(8,128)(2,1)S(1)}, bf16[2,48,1536]{2,1,0:T(8,128)(2,1)S(1)}, u32[]{:S(2)}, u32[]{:S(2)}) %collective-permute-start.5) | collective-permute-done | bytes 294944 | tf_op jit(solution)/shard_map/ppermute | solution.py:109
  40.9 1.5 collective-permute-start.10
  42.4 21.6 %collective-permute-done.7.refs_1_ = bf16[8,48,1664]{2,1,0:T(8,128)(2,1)S(1)} collective-permute-done((bf16[8,48,1664]{2,1,0:T(8,128)(2,1)S(1)}, bf16[8,48,1664]{2,1,0:T(8,128)(2,1)S(1)}, u32[]{:S(2)}, u32[]{:S(2)}) %collective-permute-start.7) | collective-permute-done | bytes 1277984 | tf_op jit(solution)/shard_map/ppermute | solution.py:109
  65.9 14.5 %collective-permute-done.16 = bf16[4,192,384]{2,1,0:T(8,128)(2,1)S(1)} collective-permute-done((bf16[4,192,384]{2,1,0:T(8,128)(2,1)S(1)}, bf16[4,192,384]{2,1,0:T(8,128)(2,1)S(1)}, u32[]{:S(2)}, u32[]{:S(2)}) %collective-permute-start.16) | collective-permute-done | bytes 589856 | tf_op jit(solution)/shard_map/ppermute | solution.py:109
  81.6 8.5 %attend.2 = (bf16[1024,2304]{1,0:T(8,128)(2,1)}, bf16[8,6,128,256]{3,2,1,0:T(8,128)(2,1)}, bf16[1024,768]{1,0:T(8,128)(2,1)}, f32[1024,768]{1,0:T(8,128)}, f32[1...) custom-call(s32[4]{0:T(128)S(1)} %pad_add_fusion.where_ref, ...), custom_call_target="tpu_custom_call" | custom-call | flops 7000000000 | bytes 21000000 | tf_op jit(solution)/shard_map/attend/pallas_call | solution.py:432
  90.7 7.7 %attend.3 = (bf16[1024,2304]{1,0:T(8,128)(2,1)}, bf16[8,6,128,256]{3,2,1,0:T(8,128)(2,1)}, bf16[1024,768]{1,0:T(8,128)(2,1)}, f32[1024,768]{1,0:T(8,128)}, f32[1...) custom-call(s32[4]{0:T(128)S(1)} %pad_add_fusion.where_ref, ...), custom_call_target="tpu_custom_call", output_to_operand_aliasing={{0}: (3, {}), {1}: (4, {}), {2}: (5, {}), {3}: (6, {}), {4}... | custom-call | flops 7000000000 | bytes 21000000 | tf_op jit(solution)/shard_map/attend/pallas_call | solution.py:432
  101.0 6.4 %up.2 = (bf16[1024,3072]{1,0:T(8,128)(2,1)S(1)}, bf16[1024,3072]{1,0:T(8,128)(2,1)}) custom-call(s32[4]{0:T(128)S(1)} %pad_add_fusion.where_ref, bf16[1024,768]{1,0:T(8,128)(2,1)S(1)} %copy-done.8, bf16[768,3072]{1,0:T(8,128)(2,1)S(1)} %bitcast.37, f32[128,768]{1,0:T(8,128)S(1)} %get-tuple-element.186.vec_ref), custom_call_target="tpu_custom_call" | custom-call | flops 8000000000 | bytes 24000000 | tf_op jit(solution)/shard_map/up/pallas_call | solution.py:455
  108.5 2.6 first_rows.1.refs_0_
  111.1 1.7 collective-permute-start.20
  113.0 2.6 collective-permute-start.22
  115.6 6.7 %up.3 = (bf16[1024,3072]{1,0:T(8,128)(2,1)S(1)}, bf16[1024,3072]{1,0:T(8,128)(2,1)}) custom-call(s32[4]{0:T(128)S(1)} %pad_add_fusion.where_ref, bf16[1024,768]{1,0:T(8,128)(2,1)S(1)} %copy-done.8, bf16[768,3072]{1,0:T(8,128)(2,1)S(1)} %bitcast.39, f32[128,768]{1,0:T(8,128)S(1)} %get-tuple-element.186.vec_ref, ...), custom_call_target="tpu_custom_call", output_to_operand_aliasing={{0}: (4, {}), {1}: (5, {})} | custom-call | flops 8000000000 | bytes 24000000 | tf_op jit(solution)/shard_map/up/pallas_call | solution.py:455
  124.6 1.5 collective-permute-start.25
  127.3 8.6 %down.1 = (bf16[512,768]{1,0:T(8,128)(2,1)}, bf16[512,768]{1,0:T(8,128)(2,1)S(1)}, f32[1024,768]{1,0:T(8,128)S(1)}, f32[1024,1]{1,0:T(8,128)S(1)}) custom-call(s32[4]{0:T(128)S(1)} %pad_add_fusion.where_ref, bf16[1024,3072]{1,0:T(8,128)(2,1)S(1)} %get-tuple-element.200.act_ref, bf16[3072,768]{1,0:T(8,128)(2,1)S(1)} %bitcast.42, ...), custom_call_target="tpu_custom_call" | custom-call | flops 8000000000 | bytes 24000000 | tf_op jit(solution)/shard_map/down/pallas_call | solution.py:481
  135.9 1.6 copy-done.13
  138.5 1.8 collective-permute-done.28.refs_1_
  140.4 1.9 contrast.1
  142.2 11.0 %top.1 = (f32[1024,768]{1,0:T(8,128)}, bf16[1024,768]{1,0:T(8,128)(2,1)S(1)}, f32[8,768]{1,0:T(8,128)S(1)}, bf16[3072,384]{1,0:T(8,128)(2,1)S(1)}, bf16[3072,384]{1,0:T(8,128)(2,1)S(1)}) custom-call(s32[4]{0:T(128)S(1)} %pad_add_fusion.where_ref, bf16[1024,768]{1,0:T(8,128)(2,1)S(1)} %pad_maximum_fusion.cot_ref, f32[32,768]{1,0:T(8,128)S(1)} %get-tuple-element.213.cls_ref, ...), custom_call_target="tpu_custom_call" | custom-call | flops 44000002048 | bytes 132000000 | tf_op jit(solution)/shard_map/top/pallas_call | solution.py:625
  153.4 19.5 %gelu_back.1 = (f32[1024,768]{1,0:T(8,128)S(1)}, f32[8,768]{1,0:T(8,128)S(1)}, bf16[768,1536]{1,0:T(8,128)(2,1)S(1)}, bf16[768,1536]{1,0:T(8,128)(2,1)S(1)}) custom-call(s32[4]{0:T(128)S(1)} %pad_add_fusion.where_ref, bf16[1024,768]{1,0:T(8,128)(2,1)S(1)} %get-tuple-element.216.gs_ref, bf16[3072,768]{1,0:T(8,128)(2,1)} %bitcast.43, ...), custom_call_target="tpu_custom_call" | custom-call | flops 80000000000 | bytes 240000000 | tf_op jit(solution)/shard_map/gelu_back/pallas_call | solution.py:662
  175.4 6.3 %hidden_back.1 = (bf16[1024,768]{1,0:T(8,128)(2,1)S(1)}, bf16[1024,768]{1,0:T(8,128)(2,1)S(1)}, f32[8,768]{1,0:T(8,128)S(1)}) custom-call(s32[4]{0:T(128)S(1)} %pad_add_fusion.where_ref, f32[1024,768]{1,0:T(8,128)S(1)} %get-tuple-element.221.acc_ref, f32[1024,768]{1,0:T(8,128)} %get-tuple-element.215.second_ref, f32[1024,768]{1,0:T(8,128)} %get-tuple-element.183.hat_ref, ...), custom_call_target="tpu_custom_call" | custom-call | flops 20000000000 | bytes 60000000 | tf_op jit(solution)/shard_map/hidden_back/pallas_call | solution.py:684
  184.1 10.8 %far_back.1 = (bf16[512,1536]{1,0:T(8,128)(2,1)S(1)}, bf16[512,768]{1,0:T(8,128)(2,1)S(1)}, bf16[512,768]{1,0:T(8,128)(2,1)S(1)}) custom-call(s32[4]{0:T(128)S(1)} %pad_add_fusion.where_ref, bf16[1024,768]{1,0:T(8,128)(2,1)S(1)} %get-tuple-element.231.ga_ref, bf16[1024,2304]{1,0:T(8,128)(2,1)} %get-tuple-element.180.proj_ref, ...), custom_call_target="tpu_custom_call" | custom-call | flops 44000002048 | bytes 132000000 | tf_op jit(solution)/shard_map/far_back/pallas_call | solution.py:791
  195.0 5.5 %attend_back.2.near_ref.first_near_ref.a_ref = bf16[512,1536]{1,0:T(8,128)(2,1)S(1)} custom-call(s32[4]{0:T(128)S(1)} %pad_add_fusion.where_ref, bf16[1024,768]{1,0:T(8,128)(2,1)S(1)} %get-tuple-element.231.ga_ref, bf16[1024,2304]{1,0:T(8,128)(2,1)} %get-tuple-element.180.proj_ref, bf16[8,6,128,256]{3,2,1,0:T(8,128)(2,1)} %get-tuple-element.181.probs_ref), custom_call_target="tpu_custom_call" | custom-call | flops 20000000000 | bytes 60000000 | tf_op jit(solution)/shard_map/attend_back/pallas_call | solution.py:726
  200.5 5.6 %first_weights.1 = (bf16[768,1152]{1,0:T(8,128)(2,1)S(1)}, bf16[768,1152]{1,0:T(8,128)(2,1)S(1)}) custom-call(s32[4]{0:T(128)S(1)} %pad_add_fusion.where_ref, bf16[512,768]{1,0:T(8,128)(2,1)S(1)} %copy-done.4, bf16[512,768]{1,0:T(8,128)(2,1)S(1)} %copy-done.6, bf16[512,1536]{1,0:T(8,128)(2,1)S(1)} %attend_back.2.near_ref.first_near_ref.a_ref, ...), custom_call_target="tpu_custom_call" | custom-call | flops 20000000000 | bytes 60000000 | tf_op jit(solution)/shard_map/first_weights/pallas_call | solution.py:769
  207.1 1.6 collective-permute-start.34
  210.1 4.0 %collective-permute-done.33 = bf16[512,768]{1,0:T(8,128)(2,1)} collective-permute-done((bf16[512,768]{1,0:T(8,128)(2,1)S(1)}, bf16[512,768]{1,0:T(8,128)(2,1)}, u32[]{:S(2)}, u32[]{:S(2)}) %collective-permute-start.33) | collective-permute-done | bytes 786464 | tf_op jit(solution)/shard_map/ppermute | solution.py:109
  214.0 3.9 %attend_back.3.near_ref.b_ref = bf16[512,768]{1,0:T(8,128)(2,1)S(1)} custom-call(s32[4]{0:T(128)S(1)} %pad_add_fusion.where_ref, bf16[1024,768]{1,0:T(8,128)(2,1)S(1)} %get-tuple-element.231.ga_ref, bf16[1024,2304]{1,0:T(8,128)(2,1)} %get-tuple-element.180.proj_ref, bf16[8,6,128,256]{3,2,1,0:T(8,128)(2,1)} %get-tuple-element.181.probs_ref), custom_call_target="tpu_custom_call" | custom-call | flops 10000000000 | bytes 30000000 | tf_op jit(solution)/shard_map/attend_back/pallas_call | solution.py:726
  218.7 1.6 collective-permute-start.39
  224.0 4.7 %collective-permute-start.40 = (bf16[2,48,1536]{2,1,0:T(8,128)(2,1)S(1)}, bf16[2,48,1536]{2,1,0:T(8,128)(2,1)S(1)}, u32[]{:S(2)}, u32[]{:S(2)}) collective-permute-start(bf16[2,48,1536]{2,1,0:T(8,128)(2,1)S(1)} %get-tuple-element.259), channel_id=1, source_target_pairs={{0,16},{1,17},{2,18},{3,19},{4,20},{5,21},{6,22},{7,23},{8,24},{9,... | collective-permute-start | bytes 884744 | tf_op jit(solution)/shard_map/ppermute | solution.py:109
  228.7 2.5 last_weights.1
  231.3 4.4 %token_back.1 = f32[512,768]{1,0:T(8,128)S(1)} custom-call(s32[4]{0:T(128)S(1)} %pad_add_fusion.where_ref, bf16[512,1536]{1,0:T(8,128)(2,1)S(1)} %attend_back.2.near_ref.first_near_ref.a_ref, bf16[512,768]{1,0:T(8,128)(2,1)S(1)} %attend_back.3.near_ref.b_ref, bf16[768,3328]{1,0:T(8,128)(2,1)} %bitcast.36, bf16[1024,768]{1,0:T(8,128)(2,1)} %copy-done.15), custom_call_target="tpu_custom_call" | custom-call | flops 16000000000 | bytes 48000000 | tf_op jit(solution)/shard_map/token_back/pallas_call | solution.py:800
  236.5 1.6 collective-permute-start.41
  239.7 1.7 collective-permute-done.39.r_ref
  242.1 4.2 %collective-permute-done.40.r_ref = bf16[2,48,1536]{2,1,0:T(8,128)(2,1)S(1)} collective-permute-done((bf16[2,48,1536]{2,1,0:T(8,128)(2,1)S(1)}, bf16[2,48,1536]{2,1,0:T(8,128)(2,1)S(1)}, u32[]{:S(2)}, u32[]{:S(2)}) %collective-permute-start.40) | collective-permute-done | bytes 294944 | tf_op jit(solution)/shard_map/ppermute | solution.py:109
  247.0 1.8 collective-permute-done.41.r_ref
  252.4 1.6 collective-permute-start.46
  257.4 2.7 collective-permute-done.45.r_ref
  261.3 2.0 collective-permute-start.49
  263.4 1.6 finish.3
  265.1 1.6 finish.4
  267.7 1.8 collective-permute-start.51
  269.6 3.0 %convert_select_fusion = (f32[512,768]{1,0:T(8,128)}, f32[512,768]{1,0:T(8,128)}) fusion(f32[512,768]{1,0:T(8,128)S(1)} %token_back.1, bf16[512,768]{1,0:T(8,128)(2,1)} %collective-permute-done.33, pred[]{:T(512)S(6)} %eq.2), kind=kLoop, calls=%fused_computation | loop fusion | flops 1179648 | bytes 5505025 | tf_op jit(solution)/shard_map/jit(_where)/select_n | solution.py:818
  275.8 1.8 finish.5
  (178 shorter events, 41.0 us)
Async XLA Ops:
  3.8 7.8 %collective-permute-start = (bf16[1,48,1664]{2,1,0:T(8,128)(2,1)S(1)}, bf16[1,48,1664]{2,1,0:T(8,128)(2,1)S(1)}, u32[]{:S(2)}, u32[]{:S(2)}) collective-permute-start(bf16[1,48,1664]{2,1,0:T(8,128)(2,1)S(1)} %get-tuple-element.159), channel_id=1, source_target_pairs={{0,8},{1,9},{2,10},{3,11},{4,12},{5,13},{6,14},{7,15},{8,0},{9,1},... | collective-permute-start | bytes 479240 | tf_op jit(solution)/shard_map/ppermute | solution.py:109
  6.9 16.8 %collective-permute-start.2 = (bf16[1,48,1664]{2,1,0:T(8,128)(2,1)S(1)}, bf16[1,48,1664]{2,1,0:T(8,128)(2,1)S(1)}, u32[]{:S(2)}, u32[]{:S(2)}) collective-permute-start(bf16[1,48,1664]{2,1,0:T(8,128)(2,1)S(1)} %get-tuple-element.159), channel_id=1, source_target_pairs={{0,24},{1,25},{2,26},{3,27},{4,28},{5,29},{6,30},{7,31},{8,16},{9,... | collective-permute-start | bytes 479240 | tf_op jit(solution)/shard_map/ppermute | solution.py:109
  9.4 14.3 %collective-permute-start.1 = (bf16[1,48,1664]{2,1,0:T(8,128)(2,1)S(1)}, bf16[1,48,1664]{2,1,0:T(8,128)(2,1)S(1)}, u32[]{:S(2)}, u32[]{:S(2)}) collective-permute-start(bf16[1,48,1664]{2,1,0:T(8,128)(2,1)S(1)} %get-tuple-element.158), channel_id=1, source_target_pairs={{0,16},{1,17},{2,18},{3,19},{4,20},{5,21},{6,22},{7,23},{8,24},{9,... | collective-permute-start | bytes 479240 | tf_op jit(solution)/shard_map/ppermute | solution.py:109
  9.5 15.8 %collective-permute-start.4 = (bf16[1,48,1536]{2,1,0:T(8,128)(2,1)S(1)}, bf16[1,48,1536]{2,1,0:T(8,128)(2,1)S(1)}, u32[]{:S(2)}, u32[]{:S(2)}) collective-permute-start(bf16[1,48,1536]{2,1,0:T(8,128)(2,1)S(1)} %get-tuple-element.161), channel_id=1, source_target_pairs={{0,8},{1,9},{2,10},{3,11},{4,12},{5,13},{6,14},{7,15},{8,0},{9,1},... | collective-permute-start | bytes 442376 | tf_op jit(solution)/shard_map/ppermute | solution.py:109
  11.3 14.2 %collective-permute-start.6 = (bf16[1,192,384]{2,1,0:T(8,128)(2,1)S(1)}, bf16[1,192,384]{2,1,0:T(8,128)(2,1)S(1)}, u32[]{:S(2)}, u32[]{:S(2)}) collective-permute-start(bf16[1,192,384]{2,1,0:T(8,128)(2,1)S(1)} %get-tuple-element.163), channel_id=1, source_target_pairs={{0,8},{1,9},{2,10},{3,11},{4,12},{5,13},{6,14},{7,15},{8,0},{9,1},... | collective-permute-start | bytes 442376 | tf_op jit(solution)/shard_map/ppermute | solution.py:109
  23.8 16.4 %collective-permute-start.3 = (bf16[4,48,1664]{2,1,0:T(8,128)(2,1)S(1)}, bf16[4,48,1664]{2,1,0:T(8,128)(2,1)S(1)}, u32[]{:S(2)}, u32[]{:S(2)}) collective-permute-start(bf16[4,48,1664]{2,1,0:T(8,128)(2,1)S(1)} %get-tuple-element.339), channel_id=1, source_target_pairs={{0,2},{1,5},{2,0},{3,7},{4,6},{5,1},{6,4},{7,3},{8,10},{9,13},{10,... | collective-permute-start | bytes 1916936 | tf_op jit(solution)/shard_map/ppermute | solution.py:109
  25.4 14.8 %collective-permute-start.5 = (bf16[2,48,1536]{2,1,0:T(8,128)(2,1)S(1)}, bf16[2,48,1536]{2,1,0:T(8,128)(2,1)S(1)}, u32[]{:S(2)}, u32[]{:S(2)}) collective-permute-start(bf16[2,48,1536]{2,1,0:T(8,128)(2,1)S(1)} %pad_maximum_fusion.1), channel_id=1, source_target_pairs={{0,16},{1,17},{2,18},{3,19},{4,20},{5,21},{6,22},{7,23},{8,24},{9,... | collective-permute-start | bytes 884744 | tf_op jit(solution)/shard_map/ppermute | solution.py:109
  40.3 23.6 %collective-permute-start.7 = (bf16[8,48,1664]{2,1,0:T(8,128)(2,1)S(1)}, bf16[8,48,1664]{2,1,0:T(8,128)(2,1)S(1)}, u32[]{:S(2)}, u32[]{:S(2)}) collective-permute-start(bf16[8,48,1664]{2,1,0:T(8,128)(2,1)S(1)} %constant_dynamic-update-slice_fusion.4.refs_0_), channel_id=1, source_target_pairs={{0,4},{1,3},{2,6},{3,1},{4,0},{5,7},{6,2},{7,5},{8,12},{9,11},{10,... | collective-permute-start | bytes 3833864 | tf_op jit(solution)/shard_map/ppermute | solution.py:109
  40.9 23.2 %collective-permute-start.10 = (bf16[4,48,1536]{2,1,0:T(8,128)(2,1)S(1)}, bf16[4,48,1536]{2,1,0:T(8,128)(2,1)S(1)}, u32[]{:S(2)}, u32[]{:S(2)}) collective-permute-start(bf16[4,48,1536]{2,1,0:T(8,128)(2,1)S(1)} %get-tuple-element.336), channel_id=1, source_target_pairs={{0,2},{1,5},{2,0},{3,7},{4,6},{5,1},{6,4},{7,3},{8,10},{9,13},{10,... | collective-permute-start | bytes 1769480 | tf_op jit(solution)/shard_map/ppermute | solution.py:109
  42.4 21.6 %collective-permute-start.11 = (bf16[2,192,384]{2,1,0:T(8,128)(2,1)S(1)}, bf16[2,192,384]{2,1,0:T(8,128)(2,1)S(1)}, u32[]{:S(2)}, u32[]{:S(2)}) collective-permute-start(bf16[2,192,384]{2,1,0:T(8,128)(2,1)S(1)} %constant_dynamic-update-slice_fusion.11), channel_id=1, source_target_pairs={{0,16},{1,17},{2,18},{3,19},{4,20},{5,21},{6,22},{7,23},{8,24},{9,... | collective-permute-start | bytes 884744 | tf_op jit(solution)/shard_map/ppermute | solution.py:109
  42.4 38.2 %collective-permute-start.8 = (bf16[8,48,1664]{2,1,0:T(8,128)(2,1)S(1)}, bf16[8,48,1664]{2,1,0:T(8,128)(2,1)S(1)}, u32[]{:S(2)}, u32[]{:S(2)}) collective-permute-start(bf16[8,48,1664]{2,1,0:T(8,128)(2,1)S(1)} %constant_dynamic-update-slice_fusion.4.refs_0_), channel_id=1, source_target_pairs={{0,1},{1,0},{2,3},{3,2},{4,5},{5,4},{6,7},{7,6},{8,9},{9,8},{10,11... | collective-permute-start | bytes 3833864 | tf_op jit(solution)/shard_map/ppermute | solution.py:109
  64.0 16.6 %collective-permute-start.9 = (bf16[8,48,1664]{2,1,0:T(8,128)(2,1)S(1)}, bf16[8,48,1664]{2,1,0:T(8,128)(2,1)S(1)}, u32[]{:S(2)}, u32[]{:S(2)}) collective-permute-start(bf16[8,48,1664]{2,1,0:T(8,128)(2,1)S(1)} %collective-permute-done.7.refs_1_), channel_id=1, source_target_pairs={{0,1},{1,0},{2,3},{3,2},{4,5},{5,4},{6,7},{7,6},{8,9},{9,8},{10,11... | collective-permute-start | bytes 3833864 | tf_op jit(solution)/shard_map/ppermute | solution.py:109
  64.1 16.3 %collective-permute-start.16 = (bf16[4,192,384]{2,1,0:T(8,128)(2,1)S(1)}, bf16[4,192,384]{2,1,0:T(8,128)(2,1)S(1)}, u32[]{:S(2)}, u32[]{:S(2)}) collective-permute-start(bf16[4,192,384]{2,1,0:T(8,128)(2,1)S(1)} %constant_dynamic-update-slice_fusion.16), channel_id=1, source_target_pairs={{0,2},{1,5},{2,0},{3,7},{4,6},{5,1},{6,4},{7,3},{8,10},{9,13},{10,... | collective-permute-start | bytes 1769480 | tf_op jit(solution)/shard_map/ppermute | solution.py:109
  65.0 25.1 %collective-permute-start.13 = (bf16[8,48,1536]{2,1,0:T(8,128)(2,1)S(1)}, bf16[8,48,1536]{2,1,0:T(8,128)(2,1)S(1)}, u32[]{:S(2)}, u32[]{:S(2)}) collective-permute-start(bf16[8,48,1536]{2,1,0:T(8,128)(2,1)S(1)} %constant_dynamic-update-slice_fusion.13.refs_0_), channel_id=1, source_target_pairs={{0,4},{1,3},{2,6},{3,1},{4,0},{5,7},{6,2},{7,5},{8,12},{9,11},{10,... | collective-permute-start | bytes 3538952 | tf_op jit(solution)/shard_map/ppermute | solution.py:109
  65.7 25.0 %collective-permute-start.12 = (bf16[512,768]{1,0:T(8,128)(2,1)S(1)}, bf16[512,768]{1,0:T(8,128)(2,1)S(1)}, u32[]{:S(2)}, u32[]{:S(2)}) collective-permute-start(bf16[512,768]{1,0:T(8,128)(2,1)S(1)} %get-tuple-element.179), channel_id=1, source_target_pairs={{0,8},{1,9},{2,10},{3,11},{4,12},{5,13},{6,14},{7,15},{8,0},{9,1},... | collective-permute-start | bytes 2359304 | tf_op jit(solution)/shard_map/ppermute | solution.py:109
  80.5 18.4 %collective-permute-start.17 = (bf16[8,192,384]{2,1,0:T(8,128)(2,1)S(1)}, bf16[8,192,384]{2,1,0:T(8,128)(2,1)S(1)}, u32[]{:S(2)}, u32[]{:S(2)}) collective-permute-start(bf16[8,192,384]{2,1,0:T(8,128)(2,1)S(1)} %constant_dynamic-update-slice_fusion.18.refs_0_), channel_id=1, source_target_pairs={{0,4},{1,3},{2,6},{3,1},{4,0},{5,7},{6,2},{7,5},{8,12},{9,11},{10,... | collective-permute-start | bytes 3538952 | tf_op jit(solution)/shard_map/ppermute | solution.py:109
  90.1 9.6 %collective-permute-start.15 = (bf16[8,48,1536]{2,1,0:T(8,128)(2,1)S(1)}, bf16[8,48,1536]{2,1,0:T(8,128)(2,1)S(1)}, u32[]{:S(2)}, u32[]{:S(2)}) collective-permute-start(bf16[8,48,1536]{2,1,0:T(8,128)(2,1)S(1)} %collective-permute-done.13.refs_1_), channel_id=1, source_target_pairs={{0,1},{1,0},{2,3},{3,2},{4,5},{5,4},{6,7},{7,6},{8,9},{9,8},{10,11... | collective-permute-start | bytes 3538952 | tf_op jit(solution)/shard_map/ppermute | solution.py:109
  90.2 9.5 %collective-permute-start.14 = (bf16[8,48,1536]{2,1,0:T(8,128)(2,1)S(1)}, bf16[8,48,1536]{2,1,0:T(8,128)(2,1)S(1)}, u32[]{:S(2)}, u32[]{:S(2)}) collective-permute-start(bf16[8,48,1536]{2,1,0:T(8,128)(2,1)S(1)} %constant_dynamic-update-slice_fusion.13.refs_0_), channel_id=1, source_target_pairs={{0,1},{1,0},{2,3},{3,2},{4,5},{5,4},{6,7},{7,6},{8,9},{9,8},{10,11... | collective-permute-start | bytes 3538952 | tf_op jit(solution)/shard_map/ppermute | solution.py:109
  98.9 8.5 %collective-permute-start.19 = (bf16[8,192,384]{2,1,0:T(8,128)(2,1)S(1)}, bf16[8,192,384]{2,1,0:T(8,128)(2,1)S(1)}, u32[]{:S(2)}, u32[]{:S(2)}) collective-permute-start(bf16[8,192,384]{2,1,0:T(8,128)(2,1)S(1)} %collective-permute-done.17.refs_1_), channel_id=1, source_target_pairs={{0,1},{1,0},{2,3},{3,2},{4,5},{5,4},{6,7},{7,6},{8,9},{9,8},{10,11... | collective-permute-start | bytes 3538952 | tf_op jit(solution)/shard_map/ppermute | solution.py:109
  99.0 8.4 %collective-permute-start.18 = (bf16[8,192,384]{2,1,0:T(8,128)(2,1)S(1)}, bf16[8,192,384]{2,1,0:T(8,128)(2,1)S(1)}, u32[]{:S(2)}, u32[]{:S(2)}) collective-permute-start(bf16[8,192,384]{2,1,0:T(8,128)(2,1)S(1)} %constant_dynamic-update-slice_fusion.18.refs_0_), channel_id=1, source_target_pairs={{0,1},{1,0},{2,3},{3,2},{4,5},{5,4},{6,7},{7,6},{8,9},{9,8},{10,11... | collective-permute-start | bytes 3538952 | tf_op jit(solution)/shard_map/ppermute | solution.py:109
  99.6 38.6 %collective-permute-start.27 = (bf16[512,768]{1,0:T(8,128)(2,1)S(1)}, bf16[512,768]{1,0:T(8,128)(2,1)S(1)}, u32[]{:S(2)}, u32[]{:S(2)}) collective-permute-start(bf16[512,768]{1,0:T(8,128)(2,1)S(1)} %get-tuple-element.210), channel_id=1, source_target_pairs={{0,8},{1,9},{2,10},{3,11},{4,12},{5,13},{6,14},{7,15},{8,0},{9,1},... | collective-permute-start | bytes 2359304 | tf_op jit(solution)/shard_map/ppermute | solution.py:109
  111.1 11.8 %collective-permute-start.20 = (bf16[32,896]{1,0:T(8,128)(2,1)S(1)}, bf16[32,896]{1,0:T(8,128)(2,1)S(1)}, u32[]{:S(2)}, u32[]{:S(2)}) collective-permute-start(bf16[32,896]{1,0:T(8,128)(2,1)S(1)} %first_rows.1.refs_0_), channel_id=1, source_target_pairs={{0,8},{1,9},{2,10},{3,11},{4,12},{5,13},{6,14},{7,15},{8,0},{9,1},... | collective-permute-start | bytes 172040 | tf_op jit(solution)/shard_map/ppermute | solution.py:109
  112.8 10.1 %collective-permute-start.21 = (bf16[32,896]{1,0:T(8,128)(2,1)S(1)}, bf16[32,896]{1,0:T(8,128)(2,1)S(1)}, u32[]{:S(2)}, u32[]{:S(2)}) collective-permute-start(bf16[32,896]{1,0:T(8,128)(2,1)S(1)} %first_rows.1.refs_0_), channel_id=1, source_target_pairs={{0,16},{1,17},{2,18},{3,19},{4,20},{5,21},{6,22},{7,23},{8,24},{9,... | collective-permute-start | bytes 172040 | tf_op jit(solution)/shard_map/ppermute | solution.py:109
  113.0 10.0 %collective-permute-start.22 = (bf16[32,896]{1,0:T(8,128)(2,1)S(1)}, bf16[32,896]{1,0:T(8,128)(2,1)S(1)}, u32[]{:S(2)}, u32[]{:S(2)}) collective-permute-start(bf16[32,896]{1,0:T(8,128)(2,1)S(1)} %first_rows.1.refs_0_), channel_id=1, source_target_pairs={{0,24},{1,25},{2,26},{3,27},{4,28},{5,29},{6,30},{7,31},{8,16},{9,... | collective-permute-start | bytes 172040 | tf_op jit(solution)/shard_map/ppermute | solution.py:109
  123.8 13.8 %collective-permute-start.24 = (bf16[2,48,896]{2,1,0:T(8,128)(2,1)S(1)}, bf16[2,48,896]{2,1,0:T(8,128)(2,1)S(1)}, u32[]{:S(2)}, u32[]{:S(2)}) collective-permute-start(bf16[2,48,896]{2,1,0:T(8,128)(2,1)S(1)} %pack.1.refs_0_), channel_id=1, source_target_pairs={{0,2},{1,3},{2,0},{3,1},{4,6},{5,7},{6,4},{7,5},{8,10},{9,11},{10,... | collective-permute-start | bytes 516104 | tf_op jit(solution)/shard_map/ppermute | solution.py:109
  124.6 13.0 %collective-permute-start.25 = (bf16[2,48,896]{2,1,0:T(8,128)(2,1)S(1)}, bf16[2,48,896]{2,1,0:T(8,128)(2,1)S(1)}, u32[]{:S(2)}, u32[]{:S(2)}) collective-permute-start(bf16[2,48,896]{2,1,0:T(8,128)(2,1)S(1)} %pack.1.refs_0_), channel_id=1, source_target_pairs={{0,4},{1,5},{2,6},{3,7},{4,0},{5,1},{6,2},{7,3},{8,12},{9,13},{10,... | collective-permute-start | bytes 516104 | tf_op jit(solution)/shard_map/ppermute | solution.py:109
  126.1 11.5 %collective-permute-start.26 = (bf16[2,48,896]{2,1,0:T(8,128)(2,1)S(1)}, bf16[2,48,896]{2,1,0:T(8,128)(2,1)S(1)}, u32[]{:S(2)}, u32[]{:S(2)}) collective-permute-start(bf16[2,48,896]{2,1,0:T(8,128)(2,1)S(1)} %pack.1.refs_0_), channel_id=1, source_target_pairs={{0,6},{1,7},{2,4},{3,5},{4,2},{5,3},{6,0},{7,1},{8,14},{9,15},{10,... | collective-permute-start | bytes 516104 | tf_op jit(solution)/shard_map/ppermute | solution.py:109
  138.4 34.5 %collective-permute-start.23 = (bf16[512,768]{1,0:T(8,128)(2,1)S(1)}, bf16[512,768]{1,0:T(8,128)(2,1)S(1)}, u32[]{:S(2)}, u32[]{:S(2)}) collective-permute-start(bf16[512,768]{1,0:T(8,128)(2,1)S(1)} %get-tuple-element.205), channel_id=1, source_target_pairs={{0,8},{1,9},{2,10},{3,11},{4,12},{5,13},{6,14},{7,15},{8,0},{9,1},... | collective-permute-start | bytes 2359304 | tf_op jit(solution)/shard_map/ppermute | solution.py:109
  153.2 20.1 %collective-permute-start.29 = (bf16[16,192,384]{2,1,0:T(8,128)(2,1)S(1)}, bf16[16,192,384]{2,1,0:T(8,128)(2,1)S(1)}, u32[]{:S(2)}, u32[]{:S(2)}) collective-permute-start(bf16[16,192,384]{2,1,0:T(8,128)(2,1)S(1)} %bitcast.45), channel_id=1, source_target_pairs={{0,1},{1,0},{2,3},{3,2},{4,5},{5,4},{6,7},{7,6},{8,9},{9,8},{10,11... | collective-permute-start | bytes 7077896 | tf_op jit(solution)/shard_map/ppermute | solution.py:109
  172.9 8.7 %collective-permute-start.30 = (bf16[16,48,1536]{2,1,0:T(8,128)(2,1)S(1)}, bf16[16,48,1536]{2,1,0:T(8,128)(2,1)S(1)}, u32[]{:S(2)}, u32[]{:S(2)}) collective-permute-start(bf16[16,48,1536]{2,1,0:T(8,128)(2,1)S(1)} %bitcast.44), channel_id=1, source_target_pairs={{0,1},{1,0},{2,3},{3,2},{4,5},{5,4},{6,7},{7,6},{8,9},{9,8},{10,11... | collective-permute-start | bytes 7077896 | tf_op jit(solution)/shard_map/ppermute | solution.py:109
  174.5 31.7 %collective-permute-start.31 = (bf16[8,192,384]{2,1,0:T(8,128)(2,1)S(1)}, bf16[8,192,384]{2,1,0:T(8,128)(2,1)S(1)}, u32[]{:S(2)}, u32[]{:S(2)}) collective-permute-start(bf16[8,192,384]{2,1,0:T(8,128)(2,1)S(1)} %get-tuple-element.227), channel_id=1, source_target_pairs={{0,2},{1,5},{2,0},{3,7},{4,6},{5,1},{6,4},{7,3},{8,10},{9,13},{10,... | collective-permute-start | bytes 3538952 | tf_op jit(solution)/shard_map/ppermute | solution.py:109
  182.8 25.9 %collective-permute-start.32 = (bf16[8,48,1536]{2,1,0:T(8,128)(2,1)S(1)}, bf16[8,48,1536]{2,1,0:T(8,128)(2,1)S(1)}, u32[]{:S(2)}, u32[]{:S(2)}) collective-permute-start(bf16[8,48,1536]{2,1,0:T(8,128)(2,1)S(1)} %get-tuple-element.234), channel_id=1, source_target_pairs={{0,2},{1,5},{2,0},{3,7},{4,6},{5,1},{6,4},{7,3},{8,10},{9,13},{10,... | collective-permute-start | bytes 3538952 | tf_op jit(solution)/shard_map/ppermute | solution.py:109
  194.8 19.2 %collective-permute-start.33 = (bf16[512,768]{1,0:T(8,128)(2,1)S(1)}, bf16[512,768]{1,0:T(8,128)(2,1)}, u32[]{:S(2)}, u32[]{:S(2)}) collective-permute-start(bf16[512,768]{1,0:T(8,128)(2,1)S(1)} %get-tuple-element.239), channel_id=1, source_target_pairs={{0,8},{1,9},{2,10},{3,11},{4,12},{5,13},{6,14},{7,15},{8,0},{9,1},... | collective-permute-start | bytes 2359304 | tf_op jit(solution)/shard_map/ppermute | solution.py:109
  206.2 14.2 %collective-permute-start.35 = (bf16[16,48,1152]{2,1,0:T(8,128)(2,1)S(1)}, bf16[16,48,1152]{2,1,0:T(8,128)(2,1)S(1)}, u32[]{:S(2)}, u32[]{:S(2)}) collective-permute-start(bf16[16,48,1152]{2,1,0:T(8,128)(2,1)S(1)} %bitcast.46), channel_id=1, source_target_pairs={{0,1},{1,0},{2,3},{3,2},{4,5},{5,4},{6,7},{7,6},{8,9},{9,8},{10,11... | collective-permute-start | bytes 5308424 | tf_op jit(solution)/shard_map/ppermute | solution.py:109
  207.1 10.9 %collective-permute-start.34 = (bf16[4,192,384]{2,1,0:T(8,128)(2,1)S(1)}, bf16[4,192,384]{2,1,0:T(8,128)(2,1)S(1)}, u32[]{:S(2)}, u32[]{:S(2)}) collective-permute-start(bf16[4,192,384]{2,1,0:T(8,128)(2,1)S(1)} %get-tuple-element.245), channel_id=1, source_target_pairs={{0,4},{1,3},{2,6},{3,1},{4,0},{5,7},{6,2},{7,5},{8,12},{9,11},{10,... | collective-permute-start | bytes 1769480 | tf_op jit(solution)/shard_map/ppermute | solution.py:109
  209.5 13.8 %collective-permute-start.36 = (bf16[4,48,1536]{2,1,0:T(8,128)(2,1)S(1)}, bf16[4,48,1536]{2,1,0:T(8,128)(2,1)S(1)}, u32[]{:S(2)}, u32[]{:S(2)}) collective-permute-start(bf16[4,48,1536]{2,1,0:T(8,128)(2,1)S(1)} %get-tuple-element.248), channel_id=1, source_target_pairs={{0,4},{1,3},{2,6},{3,1},{4,0},{5,7},{6,2},{7,5},{8,12},{9,11},{10,... | collective-permute-start | bytes 1769480 | tf_op jit(solution)/shard_map/ppermute | solution.py:109
  218.7 22.7 %collective-permute-start.39 = (bf16[2,192,384]{2,1,0:T(8,128)(2,1)S(1)}, bf16[2,192,384]{2,1,0:T(8,128)(2,1)S(1)}, u32[]{:S(2)}, u32[]{:S(2)}) collective-permute-start(bf16[2,192,384]{2,1,0:T(8,128)(2,1)S(1)} %get-tuple-element.253), channel_id=1, source_target_pairs={{0,16},{1,17},{2,18},{3,19},{4,20},{5,21},{6,22},{7,23},{8,24},{9,... | collective-permute-start | bytes 884744 | tf_op jit(solution)/shard_map/ppermute | solution.py:109
  221.3 14.4 %collective-permute-start.37 = (bf16[8,48,1152]{2,1,0:T(8,128)(2,1)S(1)}, bf16[8,48,1152]{2,1,0:T(8,128)(2,1)S(1)}, u32[]{:S(2)}, u32[]{:S(2)}) collective-permute-start(bf16[8,48,1152]{2,1,0:T(8,128)(2,1)S(1)} %get-tuple-element.256), channel_id=1, source_target_pairs={{0,2},{1,5},{2,0},{3,7},{4,6},{5,1},{6,4},{7,3},{8,10},{9,13},{10,... | collective-permute-start | bytes 2654216 | tf_op jit(solution)/shard_map/ppermute | solution.py:109
  224.0 22.3 %collective-permute-start.40 = (bf16[2,48,1536]{2,1,0:T(8,128)(2,1)S(1)}, bf16[2,48,1536]{2,1,0:T(8,128)(2,1)S(1)}, u32[]{:S(2)}, u32[]{:S(2)}) collective-permute-start(bf16[2,48,1536]{2,1,0:T(8,128)(2,1)S(1)} %get-tuple-element.259), channel_id=1, source_target_pairs={{0,16},{1,17},{2,18},{3,19},{4,20},{5,21},{6,22},{7,23},{8,24},{9,... | collective-permute-start | bytes 884744 | tf_op jit(solution)/shard_map/ppermute | solution.py:109
  236.5 12.3 %collective-permute-start.41 = (bf16[4,48,1152]{2,1,0:T(8,128)(2,1)S(1)}, bf16[4,48,1152]{2,1,0:T(8,128)(2,1)S(1)}, u32[]{:S(2)}, u32[]{:S(2)}) collective-permute-start(bf16[4,48,1152]{2,1,0:T(8,128)(2,1)S(1)} %get-tuple-element.266), channel_id=1, source_target_pairs={{0,4},{1,3},{2,6},{3,1},{4,0},{5,7},{6,2},{7,5},{8,12},{9,11},{10,... | collective-permute-start | bytes 1327112 | tf_op jit(solution)/shard_map/ppermute | solution.py:109
  238.8 11.6 %collective-permute-start.42 = (bf16[8,48,512]{2,1,0:T(8,128)(2,1)S(1)}, bf16[8,48,512]{2,1,0:T(8,128)(2,1)S(1)}, u32[]{:S(2)}, u32[]{:S(2)}) collective-permute-start(bf16[8,48,512]{2,1,0:T(8,128)(2,1)S(1)} %get-tuple-element.269), channel_id=1, source_target_pairs={{0,2},{1,5},{2,0},{3,7},{4,6},{5,1},{6,4},{7,3},{8,10},{9,13},{10,... | collective-permute-start | bytes 1179656 | tf_op jit(solution)/shard_map/ppermute | solution.py:109
  242.0 9.7 %collective-permute-start.43 = (bf16[1,192,384]{2,1,0:T(8,128)(2,1)S(1)}, bf16[1,192,384]{2,1,0:T(8,128)(2,1)S(1)}, u32[]{:S(2)}, u32[]{:S(2)}) collective-permute-start(bf16[1,192,384]{2,1,0:T(8,128)(2,1)S(1)} %get-tuple-element.272), channel_id=1, source_target_pairs={{0,8},{1,9},{2,10},{3,11},{4,12},{5,13},{6,14},{7,15},{8,0},{9,1},... | collective-permute-start | bytes 442376 | tf_op jit(solution)/shard_map/ppermute | solution.py:109
  247.0 8.9 %collective-permute-start.44 = (bf16[1,48,1536]{2,1,0:T(8,128)(2,1)S(1)}, bf16[1,48,1536]{2,1,0:T(8,128)(2,1)S(1)}, u32[]{:S(2)}, u32[]{:S(2)}) collective-permute-start(bf16[1,48,1536]{2,1,0:T(8,128)(2,1)S(1)} %get-tuple-element.275), channel_id=1, source_target_pairs={{0,8},{1,9},{2,10},{3,11},{4,12},{5,13},{6,14},{7,15},{8,0},{9,1},... | collective-permute-start | bytes 442376 | tf_op jit(solution)/shard_map/ppermute | solution.py:109
  249.5 10.6 %collective-permute-start.45 = (bf16[2,48,1152]{2,1,0:T(8,128)(2,1)S(1)}, bf16[2,48,1152]{2,1,0:T(8,128)(2,1)S(1)}, u32[]{:S(2)}, u32[]{:S(2)}) collective-permute-start(bf16[2,48,1152]{2,1,0:T(8,128)(2,1)S(1)} %get-tuple-element.278), channel_id=1, source_target_pairs={{0,16},{1,17},{2,18},{3,19},{4,20},{5,21},{6,22},{7,23},{8,24},{9,... | collective-permute-start | bytes 663560 | tf_op jit(solution)/shard_map/ppermute | solution.py:109
  252.3 11.1 %collective-permute-start.47 = (bf16[2,192,384]{2,1,0:T(8,128)(2,1)S(1)}, bf16[2,192,384]{2,1,0:T(8,128)(2,1)S(1)}, u32[]{:S(2)}, u32[]{:S(2)}) collective-permute-start(bf16[2,192,384]{2,1,0:T(8,128)(2,1)S(1)} %add_last.4.refs_0_), channel_id=1, source_target_pairs={{0,1},{1,0},{2,3},{3,2},{4,5},{5,4},{6,7},{7,6},{8,9},{9,8},{10,11... | collective-permute-start | bytes 884744 | tf_op jit(solution)/shard_map/ppermute | solution.py:109
  252.4 8.4 %collective-permute-start.46 = (bf16[4,48,512]{2,1,0:T(8,128)(2,1)S(1)}, bf16[4,48,512]{2,1,0:T(8,128)(2,1)S(1)}, u32[]{:S(2)}, u32[]{:S(2)}) collective-permute-start(bf16[4,48,512]{2,1,0:T(8,128)(2,1)S(1)} %get-tuple-element.281), channel_id=1, source_target_pairs={{0,4},{1,3},{2,6},{3,1},{4,0},{5,7},{6,2},{7,5},{8,12},{9,11},{10,... | collective-permute-start | bytes 589832 | tf_op jit(solution)/shard_map/ppermute | solution.py:109
  257.3 7.7 %collective-permute-start.48 = (bf16[2,48,1536]{2,1,0:T(8,128)(2,1)S(1)}, bf16[2,48,1536]{2,1,0:T(8,128)(2,1)S(1)}, u32[]{:S(2)}, u32[]{:S(2)}) collective-permute-start(bf16[2,48,1536]{2,1,0:T(8,128)(2,1)S(1)} %add_last.5.refs_0_), channel_id=1, source_target_pairs={{0,1},{1,0},{2,3},{3,2},{4,5},{5,4},{6,7},{7,6},{8,9},{9,8},{10,11... | collective-permute-start | bytes 884744 | tf_op jit(solution)/shard_map/ppermute | solution.py:109
  260.7 11.9 %collective-permute-start.50 = (bf16[1,48,1152]{2,1,0:T(8,128)(2,1)S(1)}, bf16[1,48,1152]{2,1,0:T(8,128)(2,1)S(1)}, u32[]{:S(2)}, u32[]{:S(2)}) collective-permute-start(bf16[1,48,1152]{2,1,0:T(8,128)(2,1)S(1)} %get-tuple-element.286), channel_id=1, source_target_pairs={{0,8},{1,9},{2,10},{3,11},{4,12},{5,13},{6,14},{7,15},{8,0},{9,1},... | collective-permute-start | bytes 331784 | tf_op jit(solution)/shard_map/ppermute | solution.py:109
  (30 other events, 196.7 us)

commit v6 on v5

--- a/solution.py
+++ b/solution.py
@@ -151,8 +151,7 @@
     core, tower = (where_ref[1], where_ref[2])
     spare = full_ref.shape[2] - AT_VEC
 
-    def turned(ref, t, at):
-        rows = ref[t][0].astype(F32)
+    def turned(rows, at):
         i = lax.broadcasted_iota(jnp.int32, (rows.shape[0], spare), 0)
         j = lax.broadcasted_iota(jnp.int32, (rows.shape[0], spare), 1)
         return t_dot(rows.astype(BF), jnp.where(i + at == j, 1.0, 0.0).astype(BF))
@@ -160,7 +159,10 @@
         t = pl.ds(tower if n == 0 else 1 - tower, 1)
         full_ref[:, :, :AT_OUT] = qkv_ref[t]
         full_ref[:, :, AT_OUT:AT_VEC] = out_ref[t]
-        full_ref[0, :, AT_VEC:] = (turned(bias_ref, t, 0) + turned(gain_ref, t, bias_ref.shape[1])).astype(BF)
+        biases = bias_ref[...].astype(F32)
+        biases = jnp.where(tower == n, biases[:, 0, :], biases[:, 1, :])
+        gains = gain_ref[t][0].astype(F32)
+        full_ref[0, :, AT_VEC:] = (turned(biases, 0) + turned(gains, biases.shape[0])).astype(BF)
         for c, ref in enumerate((full_ref, up_ref, down_ref)):
             put = outs[2 * c + n]
 
@@ -303,7 +305,7 @@
         return out
 
     def three(self):
-        self.line()
+        self.out = self.line()
 
     def four(self):
         while self.kk.shape[0] > 1:
@@ -342,11 +344,15 @@
 def turn(part_ref, lanes, at, bias_ref, gain_ref):
     for t in range(2):
         columns = part_ref[t, :, lanes]
-        for ref, start in ((bias_ref, 0), (gain_ref, bias_ref.shape[1])):
-            n = ref.shape[1]
+        count = bias_ref.shape[0]
+        for start, n in ((0, count), (count, gain_ref.shape[1])):
             i = lax.broadcasted_iota(jnp.int32, (n, columns.shape[1]), 0)
             j = lax.broadcasted_iota(jnp.int32, (n, columns.shape[1]), 1)
-            ref[t] = dot_t(jnp.where(i + start == j + at, 1.0, 0.0).astype(BF), columns)
+            rows = dot_t(jnp.where(i + start == j + at, 1.0, 0.0).astype(BF), columns)
+            if start == 0:
+                bias_ref[:, t, :] = rows
+            else:
+                gain_ref[t] = rows
 
 
 def finish(plan, order, chunks, spans, shapes, vec=-1):
@@ -818,7 +824,7 @@
         b = jnp.where(tower == 0, back, own)
         return (a.reshape(query_tokens.shape), b.reshape(passage_tokens.shape))
     order = Order(where)
-    mine, other, mine2, other2, mine3, other3 = shards_of(plan, order, w_qkv, w_out, biases, gains, w_up, w_down)
+    mine, other, mine2, other2, mine3, other3 = shards_of(plan, order, w_qkv, w_out, jnp.swapaxes(biases, 0, 1), gains, w_up, w_down)
     z1 = gather_line(plan, mine, other)
     both2 = jnp.concatenate([mine2, send(other2, swap)], 0)
     both3 = jnp.concatenate([mine3, send(other3, swap)], 0)
@@ -886,10 +892,10 @@
     b_part.two()
     down_part.last()
     up_part.last()
+    b_part.three()
     a_part.four()
-    b_part.three()
-    grad_down, = finish(plan, order, [down_part], [[(0, D, 0, 0)]], [w_down.shape])
-    grad_up, = finish(plan, order, [up_part], [[(0, FF, 0, 0)]], [w_up.shape])
+    (grad_down,) = finish(plan, order, [down_part], [[(0, D, 0, 0)]], [w_down.shape])
+    (grad_up,) = finish(plan, order, [up_part], [[(0, FF, 0, 0)]], [w_up.shape])
     b_part.four()
     a_part.last()
     b_part.last()
@@ -898,9 +904,9 @@
     qa, qb = (split * 128, D - split * 128)
     spans_a = [(0, D, 1, 0)] + [(D + j * qa, qa, 0, j * D) for j in range(3)]
     spans_b = [(j * qb, qb, 0, j * D + qa) for j in range(3)] + [(3 * qb, 128, 2, 0)]
-    shapes = [w_qkv.shape, w_out.shape, biases.shape, gains.shape]
+    shapes = [w_qkv.shape, w_out.shape, (biases.shape[1], 2, biases.shape[2]), gains.shape]
     grads = finish(plan, order, [a_part, b_part], [spans_a, spans_b], shapes, 2)
-    return (query_out, passage_out, query_grad, passage_grad, query_loss, grads[0], grads[1], grad_up, grad_down, grads[2], grads[3])
+    return (query_out, passage_out, query_grad, passage_grad, query_loss, grads[0], grads[1], grad_up, grad_down, jnp.swapaxes(grads[2], 0, 1), grads[3])
 
 
 def solution(mesh):

time: 282 us -> 277 us (0.982)
    unnamed x58 -> x56, local copies, waits for them, and re-layouts: 6.05 us -> 4.19 us
  transfers between devices with their start and end apart: 54 -> 54, of which waited for: 14 -> 14; matrix products, arithmetic and copies ran while one was open for 2% -> 2% of each run, Pallas kernels for 48% -> 49%
where the time goes in v6:
time: 277 us; the launch traced here: 274 us
  Pallas kernels  137 us (49%)
  waiting for transfers between devices  80.5 us (29%)
  starting transfers between devices  43.5 us (16%)
  local copies, waits for them, and re-layouts  5.72 us (2%)
  other arithmetic  4.87 us (2%)
    ppermute x54, waiting for transfers between devices, send(): return lax.ppermute(v, AXES, pairs)  80.5 us
    ppermute x54, starting transfers between devices, send(): return lax.ppermute(v, AXES, pairs)  43.5 us
    pallas_call x1, Pallas kernels, gelu_back(): pl.pallas_call(partial(gelu_back_kernel, reps, column), out_shape=(shape(...  19.5 us
    pallas_call x22, Pallas kernels, in_vmem(): pl.pallas_call(kernel, out_shape=tuple((shape(*o) for o in outs)), in_spe...  19.4 us
    pallas_call x2, Pallas kernels, attend(): pl.pallas_call(partial(attend_kernel, part), grid=(steps,), out_shape=(fa...  16.2 us
    pallas_call x2, Pallas kernels, up(): pl.pallas_call(partial(up_kernel, first), grid=(steps,), out_shape=(shape...  13.1 us
    pallas_call x1, Pallas kernels, top(): pl.pallas_call(top_kernel, grid=(FF // D,), out_shape=(far((rows, D), F32...  11 us
    pallas_call x1, Pallas kernels, far_back(): pl.pallas_call(partial(far_back_kernel, count), grid=(steps,), out_shape=...  10.8 us
  transfers between devices with their start and end apart: 54, of which 14 were waited for; matrix products, arithmetic and copies ran while one was open for 2% of the time, Pallas kernels for 49%

profile of v6, /device:TPU:0, one launch (start us, length us, event | category | flops | bytes accessed | tf_op | source)
XLA Modules:
  0.0 274.1 jit_solution(105526728516839356)
XLA Ops:
  0.7 1.8 shards.1
  2.5 3.1 %collective-permute-start = (bf16[1,48,1664]{2,1,0:T(8,128)(2,1)S(1)}, bf16[1,48,1664]{2,1,0:T(8,128)(2,1)S(1)}, u32[]{:S(2)}, u32[]{:S(2)}) collective-permute-start(bf16[1,48,1664]{2,1,0:T(8,128)(2,1)S(1)} %get-tuple-element.159), channel_id=1, source_target_pairs={{0,8},{1,9},{2,10},{3,11},{4,12},{5,13},{6,14},{7,15},{8,0},{9,1},... | collective-permute-start | bytes 479240 | tf_op jit(solution)/shard_map/ppermute | solution.py:109
  5.6 2.5 collective-permute-start.2
  8.2 1.8 collective-permute-start.4
  10.3 12.1 %collective-permute-done.1 = bf16[1,48,1664]{2,1,0:T(8,128)(2,1)S(1)} collective-permute-done((bf16[1,48,1664]{2,1,0:T(8,128)(2,1)S(1)}, bf16[1,48,1664]{2,1,0:T(8,128)(2,1)S(1)}, u32[]{:S(2)}, u32[]{:S(2)}) %collective-permute-start.1) | collective-permute-done | bytes 159776 | tf_op jit(solution)/shard_map/ppermute | solution.py:109
  22.5 1.6 collective-permute-start.3
  24.2 14.6 %collective-permute-done.5 = bf16[2,48,1536]{2,1,0:T(8,128)(2,1)S(1)} collective-permute-done((bf16[2,48,1536]{2,1,0:T(8,128)(2,1)S(1)}, bf16[2,48,1536]{2,1,0:T(8,128)(2,1)S(1)}, u32[]{:S(2)}, u32[]{:S(2)}) %collective-permute-start.5) | collective-permute-done | bytes 294944 | tf_op jit(solution)/shard_map/ppermute | solution.py:109
  39.6 1.5 collective-permute-start.10
  41.1 21.6 %collective-permute-done.7.refs_1_ = bf16[8,48,1664]{2,1,0:T(8,128)(2,1)S(1)} collective-permute-done((bf16[8,48,1664]{2,1,0:T(8,128)(2,1)S(1)}, bf16[8,48,1664]{2,1,0:T(8,128)(2,1)S(1)}, u32[]{:S(2)}, u32[]{:S(2)}) %collective-permute-start.7) | collective-permute-done | bytes 1277984 | tf_op jit(solution)/shard_map/ppermute | solution.py:109
  64.6 14.5 %collective-permute-done.16 = bf16[4,192,384]{2,1,0:T(8,128)(2,1)S(1)} collective-permute-done((bf16[4,192,384]{2,1,0:T(8,128)(2,1)S(1)}, bf16[4,192,384]{2,1,0:T(8,128)(2,1)S(1)}, u32[]{:S(2)}, u32[]{:S(2)}) %collective-permute-start.16) | collective-permute-done | bytes 589856 | tf_op jit(solution)/shard_map/ppermute | solution.py:109
  80.3 8.5 %attend.2 = (bf16[1024,2304]{1,0:T(8,128)(2,1)}, bf16[8,6,128,256]{3,2,1,0:T(8,128)(2,1)}, bf16[1024,768]{1,0:T(8,128)(2,1)}, f32[1024,768]{1,0:T(8,128)}, f32[1...) custom-call(s32[4]{0:T(128)S(1)} %pad_add_fusion.where_ref, ...), custom_call_target="tpu_custom_call" | custom-call | flops 7000000000 | bytes 21000000 | tf_op jit(solution)/shard_map/attend/pallas_call | solution.py:438
  89.4 7.7 %attend.3 = (bf16[1024,2304]{1,0:T(8,128)(2,1)}, bf16[8,6,128,256]{3,2,1,0:T(8,128)(2,1)}, bf16[1024,768]{1,0:T(8,128)(2,1)}, f32[1024,768]{1,0:T(8,128)}, f32[1...) custom-call(s32[4]{0:T(128)S(1)} %pad_add_fusion.where_ref, ...), custom_call_target="tpu_custom_call", output_to_operand_aliasing={{0}: (3, {}), {1}: (4, {}), {2}: (5, {}), {3}: (6, {}), {4}... | custom-call | flops 7000000000 | bytes 21000000 | tf_op jit(solution)/shard_map/attend/pallas_call | solution.py:438
  99.7 6.4 %up.2 = (bf16[1024,3072]{1,0:T(8,128)(2,1)S(1)}, bf16[1024,3072]{1,0:T(8,128)(2,1)}) custom-call(s32[4]{0:T(128)S(1)} %pad_add_fusion.where_ref, bf16[1024,768]{1,0:T(8,128)(2,1)S(1)} %copy-done.8, bf16[768,3072]{1,0:T(8,128)(2,1)S(1)} %bitcast.39, f32[128,768]{1,0:T(8,128)S(1)} %get-tuple-element.186.vec_ref), custom_call_target="tpu_custom_call" | custom-call | flops 8000000000 | bytes 24000000 | tf_op jit(solution)/shard_map/up/pallas_call | solution.py:461
  107.2 2.6 first_rows.1.refs_0_
  109.8 1.7 collective-permute-start.20
  111.7 2.6 collective-permute-start.22
  114.3 6.7 %up.3 = (bf16[1024,3072]{1,0:T(8,128)(2,1)S(1)}, bf16[1024,3072]{1,0:T(8,128)(2,1)}) custom-call(s32[4]{0:T(128)S(1)} %pad_add_fusion.where_ref, bf16[1024,768]{1,0:T(8,128)(2,1)S(1)} %copy-done.8, bf16[768,3072]{1,0:T(8,128)(2,1)S(1)} %bitcast.41, f32[128,768]{1,0:T(8,128)S(1)} %get-tuple-element.186.vec_ref, ...), custom_call_target="tpu_custom_call", output_to_operand_aliasing={{0}: (4, {}), {1}: (5, {})} | custom-call | flops 8000000000 | bytes 24000000 | tf_op jit(solution)/shard_map/up/pallas_call | solution.py:461
  123.3 1.5 collective-permute-start.25
  126.0 8.6 %down.1 = (bf16[512,768]{1,0:T(8,128)(2,1)}, bf16[512,768]{1,0:T(8,128)(2,1)S(1)}, f32[1024,768]{1,0:T(8,128)S(1)}, f32[1024,1]{1,0:T(8,128)S(1)}) custom-call(s32[4]{0:T(128)S(1)} %pad_add_fusion.where_ref, bf16[1024,3072]{1,0:T(8,128)(2,1)S(1)} %get-tuple-element.200.act_ref, bf16[3072,768]{1,0:T(8,128)(2,1)S(1)} %bitcast.44, ...), custom_call_target="tpu_custom_call" | custom-call | flops 8000000000 | bytes 24000000 | tf_op jit(solution)/shard_map/down/pallas_call | solution.py:487
  134.6 1.6 copy-done.13
  137.2 1.8 collective-permute-done.28.refs_1_
  139.1 1.9 contrast.1
  140.9 11.0 %top.1 = (f32[1024,768]{1,0:T(8,128)}, bf16[1024,768]{1,0:T(8,128)(2,1)S(1)}, f32[8,768]{1,0:T(8,128)S(1)}, bf16[3072,384]{1,0:T(8,128)(2,1)S(1)}, bf16[3072,384]{1,0:T(8,128)(2,1)S(1)}) custom-call(s32[4]{0:T(128)S(1)} %pad_add_fusion.where_ref, bf16[1024,768]{1,0:T(8,128)(2,1)S(1)} %pad_maximum_fusion.cot_ref, f32[32,768]{1,0:T(8,128)S(1)} %get-tuple-element.213.cls_ref, ...), custom_call_target="tpu_custom_call" | custom-call | flops 44000002048 | bytes 132000000 | tf_op jit(solution)/shard_map/top/pallas_call | solution.py:631
  152.1 19.5 %gelu_back.1 = (f32[1024,768]{1,0:T(8,128)S(1)}, f32[8,768]{1,0:T(8,128)S(1)}, bf16[768,1536]{1,0:T(8,128)(2,1)S(1)}, bf16[768,1536]{1,0:T(8,128)(2,1)S(1)}) custom-call(s32[4]{0:T(128)S(1)} %pad_add_fusion.where_ref, bf16[1024,768]{1,0:T(8,128)(2,1)S(1)} %get-tuple-element.216.gs_ref, bf16[3072,768]{1,0:T(8,128)(2,1)} %bitcast.45, ...), custom_call_target="tpu_custom_call" | custom-call | flops 80000000000 | bytes 240000000 | tf_op jit(solution)/shard_map/gelu_back/pallas_call | solution.py:668
  174.1 6.3 %hidden_back.1 = (bf16[1024,768]{1,0:T(8,128)(2,1)S(1)}, bf16[1024,768]{1,0:T(8,128)(2,1)S(1)}, f32[8,768]{1,0:T(8,128)S(1)}) custom-call(s32[4]{0:T(128)S(1)} %pad_add_fusion.where_ref, f32[1024,768]{1,0:T(8,128)S(1)} %get-tuple-element.221.acc_ref, f32[1024,768]{1,0:T(8,128)} %get-tuple-element.215.second_ref, f32[1024,768]{1,0:T(8,128)} %get-tuple-element.183.hat_ref, ...), custom_call_target="tpu_custom_call" | custom-call | flops 20000000000 | bytes 60000000 | tf_op jit(solution)/shard_map/hidden_back/pallas_call | solution.py:690
  181.5 1.3 collective-permute-start.32
  182.8 10.8 %far_back.1 = (bf16[512,1536]{1,0:T(8,128)(2,1)S(1)}, bf16[512,768]{1,0:T(8,128)(2,1)S(1)}, bf16[512,768]{1,0:T(8,128)(2,1)S(1)}) custom-call(s32[4]{0:T(128)S(1)} %pad_add_fusion.where_ref, bf16[1024,768]{1,0:T(8,128)(2,1)S(1)} %get-tuple-element.231.ga_ref, bf16[1024,2304]{1,0:T(8,128)(2,1)} %get-tuple-element.180.proj_ref, ...), custom_call_target="tpu_custom_call" | custom-call | flops 44000002048 | bytes 132000000 | tf_op jit(solution)/shard_map/far_back/pallas_call | solution.py:797
  193.7 5.5 %attend_back.2.near_ref.first_near_ref.a_ref = bf16[512,1536]{1,0:T(8,128)(2,1)S(1)} custom-call(s32[4]{0:T(128)S(1)} %pad_add_fusion.where_ref, bf16[1024,768]{1,0:T(8,128)(2,1)S(1)} %get-tuple-element.231.ga_ref, bf16[1024,2304]{1,0:T(8,128)(2,1)} %get-tuple-element.180.proj_ref, bf16[8,6,128,256]{3,2,1,0:T(8,128)(2,1)} %get-tuple-element.181.probs_ref), custom_call_target="tpu_custom_call" | custom-call | flops 20000000000 | bytes 60000000 | tf_op jit(solution)/shard_map/attend_back/pallas_call | solution.py:732
  199.2 5.6 %first_weights.1 = (bf16[768,1152]{1,0:T(8,128)(2,1)S(1)}, bf16[768,1152]{1,0:T(8,128)(2,1)S(1)}) custom-call(s32[4]{0:T(128)S(1)} %pad_add_fusion.where_ref, bf16[512,768]{1,0:T(8,128)(2,1)S(1)} %copy-done.4, bf16[512,768]{1,0:T(8,128)(2,1)S(1)} %copy-done.6, bf16[512,1536]{1,0:T(8,128)(2,1)S(1)} %attend_back.2.near_ref.first_near_ref.a_ref, ...), custom_call_target="tpu_custom_call" | custom-call | flops 20000000000 | bytes 60000000 | tf_op jit(solution)/shard_map/first_weights/pallas_call | solution.py:775
  205.8 1.6 collective-permute-start.34
  208.8 4.0 %collective-permute-done.33 = bf16[512,768]{1,0:T(8,128)(2,1)} collective-permute-done((bf16[512,768]{1,0:T(8,128)(2,1)S(1)}, bf16[512,768]{1,0:T(8,128)(2,1)}, u32[]{:S(2)}, u32[]{:S(2)}) %collective-permute-start.33) | collective-permute-done | bytes 786464 | tf_op jit(solution)/shard_map/ppermute | solution.py:109
  212.7 3.9 %attend_back.3.near_ref.b_ref = bf16[512,768]{1,0:T(8,128)(2,1)S(1)} custom-call(s32[4]{0:T(128)S(1)} %pad_add_fusion.where_ref, bf16[1024,768]{1,0:T(8,128)(2,1)S(1)} %get-tuple-element.231.ga_ref, bf16[1024,2304]{1,0:T(8,128)(2,1)} %get-tuple-element.180.proj_ref, bf16[8,6,128,256]{3,2,1,0:T(8,128)(2,1)} %get-tuple-element.181.probs_ref), custom_call_target="tpu_custom_call" | custom-call | flops 10000000000 | bytes 30000000 | tf_op jit(solution)/shard_map/attend_back/pallas_call | solution.py:732
  217.4 1.6 collective-permute-start.39
  222.7 4.7 %collective-permute-start.40 = (bf16[2,48,1536]{2,1,0:T(8,128)(2,1)S(1)}, bf16[2,48,1536]{2,1,0:T(8,128)(2,1)S(1)}, u32[]{:S(2)}, u32[]{:S(2)}) collective-permute-start(bf16[2,48,1536]{2,1,0:T(8,128)(2,1)S(1)} %get-tuple-element.259), channel_id=1, source_target_pairs={{0,16},{1,17},{2,18},{3,19},{4,20},{5,21},{6,22},{7,23},{8,24},{9,... | collective-permute-start | bytes 884744 | tf_op jit(solution)/shard_map/ppermute | solution.py:109
  227.5 2.5 last_weights.1
  230.0 4.4 %token_back.1 = f32[512,768]{1,0:T(8,128)S(1)} custom-call(s32[4]{0:T(128)S(1)} %pad_add_fusion.where_ref, bf16[512,1536]{1,0:T(8,128)(2,1)S(1)} %attend_back.2.near_ref.first_near_ref.a_ref, bf16[512,768]{1,0:T(8,128)(2,1)S(1)} %attend_back.3.near_ref.b_ref, bf16[768,3328]{1,0:T(8,128)(2,1)} %bitcast.38, bf16[1024,768]{1,0:T(8,128)(2,1)} %copy-done.15), custom_call_target="tpu_custom_call" | custom-call | flops 16000000000 | bytes 48000000 | tf_op jit(solution)/shard_map/token_back/pallas_call | solution.py:806
  235.2 1.6 collective-permute-start.41
  238.4 1.7 collective-permute-done.39.r_ref
  240.8 4.2 %collective-permute-done.40.r_ref = bf16[2,48,1536]{2,1,0:T(8,128)(2,1)S(1)} collective-permute-done((bf16[2,48,1536]{2,1,0:T(8,128)(2,1)S(1)}, bf16[2,48,1536]{2,1,0:T(8,128)(2,1)S(1)}, u32[]{:S(2)}, u32[]{:S(2)}) %collective-permute-start.40) | collective-permute-done | bytes 294944 | tf_op jit(solution)/shard_map/ppermute | solution.py:109
  245.7 1.8 collective-permute-done.41.r_ref
  250.4 1.5 collective-permute-start.45
  257.1 2.2 collective-permute-start.49
  260.2 1.6 finish.3
  261.9 1.6 finish.4
  263.5 1.5 collective-permute-done.49.r_ref
  265.9 3.0 %convert_select_fusion = (f32[512,768]{1,0:T(8,128)}, f32[512,768]{1,0:T(8,128)}) fusion(f32[512,768]{1,0:T(8,128)S(1)} %token_back.1, bf16[512,768]{1,0:T(8,128)(2,1)} %collective-permute-done.33, pred[]{:T(512)S(6)} %eq.2), kind=kLoop, calls=%fused_computation | loop fusion | flops 1179648 | bytes 5505025 | tf_op jit(solution)/shard_map/jit(_where)/select_n | solution.py:824
  270.9 1.2 broadcast_select_fusion
  272.1 1.8 finish.5
  (176 shorter events, 38.5 us)
Async XLA Ops:
  2.5 7.8 %collective-permute-start = (bf16[1,48,1664]{2,1,0:T(8,128)(2,1)S(1)}, bf16[1,48,1664]{2,1,0:T(8,128)(2,1)S(1)}, u32[]{:S(2)}, u32[]{:S(2)}) collective-permute-start(bf16[1,48,1664]{2,1,0:T(8,128)(2,1)S(1)} %get-tuple-element.159), channel_id=1, source_target_pairs={{0,8},{1,9},{2,10},{3,11},{4,12},{5,13},{6,14},{7,15},{8,0},{9,1},... | collective-permute-start | bytes 479240 | tf_op jit(solution)/shard_map/ppermute | solution.py:109
  5.6 16.8 %collective-permute-start.2 = (bf16[1,48,1664]{2,1,0:T(8,128)(2,1)S(1)}, bf16[1,48,1664]{2,1,0:T(8,128)(2,1)S(1)}, u32[]{:S(2)}, u32[]{:S(2)}) collective-permute-start(bf16[1,48,1664]{2,1,0:T(8,128)(2,1)S(1)} %get-tuple-element.159), channel_id=1, source_target_pairs={{0,24},{1,25},{2,26},{3,27},{4,28},{5,29},{6,30},{7,31},{8,16},{9,... | collective-permute-start | bytes 479240 | tf_op jit(solution)/shard_map/ppermute | solution.py:109
  8.1 14.3 %collective-permute-start.1 = (bf16[1,48,1664]{2,1,0:T(8,128)(2,1)S(1)}, bf16[1,48,1664]{2,1,0:T(8,128)(2,1)S(1)}, u32[]{:S(2)}, u32[]{:S(2)}) collective-permute-start(bf16[1,48,1664]{2,1,0:T(8,128)(2,1)S(1)} %get-tuple-element.158), channel_id=1, source_target_pairs={{0,16},{1,17},{2,18},{3,19},{4,20},{5,21},{6,22},{7,23},{8,24},{9,... | collective-permute-start | bytes 479240 | tf_op jit(solution)/shard_map/ppermute | solution.py:109
  8.2 15.8 %collective-permute-start.4 = (bf16[1,48,1536]{2,1,0:T(8,128)(2,1)S(1)}, bf16[1,48,1536]{2,1,0:T(8,128)(2,1)S(1)}, u32[]{:S(2)}, u32[]{:S(2)}) collective-permute-start(bf16[1,48,1536]{2,1,0:T(8,128)(2,1)S(1)} %get-tuple-element.161), channel_id=1, source_target_pairs={{0,8},{1,9},{2,10},{3,11},{4,12},{5,13},{6,14},{7,15},{8,0},{9,1},... | collective-permute-start | bytes 442376 | tf_op jit(solution)/shard_map/ppermute | solution.py:109
  10.0 14.2 %collective-permute-start.6 = (bf16[1,192,384]{2,1,0:T(8,128)(2,1)S(1)}, bf16[1,192,384]{2,1,0:T(8,128)(2,1)S(1)}, u32[]{:S(2)}, u32[]{:S(2)}) collective-permute-start(bf16[1,192,384]{2,1,0:T(8,128)(2,1)S(1)} %get-tuple-element.163), channel_id=1, source_target_pairs={{0,8},{1,9},{2,10},{3,11},{4,12},{5,13},{6,14},{7,15},{8,0},{9,1},... | collective-permute-start | bytes 442376 | tf_op jit(solution)/shard_map/ppermute | solution.py:109
  22.5 16.4 %collective-permute-start.3 = (bf16[4,48,1664]{2,1,0:T(8,128)(2,1)S(1)}, bf16[4,48,1664]{2,1,0:T(8,128)(2,1)S(1)}, u32[]{:S(2)}, u32[]{:S(2)}) collective-permute-start(bf16[4,48,1664]{2,1,0:T(8,128)(2,1)S(1)} %get-tuple-element.317), channel_id=1, source_target_pairs={{0,2},{1,5},{2,0},{3,7},{4,6},{5,1},{6,4},{7,3},{8,10},{9,13},{10,... | collective-permute-start | bytes 1916936 | tf_op jit(solution)/shard_map/ppermute | solution.py:109
  24.1 14.8 %collective-permute-start.5 = (bf16[2,48,1536]{2,1,0:T(8,128)(2,1)S(1)}, bf16[2,48,1536]{2,1,0:T(8,128)(2,1)S(1)}, u32[]{:S(2)}, u32[]{:S(2)}) collective-permute-start(bf16[2,48,1536]{2,1,0:T(8,128)(2,1)S(1)} %pad_maximum_fusion.1), channel_id=1, source_target_pairs={{0,16},{1,17},{2,18},{3,19},{4,20},{5,21},{6,22},{7,23},{8,24},{9,... | collective-permute-start | bytes 884744 | tf_op jit(solution)/shard_map/ppermute | solution.py:109
  39.0 23.6 %collective-permute-start.7 = (bf16[8,48,1664]{2,1,0:T(8,128)(2,1)S(1)}, bf16[8,48,1664]{2,1,0:T(8,128)(2,1)S(1)}, u32[]{:S(2)}, u32[]{:S(2)}) collective-permute-start(bf16[8,48,1664]{2,1,0:T(8,128)(2,1)S(1)} %constant_dynamic-update-slice_fusion.4.refs_0_), channel_id=1, source_target_pairs={{0,4},{1,3},{2,6},{3,1},{4,0},{5,7},{6,2},{7,5},{8,12},{9,11},{10,... | collective-permute-start | bytes 3833864 | tf_op jit(solution)/shard_map/ppermute | solution.py:109
  39.6 23.2 %collective-permute-start.10 = (bf16[4,48,1536]{2,1,0:T(8,128)(2,1)S(1)}, bf16[4,48,1536]{2,1,0:T(8,128)(2,1)S(1)}, u32[]{:S(2)}, u32[]{:S(2)}) collective-permute-start(bf16[4,48,1536]{2,1,0:T(8,128)(2,1)S(1)} %get-tuple-element.314), channel_id=1, source_target_pairs={{0,2},{1,5},{2,0},{3,7},{4,6},{5,1},{6,4},{7,3},{8,10},{9,13},{10,... | collective-permute-start | bytes 1769480 | tf_op jit(solution)/shard_map/ppermute | solution.py:109
  41.1 21.6 %collective-permute-start.11 = (bf16[2,192,384]{2,1,0:T(8,128)(2,1)S(1)}, bf16[2,192,384]{2,1,0:T(8,128)(2,1)S(1)}, u32[]{:S(2)}, u32[]{:S(2)}) collective-permute-start(bf16[2,192,384]{2,1,0:T(8,128)(2,1)S(1)} %constant_dynamic-update-slice_fusion.11), channel_id=1, source_target_pairs={{0,16},{1,17},{2,18},{3,19},{4,20},{5,21},{6,22},{7,23},{8,24},{9,... | collective-permute-start | bytes 884744 | tf_op jit(solution)/shard_map/ppermute | solution.py:109
  41.1 38.2 %collective-permute-start.8 = (bf16[8,48,1664]{2,1,0:T(8,128)(2,1)S(1)}, bf16[8,48,1664]{2,1,0:T(8,128)(2,1)S(1)}, u32[]{:S(2)}, u32[]{:S(2)}) collective-permute-start(bf16[8,48,1664]{2,1,0:T(8,128)(2,1)S(1)} %constant_dynamic-update-slice_fusion.4.refs_0_), channel_id=1, source_target_pairs={{0,1},{1,0},{2,3},{3,2},{4,5},{5,4},{6,7},{7,6},{8,9},{9,8},{10,11... | collective-permute-start | bytes 3833864 | tf_op jit(solution)/shard_map/ppermute | solution.py:109
  62.7 16.6 %collective-permute-start.9 = (bf16[8,48,1664]{2,1,0:T(8,128)(2,1)S(1)}, bf16[8,48,1664]{2,1,0:T(8,128)(2,1)S(1)}, u32[]{:S(2)}, u32[]{:S(2)}) collective-permute-start(bf16[8,48,1664]{2,1,0:T(8,128)(2,1)S(1)} %collective-permute-done.7.refs_1_), channel_id=1, source_target_pairs={{0,1},{1,0},{2,3},{3,2},{4,5},{5,4},{6,7},{7,6},{8,9},{9,8},{10,11... | collective-permute-start | bytes 3833864 | tf_op jit(solution)/shard_map/ppermute | solution.py:109
  62.8 16.3 %collective-permute-start.16 = (bf16[4,192,384]{2,1,0:T(8,128)(2,1)S(1)}, bf16[4,192,384]{2,1,0:T(8,128)(2,1)S(1)}, u32[]{:S(2)}, u32[]{:S(2)}) collective-permute-start(bf16[4,192,384]{2,1,0:T(8,128)(2,1)S(1)} %constant_dynamic-update-slice_fusion.16), channel_id=1, source_target_pairs={{0,2},{1,5},{2,0},{3,7},{4,6},{5,1},{6,4},{7,3},{8,10},{9,13},{10,... | collective-permute-start | bytes 1769480 | tf_op jit(solution)/shard_map/ppermute | solution.py:109
  63.7 25.1 %collective-permute-start.13 = (bf16[8,48,1536]{2,1,0:T(8,128)(2,1)S(1)}, bf16[8,48,1536]{2,1,0:T(8,128)(2,1)S(1)}, u32[]{:S(2)}, u32[]{:S(2)}) collective-permute-start(bf16[8,48,1536]{2,1,0:T(8,128)(2,1)S(1)} %constant_dynamic-update-slice_fusion.13.refs_0_), channel_id=1, source_target_pairs={{0,4},{1,3},{2,6},{3,1},{4,0},{5,7},{6,2},{7,5},{8,12},{9,11},{10,... | collective-permute-start | bytes 3538952 | tf_op jit(solution)/shard_map/ppermute | solution.py:109
  64.4 25.0 %collective-permute-start.12 = (bf16[512,768]{1,0:T(8,128)(2,1)S(1)}, bf16[512,768]{1,0:T(8,128)(2,1)S(1)}, u32[]{:S(2)}, u32[]{:S(2)}) collective-permute-start(bf16[512,768]{1,0:T(8,128)(2,1)S(1)} %get-tuple-element.179), channel_id=1, source_target_pairs={{0,8},{1,9},{2,10},{3,11},{4,12},{5,13},{6,14},{7,15},{8,0},{9,1},... | collective-permute-start | bytes 2359304 | tf_op jit(solution)/shard_map/ppermute | solution.py:109
  79.2 18.4 %collective-permute-start.17 = (bf16[8,192,384]{2,1,0:T(8,128)(2,1)S(1)}, bf16[8,192,384]{2,1,0:T(8,128)(2,1)S(1)}, u32[]{:S(2)}, u32[]{:S(2)}) collective-permute-start(bf16[8,192,384]{2,1,0:T(8,128)(2,1)S(1)} %constant_dynamic-update-slice_fusion.18.refs_0_), channel_id=1, source_target_pairs={{0,4},{1,3},{2,6},{3,1},{4,0},{5,7},{6,2},{7,5},{8,12},{9,11},{10,... | collective-permute-start | bytes 3538952 | tf_op jit(solution)/shard_map/ppermute | solution.py:109
  88.8 9.6 %collective-permute-start.15 = (bf16[8,48,1536]{2,1,0:T(8,128)(2,1)S(1)}, bf16[8,48,1536]{2,1,0:T(8,128)(2,1)S(1)}, u32[]{:S(2)}, u32[]{:S(2)}) collective-permute-start(bf16[8,48,1536]{2,1,0:T(8,128)(2,1)S(1)} %collective-permute-done.13.refs_1_), channel_id=1, source_target_pairs={{0,1},{1,0},{2,3},{3,2},{4,5},{5,4},{6,7},{7,6},{8,9},{9,8},{10,11... | collective-permute-start | bytes 3538952 | tf_op jit(solution)/shard_map/ppermute | solution.py:109
  88.9 9.6 %collective-permute-start.14 = (bf16[8,48,1536]{2,1,0:T(8,128)(2,1)S(1)}, bf16[8,48,1536]{2,1,0:T(8,128)(2,1)S(1)}, u32[]{:S(2)}, u32[]{:S(2)}) collective-permute-start(bf16[8,48,1536]{2,1,0:T(8,128)(2,1)S(1)} %constant_dynamic-update-slice_fusion.13.refs_0_), channel_id=1, source_target_pairs={{0,1},{1,0},{2,3},{3,2},{4,5},{5,4},{6,7},{7,6},{8,9},{9,8},{10,11... | collective-permute-start | bytes 3538952 | tf_op jit(solution)/shard_map/ppermute | solution.py:109
  97.6 8.5 %collective-permute-start.19 = (bf16[8,192,384]{2,1,0:T(8,128)(2,1)S(1)}, bf16[8,192,384]{2,1,0:T(8,128)(2,1)S(1)}, u32[]{:S(2)}, u32[]{:S(2)}) collective-permute-start(bf16[8,192,384]{2,1,0:T(8,128)(2,1)S(1)} %collective-permute-done.17.refs_1_), channel_id=1, source_target_pairs={{0,1},{1,0},{2,3},{3,2},{4,5},{5,4},{6,7},{7,6},{8,9},{9,8},{10,11... | collective-permute-start | bytes 3538952 | tf_op jit(solution)/shard_map/ppermute | solution.py:109
  97.7 8.4 %collective-permute-start.18 = (bf16[8,192,384]{2,1,0:T(8,128)(2,1)S(1)}, bf16[8,192,384]{2,1,0:T(8,128)(2,1)S(1)}, u32[]{:S(2)}, u32[]{:S(2)}) collective-permute-start(bf16[8,192,384]{2,1,0:T(8,128)(2,1)S(1)} %constant_dynamic-update-slice_fusion.18.refs_0_), channel_id=1, source_target_pairs={{0,1},{1,0},{2,3},{3,2},{4,5},{5,4},{6,7},{7,6},{8,9},{9,8},{10,11... | collective-permute-start | bytes 3538952 | tf_op jit(solution)/shard_map/ppermute | solution.py:109
  98.3 38.6 %collective-permute-start.27 = (bf16[512,768]{1,0:T(8,128)(2,1)S(1)}, bf16[512,768]{1,0:T(8,128)(2,1)S(1)}, u32[]{:S(2)}, u32[]{:S(2)}) collective-permute-start(bf16[512,768]{1,0:T(8,128)(2,1)S(1)} %get-tuple-element.210), channel_id=1, source_target_pairs={{0,8},{1,9},{2,10},{3,11},{4,12},{5,13},{6,14},{7,15},{8,0},{9,1},... | collective-permute-start | bytes 2359304 | tf_op jit(solution)/shard_map/ppermute | solution.py:109
  109.8 11.8 %collective-permute-start.20 = (bf16[32,896]{1,0:T(8,128)(2,1)S(1)}, bf16[32,896]{1,0:T(8,128)(2,1)S(1)}, u32[]{:S(2)}, u32[]{:S(2)}) collective-permute-start(bf16[32,896]{1,0:T(8,128)(2,1)S(1)} %first_rows.1.refs_0_), channel_id=1, source_target_pairs={{0,8},{1,9},{2,10},{3,11},{4,12},{5,13},{6,14},{7,15},{8,0},{9,1},... | collective-permute-start | bytes 172040 | tf_op jit(solution)/shard_map/ppermute | solution.py:109
  111.5 10.1 %collective-permute-start.21 = (bf16[32,896]{1,0:T(8,128)(2,1)S(1)}, bf16[32,896]{1,0:T(8,128)(2,1)S(1)}, u32[]{:S(2)}, u32[]{:S(2)}) collective-permute-start(bf16[32,896]{1,0:T(8,128)(2,1)S(1)} %first_rows.1.refs_0_), channel_id=1, source_target_pairs={{0,16},{1,17},{2,18},{3,19},{4,20},{5,21},{6,22},{7,23},{8,24},{9,... | collective-permute-start | bytes 172040 | tf_op jit(solution)/shard_map/ppermute | solution.py:109
  111.7 10.0 %collective-permute-start.22 = (bf16[32,896]{1,0:T(8,128)(2,1)S(1)}, bf16[32,896]{1,0:T(8,128)(2,1)S(1)}, u32[]{:S(2)}, u32[]{:S(2)}) collective-permute-start(bf16[32,896]{1,0:T(8,128)(2,1)S(1)} %first_rows.1.refs_0_), channel_id=1, source_target_pairs={{0,24},{1,25},{2,26},{3,27},{4,28},{5,29},{6,30},{7,31},{8,16},{9,... | collective-permute-start | bytes 172040 | tf_op jit(solution)/shard_map/ppermute | solution.py:109
  122.5 13.8 %collective-permute-start.24 = (bf16[2,48,896]{2,1,0:T(8,128)(2,1)S(1)}, bf16[2,48,896]{2,1,0:T(8,128)(2,1)S(1)}, u32[]{:S(2)}, u32[]{:S(2)}) collective-permute-start(bf16[2,48,896]{2,1,0:T(8,128)(2,1)S(1)} %pack.1.refs_0_), channel_id=1, source_target_pairs={{0,2},{1,3},{2,0},{3,1},{4,6},{5,7},{6,4},{7,5},{8,10},{9,11},{10,... | collective-permute-start | bytes 516104 | tf_op jit(solution)/shard_map/ppermute | solution.py:109
  123.3 13.0 %collective-permute-start.25 = (bf16[2,48,896]{2,1,0:T(8,128)(2,1)S(1)}, bf16[2,48,896]{2,1,0:T(8,128)(2,1)S(1)}, u32[]{:S(2)}, u32[]{:S(2)}) collective-permute-start(bf16[2,48,896]{2,1,0:T(8,128)(2,1)S(1)} %pack.1.refs_0_), channel_id=1, source_target_pairs={{0,4},{1,5},{2,6},{3,7},{4,0},{5,1},{6,2},{7,3},{8,12},{9,13},{10,... | collective-permute-start | bytes 516104 | tf_op jit(solution)/shard_map/ppermute | solution.py:109
  124.8 11.5 %collective-permute-start.26 = (bf16[2,48,896]{2,1,0:T(8,128)(2,1)S(1)}, bf16[2,48,896]{2,1,0:T(8,128)(2,1)S(1)}, u32[]{:S(2)}, u32[]{:S(2)}) collective-permute-start(bf16[2,48,896]{2,1,0:T(8,128)(2,1)S(1)} %pack.1.refs_0_), channel_id=1, source_target_pairs={{0,6},{1,7},{2,4},{3,5},{4,2},{5,3},{6,0},{7,1},{8,14},{9,15},{10,... | collective-permute-start | bytes 516104 | tf_op jit(solution)/shard_map/ppermute | solution.py:109
  137.1 34.5 %collective-permute-start.23 = (bf16[512,768]{1,0:T(8,128)(2,1)S(1)}, bf16[512,768]{1,0:T(8,128)(2,1)S(1)}, u32[]{:S(2)}, u32[]{:S(2)}) collective-permute-start(bf16[512,768]{1,0:T(8,128)(2,1)S(1)} %get-tuple-element.205), channel_id=1, source_target_pairs={{0,8},{1,9},{2,10},{3,11},{4,12},{5,13},{6,14},{7,15},{8,0},{9,1},... | collective-permute-start | bytes 2359304 | tf_op jit(solution)/shard_map/ppermute | solution.py:109
  151.9 20.1 %collective-permute-start.29 = (bf16[16,192,384]{2,1,0:T(8,128)(2,1)S(1)}, bf16[16,192,384]{2,1,0:T(8,128)(2,1)S(1)}, u32[]{:S(2)}, u32[]{:S(2)}) collective-permute-start(bf16[16,192,384]{2,1,0:T(8,128)(2,1)S(1)} %bitcast.47), channel_id=1, source_target_pairs={{0,1},{1,0},{2,3},{3,2},{4,5},{5,4},{6,7},{7,6},{8,9},{9,8},{10,11... | collective-permute-start | bytes 7077896 | tf_op jit(solution)/shard_map/ppermute | solution.py:109
  171.6 8.7 %collective-permute-start.30 = (bf16[16,48,1536]{2,1,0:T(8,128)(2,1)S(1)}, bf16[16,48,1536]{2,1,0:T(8,128)(2,1)S(1)}, u32[]{:S(2)}, u32[]{:S(2)}) collective-permute-start(bf16[16,48,1536]{2,1,0:T(8,128)(2,1)S(1)} %bitcast.46), channel_id=1, source_target_pairs={{0,1},{1,0},{2,3},{3,2},{4,5},{5,4},{6,7},{7,6},{8,9},{9,8},{10,11... | collective-permute-start | bytes 7077896 | tf_op jit(solution)/shard_map/ppermute | solution.py:109
  173.2 31.7 %collective-permute-start.31 = (bf16[8,192,384]{2,1,0:T(8,128)(2,1)S(1)}, bf16[8,192,384]{2,1,0:T(8,128)(2,1)S(1)}, u32[]{:S(2)}, u32[]{:S(2)}) collective-permute-start(bf16[8,192,384]{2,1,0:T(8,128)(2,1)S(1)} %get-tuple-element.227), channel_id=1, source_target_pairs={{0,2},{1,5},{2,0},{3,7},{4,6},{5,1},{6,4},{7,3},{8,10},{9,13},{10,... | collective-permute-start | bytes 3538952 | tf_op jit(solution)/shard_map/ppermute | solution.py:109
  181.5 25.9 %collective-permute-start.32 = (bf16[8,48,1536]{2,1,0:T(8,128)(2,1)S(1)}, bf16[8,48,1536]{2,1,0:T(8,128)(2,1)S(1)}, u32[]{:S(2)}, u32[]{:S(2)}) collective-permute-start(bf16[8,48,1536]{2,1,0:T(8,128)(2,1)S(1)} %get-tuple-element.234), channel_id=1, source_target_pairs={{0,2},{1,5},{2,0},{3,7},{4,6},{5,1},{6,4},{7,3},{8,10},{9,13},{10,... | collective-permute-start | bytes 3538952 | tf_op jit(solution)/shard_map/ppermute | solution.py:109
  193.5 19.2 %collective-permute-start.33 = (bf16[512,768]{1,0:T(8,128)(2,1)S(1)}, bf16[512,768]{1,0:T(8,128)(2,1)}, u32[]{:S(2)}, u32[]{:S(2)}) collective-permute-start(bf16[512,768]{1,0:T(8,128)(2,1)S(1)} %get-tuple-element.239), channel_id=1, source_target_pairs={{0,8},{1,9},{2,10},{3,11},{4,12},{5,13},{6,14},{7,15},{8,0},{9,1},... | collective-permute-start | bytes 2359304 | tf_op jit(solution)/shard_map/ppermute | solution.py:109
  204.9 14.2 %collective-permute-start.35 = (bf16[16,48,1152]{2,1,0:T(8,128)(2,1)S(1)}, bf16[16,48,1152]{2,1,0:T(8,128)(2,1)S(1)}, u32[]{:S(2)}, u32[]{:S(2)}) collective-permute-start(bf16[16,48,1152]{2,1,0:T(8,128)(2,1)S(1)} %bitcast.48), channel_id=1, source_target_pairs={{0,1},{1,0},{2,3},{3,2},{4,5},{5,4},{6,7},{7,6},{8,9},{9,8},{10,11... | collective-permute-start | bytes 5308424 | tf_op jit(solution)/shard_map/ppermute | solution.py:109
  205.8 10.9 %collective-permute-start.34 = (bf16[4,192,384]{2,1,0:T(8,128)(2,1)S(1)}, bf16[4,192,384]{2,1,0:T(8,128)(2,1)S(1)}, u32[]{:S(2)}, u32[]{:S(2)}) collective-permute-start(bf16[4,192,384]{2,1,0:T(8,128)(2,1)S(1)} %get-tuple-element.245), channel_id=1, source_target_pairs={{0,4},{1,3},{2,6},{3,1},{4,0},{5,7},{6,2},{7,5},{8,12},{9,11},{10,... | collective-permute-start | bytes 1769480 | tf_op jit(solution)/shard_map/ppermute | solution.py:109
  208.2 13.8 %collective-permute-start.36 = (bf16[4,48,1536]{2,1,0:T(8,128)(2,1)S(1)}, bf16[4,48,1536]{2,1,0:T(8,128)(2,1)S(1)}, u32[]{:S(2)}, u32[]{:S(2)}) collective-permute-start(bf16[4,48,1536]{2,1,0:T(8,128)(2,1)S(1)} %get-tuple-element.248), channel_id=1, source_target_pairs={{0,4},{1,3},{2,6},{3,1},{4,0},{5,7},{6,2},{7,5},{8,12},{9,11},{10,... | collective-permute-start | bytes 1769480 | tf_op jit(solution)/shard_map/ppermute | solution.py:109
  217.4 22.7 %collective-permute-start.39 = (bf16[2,192,384]{2,1,0:T(8,128)(2,1)S(1)}, bf16[2,192,384]{2,1,0:T(8,128)(2,1)S(1)}, u32[]{:S(2)}, u32[]{:S(2)}) collective-permute-start(bf16[2,192,384]{2,1,0:T(8,128)(2,1)S(1)} %get-tuple-element.253), channel_id=1, source_target_pairs={{0,16},{1,17},{2,18},{3,19},{4,20},{5,21},{6,22},{7,23},{8,24},{9,... | collective-permute-start | bytes 884744 | tf_op jit(solution)/shard_map/ppermute | solution.py:109
  220.0 14.5 %collective-permute-start.37 = (bf16[8,48,1152]{2,1,0:T(8,128)(2,1)S(1)}, bf16[8,48,1152]{2,1,0:T(8,128)(2,1)S(1)}, u32[]{:S(2)}, u32[]{:S(2)}) collective-permute-start(bf16[8,48,1152]{2,1,0:T(8,128)(2,1)S(1)} %get-tuple-element.256), channel_id=1, source_target_pairs={{0,2},{1,5},{2,0},{3,7},{4,6},{5,1},{6,4},{7,3},{8,10},{9,13},{10,... | collective-permute-start | bytes 2654216 | tf_op jit(solution)/shard_map/ppermute | solution.py:109
  222.7 22.3 %collective-permute-start.40 = (bf16[2,48,1536]{2,1,0:T(8,128)(2,1)S(1)}, bf16[2,48,1536]{2,1,0:T(8,128)(2,1)S(1)}, u32[]{:S(2)}, u32[]{:S(2)}) collective-permute-start(bf16[2,48,1536]{2,1,0:T(8,128)(2,1)S(1)} %get-tuple-element.259), channel_id=1, source_target_pairs={{0,16},{1,17},{2,18},{3,19},{4,20},{5,21},{6,22},{7,23},{8,24},{9,... | collective-permute-start | bytes 884744 | tf_op jit(solution)/shard_map/ppermute | solution.py:109
  229.9 6.8 %collective-permute-start.38 = (bf16[16,48,512]{2,1,0:T(8,128)(2,1)S(1)}, bf16[16,48,512]{2,1,0:T(8,128)(2,1)S(1)}, u32[]{:S(2)}, u32[]{:S(2)}) collective-permute-start(bf16[16,48,512]{2,1,0:T(8,128)(2,1)S(1)} %bitcast.49), channel_id=1, source_target_pairs={{0,1},{1,0},{2,3},{3,2},{4,5},{5,4},{6,7},{7,6},{8,9},{9,8},{10,11... | collective-permute-start | bytes 2359304 | tf_op jit(solution)/shard_map/ppermute | solution.py:109
  235.2 12.3 %collective-permute-start.41 = (bf16[4,48,1152]{2,1,0:T(8,128)(2,1)S(1)}, bf16[4,48,1152]{2,1,0:T(8,128)(2,1)S(1)}, u32[]{:S(2)}, u32[]{:S(2)}) collective-permute-start(bf16[4,48,1152]{2,1,0:T(8,128)(2,1)S(1)} %get-tuple-element.266), channel_id=1, source_target_pairs={{0,4},{1,3},{2,6},{3,1},{4,0},{5,7},{6,2},{7,5},{8,12},{9,11},{10,... | collective-permute-start | bytes 1327112 | tf_op jit(solution)/shard_map/ppermute | solution.py:109
  237.5 11.6 %collective-permute-start.42 = (bf16[8,48,512]{2,1,0:T(8,128)(2,1)S(1)}, bf16[8,48,512]{2,1,0:T(8,128)(2,1)S(1)}, u32[]{:S(2)}, u32[]{:S(2)}) collective-permute-start(bf16[8,48,512]{2,1,0:T(8,128)(2,1)S(1)} %get-tuple-element.269), channel_id=1, source_target_pairs={{0,2},{1,5},{2,0},{3,7},{4,6},{5,1},{6,4},{7,3},{8,10},{9,13},{10,... | collective-permute-start | bytes 1179656 | tf_op jit(solution)/shard_map/ppermute | solution.py:109
  240.7 11.2 %collective-permute-start.43 = (bf16[1,192,384]{2,1,0:T(8,128)(2,1)S(1)}, bf16[1,192,384]{2,1,0:T(8,128)(2,1)S(1)}, u32[]{:S(2)}, u32[]{:S(2)}) collective-permute-start(bf16[1,192,384]{2,1,0:T(8,128)(2,1)S(1)} %get-tuple-element.272), channel_id=1, source_target_pairs={{0,8},{1,9},{2,10},{3,11},{4,12},{5,13},{6,14},{7,15},{8,0},{9,1},... | collective-permute-start | bytes 442376 | tf_op jit(solution)/shard_map/ppermute | solution.py:109
  245.6 8.8 %collective-permute-start.44 = (bf16[1,48,1536]{2,1,0:T(8,128)(2,1)S(1)}, bf16[1,48,1536]{2,1,0:T(8,128)(2,1)S(1)}, u32[]{:S(2)}, u32[]{:S(2)}) collective-permute-start(bf16[1,48,1536]{2,1,0:T(8,128)(2,1)S(1)} %get-tuple-element.275), channel_id=1, source_target_pairs={{0,8},{1,9},{2,10},{3,11},{4,12},{5,13},{6,14},{7,15},{8,0},{9,1},... | collective-permute-start | bytes 442376 | tf_op jit(solution)/shard_map/ppermute | solution.py:109
  248.2 11.1 %collective-permute-start.46 = (bf16[2,48,1152]{2,1,0:T(8,128)(2,1)S(1)}, bf16[2,48,1152]{2,1,0:T(8,128)(2,1)S(1)}, u32[]{:S(2)}, u32[]{:S(2)}) collective-permute-start(bf16[2,48,1152]{2,1,0:T(8,128)(2,1)S(1)} %get-tuple-element.278), channel_id=1, source_target_pairs={{0,16},{1,17},{2,18},{3,19},{4,20},{5,21},{6,22},{7,23},{8,24},{9,... | collective-permute-start | bytes 663560 | tf_op jit(solution)/shard_map/ppermute | solution.py:109
  252.5 7.7 %collective-permute-start.47 = (bf16[2,192,384]{2,1,0:T(8,128)(2,1)S(1)}, bf16[2,192,384]{2,1,0:T(8,128)(2,1)S(1)}, u32[]{:S(2)}, u32[]{:S(2)}) collective-permute-start(bf16[2,192,384]{2,1,0:T(8,128)(2,1)S(1)} %add_last.4.refs_0_), channel_id=1, source_target_pairs={{0,1},{1,0},{2,3},{3,2},{4,5},{5,4},{6,7},{7,6},{8,9},{9,8},{10,11... | collective-permute-start | bytes 884744 | tf_op jit(solution)/shard_map/ppermute | solution.py:109
  257.1 7.9 %collective-permute-start.49 = (bf16[2,48,512]{2,1,0:T(8,128)(2,1)S(1)}, bf16[2,48,512]{2,1,0:T(8,128)(2,1)S(1)}, u32[]{:S(2)}, u32[]{:S(2)}) collective-permute-start(bf16[2,48,512]{2,1,0:T(8,128)(2,1)S(1)} %get-tuple-element.286), channel_id=1, source_target_pairs={{0,16},{1,17},{2,18},{3,19},{4,20},{5,21},{6,22},{7,23},{8,24},{9,... | collective-permute-start | bytes 294920 | tf_op jit(solution)/shard_map/ppermute | solution.py:109
  259.9 9.0 %collective-permute-start.50 = (bf16[1,48,1152]{2,1,0:T(8,128)(2,1)S(1)}, bf16[1,48,1152]{2,1,0:T(8,128)(2,1)S(1)}, u32[]{:S(2)}, u32[]{:S(2)}) collective-permute-start(bf16[1,48,1152]{2,1,0:T(8,128)(2,1)S(1)} %get-tuple-element.289), channel_id=1, source_target_pairs={{0,8},{1,9},{2,10},{3,11},{4,12},{5,13},{6,14},{7,15},{8,0},{9,1},... | collective-permute-start | bytes 331784 | tf_op jit(solution)/shard_map/ppermute | solution.py:109
  (30 other events, 193.3 us)

commit v7 on v6

--- a/solution.py
+++ b/solution.py
@@ -856,8 +856,8 @@
     down_part = Scatter(plan, order, g_down, w_down.shape[1])
     acc, sums_up, g_up = order.done(gelu_back(plan, order, gs, w_three, slope, norm, w_two))
     up_part = Scatter(plan, order, g_up, w_up.shape[1])
+    down_part.one()
     order.done(out_back)
-    down_part.one()
     go, ga, sums = order.done(hidden_back(order, acc, second, hat1, rstd1, w_one, vec))
     up_part.one()
     split = 4

time: 277 us -> 276 us (level)
  transfers between devices with their start and end apart: 54 -> 54, of which waited for: 14 -> 15; matrix products, arithmetic and copies ran while one was open for 2% -> 2% of each run, Pallas kernels for 49% -> 49%
where the time goes in v7:
time: 276 us; the launch traced here: 272 us
  Pallas kernels  137 us (50%)
  waiting for transfers between devices  82.1 us (30%)
  starting transfers between devices  42 us (15%)
  local copies, waits for them, and re-layouts  4.75 us (2%)
  other arithmetic  3.78 us (1%)
    ppermute x54, waiting for transfers between devices, send(): return lax.ppermute(v, AXES, pairs)  82.1 us
    ppermute x54, starting transfers between devices, send(): return lax.ppermute(v, AXES, pairs)  42 us
    pallas_call x1, Pallas kernels, gelu_back(): pl.pallas_call(partial(gelu_back_kernel, reps, column), out_shape=(shape(...  19.5 us
    pallas_call x22, Pallas kernels, in_vmem(): pl.pallas_call(kernel, out_shape=tuple((shape(*o) for o in outs)), in_spe...  19.4 us
    pallas_call x2, Pallas kernels, attend(): pl.pallas_call(partial(attend_kernel, part), grid=(steps,), out_shape=(fa...  16.2 us
    pallas_call x2, Pallas kernels, up(): pl.pallas_call(partial(up_kernel, first), grid=(steps,), out_shape=(shape...  12.9 us
    pallas_call x1, Pallas kernels, top(): pl.pallas_call(top_kernel, grid=(FF // D,), out_shape=(far((rows, D), F32...  11 us
    pallas_call x1, Pallas kernels, far_back(): pl.pallas_call(partial(far_back_kernel, count), grid=(steps,), out_shape=...  10.8 us
  transfers between devices with their start and end apart: 54, of which 15 were waited for; matrix products, arithmetic and copies ran while one was open for 2% of the time, Pallas kernels for 49%

profile of v7, /device:TPU:0, one launch (start us, length us, event | category | flops | bytes accessed | tf_op | source)
XLA Modules:
  0.0 272.4 jit_solution(4503701954217033825)
XLA Ops:
  0.7 1.8 shards.1
  2.5 3.1 %collective-permute-start = (bf16[1,48,1664]{2,1,0:T(8,128)(2,1)S(1)}, bf16[1,48,1664]{2,1,0:T(8,128)(2,1)S(1)}, u32[]{:S(2)}, u32[]{:S(2)}) collective-permute-start(bf16[1,48,1664]{2,1,0:T(8,128)(2,1)S(1)} %get-tuple-element.159), channel_id=1, source_target_pairs={{0,8},{1,9},{2,10},{3,11},{4,12},{5,13},{6,14},{7,15},{8,0},{9,1},... | collective-permute-start | bytes 479240 | tf_op jit(solution)/shard_map/ppermute | solution.py:109
  5.6 2.5 collective-permute-start.2
  8.2 1.8 collective-permute-start.4
  10.3 12.1 %collective-permute-done.1 = bf16[1,48,1664]{2,1,0:T(8,128)(2,1)S(1)} collective-permute-done((bf16[1,48,1664]{2,1,0:T(8,128)(2,1)S(1)}, bf16[1,48,1664]{2,1,0:T(8,128)(2,1)S(1)}, u32[]{:S(2)}, u32[]{:S(2)}) %collective-permute-start.1) | collective-permute-done | bytes 159776 | tf_op jit(solution)/shard_map/ppermute | solution.py:109
  22.5 1.6 collective-permute-start.3
  24.2 14.6 %collective-permute-done.5 = bf16[2,48,1536]{2,1,0:T(8,128)(2,1)S(1)} collective-permute-done((bf16[2,48,1536]{2,1,0:T(8,128)(2,1)S(1)}, bf16[2,48,1536]{2,1,0:T(8,128)(2,1)S(1)}, u32[]{:S(2)}, u32[]{:S(2)}) %collective-permute-start.5) | collective-permute-done | bytes 294944 | tf_op jit(solution)/shard_map/ppermute | solution.py:109
  39.6 1.5 collective-permute-start.10
  41.1 21.6 %collective-permute-done.7.refs_1_ = bf16[8,48,1664]{2,1,0:T(8,128)(2,1)S(1)} collective-permute-done((bf16[8,48,1664]{2,1,0:T(8,128)(2,1)S(1)}, bf16[8,48,1664]{2,1,0:T(8,128)(2,1)S(1)}, u32[]{:S(2)}, u32[]{:S(2)}) %collective-permute-start.7) | collective-permute-done | bytes 1277984 | tf_op jit(solution)/shard_map/ppermute | solution.py:109
  64.6 14.5 %collective-permute-done.16 = bf16[4,192,384]{2,1,0:T(8,128)(2,1)S(1)} collective-permute-done((bf16[4,192,384]{2,1,0:T(8,128)(2,1)S(1)}, bf16[4,192,384]{2,1,0:T(8,128)(2,1)S(1)}, u32[]{:S(2)}, u32[]{:S(2)}) %collective-permute-start.16) | collective-permute-done | bytes 589856 | tf_op jit(solution)/shard_map/ppermute | solution.py:109
  80.3 8.5 %attend.2 = (bf16[1024,2304]{1,0:T(8,128)(2,1)}, bf16[8,6,128,256]{3,2,1,0:T(8,128)(2,1)}, bf16[1024,768]{1,0:T(8,128)(2,1)}, f32[1024,768]{1,0:T(8,128)}, f32[1...) custom-call(s32[4]{0:T(128)S(1)} %pad_add_fusion.where_ref, ...), custom_call_target="tpu_custom_call" | custom-call | flops 7000000000 | bytes 21000000 | tf_op jit(solution)/shard_map/attend/pallas_call | solution.py:438
  89.4 7.7 %attend.3 = (bf16[1024,2304]{1,0:T(8,128)(2,1)}, bf16[8,6,128,256]{3,2,1,0:T(8,128)(2,1)}, bf16[1024,768]{1,0:T(8,128)(2,1)}, f32[1024,768]{1,0:T(8,128)}, f32[1...) custom-call(s32[4]{0:T(128)S(1)} %pad_add_fusion.where_ref, ...), custom_call_target="tpu_custom_call", output_to_operand_aliasing={{0}: (3, {}), {1}: (4, {}), {2}: (5, {}), {3}: (6, {}), {4}... | custom-call | flops 7000000000 | bytes 21000000 | tf_op jit(solution)/shard_map/attend/pallas_call | solution.py:438
  99.7 6.3 %up.2 = (bf16[1024,3072]{1,0:T(8,128)(2,1)S(1)}, bf16[1024,3072]{1,0:T(8,128)(2,1)}) custom-call(s32[4]{0:T(128)S(1)} %pad_add_fusion.where_ref, bf16[1024,768]{1,0:T(8,128)(2,1)S(1)} %copy-done.8, bf16[768,3072]{1,0:T(8,128)(2,1)S(1)} %bitcast.39, f32[128,768]{1,0:T(8,128)S(1)} %get-tuple-element.186.vec_ref), custom_call_target="tpu_custom_call" | custom-call | flops 8000000000 | bytes 24000000 | tf_op jit(solution)/shard_map/up/pallas_call | solution.py:461
  107.1 2.6 first_rows.1.refs_0_
  109.8 1.7 collective-permute-start.20
  111.6 2.6 collective-permute-start.22
  114.2 6.5 %up.3 = (bf16[1024,3072]{1,0:T(8,128)(2,1)S(1)}, bf16[1024,3072]{1,0:T(8,128)(2,1)}) custom-call(s32[4]{0:T(128)S(1)} %pad_add_fusion.where_ref, bf16[1024,768]{1,0:T(8,128)(2,1)S(1)} %copy-done.8, bf16[768,3072]{1,0:T(8,128)(2,1)S(1)} %bitcast.41, f32[128,768]{1,0:T(8,128)S(1)} %get-tuple-element.186.vec_ref, ...), custom_call_target="tpu_custom_call", output_to_operand_aliasing={{0}: (4, {}), {1}: (5, {})} | custom-call | flops 8000000000 | bytes 24000000 | tf_op jit(solution)/shard_map/up/pallas_call | solution.py:461
  123.3 1.5 collective-permute-start.25
  124.8 1.2 collective-permute-start.26
  126.0 8.6 %down.1 = (bf16[512,768]{1,0:T(8,128)(2,1)}, bf16[512,768]{1,0:T(8,128)(2,1)S(1)}, f32[1024,768]{1,0:T(8,128)S(1)}, f32[1024,1]{1,0:T(8,128)S(1)}) custom-call(s32[4]{0:T(128)S(1)} %pad_add_fusion.where_ref, bf16[1024,3072]{1,0:T(8,128)(2,1)S(1)} %get-tuple-element.200.act_ref, bf16[3072,768]{1,0:T(8,128)(2,1)S(1)} %bitcast.44, ...), custom_call_target="tpu_custom_call" | custom-call | flops 8000000000 | bytes 24000000 | tf_op jit(solution)/shard_map/down/pallas_call | solution.py:487
  136.2 1.2 collective-permute-done.28.refs_1_
  137.4 1.9 contrast.1
  139.3 11.0 %top.1 = (f32[1024,768]{1,0:T(8,128)}, bf16[1024,768]{1,0:T(8,128)(2,1)S(1)}, f32[8,768]{1,0:T(8,128)S(1)}, bf16[3072,384]{1,0:T(8,128)(2,1)S(1)}, bf16[3072,384]{1,0:T(8,128)(2,1)S(1)}) custom-call(s32[4]{0:T(128)S(1)} %pad_add_fusion.where_ref, bf16[1024,768]{1,0:T(8,128)(2,1)S(1)} %pad_maximum_fusion.cot_ref, f32[32,768]{1,0:T(8,128)S(1)} %get-tuple-element.213.cls_ref, ...), custom_call_target="tpu_custom_call" | custom-call | flops 44000002048 | bytes 132000000 | tf_op jit(solution)/shard_map/top/pallas_call | solution.py:631
  150.4 19.5 %gelu_back.1 = (f32[1024,768]{1,0:T(8,128)S(1)}, f32[8,768]{1,0:T(8,128)S(1)}, bf16[768,1536]{1,0:T(8,128)(2,1)S(1)}, bf16[768,1536]{1,0:T(8,128)(2,1)S(1)}) custom-call(s32[4]{0:T(128)S(1)} %pad_add_fusion.where_ref, bf16[1024,768]{1,0:T(8,128)(2,1)S(1)} %get-tuple-element.216.gs_ref, bf16[3072,768]{1,0:T(8,128)(2,1)} %bitcast.45, ...), custom_call_target="tpu_custom_call" | custom-call | flops 80000000000 | bytes 240000000 | tf_op jit(solution)/shard_map/gelu_back/pallas_call | solution.py:668
  172.3 6.6 %hidden_back.1 = (bf16[1024,768]{1,0:T(8,128)(2,1)S(1)}, bf16[1024,768]{1,0:T(8,128)(2,1)S(1)}, f32[8,768]{1,0:T(8,128)S(1)}) custom-call(s32[4]{0:T(128)S(1)} %pad_add_fusion.where_ref, f32[1024,768]{1,0:T(8,128)S(1)} %get-tuple-element.221.acc_ref, f32[1024,768]{1,0:T(8,128)} %get-tuple-element.215.second_ref, f32[1024,768]{1,0:T(8,128)} %get-tuple-element.183.hat_ref, ...), custom_call_target="tpu_custom_call" | custom-call | flops 20000000000 | bytes 60000000 | tf_op jit(solution)/shard_map/hidden_back/pallas_call | solution.py:690
  180.1 1.3 collective-permute-start.32
  181.3 10.8 %far_back.1 = (bf16[512,1536]{1,0:T(8,128)(2,1)S(1)}, bf16[512,768]{1,0:T(8,128)(2,1)S(1)}, bf16[512,768]{1,0:T(8,128)(2,1)S(1)}) custom-call(s32[4]{0:T(128)S(1)} %pad_add_fusion.where_ref, bf16[1024,768]{1,0:T(8,128)(2,1)S(1)} %get-tuple-element.231.ga_ref, bf16[1024,2304]{1,0:T(8,128)(2,1)} %get-tuple-element.180.proj_ref, ...), custom_call_target="tpu_custom_call" | custom-call | flops 44000002048 | bytes 132000000 | tf_op jit(solution)/shard_map/far_back/pallas_call | solution.py:797
  193.0 5.5 %attend_back.2.near_ref.first_near_ref.a_ref = bf16[512,1536]{1,0:T(8,128)(2,1)S(1)} custom-call(s32[4]{0:T(128)S(1)} %pad_add_fusion.where_ref, bf16[1024,768]{1,0:T(8,128)(2,1)S(1)} %get-tuple-element.231.ga_ref, bf16[1024,2304]{1,0:T(8,128)(2,1)} %get-tuple-element.180.proj_ref, bf16[8,6,128,256]{3,2,1,0:T(8,128)(2,1)} %get-tuple-element.181.probs_ref), custom_call_target="tpu_custom_call" | custom-call | flops 20000000000 | bytes 60000000 | tf_op jit(solution)/shard_map/attend_back/pallas_call | solution.py:732
  198.5 5.6 %first_weights.1 = (bf16[768,1152]{1,0:T(8,128)(2,1)S(1)}, bf16[768,1152]{1,0:T(8,128)(2,1)S(1)}) custom-call(s32[4]{0:T(128)S(1)} %pad_add_fusion.where_ref, bf16[512,768]{1,0:T(8,128)(2,1)S(1)} %copy-done.4, bf16[512,768]{1,0:T(8,128)(2,1)S(1)} %copy-done.6, bf16[512,1536]{1,0:T(8,128)(2,1)S(1)} %attend_back.2.near_ref.first_near_ref.a_ref, ...), custom_call_target="tpu_custom_call" | custom-call | flops 20000000000 | bytes 60000000 | tf_op jit(solution)/shard_map/first_weights/pallas_call | solution.py:775
  205.1 1.6 collective-permute-start.34
  208.0 3.1 %collective-permute-done.33 = bf16[512,768]{1,0:T(8,128)(2,1)S(1)} collective-permute-done((bf16[512,768]{1,0:T(8,128)(2,1)S(1)}, bf16[512,768]{1,0:T(8,128)(2,1)S(1)}, u32[]{:S(2)}, u32[]{:S(2)}) %collective-permute-start.33) | collective-permute-done | bytes 786464 | tf_op jit(solution)/shard_map/ppermute | solution.py:109
  211.2 4.2 %attend_back.3.near_ref.b_ref = bf16[512,768]{1,0:T(8,128)(2,1)S(1)} custom-call(s32[4]{0:T(128)S(1)} %pad_add_fusion.where_ref, bf16[1024,768]{1,0:T(8,128)(2,1)S(1)} %get-tuple-element.231.ga_ref, bf16[1024,2304]{1,0:T(8,128)(2,1)} %get-tuple-element.180.proj_ref, bf16[8,6,128,256]{3,2,1,0:T(8,128)(2,1)} %get-tuple-element.181.probs_ref), custom_call_target="tpu_custom_call" | custom-call | flops 10000000000 | bytes 30000000 | tf_op jit(solution)/shard_map/attend_back/pallas_call | solution.py:732
  216.1 1.4 collective-permute-start.39
  219.4 2.6 collective-permute-done.36.r_ref
  222.7 2.6 collective-permute-start.40
  225.3 2.5 last_weights.1
  227.9 4.4 %token_back.1 = f32[512,768]{1,0:T(8,128)S(1)} custom-call(s32[4]{0:T(128)S(1)} %pad_add_fusion.where_ref, bf16[512,1536]{1,0:T(8,128)(2,1)S(1)} %attend_back.2.near_ref.first_near_ref.a_ref, bf16[512,768]{1,0:T(8,128)(2,1)S(1)} %attend_back.3.near_ref.b_ref, bf16[768,3328]{1,0:T(8,128)(2,1)} %bitcast.38, bf16[1024,768]{1,0:T(8,128)(2,1)} %copy-done.15), custom_call_target="tpu_custom_call" | custom-call | flops 16000000000 | bytes 48000000 | tf_op jit(solution)/shard_map/token_back/pallas_call | solution.py:806
  233.1 1.6 collective-permute-start.41
  236.3 2.4 collective-permute-done.39.r_ref
  239.4 4.9 %collective-permute-done.40.r_ref = bf16[2,48,1536]{2,1,0:T(8,128)(2,1)S(1)} collective-permute-done((bf16[2,48,1536]{2,1,0:T(8,128)(2,1)S(1)}, bf16[2,48,1536]{2,1,0:T(8,128)(2,1)S(1)}, u32[]{:S(2)}, u32[]{:S(2)}) %collective-permute-start.40) | collective-permute-done | bytes 294944 | tf_op jit(solution)/shard_map/ppermute | solution.py:109
  246.0 2.3 collective-permute-start.46
  249.7 1.5 collective-permute-start.45
  259.5 1.6 finish.3
  261.1 1.6 finish.4
  264.7 1.9 convert_select_fusion
  267.2 1.3 collective-permute-done.51.got_ref
  269.2 1.2 broadcast_select_fusion
  270.4 1.8 finish.5
  (180 shorter events, 39.8 us)
Async XLA Ops:
  2.5 7.8 %collective-permute-start = (bf16[1,48,1664]{2,1,0:T(8,128)(2,1)S(1)}, bf16[1,48,1664]{2,1,0:T(8,128)(2,1)S(1)}, u32[]{:S(2)}, u32[]{:S(2)}) collective-permute-start(bf16[1,48,1664]{2,1,0:T(8,128)(2,1)S(1)} %get-tuple-element.159), channel_id=1, source_target_pairs={{0,8},{1,9},{2,10},{3,11},{4,12},{5,13},{6,14},{7,15},{8,0},{9,1},... | collective-permute-start | bytes 479240 | tf_op jit(solution)/shard_map/ppermute | solution.py:109
  5.6 16.8 %collective-permute-start.2 = (bf16[1,48,1664]{2,1,0:T(8,128)(2,1)S(1)}, bf16[1,48,1664]{2,1,0:T(8,128)(2,1)S(1)}, u32[]{:S(2)}, u32[]{:S(2)}) collective-permute-start(bf16[1,48,1664]{2,1,0:T(8,128)(2,1)S(1)} %get-tuple-element.159), channel_id=1, source_target_pairs={{0,24},{1,25},{2,26},{3,27},{4,28},{5,29},{6,30},{7,31},{8,16},{9,... | collective-permute-start | bytes 479240 | tf_op jit(solution)/shard_map/ppermute | solution.py:109
  8.1 14.3 %collective-permute-start.1 = (bf16[1,48,1664]{2,1,0:T(8,128)(2,1)S(1)}, bf16[1,48,1664]{2,1,0:T(8,128)(2,1)S(1)}, u32[]{:S(2)}, u32[]{:S(2)}) collective-permute-start(bf16[1,48,1664]{2,1,0:T(8,128)(2,1)S(1)} %get-tuple-element.158), channel_id=1, source_target_pairs={{0,16},{1,17},{2,18},{3,19},{4,20},{5,21},{6,22},{7,23},{8,24},{9,... | collective-permute-start | bytes 479240 | tf_op jit(solution)/shard_map/ppermute | solution.py:109
  8.2 15.8 %collective-permute-start.4 = (bf16[1,48,1536]{2,1,0:T(8,128)(2,1)S(1)}, bf16[1,48,1536]{2,1,0:T(8,128)(2,1)S(1)}, u32[]{:S(2)}, u32[]{:S(2)}) collective-permute-start(bf16[1,48,1536]{2,1,0:T(8,128)(2,1)S(1)} %get-tuple-element.161), channel_id=1, source_target_pairs={{0,8},{1,9},{2,10},{3,11},{4,12},{5,13},{6,14},{7,15},{8,0},{9,1},... | collective-permute-start | bytes 442376 | tf_op jit(solution)/shard_map/ppermute | solution.py:109
  10.0 14.2 %collective-permute-start.6 = (bf16[1,192,384]{2,1,0:T(8,128)(2,1)S(1)}, bf16[1,192,384]{2,1,0:T(8,128)(2,1)S(1)}, u32[]{:S(2)}, u32[]{:S(2)}) collective-permute-start(bf16[1,192,384]{2,1,0:T(8,128)(2,1)S(1)} %get-tuple-element.163), channel_id=1, source_target_pairs={{0,8},{1,9},{2,10},{3,11},{4,12},{5,13},{6,14},{7,15},{8,0},{9,1},... | collective-permute-start | bytes 442376 | tf_op jit(solution)/shard_map/ppermute | solution.py:109
  22.5 16.4 %collective-permute-start.3 = (bf16[4,48,1664]{2,1,0:T(8,128)(2,1)S(1)}, bf16[4,48,1664]{2,1,0:T(8,128)(2,1)S(1)}, u32[]{:S(2)}, u32[]{:S(2)}) collective-permute-start(bf16[4,48,1664]{2,1,0:T(8,128)(2,1)S(1)} %get-tuple-element.317), channel_id=1, source_target_pairs={{0,2},{1,5},{2,0},{3,7},{4,6},{5,1},{6,4},{7,3},{8,10},{9,13},{10,... | collective-permute-start | bytes 1916936 | tf_op jit(solution)/shard_map/ppermute | solution.py:109
  24.1 14.8 %collective-permute-start.5 = (bf16[2,48,1536]{2,1,0:T(8,128)(2,1)S(1)}, bf16[2,48,1536]{2,1,0:T(8,128)(2,1)S(1)}, u32[]{:S(2)}, u32[]{:S(2)}) collective-permute-start(bf16[2,48,1536]{2,1,0:T(8,128)(2,1)S(1)} %pad_maximum_fusion.1), channel_id=1, source_target_pairs={{0,16},{1,17},{2,18},{3,19},{4,20},{5,21},{6,22},{7,23},{8,24},{9,... | collective-permute-start | bytes 884744 | tf_op jit(solution)/shard_map/ppermute | solution.py:109
  39.0 23.6 %collective-permute-start.7 = (bf16[8,48,1664]{2,1,0:T(8,128)(2,1)S(1)}, bf16[8,48,1664]{2,1,0:T(8,128)(2,1)S(1)}, u32[]{:S(2)}, u32[]{:S(2)}) collective-permute-start(bf16[8,48,1664]{2,1,0:T(8,128)(2,1)S(1)} %constant_dynamic-update-slice_fusion.4.refs_0_), channel_id=1, source_target_pairs={{0,4},{1,3},{2,6},{3,1},{4,0},{5,7},{6,2},{7,5},{8,12},{9,11},{10,... | collective-permute-start | bytes 3833864 | tf_op jit(solution)/shard_map/ppermute | solution.py:109
  39.6 23.2 %collective-permute-start.10 = (bf16[4,48,1536]{2,1,0:T(8,128)(2,1)S(1)}, bf16[4,48,1536]{2,1,0:T(8,128)(2,1)S(1)}, u32[]{:S(2)}, u32[]{:S(2)}) collective-permute-start(bf16[4,48,1536]{2,1,0:T(8,128)(2,1)S(1)} %get-tuple-element.314), channel_id=1, source_target_pairs={{0,2},{1,5},{2,0},{3,7},{4,6},{5,1},{6,4},{7,3},{8,10},{9,13},{10,... | collective-permute-start | bytes 1769480 | tf_op jit(solution)/shard_map/ppermute | solution.py:109
  41.1 21.6 %collective-permute-start.11 = (bf16[2,192,384]{2,1,0:T(8,128)(2,1)S(1)}, bf16[2,192,384]{2,1,0:T(8,128)(2,1)S(1)}, u32[]{:S(2)}, u32[]{:S(2)}) collective-permute-start(bf16[2,192,384]{2,1,0:T(8,128)(2,1)S(1)} %constant_dynamic-update-slice_fusion.11), channel_id=1, source_target_pairs={{0,16},{1,17},{2,18},{3,19},{4,20},{5,21},{6,22},{7,23},{8,24},{9,... | collective-permute-start | bytes 884744 | tf_op jit(solution)/shard_map/ppermute | solution.py:109
  41.1 38.2 %collective-permute-start.8 = (bf16[8,48,1664]{2,1,0:T(8,128)(2,1)S(1)}, bf16[8,48,1664]{2,1,0:T(8,128)(2,1)S(1)}, u32[]{:S(2)}, u32[]{:S(2)}) collective-permute-start(bf16[8,48,1664]{2,1,0:T(8,128)(2,1)S(1)} %constant_dynamic-update-slice_fusion.4.refs_0_), channel_id=1, source_target_pairs={{0,1},{1,0},{2,3},{3,2},{4,5},{5,4},{6,7},{7,6},{8,9},{9,8},{10,11... | collective-permute-start | bytes 3833864 | tf_op jit(solution)/shard_map/ppermute | solution.py:109
  62.7 16.6 %collective-permute-start.9 = (bf16[8,48,1664]{2,1,0:T(8,128)(2,1)S(1)}, bf16[8,48,1664]{2,1,0:T(8,128)(2,1)S(1)}, u32[]{:S(2)}, u32[]{:S(2)}) collective-permute-start(bf16[8,48,1664]{2,1,0:T(8,128)(2,1)S(1)} %collective-permute-done.7.refs_1_), channel_id=1, source_target_pairs={{0,1},{1,0},{2,3},{3,2},{4,5},{5,4},{6,7},{7,6},{8,9},{9,8},{10,11... | collective-permute-start | bytes 3833864 | tf_op jit(solution)/shard_map/ppermute | solution.py:109
  62.8 16.3 %collective-permute-start.16 = (bf16[4,192,384]{2,1,0:T(8,128)(2,1)S(1)}, bf16[4,192,384]{2,1,0:T(8,128)(2,1)S(1)}, u32[]{:S(2)}, u32[]{:S(2)}) collective-permute-start(bf16[4,192,384]{2,1,0:T(8,128)(2,1)S(1)} %constant_dynamic-update-slice_fusion.16), channel_id=1, source_target_pairs={{0,2},{1,5},{2,0},{3,7},{4,6},{5,1},{6,4},{7,3},{8,10},{9,13},{10,... | collective-permute-start | bytes 1769480 | tf_op jit(solution)/shard_map/ppermute | solution.py:109
  63.7 25.1 %collective-permute-start.13 = (bf16[8,48,1536]{2,1,0:T(8,128)(2,1)S(1)}, bf16[8,48,1536]{2,1,0:T(8,128)(2,1)S(1)}, u32[]{:S(2)}, u32[]{:S(2)}) collective-permute-start(bf16[8,48,1536]{2,1,0:T(8,128)(2,1)S(1)} %constant_dynamic-update-slice_fusion.13.refs_0_), channel_id=1, source_target_pairs={{0,4},{1,3},{2,6},{3,1},{4,0},{5,7},{6,2},{7,5},{8,12},{9,11},{10,... | collective-permute-start | bytes 3538952 | tf_op jit(solution)/shard_map/ppermute | solution.py:109
  64.4 25.0 %collective-permute-start.12 = (bf16[512,768]{1,0:T(8,128)(2,1)S(1)}, bf16[512,768]{1,0:T(8,128)(2,1)S(1)}, u32[]{:S(2)}, u32[]{:S(2)}) collective-permute-start(bf16[512,768]{1,0:T(8,128)(2,1)S(1)} %get-tuple-element.179), channel_id=1, source_target_pairs={{0,8},{1,9},{2,10},{3,11},{4,12},{5,13},{6,14},{7,15},{8,0},{9,1},... | collective-permute-start | bytes 2359304 | tf_op jit(solution)/shard_map/ppermute | solution.py:109
  79.2 18.4 %collective-permute-start.17 = (bf16[8,192,384]{2,1,0:T(8,128)(2,1)S(1)}, bf16[8,192,384]{2,1,0:T(8,128)(2,1)S(1)}, u32[]{:S(2)}, u32[]{:S(2)}) collective-permute-start(bf16[8,192,384]{2,1,0:T(8,128)(2,1)S(1)} %constant_dynamic-update-slice_fusion.18.refs_0_), channel_id=1, source_target_pairs={{0,4},{1,3},{2,6},{3,1},{4,0},{5,7},{6,2},{7,5},{8,12},{9,11},{10,... | collective-permute-start | bytes 3538952 | tf_op jit(solution)/shard_map/ppermute | solution.py:109
  88.8 9.6 %collective-permute-start.15 = (bf16[8,48,1536]{2,1,0:T(8,128)(2,1)S(1)}, bf16[8,48,1536]{2,1,0:T(8,128)(2,1)S(1)}, u32[]{:S(2)}, u32[]{:S(2)}) collective-permute-start(bf16[8,48,1536]{2,1,0:T(8,128)(2,1)S(1)} %collective-permute-done.13.refs_1_), channel_id=1, source_target_pairs={{0,1},{1,0},{2,3},{3,2},{4,5},{5,4},{6,7},{7,6},{8,9},{9,8},{10,11... | collective-permute-start | bytes 3538952 | tf_op jit(solution)/shard_map/ppermute | solution.py:109
  88.9 9.6 %collective-permute-start.14 = (bf16[8,48,1536]{2,1,0:T(8,128)(2,1)S(1)}, bf16[8,48,1536]{2,1,0:T(8,128)(2,1)S(1)}, u32[]{:S(2)}, u32[]{:S(2)}) collective-permute-start(bf16[8,48,1536]{2,1,0:T(8,128)(2,1)S(1)} %constant_dynamic-update-slice_fusion.13.refs_0_), channel_id=1, source_target_pairs={{0,1},{1,0},{2,3},{3,2},{4,5},{5,4},{6,7},{7,6},{8,9},{9,8},{10,11... | collective-permute-start | bytes 3538952 | tf_op jit(solution)/shard_map/ppermute | solution.py:109
  97.6 8.5 %collective-permute-start.19 = (bf16[8,192,384]{2,1,0:T(8,128)(2,1)S(1)}, bf16[8,192,384]{2,1,0:T(8,128)(2,1)S(1)}, u32[]{:S(2)}, u32[]{:S(2)}) collective-permute-start(bf16[8,192,384]{2,1,0:T(8,128)(2,1)S(1)} %collective-permute-done.17.refs_1_), channel_id=1, source_target_pairs={{0,1},{1,0},{2,3},{3,2},{4,5},{5,4},{6,7},{7,6},{8,9},{9,8},{10,11... | collective-permute-start | bytes 3538952 | tf_op jit(solution)/shard_map/ppermute | solution.py:109
  97.7 8.3 %collective-permute-start.18 = (bf16[8,192,384]{2,1,0:T(8,128)(2,1)S(1)}, bf16[8,192,384]{2,1,0:T(8,128)(2,1)S(1)}, u32[]{:S(2)}, u32[]{:S(2)}) collective-permute-start(bf16[8,192,384]{2,1,0:T(8,128)(2,1)S(1)} %constant_dynamic-update-slice_fusion.18.refs_0_), channel_id=1, source_target_pairs={{0,1},{1,0},{2,3},{3,2},{4,5},{5,4},{6,7},{7,6},{8,9},{9,8},{10,11... | collective-permute-start | bytes 3538952 | tf_op jit(solution)/shard_map/ppermute | solution.py:109
  98.3 37.0 %collective-permute-start.27 = (bf16[512,768]{1,0:T(8,128)(2,1)S(1)}, bf16[512,768]{1,0:T(8,128)(2,1)S(1)}, u32[]{:S(2)}, u32[]{:S(2)}) collective-permute-start(bf16[512,768]{1,0:T(8,128)(2,1)S(1)} %get-tuple-element.210), channel_id=1, source_target_pairs={{0,8},{1,9},{2,10},{3,11},{4,12},{5,13},{6,14},{7,15},{8,0},{9,1},... | collective-permute-start | bytes 2359304 | tf_op jit(solution)/shard_map/ppermute | solution.py:109
  109.8 11.9 %collective-permute-start.20 = (bf16[32,896]{1,0:T(8,128)(2,1)S(1)}, bf16[32,896]{1,0:T(8,128)(2,1)S(1)}, u32[]{:S(2)}, u32[]{:S(2)}) collective-permute-start(bf16[32,896]{1,0:T(8,128)(2,1)S(1)} %first_rows.1.refs_0_), channel_id=1, source_target_pairs={{0,8},{1,9},{2,10},{3,11},{4,12},{5,13},{6,14},{7,15},{8,0},{9,1},... | collective-permute-start | bytes 172040 | tf_op jit(solution)/shard_map/ppermute | solution.py:109
  111.5 10.2 %collective-permute-start.21 = (bf16[32,896]{1,0:T(8,128)(2,1)S(1)}, bf16[32,896]{1,0:T(8,128)(2,1)S(1)}, u32[]{:S(2)}, u32[]{:S(2)}) collective-permute-start(bf16[32,896]{1,0:T(8,128)(2,1)S(1)} %first_rows.1.refs_0_), channel_id=1, source_target_pairs={{0,16},{1,17},{2,18},{3,19},{4,20},{5,21},{6,22},{7,23},{8,24},{9,... | collective-permute-start | bytes 172040 | tf_op jit(solution)/shard_map/ppermute | solution.py:109
  111.6 10.1 %collective-permute-start.22 = (bf16[32,896]{1,0:T(8,128)(2,1)S(1)}, bf16[32,896]{1,0:T(8,128)(2,1)S(1)}, u32[]{:S(2)}, u32[]{:S(2)}) collective-permute-start(bf16[32,896]{1,0:T(8,128)(2,1)S(1)} %first_rows.1.refs_0_), channel_id=1, source_target_pairs={{0,24},{1,25},{2,26},{3,27},{4,28},{5,29},{6,30},{7,31},{8,16},{9,... | collective-permute-start | bytes 172040 | tf_op jit(solution)/shard_map/ppermute | solution.py:109
  122.5 12.2 %collective-permute-start.24 = (bf16[2,48,896]{2,1,0:T(8,128)(2,1)S(1)}, bf16[2,48,896]{2,1,0:T(8,128)(2,1)S(1)}, u32[]{:S(2)}, u32[]{:S(2)}) collective-permute-start(bf16[2,48,896]{2,1,0:T(8,128)(2,1)S(1)} %pack.1.refs_0_), channel_id=1, source_target_pairs={{0,2},{1,3},{2,0},{3,1},{4,6},{5,7},{6,4},{7,5},{8,10},{9,11},{10,... | collective-permute-start | bytes 516104 | tf_op jit(solution)/shard_map/ppermute | solution.py:109
  123.3 11.4 %collective-permute-start.25 = (bf16[2,48,896]{2,1,0:T(8,128)(2,1)S(1)}, bf16[2,48,896]{2,1,0:T(8,128)(2,1)S(1)}, u32[]{:S(2)}, u32[]{:S(2)}) collective-permute-start(bf16[2,48,896]{2,1,0:T(8,128)(2,1)S(1)} %pack.1.refs_0_), channel_id=1, source_target_pairs={{0,4},{1,5},{2,6},{3,7},{4,0},{5,1},{6,2},{7,3},{8,12},{9,13},{10,... | collective-permute-start | bytes 516104 | tf_op jit(solution)/shard_map/ppermute | solution.py:109
  124.8 9.8 %collective-permute-start.26 = (bf16[2,48,896]{2,1,0:T(8,128)(2,1)S(1)}, bf16[2,48,896]{2,1,0:T(8,128)(2,1)S(1)}, u32[]{:S(2)}, u32[]{:S(2)}) collective-permute-start(bf16[2,48,896]{2,1,0:T(8,128)(2,1)S(1)} %pack.1.refs_0_), channel_id=1, source_target_pairs={{0,6},{1,7},{2,4},{3,5},{4,2},{5,3},{6,0},{7,1},{8,14},{9,15},{10,... | collective-permute-start | bytes 516104 | tf_op jit(solution)/shard_map/ppermute | solution.py:109
  136.2 36.1 %collective-permute-start.23 = (bf16[512,768]{1,0:T(8,128)(2,1)S(1)}, bf16[512,768]{1,0:T(8,128)(2,1)S(1)}, u32[]{:S(2)}, u32[]{:S(2)}) collective-permute-start(bf16[512,768]{1,0:T(8,128)(2,1)S(1)} %get-tuple-element.205), channel_id=1, source_target_pairs={{0,8},{1,9},{2,10},{3,11},{4,12},{5,13},{6,14},{7,15},{8,0},{9,1},... | collective-permute-start | bytes 2359304 | tf_op jit(solution)/shard_map/ppermute | solution.py:109
  150.3 20.1 %collective-permute-start.29 = (bf16[16,192,384]{2,1,0:T(8,128)(2,1)S(1)}, bf16[16,192,384]{2,1,0:T(8,128)(2,1)S(1)}, u32[]{:S(2)}, u32[]{:S(2)}) collective-permute-start(bf16[16,192,384]{2,1,0:T(8,128)(2,1)S(1)} %bitcast.47), channel_id=1, source_target_pairs={{0,1},{1,0},{2,3},{3,2},{4,5},{5,4},{6,7},{7,6},{8,9},{9,8},{10,11... | collective-permute-start | bytes 7077896 | tf_op jit(solution)/shard_map/ppermute | solution.py:109
  169.9 9.0 %collective-permute-start.30 = (bf16[16,48,1536]{2,1,0:T(8,128)(2,1)S(1)}, bf16[16,48,1536]{2,1,0:T(8,128)(2,1)S(1)}, u32[]{:S(2)}, u32[]{:S(2)}) collective-permute-start(bf16[16,48,1536]{2,1,0:T(8,128)(2,1)S(1)} %bitcast.46), channel_id=1, source_target_pairs={{0,1},{1,0},{2,3},{3,2},{4,5},{5,4},{6,7},{7,6},{8,9},{9,8},{10,11... | collective-permute-start | bytes 7077896 | tf_op jit(solution)/shard_map/ppermute | solution.py:109
  171.5 32.8 %collective-permute-start.31 = (bf16[8,192,384]{2,1,0:T(8,128)(2,1)S(1)}, bf16[8,192,384]{2,1,0:T(8,128)(2,1)S(1)}, u32[]{:S(2)}, u32[]{:S(2)}) collective-permute-start(bf16[8,192,384]{2,1,0:T(8,128)(2,1)S(1)} %get-tuple-element.226), channel_id=1, source_target_pairs={{0,2},{1,5},{2,0},{3,7},{4,6},{5,1},{6,4},{7,3},{8,10},{9,13},{10,... | collective-permute-start | bytes 3538952 | tf_op jit(solution)/shard_map/ppermute | solution.py:109
  180.1 26.6 %collective-permute-start.32 = (bf16[8,48,1536]{2,1,0:T(8,128)(2,1)S(1)}, bf16[8,48,1536]{2,1,0:T(8,128)(2,1)S(1)}, u32[]{:S(2)}, u32[]{:S(2)}) collective-permute-start(bf16[8,48,1536]{2,1,0:T(8,128)(2,1)S(1)} %get-tuple-element.234), channel_id=1, source_target_pairs={{0,2},{1,5},{2,0},{3,7},{4,6},{5,1},{6,4},{7,3},{8,10},{9,13},{10,... | collective-permute-start | bytes 3538952 | tf_op jit(solution)/shard_map/ppermute | solution.py:109
  192.1 19.1 %collective-permute-start.33 = (bf16[512,768]{1,0:T(8,128)(2,1)S(1)}, bf16[512,768]{1,0:T(8,128)(2,1)S(1)}, u32[]{:S(2)}, u32[]{:S(2)}) collective-permute-start(bf16[512,768]{1,0:T(8,128)(2,1)S(1)} %get-tuple-element.239), channel_id=1, source_target_pairs={{0,8},{1,9},{2,10},{3,11},{4,12},{5,13},{6,14},{7,15},{8,0},{9,1},... | collective-permute-start | bytes 2359304 | tf_op jit(solution)/shard_map/ppermute | solution.py:109
  204.2 13.4 %collective-permute-start.35 = (bf16[16,48,1152]{2,1,0:T(8,128)(2,1)S(1)}, bf16[16,48,1152]{2,1,0:T(8,128)(2,1)S(1)}, u32[]{:S(2)}, u32[]{:S(2)}) collective-permute-start(bf16[16,48,1152]{2,1,0:T(8,128)(2,1)S(1)} %bitcast.48), channel_id=1, source_target_pairs={{0,1},{1,0},{2,3},{3,2},{4,5},{5,4},{6,7},{7,6},{8,9},{9,8},{10,11... | collective-permute-start | bytes 5308424 | tf_op jit(solution)/shard_map/ppermute | solution.py:109
  205.1 10.4 %collective-permute-start.34 = (bf16[4,192,384]{2,1,0:T(8,128)(2,1)S(1)}, bf16[4,192,384]{2,1,0:T(8,128)(2,1)S(1)}, u32[]{:S(2)}, u32[]{:S(2)}) collective-permute-start(bf16[4,192,384]{2,1,0:T(8,128)(2,1)S(1)} %get-tuple-element.245), channel_id=1, source_target_pairs={{0,4},{1,3},{2,6},{3,1},{4,0},{5,7},{6,2},{7,5},{8,12},{9,11},{10,... | collective-permute-start | bytes 1769480 | tf_op jit(solution)/shard_map/ppermute | solution.py:109
  207.5 14.6 %collective-permute-start.36 = (bf16[4,48,1536]{2,1,0:T(8,128)(2,1)S(1)}, bf16[4,48,1536]{2,1,0:T(8,128)(2,1)S(1)}, u32[]{:S(2)}, u32[]{:S(2)}) collective-permute-start(bf16[4,48,1536]{2,1,0:T(8,128)(2,1)S(1)} %get-tuple-element.248), channel_id=1, source_target_pairs={{0,4},{1,3},{2,6},{3,1},{4,0},{5,7},{6,2},{7,5},{8,12},{9,11},{10,... | collective-permute-start | bytes 1769480 | tf_op jit(solution)/shard_map/ppermute | solution.py:109
  216.1 22.5 %collective-permute-start.39 = (bf16[2,192,384]{2,1,0:T(8,128)(2,1)S(1)}, bf16[2,192,384]{2,1,0:T(8,128)(2,1)S(1)}, u32[]{:S(2)}, u32[]{:S(2)}) collective-permute-start(bf16[2,192,384]{2,1,0:T(8,128)(2,1)S(1)} %get-tuple-element.253), channel_id=1, source_target_pairs={{0,16},{1,17},{2,18},{3,19},{4,20},{5,21},{6,22},{7,23},{8,24},{9,... | collective-permute-start | bytes 884744 | tf_op jit(solution)/shard_map/ppermute | solution.py:109
  218.6 13.8 %collective-permute-start.37 = (bf16[8,48,1152]{2,1,0:T(8,128)(2,1)S(1)}, bf16[8,48,1152]{2,1,0:T(8,128)(2,1)S(1)}, u32[]{:S(2)}, u32[]{:S(2)}) collective-permute-start(bf16[8,48,1152]{2,1,0:T(8,128)(2,1)S(1)} %get-tuple-element.256), channel_id=1, source_target_pairs={{0,2},{1,5},{2,0},{3,7},{4,6},{5,1},{6,4},{7,3},{8,10},{9,13},{10,... | collective-permute-start | bytes 2654216 | tf_op jit(solution)/shard_map/ppermute | solution.py:109
  222.7 21.6 %collective-permute-start.40 = (bf16[2,48,1536]{2,1,0:T(8,128)(2,1)S(1)}, bf16[2,48,1536]{2,1,0:T(8,128)(2,1)S(1)}, u32[]{:S(2)}, u32[]{:S(2)}) collective-permute-start(bf16[2,48,1536]{2,1,0:T(8,128)(2,1)S(1)} %get-tuple-element.259), channel_id=1, source_target_pairs={{0,16},{1,17},{2,18},{3,19},{4,20},{5,21},{6,22},{7,23},{8,24},{9,... | collective-permute-start | bytes 884744 | tf_op jit(solution)/shard_map/ppermute | solution.py:109
  227.8 6.9 %collective-permute-start.38 = (bf16[16,48,512]{2,1,0:T(8,128)(2,1)S(1)}, bf16[16,48,512]{2,1,0:T(8,128)(2,1)S(1)}, u32[]{:S(2)}, u32[]{:S(2)}) collective-permute-start(bf16[16,48,512]{2,1,0:T(8,128)(2,1)S(1)} %bitcast.49), channel_id=1, source_target_pairs={{0,1},{1,0},{2,3},{3,2},{4,5},{5,4},{6,7},{7,6},{8,9},{9,8},{10,11... | collective-permute-start | bytes 2359304 | tf_op jit(solution)/shard_map/ppermute | solution.py:109
  233.1 12.3 %collective-permute-start.41 = (bf16[4,48,1152]{2,1,0:T(8,128)(2,1)S(1)}, bf16[4,48,1152]{2,1,0:T(8,128)(2,1)S(1)}, u32[]{:S(2)}, u32[]{:S(2)}) collective-permute-start(bf16[4,48,1152]{2,1,0:T(8,128)(2,1)S(1)} %get-tuple-element.266), channel_id=1, source_target_pairs={{0,4},{1,3},{2,6},{3,1},{4,0},{5,7},{6,2},{7,5},{8,12},{9,11},{10,... | collective-permute-start | bytes 1327112 | tf_op jit(solution)/shard_map/ppermute | solution.py:109
  235.4 13.0 %collective-permute-start.42 = (bf16[8,48,512]{2,1,0:T(8,128)(2,1)S(1)}, bf16[8,48,512]{2,1,0:T(8,128)(2,1)S(1)}, u32[]{:S(2)}, u32[]{:S(2)}) collective-permute-start(bf16[8,48,512]{2,1,0:T(8,128)(2,1)S(1)} %get-tuple-element.269), channel_id=1, source_target_pairs={{0,2},{1,5},{2,0},{3,7},{4,6},{5,1},{6,4},{7,3},{8,10},{9,13},{10,... | collective-permute-start | bytes 1179656 | tf_op jit(solution)/shard_map/ppermute | solution.py:109
  239.3 11.9 %collective-permute-start.43 = (bf16[1,192,384]{2,1,0:T(8,128)(2,1)S(1)}, bf16[1,192,384]{2,1,0:T(8,128)(2,1)S(1)}, u32[]{:S(2)}, u32[]{:S(2)}) collective-permute-start(bf16[1,192,384]{2,1,0:T(8,128)(2,1)S(1)} %get-tuple-element.272), channel_id=1, source_target_pairs={{0,8},{1,9},{2,10},{3,11},{4,12},{5,13},{6,14},{7,15},{8,0},{9,1},... | collective-permute-start | bytes 442376 | tf_op jit(solution)/shard_map/ppermute | solution.py:109
  244.9 8.8 %collective-permute-start.44 = (bf16[1,48,1536]{2,1,0:T(8,128)(2,1)S(1)}, bf16[1,48,1536]{2,1,0:T(8,128)(2,1)S(1)}, u32[]{:S(2)}, u32[]{:S(2)}) collective-permute-start(bf16[1,48,1536]{2,1,0:T(8,128)(2,1)S(1)} %get-tuple-element.275), channel_id=1, source_target_pairs={{0,8},{1,9},{2,10},{3,11},{4,12},{5,13},{6,14},{7,15},{8,0},{9,1},... | collective-permute-start | bytes 442376 | tf_op jit(solution)/shard_map/ppermute | solution.py:109
  246.0 12.0 %collective-permute-start.46 = (bf16[2,48,1152]{2,1,0:T(8,128)(2,1)S(1)}, bf16[2,48,1152]{2,1,0:T(8,128)(2,1)S(1)}, u32[]{:S(2)}, u32[]{:S(2)}) collective-permute-start(bf16[2,48,1152]{2,1,0:T(8,128)(2,1)S(1)} %get-tuple-element.278), channel_id=1, source_target_pairs={{0,16},{1,17},{2,18},{3,19},{4,20},{5,21},{6,22},{7,23},{8,24},{9,... | collective-permute-start | bytes 663560 | tf_op jit(solution)/shard_map/ppermute | solution.py:109
  251.8 7.7 %collective-permute-start.47 = (bf16[2,192,384]{2,1,0:T(8,128)(2,1)S(1)}, bf16[2,192,384]{2,1,0:T(8,128)(2,1)S(1)}, u32[]{:S(2)}, u32[]{:S(2)}) collective-permute-start(bf16[2,192,384]{2,1,0:T(8,128)(2,1)S(1)} %add_last.4.refs_0_), channel_id=1, source_target_pairs={{0,1},{1,0},{2,3},{3,2},{4,5},{5,4},{6,7},{7,6},{8,9},{9,8},{10,11... | collective-permute-start | bytes 884744 | tf_op jit(solution)/shard_map/ppermute | solution.py:109
  256.4 7.4 %collective-permute-start.49 = (bf16[2,48,512]{2,1,0:T(8,128)(2,1)S(1)}, bf16[2,48,512]{2,1,0:T(8,128)(2,1)S(1)}, u32[]{:S(2)}, u32[]{:S(2)}) collective-permute-start(bf16[2,48,512]{2,1,0:T(8,128)(2,1)S(1)} %get-tuple-element.286), channel_id=1, source_target_pairs={{0,16},{1,17},{2,18},{3,19},{4,20},{5,21},{6,22},{7,23},{8,24},{9,... | collective-permute-start | bytes 294920 | tf_op jit(solution)/shard_map/ppermute | solution.py:109
  258.6 8.0 %collective-permute-start.50 = (bf16[1,48,1152]{2,1,0:T(8,128)(2,1)S(1)}, bf16[1,48,1152]{2,1,0:T(8,128)(2,1)S(1)}, u32[]{:S(2)}, u32[]{:S(2)}) collective-permute-start(bf16[1,48,1152]{2,1,0:T(8,128)(2,1)S(1)} %get-tuple-element.289), channel_id=1, source_target_pairs={{0,8},{1,9},{2,10},{3,11},{4,12},{5,13},{6,14},{7,15},{8,0},{9,1},... | collective-permute-start | bytes 331784 | tf_op jit(solution)/shard_map/ppermute | solution.py:109
  (32 other events, 203.8 us)
